TPU v7x, 32 devices: a whole 2x2x4 slice. The times are simulated.
32 devices in a mesh: aux: 8 (over y, x, core), orb: 4 (over z).
Axes of the slice: x: 2, y: 2, z: 4, core: 2. Of those that a mesh axis runs over, the one named last changes fastest.
Arguments:
- density: bfloat16 [256, 256], P('orb'), may hold values from -6 to 6
- tensor_blocks: bfloat16 [4, 8, 3, 4, 4096], P('orb', 'aux'), may hold values from -0.4375 to 0.4375
- pairs: int32 [4, 8, 3], P('orb', 'aux'), may hold values from 0 to 3, as said below
- kept: int32 [4, 8], P('orb', 'aux'), may hold values from 1 to 3, as said below
Outputs:
- exchange_matrix: float32 [256, 256], P('orb')
Inputs may be any that keep to these rules, and one draw needn't show every extreme that they name: `pairs`: within one row atom block and one auxiliary block all 3 slots name different column blocks. `kept`: every auxiliary block has a row atom block whose slots are all used.
All inputs are finite; a program needn't handle non-finite values.
Results may differ from a plain program's by a relative error of at most 0.0032.
Values may be sent and summed in bfloat16 or wider, within the bound.
No kernel may reach another device: no remote copies, remote signals or barrier semaphores. Data moves between devices by JAX's collectives and lax.ppermute only.
A program may use at most 64 MiB of HBM per device.

v0:
```python
import jax
import jax.numpy as jnp
from jax import lax
from jax.sharding import PartitionSpec as P

BS = 64


def shards(density, tensor_blocks, pairs, kept):
    width = BS
    full_width = density.shape[1]
    blocks_count = full_width // width
    slots = tensor_blocks.shape[2]
    aux_width = tensor_blocks.shape[3]
    slot_index = jnp.arange(slots, dtype=jnp.int32)
    active = slot_index[None, None, :] < kept[:, :, None]
    masked = jnp.where(active[:, :, :, None, None], tensor_blocks, jnp.zeros_like(tensor_blocks))
    own_blocks = masked.reshape(slots, aux_width, width, width)
    own_pairs = pairs.reshape(slots)
    rows = lax.all_gather(density, "orb", axis=0, tiled=True)
    selected = rows.reshape(blocks_count, width, full_width)[own_pairs]
    half = jnp.einsum(
        "jpal,jlc->pac", own_blocks, selected, preferred_element_type=jnp.float32
    ).astype(jnp.bfloat16)
    half_four = half.reshape(aux_width, width, blocks_count, width)
    peer_blocks = lax.all_gather(masked, "orb", axis=0, tiled=True)
    peer_pairs = lax.all_gather(pairs, "orb", axis=0, tiled=True)
    count = peer_blocks.shape[0]
    blocks = peer_blocks.reshape(count, slots, aux_width, width, width)
    picked = jnp.take(half_four, peer_pairs.reshape(count * slots), axis=2)
    picked = picked.reshape(aux_width, width, count, slots, width)
    parts = jnp.einsum("pakjs,kjpbs->akb", picked, blocks, preferred_element_type=jnp.float32)
    summed = lax.psum(parts, "aux")
    return summed.reshape(width, full_width)


def solution(mesh):
    return jax.shard_map(
        shards,
        mesh=mesh,
        in_specs=(
            P("orb", None),
            P("orb", "aux", None, None, None),
            P("orb", "aux", None),
            P("orb", "aux"),
        ),
        out_specs=P("orb", None),
        check_vma=False,
    )
```

profile of v0, /device:TPU:0, one launch (start us, length us, event | category | flops | bytes accessed | tf_op | source)
XLA Modules:
  0.0 113.7 jit_solution(615808598978007925)
XLA Ops:
  6.5 0.0 copy-start.1
  6.5 0.0 all-reduce.2.cloned.1.call-start
  6.5 0.7 fusion.5
  7.3 0.0 copy-done.1
  7.3 12.5 %all_gather.10 = s32[4,1,3]{2,1,0:T(1,128)S(1)} all-gather(s32[1,1,3]{2,1,0:T(1,128)S(1)} %copy-done.1), channel_id=1, replica_groups=mesh['aux'=8,'orb'=4] {'orb'}, dimensions={0}, use_global_device_ids=true | all-gather | bytes 60 | tf_op jit(solution)/shard_map/all_gather | solution.py:27
  20.5 1.0 broadcast_select_fusion
  21.5 0.2 reshape.102
  21.7 0.0 copy-start
  21.7 14.4 %all_gather.9 = bf16[4,1,3,4,4096]{4,3,2,1,0:T(4,128)(2,1)S(1)} all-gather(bf16[1,1,3,4,4096]{4,3,2,1,0:T(4,128)(2,1)S(1)} %broadcast_select_fusion), channel_id=1, replica_groups=mesh['aux'=8,'orb'=4] {'orb'}, dimensions={0}, use_global_device_ids=true | all-gather | bytes 491520 | tf_op jit(solution)/shard_map/all_gather | solution.py:26
  36.1 0.1 copy.12
  36.2 0.5 broadcast.81
  36.7 0.7 reduce.3
  37.4 0.1 reshape.106
  37.5 0.0 copy-done
  37.5 13.3 %all_gather.11 = bf16[256,256]{1,0:T(8,128)(2,1)S(1)} all-gather(bf16[64,256]{1,0:T(8,128)(2,1)S(1)} %copy-done), channel_id=1, replica_groups=mesh['aux'=8,'orb'=4] {'orb'}, dimensions={0}, use_global_device_ids=true | all-gather | bytes 163840 | tf_op jit(solution)/shard_map/all_gather | solution.py:20
  50.9 0.6 gather_fusion
  51.4 0.2 fusion
  51.7 0.2 reshape.105
  51.8 0.1 copy.13
  51.9 0.2 copy.11
  52.1 0.6 reshape.100
  52.7 0.7 gather_fusion.1
  53.4 0.4 fusion.1
  53.8 0.7 copy.15
  54.5 0.0 all-reduce.2.cloned.1.call-update
  54.6 50.9 %all-reduce.2.cloned.1.call-done = f32[64,256]{1,0:T(8,128)} async-done(((f32[64,256]{1,0:T(8,128)}), f32[64,256]{1,0:T(8,128)}) %all-reduce.2.cloned.1.call-update) | async-done | bytes 65552 | tf_op jit(solution)/shard_map/psum | solution.py:33
  105.4 1.5 %copy.22 = f32[64,256]{1,0:T(8,128)} copy(f32[64,256]{1,0:T(8,128)} %all-reduce.2.cloned.1.call-done) | data formatting | bytes 131072
  (5 shorter events, 0.0 us)
Async XLA Ops:
  6.5 0.7 copy-start.1
  6.5 98.9 %all-reduce.2.cloned.1.call-start = ((), (), s32[]{:S(2)}) async-start(), calls=%async_computation | async-start | bytes 131072 | tf_op jit(solution)/shard_map/psum | solution.py:33
  21.7 15.8 %copy-start = (bf16[64,256]{1,0:T(8,128)(2,1)S(1)}, bf16[64,256]{1,0:T(8,128)(2,1)}, u32[]{:S(2)}) copy-start(bf16[64,256]{1,0:T(8,128)(2,1)} %param.4) | copy-start | bytes 98308
Sparse Core Ops, SparseCore 0:
  54.7 50.6 all-reduce.1
where the time goes:
time: 114 us
  waiting for transfers between devices  50.9 us (45%)
  blocking collectives  40.3 us (35%)
  between operations  14.1 us (12%)
  local copies, waits for them, and re-layouts  5.34 us (5%)
  other arithmetic  2.43 us (2%)
    psum x1, waiting for transfers between devices, shards(): summed = lax.psum(parts, 'aux')  50.9 us
    all_gather x1, blocking collectives, shards(): peer_blocks = lax.all_gather(masked, 'orb', axis=0, tiled=True)  14.4 us
    all_gather x1, blocking collectives, shards(): rows = lax.all_gather(density, 'orb', axis=0, tiled=True)  13.3 us
    all_gather x1, blocking collectives, shards(): peer_pairs = lax.all_gather(pairs, 'orb', axis=0, tiled=True)  12.5 us
  transfers between devices with their start and end apart: 1, of which 1 were waited for; matrix products, arithmetic and copies ran while one was open for 0% of the time, Pallas kernels for 0%

commit v1 on v0

v1 whole, which is shorter than its diff:
```python
import jax
import jax.numpy as jnp
from jax import lax
from jax.sharding import PartitionSpec as P

BS = 64


def shards(density, tensor_blocks, pairs, kept):
    width = BS
    full_width = density.shape[1]
    blocks_count = full_width // width
    slots = tensor_blocks.shape[2]
    aux_width = tensor_blocks.shape[3]
    orb = lax.axis_size("orb")
    aux = lax.axis_size("aux")
    me = lax.axis_index("orb")
    slot_index = jnp.arange(slots, dtype=jnp.int32)
    active = slot_index < kept[0, 0]
    masked = jnp.where(active[:, None, None], tensor_blocks[0, 0], 0)
    own = masked.reshape(slots, aux_width, width, width)
    flat = own.transpose(2, 0, 1, 3).reshape(width, slots * aux_width * width)
    own_pairs = pairs.reshape(slots)

    rows, peers, peer_pairs = [density], [flat], [own_pairs]
    for shift in range(1, orb):
        perm = [(i, (i + shift) % orb) for i in range(orb)]
        rows.append(lax.ppermute(density, "orb", perm))
        peers.append(lax.ppermute(flat, "orb", perm))
        peer_pairs.append(lax.ppermute(own_pairs, "orb", perm))

    stacked = jnp.stack(rows)
    selected = stacked[(me - own_pairs) % orb]
    half = jnp.einsum(
        "jpal,jlc->pac", own, selected, preferred_element_type=jnp.float32
    ).astype(jnp.bfloat16)
    half_four = half.reshape(aux_width, width, blocks_count, width)
    columns = []
    for shift in range(orb):
        picked = jnp.take(half_four, peer_pairs[shift], axis=2, mode="clip")
        picked = picked.transpose(1, 2, 0, 3).reshape(width, -1)
        columns.append(
            lax.dot_general(
                picked, peers[shift], (((1,), (1,)), ((), ())), preferred_element_type=jnp.float32
            )
        )
    order = (me - jnp.arange(orb)) % orb
    parts = jnp.stack(columns)[order].transpose(1, 0, 2).reshape(width, full_width)
    step = 1
    while step < aux:
        parts = parts + lax.ppermute(parts, "aux", [(i, i ^ step) for i in range(aux)])
        step *= 2
    return parts


def solution(mesh):
    return jax.shard_map(
        shards,
        mesh=mesh,
        in_specs=(
            P("orb", None),
            P("orb", "aux", None, None, None),
            P("orb", "aux", None),
            P("orb", "aux"),
        ),
        out_specs=P("orb", None),
        check_vma=False,
    )
```

time: 114 us -> 35.6 us (0.31)
  waiting for transfers between devices: 50.9 us -> 7.95 us
  blocking collectives: 40.3 us -> 0 us
  starting transfers between devices: 0.01 us -> 18.4 us
  between operations: 14.1 us -> 0.96 us
  other arithmetic: 2.43 us -> 1.12 us
    psum x1 -> x0, waiting for transfers between devices: 50.9 us -> none  [shards(): summed = lax.psum(parts, 'aux')]
    all_gather x3 -> x0, blocking collectives: 40.3 us -> none  [the longest x1 14.4 us: shards(): peer_blocks = lax.all_gather(masked, 'orb', axis=0, tiled=True)]
    ppermute x0 -> x12, starting transfers between devices: none -> 18.4 us  [the longest x3 6.96 us: shards(): rows.append(lax.ppermute(density, 'orb', perm))]
    ppermute x0 -> x12, waiting for transfers between devices: none -> 7.95 us  [the longest x3 6.43 us: shards(): lax.ppermute(parts, 'aux', [(i, i ^ step) for i in range(aux)])]
    gather x2 -> x6, local copies, waits for them, and re-layouts: 1.25 us -> 3.45 us  [the longest x4 2.34 us: shards(): picked = jnp.take(half_four, peer_pairs[shift], axis=2, mode='clip')]
    select_n x3, other arithmetic: 1.74 us -> 0.2 us  [the longest x1 0.18 us: shards(): masked = jnp.where(active[:, None, None], tensor_blocks[0, 0], 0)]
    unnamed x5 -> x4, local copies, waits for them, and re-layouts: 1.48 us -> 0.01 us
  transfers between devices with their start and end apart: 1 -> 12, of which waited for: 1 -> 5; matrix products, arithmetic and copies ran while one was open for 0% -> 18% of each run, Pallas kernels for 0% -> 0%
where the time goes in v1:
time: 35.6 us; the launch traced here: 35.5 us
  starting transfers between devices  18.4 us (52%)
  waiting for transfers between devices  7.95 us (22%)
  local copies, waits for them, and re-layouts  6.13 us (17%)
  other arithmetic  1.12 us (3%)
  between operations  0.96 us (3%)
  matrix products  0.88 us (2%)
    ppermute x3, starting transfers between devices, shards(): rows.append(lax.ppermute(density, 'orb', perm))  6.96 us
    ppermute x3, waiting for transfers between devices, shards(): lax.ppermute(parts, 'aux', [(i, i ^ step) for i in range(aux)])  6.43 us
    ppermute x3, starting transfers between devices, shards(): peers.append(lax.ppermute(flat, 'orb', perm))  4.91 us
    ppermute x3, starting transfers between devices, shards(): lax.ppermute(parts, 'aux', [(i, i ^ step) for i in range(aux)])  3.53 us
    ppermute x3, starting transfers between devices, shards(): peer_pairs.append(lax.ppermute(own_pairs, 'orb', perm))  3.04 us
    gather x4, local copies, waits for them, and re-layouts, shards(): picked = jnp.take(half_four, peer_pairs[shift], axis=2, mode='clip')  2.34 us
    ppermute x3, waiting for transfers between devices, shards(): peer_pairs.append(lax.ppermute(own_pairs, 'orb', perm))  1.5 us
    squeeze x1, local copies, waits for them, and re-layouts, shards(): masked = jnp.where(active[:, None, None], tensor_blocks[0, 0], 0)  1.1 us
  transfers between devices with their start and end apart: 12, of which 5 were waited for; matrix products, arithmetic and copies ran while one was open for 18% of the time, Pallas kernels for 0%

profile of v1, /device:TPU:0, one launch (start us, length us, event | category | flops | bytes accessed | tf_op | source)
XLA Modules:
  0.0 35.5 jit_solution(7154829087524635812)
XLA Ops:
  0.0 0.0 copy-start.1
  0.0 3.0 %collective-permute-start = (bf16[64,256]{1,0:T(8,128)(2,1)}, bf16[64,256]{1,0:T(8,128)(2,1)S(1)}, u32[]{:S(2)}, u32[]{:S(2)}) collective-permute-start(bf16[64,256]{1,0:T(8,128)(2,1)} %param.4), channel_id=1, source_target_pairs={{0,1},{1,2},{2,3},{3,0},{4,5},{5,6},{6,7},{7,4},{8,9},{9,10},{10,1... | collective-permute-start | bytes 98312 | tf_op jit(solution)/shard_map/ppermute | solution.py:28
  3.0 2.6 %collective-permute-start.1 = (bf16[64,256]{1,0:T(8,128)(2,1)}, bf16[64,256]{1,0:T(8,128)(2,1)S(1)}, u32[]{:S(2)}, u32[]{:S(2)}) collective-permute-start(bf16[64,256]{1,0:T(8,128)(2,1)} %param.4), channel_id=1, source_target_pairs={{0,2},{1,3},{2,0},{3,1},{4,6},{5,7},{6,4},{7,5},{8,10},{9,11},{10,... | collective-permute-start | bytes 98312 | tf_op jit(solution)/shard_map/ppermute | solution.py:28
  5.6 1.3 %collective-permute-start.2 = (bf16[64,256]{1,0:T(8,128)(2,1)}, bf16[64,256]{1,0:T(8,128)(2,1)S(1)}, u32[]{:S(2)}, u32[]{:S(2)}) collective-permute-start(bf16[64,256]{1,0:T(8,128)(2,1)} %param.4), channel_id=1, source_target_pairs={{0,3},{1,0},{2,1},{3,2},{4,7},{5,4},{6,5},{7,6},{8,11},{9,8},{10,9... | collective-permute-start | bytes 98312 | tf_op jit(solution)/shard_map/ppermute | solution.py:28
  7.0 0.0 copy-done.1
  7.0 0.2 collective-permute-start.5
  7.1 0.8 %collective-permute-start.3 = (s32[3]{0:T(128)S(1)}, s32[3]{0:T(128)S(1)}, u32[]{:S(2)}, u32[]{:S(2)}) collective-permute-start(s32[3]{0:T(128)S(1)} %bitcast.57), channel_id=1, source_target_pairs={{0,1},{1,2},{2,3},{3,0},{4,5},{5,6},{6,7},{7,4},{8,9},{9,10},{10,1... | collective-permute-start | bytes 44 | tf_op jit(solution)/shard_map/ppermute | solution.py:30
  8.0 1.1 %squeeze.7 = bf16[3,4,64,64]{3,2,1,0:T(8,128)(2,1)S(1)} reshape(bf16[1,1,3,4,4096]{4,3,2,1,0:T(4,128)(2,1)} %param.5) | data formatting | bytes 196608 | tf_op jit(solution)/shard_map/squeeze | solution.py:20
  9.8 0.2 copy_select_fusion
  9.9 0.2 fusion.15
  10.2 0.0 copy-start
  10.2 0.2 reshape.136
  10.4 1.0 %collective-permute-done.5 = s32[3]{0:T(128)S(1)} collective-permute-done((s32[3]{0:T(128)S(1)}, s32[3]{0:T(128)S(1)}, u32[]{:S(2)}, u32[]{:S(2)}) %collective-permute-start.5) | collective-permute-done | bytes 44 | tf_op jit(solution)/shard_map/ppermute | solution.py:30
  11.4 2.0 %collective-permute-start.7 = (s32[3]{0:T(128)S(1)}, s32[3]{0:T(128)S(1)}, u32[]{:S(2)}, u32[]{:S(2)}) collective-permute-start(s32[3]{0:T(128)S(1)} %bitcast.59), channel_id=1, source_target_pairs={{0,3},{1,0},{2,1},{3,2},{4,7},{5,4},{6,5},{7,6},{8,11},{9,8},{10,9... | collective-permute-start | bytes 44 | tf_op jit(solution)/shard_map/ppermute | solution.py:30
  13.4 0.0 collective-permute-done.3
  13.4 1.0 %collective-permute-start.6 = (bf16[64,768]{1,0:T(8,128)(2,1)S(1)}, bf16[64,768]{1,0:T(8,128)(2,1)S(1)}, u32[]{:S(2)}, u32[]{:S(2)}) collective-permute-start(bf16[64,768]{1,0:T(8,128)(2,1)S(1)} %reshape.136), channel_id=1, source_target_pairs={{0,2},{1,3},{2,0},{3,1},{4,6},{5,7},{6,4},{7,5},{8,10},{9,11},{10,... | collective-permute-start | bytes 294920 | tf_op jit(solution)/shard_map/ppermute | solution.py:29
  14.5 0.5 %collective-permute-done.7 = s32[3]{0:T(128)S(1)} collective-permute-done((s32[3]{0:T(128)S(1)}, s32[3]{0:T(128)S(1)}, u32[]{:S(2)}, u32[]{:S(2)}) %collective-permute-start.7) | collective-permute-done | bytes 44 | tf_op jit(solution)/shard_map/ppermute | solution.py:30
  14.9 1.5 %collective-permute-start.4 = (bf16[64,768]{1,0:T(8,128)(2,1)S(1)}, bf16[64,768]{1,0:T(8,128)(2,1)S(1)}, u32[]{:S(2)}, u32[]{:S(2)}) collective-permute-start(bf16[64,768]{1,0:T(8,128)(2,1)S(1)} %reshape.136), channel_id=1, source_target_pairs={{0,1},{1,2},{2,3},{3,0},{4,5},{5,6},{6,7},{7,4},{8,9},{9,10},{10,1... | collective-permute-start | bytes 294920 | tf_op jit(solution)/shard_map/ppermute | solution.py:29
  16.5 0.0 collective-permute-done
  16.5 2.4 %collective-permute-start.8 = (bf16[64,768]{1,0:T(8,128)(2,1)S(1)}, bf16[64,768]{1,0:T(8,128)(2,1)S(1)}, u32[]{:S(2)}, u32[]{:S(2)}) collective-permute-start(bf16[64,768]{1,0:T(8,128)(2,1)S(1)} %reshape.136), channel_id=1, source_target_pairs={{0,3},{1,0},{2,1},{3,2},{4,7},{5,4},{6,5},{7,6},{8,11},{9,8},{10,9... | collective-permute-start | bytes 294920 | tf_op jit(solution)/shard_map/ppermute | solution.py:29
  18.9 0.0 collective-permute-done.1
  18.9 0.0 collective-permute-done.2
  18.9 0.0 copy-done
  18.9 0.6 %gather_fusion = bf16[3,64,256]{2,1,0:T(8,128)(2,1)S(1)} fusion(bf16[4,64,256]{2,1,0:T(8,128)(2,1)S(1)} %pad_maximum_fusion, s32[1024]{0:T(1024)S(1)} %pad_clamp_fusion.5), kind=kCustom, calls=%fused_computation | custom fusion | bytes 196620 | tf_op jit(solution)/shard_map/gather | solution.py:33
  19.5 0.2 fusion
  19.7 0.2 reshape.133
  19.9 0.1 copy.8
  19.9 0.6 %gather_fusion.3 = bf16[3,4,64,64]{3,2,1,0:T(8,128)(2,1)S(1)} fusion(bf16[4,64,4,64]{3,1,2,0:T(8,128)(2,1)S(1)} %copy.8, s32[1024]{0:T(1024)S(1)} %pad_clamp_fusion.2), kind=kCustom, calls=%fused_computation.3 | custom fusion | bytes 196620 | tf_op jit(solution)/shard_map/jit(_take)/gather | solution.py:40
  20.5 0.2 copy.13
  20.7 0.2 reshape.137
  20.8 0.6 %gather_fusion.2 = bf16[3,4,64,64]{3,2,1,0:T(8,128)(2,1)S(1)} fusion(bf16[4,64,4,64]{3,1,2,0:T(8,128)(2,1)S(1)} %copy.8, s32[1024]{0:T(1024)S(1)} %pad_clamp_fusion.3), kind=kCustom, calls=%fused_computation.2 | custom fusion | bytes 196620 | tf_op jit(solution)/shard_map/jit(_take)/gather | solution.py:40
  21.4 0.2 copy.11
  21.6 0.2 reshape.135
  21.8 0.6 %gather_fusion.4 = bf16[3,4,64,64]{3,2,1,0:T(8,128)(2,1)S(1)} fusion(bf16[4,64,4,64]{3,1,2,0:T(8,128)(2,1)S(1)} %copy.8, s32[1024]{0:T(1024)S(1)} %pad_clamp_fusion.1), kind=kCustom, calls=%fused_computation.4 | custom fusion | bytes 196620 | tf_op jit(solution)/shard_map/jit(_take)/gather | solution.py:40
  22.4 0.2 copy.15
  22.5 0.2 reshape.138
  22.7 0.6 %gather_fusion.1 = bf16[3,4,64,64]{3,2,1,0:T(8,128)(2,1)S(1)} fusion(bf16[4,64,4,64]{3,1,2,0:T(8,128)(2,1)S(1)} %copy.8, s32[1024]{0:T(1024)S(1)} %pad_clamp_fusion.4), kind=kCustom, calls=%fused_computation.1 | custom fusion | bytes 196620 | tf_op jit(solution)/shard_map/jit(_take)/gather | solution.py:40
  23.3 0.2 convolution_bitcast_fusion.4
  23.5 0.0 collective-permute-done.6
  23.5 0.2 convolution_bitcast_fusion.2
  23.7 0.0 collective-permute-done.4
  23.7 0.2 convolution_bitcast_fusion.3
  23.8 0.0 collective-permute-done.8
  23.9 0.1 convolution_bitcast_fusion.1
  24.0 0.6 %gather_fusion.5 = f32[4,64,64]{2,1,0:T(8,128)S(1)} fusion(f32[4,64,64]{2,1,0:T(8,128)S(1)} %pad_maximum_fusion.1, s32[1024]{0:T(1024)S(1)} %pad_clamp_fusion), kind=kCustom, calls=%fused_computation.5 | custom fusion | bytes 131088 | tf_op jit(solution)/shard_map/gather | solution.py:48
  24.6 0.1 copy.16
  24.7 0.1 reshape.139
  24.8 0.1 collective-permute-start.9
  24.9 1.2 %collective-permute-done.9 = f32[64,256]{1,0:T(8,128)S(1)} collective-permute-done((f32[64,256]{1,0:T(8,128)S(1)}, f32[64,256]{1,0:T(8,128)S(1)}, u32[]{:S(2)}, u32[]{:S(2)}) %collective-permute-start.9) | collective-permute-done | bytes 65568 | tf_op jit(solution)/shard_map/ppermute | solution.py:51
  26.2 1.7 %collective-permute-start.10 = (f32[64,256]{1,0:T(8,128)S(1)}, f32[64,256]{1,0:T(8,128)S(1)}, u32[]{:S(2)}, u32[]{:S(2)}) collective-permute-start(f32[64,256]{1,0:T(8,128)S(1)} %add.59), channel_id=1, source_target_pairs={{0,8},{4,12},{8,0},{12,4},{16,24},{20,28},{24,16},{28,20},{1,9},{5... | collective-permute-start | bytes 196616 | tf_op jit(solution)/shard_map/ppermute | solution.py:51
  27.9 2.6 %collective-permute-done.10 = f32[64,256]{1,0:T(8,128)S(1)} collective-permute-done((f32[64,256]{1,0:T(8,128)S(1)}, f32[64,256]{1,0:T(8,128)S(1)}, u32[]{:S(2)}, u32[]{:S(2)}) %collective-permute-start.10) | collective-permute-done | bytes 65568 | tf_op jit(solution)/shard_map/ppermute | solution.py:51
  30.5 1.8 %collective-permute-start.11 = (f32[64,256]{1,0:T(8,128)S(1)}, f32[64,256]{1,0:T(8,128)S(1)}, u32[]{:S(2)}, u32[]{:S(2)}) collective-permute-start(f32[64,256]{1,0:T(8,128)S(1)} %add.60), channel_id=1, source_target_pairs={{0,16},{4,20},{8,24},{12,28},{16,0},{20,4},{24,8},{28,12},{1,17},{... | collective-permute-start | bytes 196616 | tf_op jit(solution)/shard_map/ppermute | solution.py:51
  32.3 2.6 %collective-permute-done.11 = f32[64,256]{1,0:T(8,128)S(1)} collective-permute-done((f32[64,256]{1,0:T(8,128)S(1)}, f32[64,256]{1,0:T(8,128)S(1)}, u32[]{:S(2)}, u32[]{:S(2)}) %collective-permute-start.11) | collective-permute-done | bytes 65568 | tf_op jit(solution)/shard_map/ppermute | solution.py:51
  34.8 0.6 %add.61 = f32[64,256]{1,0:T(8,128)} add(f32[64,256]{1,0:T(8,128)S(1)} %add.60, f32[64,256]{1,0:T(8,128)S(1)} %collective-permute-done.11) | non-fusion elementwise | flops 16384 | bytes 196608 | tf_op jit(solution)/shard_map/add | solution.py:51
  (13 shorter events, 0.1 us)
Async XLA Ops:
  0.0 7.0 %copy-start.1 = (s32[1,1,3]{2,1,0:T(1,128)S(1)}, s32[1,1,3]{2,1,0:T(1,128)}, u32[]{:S(2)}) copy-start(s32[1,1,3]{2,1,0:T(1,128)} %param.6) | copy-start | bytes 40
  0.0 16.5 %collective-permute-start = (bf16[64,256]{1,0:T(8,128)(2,1)}, bf16[64,256]{1,0:T(8,128)(2,1)S(1)}, u32[]{:S(2)}, u32[]{:S(2)}) collective-permute-start(bf16[64,256]{1,0:T(8,128)(2,1)} %param.4), channel_id=1, source_target_pairs={{0,1},{1,2},{2,3},{3,0},{4,5},{5,6},{6,7},{7,4},{8,9},{9,10},{10,1... | collective-permute-start | bytes 98312 | tf_op jit(solution)/shard_map/ppermute | solution.py:28
  3.0 15.8 %collective-permute-start.1 = (bf16[64,256]{1,0:T(8,128)(2,1)}, bf16[64,256]{1,0:T(8,128)(2,1)S(1)}, u32[]{:S(2)}, u32[]{:S(2)}) collective-permute-start(bf16[64,256]{1,0:T(8,128)(2,1)} %param.4), channel_id=1, source_target_pairs={{0,2},{1,3},{2,0},{3,1},{4,6},{5,7},{6,4},{7,5},{8,10},{9,11},{10,... | collective-permute-start | bytes 98312 | tf_op jit(solution)/shard_map/ppermute | solution.py:28
  5.6 13.2 %collective-permute-start.2 = (bf16[64,256]{1,0:T(8,128)(2,1)}, bf16[64,256]{1,0:T(8,128)(2,1)S(1)}, u32[]{:S(2)}, u32[]{:S(2)}) collective-permute-start(bf16[64,256]{1,0:T(8,128)(2,1)} %param.4), channel_id=1, source_target_pairs={{0,3},{1,0},{2,1},{3,2},{4,7},{5,4},{6,5},{7,6},{8,11},{9,8},{10,9... | collective-permute-start | bytes 98312 | tf_op jit(solution)/shard_map/ppermute | solution.py:28
  7.0 4.4 %collective-permute-start.5 = (s32[3]{0:T(128)S(1)}, s32[3]{0:T(128)S(1)}, u32[]{:S(2)}, u32[]{:S(2)}) collective-permute-start(s32[3]{0:T(128)S(1)} %bitcast.56), channel_id=1, source_target_pairs={{0,2},{1,3},{2,0},{3,1},{4,6},{5,7},{6,4},{7,5},{8,10},{9,11},{10,... | collective-permute-start | bytes 44 | tf_op jit(solution)/shard_map/ppermute | solution.py:30
  7.1 6.3 %collective-permute-start.3 = (s32[3]{0:T(128)S(1)}, s32[3]{0:T(128)S(1)}, u32[]{:S(2)}, u32[]{:S(2)}) collective-permute-start(s32[3]{0:T(128)S(1)} %bitcast.57), channel_id=1, source_target_pairs={{0,1},{1,2},{2,3},{3,0},{4,5},{5,6},{6,7},{7,4},{8,9},{9,10},{10,1... | collective-permute-start | bytes 44 | tf_op jit(solution)/shard_map/ppermute | solution.py:30
  10.2 8.7 %copy-start = (bf16[64,256]{1,0:T(8,128)(2,1)S(1)}, bf16[64,256]{1,0:T(8,128)(2,1)}, u32[]{:S(2)}) copy-start(bf16[64,256]{1,0:T(8,128)(2,1)} %param.4) | copy-start | bytes 98308
  11.4 3.5 %collective-permute-start.7 = (s32[3]{0:T(128)S(1)}, s32[3]{0:T(128)S(1)}, u32[]{:S(2)}, u32[]{:S(2)}) collective-permute-start(s32[3]{0:T(128)S(1)} %bitcast.59), channel_id=1, source_target_pairs={{0,3},{1,0},{2,1},{3,2},{4,7},{5,4},{6,5},{7,6},{8,11},{9,8},{10,9... | collective-permute-start | bytes 44 | tf_op jit(solution)/shard_map/ppermute | solution.py:30
  13.4 10.1 %collective-permute-start.6 = (bf16[64,768]{1,0:T(8,128)(2,1)S(1)}, bf16[64,768]{1,0:T(8,128)(2,1)S(1)}, u32[]{:S(2)}, u32[]{:S(2)}) collective-permute-start(bf16[64,768]{1,0:T(8,128)(2,1)S(1)} %reshape.136), channel_id=1, source_target_pairs={{0,2},{1,3},{2,0},{3,1},{4,6},{5,7},{6,4},{7,5},{8,10},{9,11},{10,... | collective-permute-start | bytes 294920 | tf_op jit(solution)/shard_map/ppermute | solution.py:29
  14.9 8.7 %collective-permute-start.4 = (bf16[64,768]{1,0:T(8,128)(2,1)S(1)}, bf16[64,768]{1,0:T(8,128)(2,1)S(1)}, u32[]{:S(2)}, u32[]{:S(2)}) collective-permute-start(bf16[64,768]{1,0:T(8,128)(2,1)S(1)} %reshape.136), channel_id=1, source_target_pairs={{0,1},{1,2},{2,3},{3,0},{4,5},{5,6},{6,7},{7,4},{8,9},{9,10},{10,1... | collective-permute-start | bytes 294920 | tf_op jit(solution)/shard_map/ppermute | solution.py:29
  16.5 7.4 %collective-permute-start.8 = (bf16[64,768]{1,0:T(8,128)(2,1)S(1)}, bf16[64,768]{1,0:T(8,128)(2,1)S(1)}, u32[]{:S(2)}, u32[]{:S(2)}) collective-permute-start(bf16[64,768]{1,0:T(8,128)(2,1)S(1)} %reshape.136), channel_id=1, source_target_pairs={{0,3},{1,0},{2,1},{3,2},{4,7},{5,4},{6,5},{7,6},{8,11},{9,8},{10,9... | collective-permute-start | bytes 294920 | tf_op jit(solution)/shard_map/ppermute | solution.py:29
  24.8 1.3 %collective-permute-start.9 = (f32[64,256]{1,0:T(8,128)S(1)}, f32[64,256]{1,0:T(8,128)S(1)}, u32[]{:S(2)}, u32[]{:S(2)}) collective-permute-start(f32[64,256]{1,0:T(8,128)S(1)} %reshape.139), channel_id=1, source_target_pairs={{0,4},{4,0},{8,12},{12,8},{16,20},{20,16},{24,28},{28,24},{1,5},{5... | collective-permute-start | bytes 196616 | tf_op jit(solution)/shard_map/ppermute | solution.py:51
  26.2 4.3 %collective-permute-start.10 = (f32[64,256]{1,0:T(8,128)S(1)}, f32[64,256]{1,0:T(8,128)S(1)}, u32[]{:S(2)}, u32[]{:S(2)}) collective-permute-start(f32[64,256]{1,0:T(8,128)S(1)} %add.59), channel_id=1, source_target_pairs={{0,8},{4,12},{8,0},{12,4},{16,24},{20,28},{24,16},{28,20},{1,9},{5... | collective-permute-start | bytes 196616 | tf_op jit(solution)/shard_map/ppermute | solution.py:51
  30.5 4.3 %collective-permute-start.11 = (f32[64,256]{1,0:T(8,128)S(1)}, f32[64,256]{1,0:T(8,128)S(1)}, u32[]{:S(2)}, u32[]{:S(2)}) collective-permute-start(f32[64,256]{1,0:T(8,128)S(1)} %add.60), channel_id=1, source_target_pairs={{0,16},{4,20},{8,24},{12,28},{16,0},{20,4},{24,8},{28,12},{1,17},{... | collective-permute-start | bytes 196616 | tf_op jit(solution)/shard_map/ppermute | solution.py:51

commit v2 on v1

v2 whole, which is shorter than its diff:
```python
import functools

import jax
import jax.numpy as jnp
from jax import lax
from jax.experimental import pallas as pl
from jax.experimental.pallas import tpu as pltpu
from jax.sharding import PartitionSpec as P

BS = 64


def half_kernel(orb, slots, aux_width, meta_ref, own_ref, *refs):
    rows, (half_ref, held) = refs[:orb], refs[orb:]
    me = lax.axis_index("orb")
    width = BS
    for shift in range(orb):
        held[shift] = rows[shift][:width]
    chosen = [held[lax.rem(me - meta_ref[j] + orb, orb)] for j in range(slots)]
    selected = jnp.concatenate(chosen, axis=0)
    own = own_ref[...]
    pieces = []
    for p in range(aux_width):
        cut = [(j * aux_width + p) * width for j in range(slots)]
        pieces.append(jnp.concatenate([own[:, c : c + width] for c in cut], axis=1))
    left = jnp.concatenate(pieces, axis=0)
    half = jnp.dot(left, selected, preferred_element_type=jnp.float32).astype(jnp.bfloat16)
    for k in range(orb):
        half_ref[k] = jnp.concatenate(
            [
                half[p * width : (p + 1) * width, k * width : (k + 1) * width]
                for p in range(aux_width)
            ],
            axis=1,
        )


def exchange_kernel(orb, slots, aux_width, meta_ref, half_ref, *refs):
    blocks, (out_ref, held) = refs[:orb], refs[orb:]
    me = lax.axis_index("orb")
    depth = aux_width * BS
    for shift in range(orb):
        total = None
        for j in range(slots):
            term = lax.dot_general(
                half_ref[meta_ref[shift * slots + j]],
                blocks[shift][:, j * depth : (j + 1) * depth],
                (((1,), (1,)), ((), ())),
                preferred_element_type=jnp.float32,
            )
            total = term if total is None else total + term
        held[lax.rem(me - shift + orb, orb)] = total
    out_ref[...] = jnp.concatenate([held[n] for n in range(orb)], axis=1)


def shards(density, tensor_blocks, pairs, kept):
    width = BS
    full_width = density.shape[1]
    slots = tensor_blocks.shape[2]
    aux_width = tensor_blocks.shape[3]
    orb = lax.axis_size("orb")
    aux = lax.axis_size("aux")
    slot_index = jnp.arange(slots, dtype=jnp.int32)
    active = slot_index < kept[0, 0]
    masked = jnp.where(active[:, None, None], tensor_blocks[0, 0], 0)
    own = masked.reshape(slots, aux_width, width, width)
    flat = own.transpose(2, 0, 1, 3).reshape(width, slots * aux_width * width)
    own_pairs = pairs.reshape(slots)
    note = jnp.zeros((8, full_width), jnp.bfloat16)
    note = note.at[0, :slots].set(own_pairs.astype(jnp.bfloat16))
    packed = jnp.concatenate([density, note], axis=0)

    rows, blocks, all_pairs = [packed], [flat], [own_pairs]
    for shift in range(1, orb):
        perm = [(i, (i + shift) % orb) for i in range(orb)]
        rows.append(lax.ppermute(packed, "orb", perm))
        blocks.append(lax.ppermute(flat, "orb", perm))
        all_pairs.append(rows[-1][width, :slots].astype(jnp.int32))

    vmem = pl.BlockSpec(memory_space=pltpu.VMEM)
    smem = pl.BlockSpec(memory_space=pltpu.SMEM)
    half = pl.pallas_call(
        functools.partial(half_kernel, orb, slots, aux_width),
        out_shape=jax.ShapeDtypeStruct((orb, width, aux_width * width), jnp.bfloat16),
        in_specs=[smem, vmem] + [vmem] * orb,
        out_specs=vmem,
        scratch_shapes=[pltpu.VMEM((orb, width, full_width), jnp.bfloat16)],
        compiler_params=pltpu.CompilerParams(vmem_limit_bytes=32 * 1024 * 1024),
        name="half",
    )(own_pairs, flat, *rows)
    parts = pl.pallas_call(
        functools.partial(exchange_kernel, orb, slots, aux_width),
        out_shape=jax.ShapeDtypeStruct((width, full_width), jnp.float32),
        in_specs=[smem, vmem] + [vmem] * orb,
        out_specs=vmem,
        scratch_shapes=[pltpu.VMEM((orb, width, width), jnp.float32)],
        compiler_params=pltpu.CompilerParams(vmem_limit_bytes=32 * 1024 * 1024),
        name="exchange",
    )(jnp.concatenate(all_pairs), half, *blocks)

    step = 1
    while step < aux:
        ways = 2 if step == 1 or step * 4 > aux else 4
        terms = [parts]
        for way in range(1, ways):
            terms.append(lax.ppermute(parts, "aux", [(i, i ^ (way * step)) for i in range(aux)]))
        while len(terms) > 1:
            terms = [terms[i] + terms[i + 1] for i in range(0, len(terms), 2)]
        parts = terms[0]
        step *= ways
    return parts


def solution(mesh):
    return jax.shard_map(
        shards,
        mesh=mesh,
        in_specs=(
            P("orb", None),
            P("orb", "aux", None, None, None),
            P("orb", "aux", None),
            P("orb", "aux"),
        ),
        out_specs=P("orb", None),
        check_vma=False,
    )
```

time: 35.6 us -> 32.1 us (0.902)
  starting transfers between devices: 18.4 us -> 13.7 us
  local copies, waits for them, and re-layouts: 6.13 us -> 1.92 us
  waiting for transfers between devices: 7.95 us -> 11.5 us
  Pallas kernels: 0 us -> 1.71 us
  other arithmetic: 1.12 us -> 2.35 us
  matrix products: 0.88 us -> 0 us
    ppermute x12 -> x10, starting transfers between devices: 18.4 us -> 13.7 us  [the longest x3 6.06 us: shards(): rows.append(lax.ppermute(packed, 'orb', perm))]
    ppermute x12 -> x10, waiting for transfers between devices: 7.95 us -> 11.5 us  [the longest x3 6.51 us: shards(): blocks.append(lax.ppermute(flat, 'orb', perm))]
    gather x6 -> x0, local copies, waits for them, and re-layouts: 3.45 us -> none  [the longest x4 2.34 us: shards(): picked = jnp.take(half_four, peer_pairs[shift], axis=2, mode='clip')]
    pallas_call x0 -> x2, Pallas kernels: none -> 1.71 us  [the longest x1 0.87 us: shards(): pl.pallas_call(functools.partial(exchange_kernel, orb, slots, aux_width),...]
    dot_general x5 -> x0, matrix products: 0.88 us -> none  [the longest x4 0.65 us: shards(): lax.dot_general(picked, peers[shift], (((1,), (1,)), ((), ())), preferred...]
    reshape x6 -> x0, local copies, waits for them, and re-layouts: 0.85 us -> none  [the longest x3 0.5 us: shards(): picked = picked.transpose(1, 2, 0, 3).reshape(width, -1)]
    concatenate x0 -> x2, other arithmetic: none -> 0.84 us  [the longest x1 0.76 us: shards(): packed = jnp.concatenate([density, note], axis=0)]
    convert_element_type x0 -> x4, other arithmetic: none -> 0.67 us  [the longest x1 0.66 us: shards(): note = note.at[0, :slots].set(own_pairs.astype(jnp.bfloat16))]
  transfers between devices with their start and end apart: 12 -> 10, of which waited for: 5 -> 6; matrix products, arithmetic and copies ran while one was open for 18% -> 5% of each run, Pallas kernels for 0% -> 3%
where the time goes in v2:
time: 32.1 us; the launch traced here: 31.9 us
  starting transfers between devices  13.7 us (43%)
  waiting for transfers between devices  11.5 us (36%)
  other arithmetic  2.35 us (7%)
  local copies, waits for them, and re-layouts  1.92 us (6%)
  Pallas kernels  1.71 us (5%)
  between operations  0.76 us (2%)
    ppermute x3, waiting for transfers between devices, shards(): blocks.append(lax.ppermute(flat, 'orb', perm))  6.51 us
    ppermute x3, starting transfers between devices, shards(): rows.append(lax.ppermute(packed, 'orb', perm))  6.06 us
    ppermute x4, waiting for transfers between devices, shards(): lax.ppermute(parts, 'aux', [(i, i ^ way * step) for i in range(aux)])  4.97 us
    ppermute x3, starting transfers between devices, shards(): blocks.append(lax.ppermute(flat, 'orb', perm))  3.99 us
    ppermute x4, starting transfers between devices, shards(): lax.ppermute(parts, 'aux', [(i, i ^ way * step) for i in range(aux)])  3.62 us
    squeeze x1, local copies, waits for them, and re-layouts, shards(): masked = jnp.where(active[:, None, None], tensor_blocks[0, 0], 0)  1.1 us
    pallas_call x1, Pallas kernels, shards(): pl.pallas_call(functools.partial(exchange_kernel, orb, slots, aux_width),...  0.87 us
    pallas_call x1, Pallas kernels, shards(): pl.pallas_call(functools.partial(half_kernel, orb, slots, aux_width), out...  0.84 us
  transfers between devices with their start and end apart: 10, of which 6 were waited for; matrix products, arithmetic and copies ran while one was open for 5% of the time, Pallas kernels for 3%

profile of v2, /device:TPU:0, one launch (start us, length us, event | category | flops | bytes accessed | tf_op | source)
XLA Modules:
  0.0 31.9 jit_solution(5221018540434627702)
XLA Ops:
  0.0 0.7 %convert_bitcast_fusion = bf16[1,3]{1,0:T(2,128)(2,1)S(1)} fusion(s32[1,1,3]{2,1,0:T(1,128)} %param.8), kind=kLoop, calls=%fused_computation.14 | loop fusion | flops 3 | bytes 18 | tf_op jit(solution)/shard_map/convert_element_type | solution.py:70
  0.7 0.8 %fusion.2.refs_0_ = bf16[72,256]{1,0:T(8,128)(2,1)S(1)} fusion(bf16[1,3]{1,0:T(2,128)(2,1)S(1)} %convert_bitcast_fusion, bf16[64,256]{1,0:T(8,128)(2,1)} %param.6), kind=kLoop, calls=%fused_computation.5 | loop fusion | flops 110592 | bytes 69638 | tf_op jit(solution)/shard_map/concatenate | solution.py:71
  1.4 5.0 %collective-permute-start.2 = (bf16[72,256]{1,0:T(8,128)(2,1)S(1)}, bf16[72,256]{1,0:T(8,128)(2,1)S(1)}, u32[]{:S(2)}, u32[]{:S(2)}) collective-permute-start(bf16[72,256]{1,0:T(8,128)(2,1)S(1)} %fusion.2.refs_0_), channel_id=1, source_target_pairs={{0,3},{1,0},{2,1},{3,2},{4,7},{5,4},{6,5},{7,6},{8,11},{9,8},{10,9... | collective-permute-start | bytes 110600 | tf_op jit(solution)/shard_map/ppermute | solution.py:76
  6.5 0.0 collective-permute-start.1
  6.5 1.0 %collective-permute-start = (bf16[72,256]{1,0:T(8,128)(2,1)S(1)}, bf16[72,256]{1,0:T(8,128)(2,1)S(1)}, u32[]{:S(2)}, u32[]{:S(2)}) collective-permute-start(bf16[72,256]{1,0:T(8,128)(2,1)S(1)} %fusion.2.refs_0_), channel_id=1, source_target_pairs={{0,1},{1,2},{2,3},{3,0},{4,5},{5,6},{6,7},{7,4},{8,9},{9,10},{10,1... | collective-permute-start | bytes 110600 | tf_op jit(solution)/shard_map/ppermute | solution.py:76
  8.2 1.1 %squeeze.10 = bf16[3,4,64,64]{3,2,1,0:T(8,128)(2,1)S(1)} reshape(bf16[1,1,3,4,4096]{4,3,2,1,0:T(4,128)(2,1)} %param.7) | data formatting | bytes 196608 | tf_op jit(solution)/shard_map/squeeze | solution.py:65
  9.3 0.2 fusion
  9.4 0.2 reshape.55.own_ref.refs_0_
  9.6 2.9 %collective-permute-start.5 = (bf16[64,768]{1,0:T(8,128)(2,1)S(1)}, bf16[64,768]{1,0:T(8,128)(2,1)S(1)}, u32[]{:S(2)}, u32[]{:S(2)}) collective-permute-start(bf16[64,768]{1,0:T(8,128)(2,1)S(1)} %reshape.55.own_ref.refs_0_), channel_id=1, source_target_pairs={{0,3},{1,0},{2,1},{3,2},{4,7},{5,4},{6,5},{7,6},{8,11},{9,8},{10,9... | collective-permute-start | bytes 294920 | tf_op jit(solution)/shard_map/ppermute | solution.py:77
  12.5 1.1 %collective-permute-start.4 = (bf16[64,768]{1,0:T(8,128)(2,1)S(1)}, bf16[64,768]{1,0:T(8,128)(2,1)S(1)}, u32[]{:S(2)}, u32[]{:S(2)}) collective-permute-start(bf16[64,768]{1,0:T(8,128)(2,1)S(1)} %reshape.55.own_ref.refs_0_), channel_id=1, source_target_pairs={{0,2},{1,3},{2,0},{3,1},{4,6},{5,7},{6,4},{7,5},{8,10},{9,11},{10,... | collective-permute-start | bytes 294920 | tf_op jit(solution)/shard_map/ppermute | solution.py:77
  13.6 0.0 collective-permute-done.2.refs_3_
  13.6 0.0 collective-permute-start.3
  13.6 0.0 collective-permute-done.1.refs_2_
  13.6 0.0 collective-permute-done.refs_1_
  13.7 0.0 copy-start
  13.7 0.6 %copy-done = s32[1,1,3]{2,1,0:T(1,128)S(1)} copy-done((s32[1,1,3]{2,1,0:T(1,128)S(1)}, s32[1,1,3]{2,1,0:T(1,128)}, u32[]{:S(2)}) %copy-start) | copy-done | bytes 36
  14.3 0.8 %half.1.half_ref = bf16[4,64,256]{2,1,0:T(8,128)(2,1)S(1)} custom-call(s32[3]{0:T(128)S(1)} %bitcast.22, bf16[64,768]{1,0:T(8,128)(2,1)S(1)} %reshape.55.own_ref.refs_0_, bf16[72,256]{1,0:T(8,128)(2,1)S(1)} %fusion.2.refs_0_, bf16[72,256]{1,0:T(8,128)(2,1)S(1)} %collective-permute-done.refs_1_, bf16[72,256]{1,0:T(8,128)(2,1)S(1)} %collective-permute-done.1.refs_2_, ...), custom_call_target="tpu_custom_call" | custom-call | tf_op jit(solution)/shard_map/half/pallas_call | solution.py:82
  15.2 0.1 pad_add_fusion.meta_ref
  15.3 0.5 %collective-permute-done.5.refs_3_ = bf16[64,768]{1,0:T(8,128)(2,1)S(1)} collective-permute-done((bf16[64,768]{1,0:T(8,128)(2,1)S(1)}, bf16[64,768]{1,0:T(8,128)(2,1)S(1)}, u32[]{:S(2)}, u32[]{:S(2)}) %collective-permute-start.5) | collective-permute-done | bytes 98336 | tf_op jit(solution)/shard_map/ppermute | solution.py:77
  15.7 6.0 %collective-permute-done.4.refs_2_ = bf16[64,768]{1,0:T(8,128)(2,1)S(1)} collective-permute-done((bf16[64,768]{1,0:T(8,128)(2,1)S(1)}, bf16[64,768]{1,0:T(8,128)(2,1)S(1)}, u32[]{:S(2)}, u32[]{:S(2)}) %collective-permute-start.4) | collective-permute-done | bytes 98336 | tf_op jit(solution)/shard_map/ppermute | solution.py:77
  21.8 0.0 collective-permute-done.3.refs_1_
  21.8 0.9 %exchange.1 = f32[64,256]{1,0:T(8,128)S(1)} custom-call(s32[12]{0:T(128)S(1)} %pad_add_fusion.meta_ref, bf16[4,64,256]{2,1,0:T(8,128)(2,1)S(1)} %half.1.half_ref, bf16[64,768]{1,0:T(8,128)(2,1)S(1)} %reshape.55.own_ref.refs_0_, bf16[64,768]{1,0:T(8,128)(2,1)S(1)} %collective-permute-done.3.refs_1_, bf16[64,768]{1,0:T(8,128)(2,1)S(1)} %collective-permute-done.4.refs_2_, ...), custom_call_target="tpu_custom_call" | custom-call | tf_op jit(solution)/shard_map/exchange/pallas_call | solution.py:91
  22.6 0.1 collective-permute-start.6
  22.7 1.2 %collective-permute-done.6 = f32[64,256]{1,0:T(8,128)S(1)} collective-permute-done((f32[64,256]{1,0:T(8,128)S(1)}, f32[64,256]{1,0:T(8,128)S(1)}, u32[]{:S(2)}, u32[]{:S(2)}) %collective-permute-start.6) | collective-permute-done | bytes 65568 | tf_op jit(solution)/shard_map/ppermute | solution.py:106
  24.0 2.5 %collective-permute-start.9 = (f32[64,256]{1,0:T(8,128)S(1)}, f32[64,256]{1,0:T(8,128)S(1)}, u32[]{:S(2)}, u32[]{:S(2)}) collective-permute-start(f32[64,256]{1,0:T(8,128)S(1)} %add.16), channel_id=1, source_target_pairs={{0,24},{4,28},{8,16},{12,20},{16,8},{20,12},{24,0},{28,4},{1,25},{... | collective-permute-start | bytes 196616 | tf_op jit(solution)/shard_map/ppermute | solution.py:106
  26.5 0.5 %collective-permute-start.8 = (f32[64,256]{1,0:T(8,128)S(1)}, f32[64,256]{1,0:T(8,128)S(1)}, u32[]{:S(2)}, u32[]{:S(2)}) collective-permute-start(f32[64,256]{1,0:T(8,128)S(1)} %add.16), channel_id=1, source_target_pairs={{0,16},{4,20},{8,24},{12,28},{16,0},{20,4},{24,8},{28,12},{1,17},{... | collective-permute-start | bytes 196616 | tf_op jit(solution)/shard_map/ppermute | solution.py:106
  27.0 0.5 %collective-permute-start.7 = (f32[64,256]{1,0:T(8,128)S(1)}, f32[64,256]{1,0:T(8,128)S(1)}, u32[]{:S(2)}, u32[]{:S(2)}) collective-permute-start(f32[64,256]{1,0:T(8,128)S(1)} %add.16), channel_id=1, source_target_pairs={{0,8},{4,12},{8,0},{12,4},{16,24},{20,28},{24,16},{28,20},{1,9},{5... | collective-permute-start | bytes 196616 | tf_op jit(solution)/shard_map/ppermute | solution.py:106
  27.5 1.7 %collective-permute-done.9 = f32[64,256]{1,0:T(8,128)S(1)} collective-permute-done((f32[64,256]{1,0:T(8,128)S(1)}, f32[64,256]{1,0:T(8,128)S(1)}, u32[]{:S(2)}, u32[]{:S(2)}) %collective-permute-start.9) | collective-permute-done | bytes 65568 | tf_op jit(solution)/shard_map/ppermute | solution.py:106
  29.2 1.5 %collective-permute-done.8 = f32[64,256]{1,0:T(8,128)S(1)} collective-permute-done((f32[64,256]{1,0:T(8,128)S(1)}, f32[64,256]{1,0:T(8,128)S(1)}, u32[]{:S(2)}, u32[]{:S(2)}) %collective-permute-start.8) | collective-permute-done | bytes 65568 | tf_op jit(solution)/shard_map/ppermute | solution.py:106
  30.8 0.5 %collective-permute-done.7 = f32[64,256]{1,0:T(8,128)S(1)} collective-permute-done((f32[64,256]{1,0:T(8,128)S(1)}, f32[64,256]{1,0:T(8,128)S(1)}, u32[]{:S(2)}, u32[]{:S(2)}) %collective-permute-start.7) | collective-permute-done | bytes 65568 | tf_op jit(solution)/shard_map/ppermute | solution.py:106
  31.3 0.6 %add_add_fusion = f32[64,256]{1,0:T(8,128)} fusion(f32[64,256]{1,0:T(8,128)S(1)} %collective-permute-done.8, f32[64,256]{1,0:T(8,128)S(1)} %collective-permute-done.9, f32[64,256]{1,0:T(8,128)S(1)} %add.16, f32[64,256]{1,0:T(8,128)S(1)} %collective-permute-done.7), kind=kLoop, calls=%fused_computation.4 | loop fusion | flops 49152 | bytes 327680 | tf_op jit(solution)/shard_map/add | solution.py:108
  (5 shorter events, 0.0 us)
Async XLA Ops:
  1.4 12.2 %collective-permute-start.2 = (bf16[72,256]{1,0:T(8,128)(2,1)S(1)}, bf16[72,256]{1,0:T(8,128)(2,1)S(1)}, u32[]{:S(2)}, u32[]{:S(2)}) collective-permute-start(bf16[72,256]{1,0:T(8,128)(2,1)S(1)} %fusion.2.refs_0_), channel_id=1, source_target_pairs={{0,3},{1,0},{2,1},{3,2},{4,7},{5,4},{6,5},{7,6},{8,11},{9,8},{10,9... | collective-permute-start | bytes 110600 | tf_op jit(solution)/shard_map/ppermute | solution.py:76
  6.5 7.2 %collective-permute-start.1 = (bf16[72,256]{1,0:T(8,128)(2,1)S(1)}, bf16[72,256]{1,0:T(8,128)(2,1)S(1)}, u32[]{:S(2)}, u32[]{:S(2)}) collective-permute-start(bf16[72,256]{1,0:T(8,128)(2,1)S(1)} %fusion.2.refs_0_), channel_id=1, source_target_pairs={{0,2},{1,3},{2,0},{3,1},{4,6},{5,7},{6,4},{7,5},{8,10},{9,11},{10,... | collective-permute-start | bytes 110600 | tf_op jit(solution)/shard_map/ppermute | solution.py:76
  6.5 7.2 %collective-permute-start = (bf16[72,256]{1,0:T(8,128)(2,1)S(1)}, bf16[72,256]{1,0:T(8,128)(2,1)S(1)}, u32[]{:S(2)}, u32[]{:S(2)}) collective-permute-start(bf16[72,256]{1,0:T(8,128)(2,1)S(1)} %fusion.2.refs_0_), channel_id=1, source_target_pairs={{0,1},{1,2},{2,3},{3,0},{4,5},{5,6},{6,7},{7,4},{8,9},{9,10},{10,1... | collective-permute-start | bytes 110600 | tf_op jit(solution)/shard_map/ppermute | solution.py:76
  9.6 6.1 %collective-permute-start.5 = (bf16[64,768]{1,0:T(8,128)(2,1)S(1)}, bf16[64,768]{1,0:T(8,128)(2,1)S(1)}, u32[]{:S(2)}, u32[]{:S(2)}) collective-permute-start(bf16[64,768]{1,0:T(8,128)(2,1)S(1)} %reshape.55.own_ref.refs_0_), channel_id=1, source_target_pairs={{0,3},{1,0},{2,1},{3,2},{4,7},{5,4},{6,5},{7,6},{8,11},{9,8},{10,9... | collective-permute-start | bytes 294920 | tf_op jit(solution)/shard_map/ppermute | solution.py:77
  12.5 9.3 %collective-permute-start.4 = (bf16[64,768]{1,0:T(8,128)(2,1)S(1)}, bf16[64,768]{1,0:T(8,128)(2,1)S(1)}, u32[]{:S(2)}, u32[]{:S(2)}) collective-permute-start(bf16[64,768]{1,0:T(8,128)(2,1)S(1)} %reshape.55.own_ref.refs_0_), channel_id=1, source_target_pairs={{0,2},{1,3},{2,0},{3,1},{4,6},{5,7},{6,4},{7,5},{8,10},{9,11},{10,... | collective-permute-start | bytes 294920 | tf_op jit(solution)/shard_map/ppermute | solution.py:77
  13.6 8.1 %collective-permute-start.3 = (bf16[64,768]{1,0:T(8,128)(2,1)S(1)}, bf16[64,768]{1,0:T(8,128)(2,1)S(1)}, u32[]{:S(2)}, u32[]{:S(2)}) collective-permute-start(bf16[64,768]{1,0:T(8,128)(2,1)S(1)} %reshape.55.own_ref.refs_0_), channel_id=1, source_target_pairs={{0,1},{1,2},{2,3},{3,0},{4,5},{5,6},{6,7},{7,4},{8,9},{9,10},{10,1... | collective-permute-start | bytes 294920 | tf_op jit(solution)/shard_map/ppermute | solution.py:77
  13.7 0.7 %copy-start = (s32[1,1,3]{2,1,0:T(1,128)S(1)}, s32[1,1,3]{2,1,0:T(1,128)}, u32[]{:S(2)}) copy-start(s32[1,1,3]{2,1,0:T(1,128)} %param.8) | copy-start | bytes 40
  22.6 1.3 %collective-permute-start.6 = (f32[64,256]{1,0:T(8,128)S(1)}, f32[64,256]{1,0:T(8,128)S(1)}, u32[]{:S(2)}, u32[]{:S(2)}) collective-permute-start(f32[64,256]{1,0:T(8,128)S(1)} %exchange.1), channel_id=1, source_target_pairs={{0,4},{4,0},{8,12},{12,8},{16,20},{20,16},{24,28},{28,24},{1,5},{5... | collective-permute-start | bytes 196616 | tf_op jit(solution)/shard_map/ppermute | solution.py:106
  24.0 5.3 %collective-permute-start.9 = (f32[64,256]{1,0:T(8,128)S(1)}, f32[64,256]{1,0:T(8,128)S(1)}, u32[]{:S(2)}, u32[]{:S(2)}) collective-permute-start(f32[64,256]{1,0:T(8,128)S(1)} %add.16), channel_id=1, source_target_pairs={{0,24},{4,28},{8,16},{12,20},{16,8},{20,12},{24,0},{28,4},{1,25},{... | collective-permute-start | bytes 196616 | tf_op jit(solution)/shard_map/ppermute | solution.py:106
  26.5 4.3 %collective-permute-start.8 = (f32[64,256]{1,0:T(8,128)S(1)}, f32[64,256]{1,0:T(8,128)S(1)}, u32[]{:S(2)}, u32[]{:S(2)}) collective-permute-start(f32[64,256]{1,0:T(8,128)S(1)} %add.16), channel_id=1, source_target_pairs={{0,16},{4,20},{8,24},{12,28},{16,0},{20,4},{24,8},{28,12},{1,17},{... | collective-permute-start | bytes 196616 | tf_op jit(solution)/shard_map/ppermute | solution.py:106
  27.0 4.3 %collective-permute-start.7 = (f32[64,256]{1,0:T(8,128)S(1)}, f32[64,256]{1,0:T(8,128)S(1)}, u32[]{:S(2)}, u32[]{:S(2)}) collective-permute-start(f32[64,256]{1,0:T(8,128)S(1)} %add.16), channel_id=1, source_target_pairs={{0,8},{4,12},{8,0},{12,4},{16,24},{20,28},{24,16},{28,20},{1,9},{5... | collective-permute-start | bytes 196616 | tf_op jit(solution)/shard_map/ppermute | solution.py:106

commit v3 on v2

v3 whole, which is shorter than its diff:
```python
import functools

import jax
import jax.numpy as jnp
from jax import lax
from jax.experimental import pallas as pl
from jax.experimental.pallas import tpu as pltpu
from jax.sharding import PartitionSpec as P

BS = 64


def half_kernel(orb, slots, aux_width, meta_ref, own_ref, *refs):
    rows, (half_ref, held) = refs[:orb], refs[orb:]
    me = lax.axis_index("orb")
    width = BS
    for shift in range(orb):
        held[lax.rem(me - shift + orb, orb)] = rows[shift][...]
    held[orb] = jnp.zeros_like(held[orb])
    selected = jnp.concatenate([held[meta_ref[j]] for j in range(slots)], axis=0)
    left = jnp.concatenate(
        [
            jnp.concatenate([own_ref[j, p] for j in range(slots)], axis=1)
            for p in range(aux_width)
        ],
        axis=0,
    )
    half = jnp.dot(left, selected, preferred_element_type=jnp.float32).astype(jnp.bfloat16)
    for k in range(orb):
        half_ref[k] = jnp.concatenate(
            [
                half[p * width : (p + 1) * width, k * width : (k + 1) * width]
                for p in range(aux_width)
            ],
            axis=1,
        )
    half_ref[orb] = jnp.zeros_like(half_ref[orb])


def exchange_kernel(orb, slots, aux_width, meta_ref, half_ref, *refs):
    blocks, (out_ref, held) = refs[:orb], refs[orb:]
    me = lax.axis_index("orb")
    for shift in range(orb):
        total = None
        for j in range(slots):
            right = jnp.concatenate([blocks[shift][j, p] for p in range(aux_width)], axis=1)
            term = lax.dot_general(
                half_ref[meta_ref[shift * slots + j]],
                right,
                (((1,), (1,)), ((), ())),
                preferred_element_type=jnp.float32,
            )
            total = term if total is None else total + term
        held[lax.rem(me - shift + orb, orb)] = total
    out_ref[...] = jnp.concatenate([held[n] for n in range(orb)], axis=1)


def shards(density, tensor_blocks, pairs, kept):
    width = BS
    full_width = density.shape[1]
    slots = tensor_blocks.shape[2]
    aux_width = tensor_blocks.shape[3]
    orb = lax.axis_size("orb")
    aux = lax.axis_size("aux")
    perms = [[(i, (i + shift) % orb) for i in range(orb)] for shift in range(orb)]
    slot_index = jnp.arange(slots, dtype=jnp.int32)
    codes = jnp.where(slot_index < kept[0, 0], pairs.reshape(slots), orb)
    rows, blocks, all_codes = [density], [tensor_blocks], [codes]
    for shift in range(1, orb):
        rows.append(lax.ppermute(density, "orb", perms[shift]))
        blocks.append(lax.ppermute(tensor_blocks, "orb", perms[shift]))
    sent, rows = lax.optimization_barrier((codes, rows))
    for shift in range(1, orb):
        all_codes.append(lax.ppermute(sent, "orb", perms[shift]))
    blocks = [b.reshape(slots, aux_width, width, width) for b in blocks]

    vmem = pl.BlockSpec(memory_space=pltpu.VMEM)
    smem = pl.BlockSpec(memory_space=pltpu.SMEM)
    half = pl.pallas_call(
        functools.partial(half_kernel, orb, slots, aux_width),
        out_shape=jax.ShapeDtypeStruct((orb + 1, width, aux_width * width), jnp.bfloat16),
        in_specs=[smem, vmem] + [vmem] * orb,
        out_specs=vmem,
        scratch_shapes=[pltpu.VMEM((orb + 1, width, full_width), jnp.bfloat16)],
        compiler_params=pltpu.CompilerParams(vmem_limit_bytes=32 * 1024 * 1024),
        name="half",
    )(codes, blocks[0], *rows)
    parts = pl.pallas_call(
        functools.partial(exchange_kernel, orb, slots, aux_width),
        out_shape=jax.ShapeDtypeStruct((width, full_width), jnp.float32),
        in_specs=[smem, vmem] + [vmem] * orb,
        out_specs=vmem,
        scratch_shapes=[pltpu.VMEM((orb, width, width), jnp.float32)],
        compiler_params=pltpu.CompilerParams(vmem_limit_bytes=32 * 1024 * 1024),
        name="exchange",
    )(jnp.concatenate(all_codes), half, *blocks)

    step = 1
    while step < aux:
        ways = 2 if step == 1 or step * 4 > aux else 4
        terms = [parts]
        for way in range(1, ways):
            terms.append(lax.ppermute(parts, "aux", [(i, i ^ (way * step)) for i in range(aux)]))
        while len(terms) > 1:
            terms = [terms[i] + terms[i + 1] for i in range(0, len(terms), 2)]
        parts = terms[0]
        step *= ways
    return parts


def solution(mesh):
    return jax.shard_map(
        shards,
        mesh=mesh,
        in_specs=(
            P("orb", None),
            P("orb", "aux", None, None, None),
            P("orb", "aux", None),
            P("orb", "aux"),
        ),
        out_specs=P("orb", None),
        check_vma=False,
    )
```

time: 32.1 us -> 34.4 us (1.072)
  starting transfers between devices: 13.7 us -> 17.1 us
  other arithmetic: 2.35 us -> 0.74 us
  local copies, waits for them, and re-layouts: 1.92 us -> 2.47 us
    ppermute x6 -> x9, starting transfers between devices: 10.1 us -> 13.5 us  [the longest x3 6.96 us: shards(): rows.append(lax.ppermute(density, 'orb', perms[shift]))]
    reshape x1 -> x4, local copies, waits for them, and re-layouts: 0.17 us -> 1.81 us  [shards(): blocks = [b.reshape(slots, aux_width, width, width) for b in blocks]]
    squeeze x1 -> x0, local copies, waits for them, and re-layouts: 1.1 us -> none  [shards(): masked = jnp.where(active[:, None, None], tensor_blocks[0, 0], 0)]
    ppermute x6 -> x9, waiting for transfers between devices: 6.52 us -> 5.43 us  [the longest x3 5.42 us: shards(): all_codes.append(lax.ppermute(sent, 'orb', perms[shift]))]
    ppermute x4, waiting for transfers between devices: 4.97 us -> 5.93 us  [shards(): lax.ppermute(parts, 'aux', [(i, i ^ way * step) for i in range(aux)])]
    concatenate x2 -> x1, other arithmetic: 0.84 us -> 0.08 us  [shards(): jnp.concatenate(all_codes)]
    convert_element_type x4 -> x0, other arithmetic: 0.67 us -> none  [the longest x1 0.66 us: shards(): note = note.at[0, :slots].set(own_pairs.astype(jnp.bfloat16))]
  transfers between devices with their start and end apart: 10 -> 13, of which waited for: 6 -> 6; matrix products, arithmetic and copies ran while one was open for 5% -> 5% of each run, Pallas kernels for 3% -> 2%
where the time goes in v3:
time: 34.4 us; the launch traced here: 34.2 us
  starting transfers between devices  17.1 us (50%)
  waiting for transfers between devices  11.4 us (33%)
  local copies, waits for them, and re-layouts  2.47 us (7%)
  Pallas kernels  1.79 us (5%)
  between operations  0.76 us (2%)
  other arithmetic  0.74 us (2%)
    ppermute x3, starting transfers between devices, shards(): rows.append(lax.ppermute(density, 'orb', perms[shift]))  6.96 us
    ppermute x4, waiting for transfers between devices, shards(): lax.ppermute(parts, 'aux', [(i, i ^ way * step) for i in range(aux)])  5.93 us
    ppermute x3, waiting for transfers between devices, shards(): all_codes.append(lax.ppermute(sent, 'orb', perms[shift]))  5.42 us
    ppermute x3, starting transfers between devices, shards(): blocks.append(lax.ppermute(tensor_blocks, 'orb', perms[shift]))  3.88 us
    ppermute x4, starting transfers between devices, shards(): lax.ppermute(parts, 'aux', [(i, i ^ way * step) for i in range(aux)])  3.62 us
    ppermute x3, starting transfers between devices, shards(): all_codes.append(lax.ppermute(sent, 'orb', perms[shift]))  2.61 us
    reshape x4, local copies, waits for them, and re-layouts, shards(): blocks = [b.reshape(slots, aux_width, width, width) for b in blocks]  1.81 us
    pallas_call x1, Pallas kernels, shards(): pl.pallas_call(functools.partial(exchange_kernel, orb, slots, aux_width),...  0.95 us
  transfers between devices with their start and end apart: 13, of which 6 were waited for; matrix products, arithmetic and copies ran while one was open for 5% of the time, Pallas kernels for 2%

profile of v3, /device:TPU:0, one launch (start us, length us, event | category | flops | bytes accessed | tf_op | source)
XLA Modules:
  0.0 34.2 jit_solution(11126334626524729575)
XLA Ops:
  0.0 3.0 %collective-permute-start = (bf16[64,256]{1,0:T(8,128)(2,1)}, bf16[64,256]{1,0:T(8,128)(2,1)S(1)}, u32[]{:S(2)}, u32[]{:S(2)}) collective-permute-start(bf16[64,256]{1,0:T(8,128)(2,1)} %refs_0_), channel_id=1, source_target_pairs={{0,1},{1,2},{2,3},{3,0},{4,5},{5,6},{6,7},{7,4},{8,9},{9,10},{10,1... | collective-permute-start | bytes 98312 | tf_op jit(solution)/shard_map/ppermute | solution.py:70
  3.0 2.6 %collective-permute-start.1 = (bf16[64,256]{1,0:T(8,128)(2,1)}, bf16[64,256]{1,0:T(8,128)(2,1)S(1)}, u32[]{:S(2)}, u32[]{:S(2)}) collective-permute-start(bf16[64,256]{1,0:T(8,128)(2,1)} %refs_0_), channel_id=1, source_target_pairs={{0,2},{1,3},{2,0},{3,1},{4,6},{5,7},{6,4},{7,5},{8,10},{9,11},{10,... | collective-permute-start | bytes 98312 | tf_op jit(solution)/shard_map/ppermute | solution.py:70
  5.6 1.3 %collective-permute-start.2 = (bf16[64,256]{1,0:T(8,128)(2,1)}, bf16[64,256]{1,0:T(8,128)(2,1)S(1)}, u32[]{:S(2)}, u32[]{:S(2)}) collective-permute-start(bf16[64,256]{1,0:T(8,128)(2,1)} %refs_0_), channel_id=1, source_target_pairs={{0,3},{1,0},{2,1},{3,2},{4,7},{5,4},{6,5},{7,6},{8,11},{9,8},{10,9... | collective-permute-start | bytes 98312 | tf_op jit(solution)/shard_map/ppermute | solution.py:70
  7.0 0.7 %collective-permute-start.6 = (bf16[1,1,3,4,4096]{4,3,2,1,0:T(4,128)(2,1)}, bf16[1,1,3,4,4096]{4,3,2,1,0:T(4,128)(2,1)S(1)}, u32[]{:S(2)}, u32[]{:S(2)}) collective-permute-start(bf16[1,1,3,4,4096]{4,3,2,1,0:T(4,128)(2,1)} %param.5), channel_id=1, source_target_pairs={{0,1},{1,2},{2,3},{3,0},{4,5},{5,6},{6,7},{7,4},{8,9},{9,10},{10,1... | collective-permute-start | bytes 294920 | tf_op jit(solution)/shard_map/ppermute | solution.py:71
  7.6 0.3 collective-permute-start.7
  8.6 0.0 copy-start.2
  8.6 0.6 %copy-done.2 = s32[1,1,3]{2,1,0:T(1,128)S(1)} copy-done((s32[1,1,3]{2,1,0:T(1,128)S(1)}, s32[1,1,3]{2,1,0:T(1,128)}, u32[]{:S(2)}) %copy-start.2) | copy-done | bytes 36
  9.3 0.0 copy-start.1
  9.3 0.0 copy-start
  9.3 1.2 %reshape.16.own_ref.refs_0_ = bf16[3,4,64,64]{3,2,1,0:T(8,128)(2,1)S(1)} reshape(bf16[1,1,3,4,4096]{4,3,2,1,0:T(4,128)(2,1)} %param.5) | data formatting | bytes 196608 | tf_op jit(solution)/shard_map/reshape | solution.py:75
  10.5 0.0 collective-permute-done.refs_1_
  10.5 0.0 copy-done.1
  10.5 2.9 %collective-permute-start.8 = (bf16[1,1,3,4,4096]{4,3,2,1,0:T(4,128)(2,1)S(1)}, bf16[1,1,3,4,4096]{4,3,2,1,0:T(4,128)(2,1)S(1)}, u32[]{:S(2)}, u32[]{:S(2)}) collective-permute-start(bf16[1,1,3,4,4096]{4,3,2,1,0:T(4,128)(2,1)S(1)} %copy-done.1), channel_id=1, source_target_pairs={{0,3},{1,0},{2,1},{3,2},{4,7},{5,4},{6,5},{7,6},{8,11},{9,8},{10,9... | collective-permute-start | bytes 294920 | tf_op jit(solution)/shard_map/ppermute | solution.py:71
  13.4 0.0 collective-permute-done.1.refs_2_
  13.4 0.0 collective-permute-done.2.refs_3_
  13.4 0.6 %collective-permute-start.3 = (s32[3]{0:T(128)S(1)}, s32[3]{0:T(128)S(1)}, u32[]{:S(2)}, u32[]{:S(2)}) collective-permute-start(s32[3]{0:T(128)S(1)} %compare_select_fusion.meta_ref), channel_id=1, source_target_pairs={{0,1},{1,2},{2,3},{3,0},{4,5},{5,6},{6,7},{7,4},{8,9},{9,10},{10,1... | collective-permute-start | bytes 44 | tf_op jit(solution)/shard_map/ppermute | solution.py:74
  14.0 1.5 %collective-permute-start.4 = (s32[3]{0:T(128)S(1)}, s32[3]{0:T(128)S(1)}, u32[]{:S(2)}, u32[]{:S(2)}) collective-permute-start(s32[3]{0:T(128)S(1)} %compare_select_fusion.meta_ref), channel_id=1, source_target_pairs={{0,2},{1,3},{2,0},{3,1},{4,6},{5,7},{6,4},{7,5},{8,10},{9,11},{10,... | collective-permute-start | bytes 44 | tf_op jit(solution)/shard_map/ppermute | solution.py:74
  15.5 0.0 copy-done
  15.5 0.8 %half.1.half_ref = bf16[5,64,256]{2,1,0:T(8,128)(2,1)S(1)} custom-call(s32[3]{0:T(128)S(1)} %compare_select_fusion.meta_ref, bf16[3,4,64,64]{3,2,1,0:T(8,128)(2,1)S(1)} %reshape.16.own_ref.refs_0_, bf16[64,256]{1,0:T(8,128)(2,1)S(1)} %copy-done, bf16[64,256]{1,0:T(8,128)(2,1)S(1)} %collective-permute-done.refs_1_, ...), custom_call_target="tpu_custom_call" | custom-call | tf_op jit(solution)/shard_map/half/pallas_call | solution.py:79
  16.3 2.4 %collective-permute-done.3 = s32[3]{0:T(128)S(1)} collective-permute-done((s32[3]{0:T(128)S(1)}, s32[3]{0:T(128)S(1)}, u32[]{:S(2)}, u32[]{:S(2)}) %collective-permute-start.3) | collective-permute-done | bytes 44 | tf_op jit(solution)/shard_map/ppermute | solution.py:74
  18.7 0.5 %collective-permute-start.5 = (s32[3]{0:T(128)S(1)}, s32[3]{0:T(128)S(1)}, u32[]{:S(2)}, u32[]{:S(2)}) collective-permute-start(s32[3]{0:T(128)S(1)} %compare_select_fusion.meta_ref), channel_id=1, source_target_pairs={{0,3},{1,0},{2,1},{3,2},{4,7},{5,4},{6,5},{7,6},{8,11},{9,8},{10,9... | collective-permute-start | bytes 44 | tf_op jit(solution)/shard_map/ppermute | solution.py:74
  19.2 0.0 collective-permute-done.4
  19.2 3.0 %collective-permute-done.5 = s32[3]{0:T(128)S(1)} collective-permute-done((s32[3]{0:T(128)S(1)}, s32[3]{0:T(128)S(1)}, u32[]{:S(2)}, u32[]{:S(2)}) %collective-permute-start.5) | collective-permute-done | bytes 44 | tf_op jit(solution)/shard_map/ppermute | solution.py:74
  22.2 0.1 pad_add_fusion.meta_ref
  22.3 0.0 collective-permute-done.6
  22.3 0.2 reshape.17.refs_1_
  22.5 0.0 collective-permute-done.7
  22.6 0.2 reshape.18.refs_2_
  22.8 0.0 collective-permute-done.8
  22.8 0.2 reshape.19.refs_3_
  23.0 1.0 %exchange.1 = f32[64,256]{1,0:T(8,128)S(1)} custom-call(s32[12]{0:T(128)S(1)} %pad_add_fusion.meta_ref, bf16[5,64,256]{2,1,0:T(8,128)(2,1)S(1)} %half.1.half_ref, bf16[3,4,64,64]{3,2,1,0:T(8,128)(2,1)S(1)} %reshape.16.own_ref.refs_0_, bf16[3,4,64,64]{3,2,1,0:T(8,128)(2,1)S(1)} %reshape.17.refs_1_, bf16[3,4,64,64]{3,2,1,0:T(8,128)(2,1)S(1)} %reshape.18.refs_2_, ...), custom_call_target="tpu_custom_call" | custom-call | tf_op jit(solution)/shard_map/exchange/pallas_call | solution.py:88
  24.0 0.1 collective-permute-start.9
  24.0 1.2 %collective-permute-done.9 = f32[64,256]{1,0:T(8,128)S(1)} collective-permute-done((f32[64,256]{1,0:T(8,128)S(1)}, f32[64,256]{1,0:T(8,128)S(1)}, u32[]{:S(2)}, u32[]{:S(2)}) %collective-permute-start.9) | collective-permute-done | bytes 65568 | tf_op jit(solution)/shard_map/ppermute | solution.py:103
  25.3 1.6 %collective-permute-start.10 = (f32[64,256]{1,0:T(8,128)S(1)}, f32[64,256]{1,0:T(8,128)S(1)}, u32[]{:S(2)}, u32[]{:S(2)}) collective-permute-start(f32[64,256]{1,0:T(8,128)S(1)} %add.12), channel_id=1, source_target_pairs={{0,8},{4,12},{8,0},{12,4},{16,24},{20,28},{24,16},{28,20},{1,9},{5... | collective-permute-start | bytes 196616 | tf_op jit(solution)/shard_map/ppermute | solution.py:103
  26.9 1.5 %collective-permute-start.11 = (f32[64,256]{1,0:T(8,128)S(1)}, f32[64,256]{1,0:T(8,128)S(1)}, u32[]{:S(2)}, u32[]{:S(2)}) collective-permute-start(f32[64,256]{1,0:T(8,128)S(1)} %add.12), channel_id=1, source_target_pairs={{0,16},{4,20},{8,24},{12,28},{16,0},{20,4},{24,8},{28,12},{1,17},{... | collective-permute-start | bytes 196616 | tf_op jit(solution)/shard_map/ppermute | solution.py:103
  28.4 0.5 %collective-permute-start.12 = (f32[64,256]{1,0:T(8,128)S(1)}, f32[64,256]{1,0:T(8,128)S(1)}, u32[]{:S(2)}, u32[]{:S(2)}) collective-permute-start(f32[64,256]{1,0:T(8,128)S(1)} %add.12), channel_id=1, source_target_pairs={{0,24},{4,28},{8,16},{12,20},{16,8},{20,12},{24,0},{28,4},{1,25},{... | collective-permute-start | bytes 196616 | tf_op jit(solution)/shard_map/ppermute | solution.py:103
  28.9 0.8 %collective-permute-done.10 = f32[64,256]{1,0:T(8,128)S(1)} collective-permute-done((f32[64,256]{1,0:T(8,128)S(1)}, f32[64,256]{1,0:T(8,128)S(1)}, u32[]{:S(2)}, u32[]{:S(2)}) %collective-permute-start.10) | collective-permute-done | bytes 65568 | tf_op jit(solution)/shard_map/ppermute | solution.py:103
  29.6 1.5 %collective-permute-done.11 = f32[64,256]{1,0:T(8,128)S(1)} collective-permute-done((f32[64,256]{1,0:T(8,128)S(1)}, f32[64,256]{1,0:T(8,128)S(1)}, u32[]{:S(2)}, u32[]{:S(2)}) %collective-permute-start.11) | collective-permute-done | bytes 65568 | tf_op jit(solution)/shard_map/ppermute | solution.py:103
  31.1 2.4 %collective-permute-done.12 = f32[64,256]{1,0:T(8,128)S(1)} collective-permute-done((f32[64,256]{1,0:T(8,128)S(1)}, f32[64,256]{1,0:T(8,128)S(1)}, u32[]{:S(2)}, u32[]{:S(2)}) %collective-permute-start.12) | collective-permute-done | bytes 65568 | tf_op jit(solution)/shard_map/ppermute | solution.py:103
  33.5 0.6 %add_add_fusion = f32[64,256]{1,0:T(8,128)} fusion(f32[64,256]{1,0:T(8,128)S(1)} %collective-permute-done.11, f32[64,256]{1,0:T(8,128)S(1)} %collective-permute-done.12, f32[64,256]{1,0:T(8,128)S(1)} %add.12, f32[64,256]{1,0:T(8,128)S(1)} %collective-permute-done.10), kind=kLoop, calls=%fused_computation | loop fusion | flops 49152 | bytes 327680 | tf_op jit(solution)/shard_map/add | solution.py:105
  (2 shorter events, 0.0 us)
Async XLA Ops:
  0.0 10.5 %collective-permute-start = (bf16[64,256]{1,0:T(8,128)(2,1)}, bf16[64,256]{1,0:T(8,128)(2,1)S(1)}, u32[]{:S(2)}, u32[]{:S(2)}) collective-permute-start(bf16[64,256]{1,0:T(8,128)(2,1)} %refs_0_), channel_id=1, source_target_pairs={{0,1},{1,2},{2,3},{3,0},{4,5},{5,6},{6,7},{7,4},{8,9},{9,10},{10,1... | collective-permute-start | bytes 98312 | tf_op jit(solution)/shard_map/ppermute | solution.py:70
  3.0 10.3 %collective-permute-start.1 = (bf16[64,256]{1,0:T(8,128)(2,1)}, bf16[64,256]{1,0:T(8,128)(2,1)S(1)}, u32[]{:S(2)}, u32[]{:S(2)}) collective-permute-start(bf16[64,256]{1,0:T(8,128)(2,1)} %refs_0_), channel_id=1, source_target_pairs={{0,2},{1,3},{2,0},{3,1},{4,6},{5,7},{6,4},{7,5},{8,10},{9,11},{10,... | collective-permute-start | bytes 98312 | tf_op jit(solution)/shard_map/ppermute | solution.py:70
  5.6 7.8 %collective-permute-start.2 = (bf16[64,256]{1,0:T(8,128)(2,1)}, bf16[64,256]{1,0:T(8,128)(2,1)S(1)}, u32[]{:S(2)}, u32[]{:S(2)}) collective-permute-start(bf16[64,256]{1,0:T(8,128)(2,1)} %refs_0_), channel_id=1, source_target_pairs={{0,3},{1,0},{2,1},{3,2},{4,7},{5,4},{6,5},{7,6},{8,11},{9,8},{10,9... | collective-permute-start | bytes 98312 | tf_op jit(solution)/shard_map/ppermute | solution.py:70
  7.0 15.4 %collective-permute-start.6 = (bf16[1,1,3,4,4096]{4,3,2,1,0:T(4,128)(2,1)}, bf16[1,1,3,4,4096]{4,3,2,1,0:T(4,128)(2,1)S(1)}, u32[]{:S(2)}, u32[]{:S(2)}) collective-permute-start(bf16[1,1,3,4,4096]{4,3,2,1,0:T(4,128)(2,1)} %param.5), channel_id=1, source_target_pairs={{0,1},{1,2},{2,3},{3,0},{4,5},{5,6},{6,7},{7,4},{8,9},{9,10},{10,1... | collective-permute-start | bytes 294920 | tf_op jit(solution)/shard_map/ppermute | solution.py:71
  7.6 14.9 %collective-permute-start.7 = (bf16[1,1,3,4,4096]{4,3,2,1,0:T(4,128)(2,1)}, bf16[1,1,3,4,4096]{4,3,2,1,0:T(4,128)(2,1)S(1)}, u32[]{:S(2)}, u32[]{:S(2)}) collective-permute-start(bf16[1,1,3,4,4096]{4,3,2,1,0:T(4,128)(2,1)} %param.5), channel_id=1, source_target_pairs={{0,2},{1,3},{2,0},{3,1},{4,6},{5,7},{6,4},{7,5},{8,10},{9,11},{10,... | collective-permute-start | bytes 294920 | tf_op jit(solution)/shard_map/ppermute | solution.py:71
  8.6 0.7 %copy-start.2 = (s32[1,1,3]{2,1,0:T(1,128)S(1)}, s32[1,1,3]{2,1,0:T(1,128)}, u32[]{:S(2)}) copy-start(s32[1,1,3]{2,1,0:T(1,128)} %param.6) | copy-start | bytes 40
  9.3 1.2 %copy-start.1 = (bf16[1,1,3,4,4096]{4,3,2,1,0:T(4,128)(2,1)S(1)}, bf16[1,1,3,4,4096]{4,3,2,1,0:T(4,128)(2,1)}, u32[]{:S(2)}) copy-start(bf16[1,1,3,4,4096]{4,3,2,1,0:T(4,128)(2,1)} %param.5) | copy-start | bytes 294916
  9.3 6.2 %copy-start = (bf16[64,256]{1,0:T(8,128)(2,1)S(1)}, bf16[64,256]{1,0:T(8,128)(2,1)}, u32[]{:S(2)}) copy-start(bf16[64,256]{1,0:T(8,128)(2,1)} %refs_0_) | copy-start | bytes 98308
  10.5 12.3 %collective-permute-start.8 = (bf16[1,1,3,4,4096]{4,3,2,1,0:T(4,128)(2,1)S(1)}, bf16[1,1,3,4,4096]{4,3,2,1,0:T(4,128)(2,1)S(1)}, u32[]{:S(2)}, u32[]{:S(2)}) collective-permute-start(bf16[1,1,3,4,4096]{4,3,2,1,0:T(4,128)(2,1)S(1)} %copy-done.1), channel_id=1, source_target_pairs={{0,3},{1,0},{2,1},{3,2},{4,7},{5,4},{6,5},{7,6},{8,11},{9,8},{10,9... | collective-permute-start | bytes 294920 | tf_op jit(solution)/shard_map/ppermute | solution.py:71
  13.4 5.3 %collective-permute-start.3 = (s32[3]{0:T(128)S(1)}, s32[3]{0:T(128)S(1)}, u32[]{:S(2)}, u32[]{:S(2)}) collective-permute-start(s32[3]{0:T(128)S(1)} %compare_select_fusion.meta_ref), channel_id=1, source_target_pairs={{0,1},{1,2},{2,3},{3,0},{4,5},{5,6},{6,7},{7,4},{8,9},{9,10},{10,1... | collective-permute-start | bytes 44 | tf_op jit(solution)/shard_map/ppermute | solution.py:74
  14.0 5.2 %collective-permute-start.4 = (s32[3]{0:T(128)S(1)}, s32[3]{0:T(128)S(1)}, u32[]{:S(2)}, u32[]{:S(2)}) collective-permute-start(s32[3]{0:T(128)S(1)} %compare_select_fusion.meta_ref), channel_id=1, source_target_pairs={{0,2},{1,3},{2,0},{3,1},{4,6},{5,7},{6,4},{7,5},{8,10},{9,11},{10,... | collective-permute-start | bytes 44 | tf_op jit(solution)/shard_map/ppermute | solution.py:74
  18.7 3.5 %collective-permute-start.5 = (s32[3]{0:T(128)S(1)}, s32[3]{0:T(128)S(1)}, u32[]{:S(2)}, u32[]{:S(2)}) collective-permute-start(s32[3]{0:T(128)S(1)} %compare_select_fusion.meta_ref), channel_id=1, source_target_pairs={{0,3},{1,0},{2,1},{3,2},{4,7},{5,4},{6,5},{7,6},{8,11},{9,8},{10,9... | collective-permute-start | bytes 44 | tf_op jit(solution)/shard_map/ppermute | solution.py:74
  24.0 1.3 %collective-permute-start.9 = (f32[64,256]{1,0:T(8,128)S(1)}, f32[64,256]{1,0:T(8,128)S(1)}, u32[]{:S(2)}, u32[]{:S(2)}) collective-permute-start(f32[64,256]{1,0:T(8,128)S(1)} %exchange.1), channel_id=1, source_target_pairs={{0,4},{4,0},{8,12},{12,8},{16,20},{20,16},{24,28},{28,24},{1,5},{5... | collective-permute-start | bytes 196616 | tf_op jit(solution)/shard_map/ppermute | solution.py:103
  25.3 4.3 %collective-permute-start.10 = (f32[64,256]{1,0:T(8,128)S(1)}, f32[64,256]{1,0:T(8,128)S(1)}, u32[]{:S(2)}, u32[]{:S(2)}) collective-permute-start(f32[64,256]{1,0:T(8,128)S(1)} %add.12), channel_id=1, source_target_pairs={{0,8},{4,12},{8,0},{12,4},{16,24},{20,28},{24,16},{28,20},{1,9},{5... | collective-permute-start | bytes 196616 | tf_op jit(solution)/shard_map/ppermute | solution.py:103
  26.9 4.3 %collective-permute-start.11 = (f32[64,256]{1,0:T(8,128)S(1)}, f32[64,256]{1,0:T(8,128)S(1)}, u32[]{:S(2)}, u32[]{:S(2)}) collective-permute-start(f32[64,256]{1,0:T(8,128)S(1)} %add.12), channel_id=1, source_target_pairs={{0,16},{4,20},{8,24},{12,28},{16,0},{20,4},{24,8},{28,12},{1,17},{... | collective-permute-start | bytes 196616 | tf_op jit(solution)/shard_map/ppermute | solution.py:103
  28.4 5.2 %collective-permute-start.12 = (f32[64,256]{1,0:T(8,128)S(1)}, f32[64,256]{1,0:T(8,128)S(1)}, u32[]{:S(2)}, u32[]{:S(2)}) collective-permute-start(f32[64,256]{1,0:T(8,128)S(1)} %add.12), channel_id=1, source_target_pairs={{0,24},{4,28},{8,16},{12,20},{16,8},{20,12},{24,0},{28,4},{1,25},{... | collective-permute-start | bytes 196616 | tf_op jit(solution)/shard_map/ppermute | solution.py:103

commit v4 on v3

v4 whole, which is shorter than its diff:
```python
import functools

import jax
import jax.numpy as jnp
from jax import lax
from jax.experimental import pallas as pl
from jax.experimental.pallas import tpu as pltpu
from jax.sharding import PartitionSpec as P

BS = 64
LANES = 128
NOTE = 16


def send_to(i, way, count):
    return i ^ way if count & (count - 1) == 0 else (i + way) % count


def source_of(i, way, count):
    return i ^ way if count & (count - 1) == 0 else lax.rem(i - way + count, count)


def pack_kernel(
    orb, pairs_hbm, kept_hbm, density_hbm, blocks_hbm, out_ref, pairs, kept, rows, blocks, sems
):
    sources = (blocks_hbm, density_hbm, pairs_hbm, kept_hbm)
    targets = (blocks, rows, pairs, kept)
    copies = [
        pltpu.make_async_copy(src, dst, sems.at[i])
        for i, (src, dst) in enumerate(zip(sources, targets))
    ]
    for copy in copies:
        copy.start()
    for copy in copies:
        copy.wait()
    slots, aux_width = blocks.shape[2:4]
    square = blocks[0, 0].reshape(slots * aux_width, BS, BS)
    tile = 0
    for pair in range(0, slots * aux_width, 2):
        both = jnp.concatenate([square[pair], square[pair + 1]], axis=1)
        out_ref[tile * BS : (tile + 1) * BS] = both
        tile += 1
    for at in range(0, rows.shape[1], LANES):
        out_ref[tile * BS : (tile + 1) * BS] = rows[:, at : at + LANES]
        tile += 1
    shape = (NOTE, LANES)
    lane = lax.broadcasted_iota(jnp.int32, shape, 1)
    note = jnp.zeros(shape, jnp.int32)
    for j in range(slots):
        note = jnp.where(lane == j, jnp.where(j < kept[0, 0], pairs[0, 0, j], orb), note)
    out_ref[tile * BS :] = note.astype(jnp.float32).astype(jnp.bfloat16)


def exchange_kernel(orb, slots, aux_width, meta_ref, *refs):
    packs, (out_ref, rows, half_ref, held) = refs[:orb], refs[orb:]
    me = lax.axis_index("orb")
    full_width = out_ref.shape[1]
    per_slot = aux_width * BS // LANES

    def tiles(way, first, count):
        return [packs[way][t * BS : (t + 1) * BS] for t in range(first, first + count)]

    for way in range(orb):
        owner = source_of(me, way, orb)
        for t, part in enumerate(tiles(way, slots * per_slot, full_width // LANES)):
            rows[owner, :, t * LANES : (t + 1) * LANES] = part
    rows[orb] = jnp.zeros_like(rows[orb])
    selected = jnp.concatenate([rows[meta_ref[j]] for j in range(slots)], axis=0)
    own = jnp.concatenate(tiles(0, 0, slots * per_slot), axis=1)
    left = []
    for p in range(aux_width):
        cuts = [(j * aux_width + p) * BS for j in range(slots)]
        left.append(jnp.concatenate([own[:, cut : cut + BS] for cut in cuts], axis=1))
    left = jnp.concatenate(left, axis=0)
    half = jnp.dot(left, selected, preferred_element_type=jnp.float32).astype(jnp.bfloat16)
    for k in range(orb):
        half_ref[k] = jnp.concatenate(
            [half[p * BS : (p + 1) * BS, k * BS : (k + 1) * BS] for p in range(aux_width)],
            axis=1,
        )
    half_ref[orb] = jnp.zeros_like(half_ref[orb])
    for way in range(orb):
        total = None
        for j in range(slots):
            term = lax.dot_general(
                half_ref[meta_ref[way * slots + j]],
                jnp.concatenate(tiles(way, j * per_slot, per_slot), axis=1),
                (((1,), (1,)), ((), ())),
                preferred_element_type=jnp.float32,
            )
            total = term if total is None else total + term
        held[source_of(me, way, orb)] = total
    out_ref[...] = jnp.concatenate([held[n] for n in range(orb)], axis=1)


def shards(density, tensor_blocks, pairs, kept):
    full_width = density.shape[1]
    slots = tensor_blocks.shape[2]
    aux_width = tensor_blocks.shape[3]
    orb = lax.axis_size("orb")
    aux = lax.axis_size("aux")
    size = (slots * aux_width * BS + full_width) // LANES * BS
    vmem = pl.BlockSpec(memory_space=pltpu.VMEM)
    smem = pl.BlockSpec(memory_space=pltpu.SMEM)
    params = pltpu.CompilerParams(vmem_limit_bytes=32 * 1024 * 1024)

    packed = pl.pallas_call(
        functools.partial(pack_kernel, orb),
        out_shape=jax.ShapeDtypeStruct((size + NOTE, LANES), jnp.bfloat16),
        in_specs=[pl.BlockSpec(memory_space=pltpu.HBM)] * 4,
        out_specs=vmem,
        scratch_shapes=[
            pltpu.SMEM(pairs.shape, jnp.int32),
            pltpu.SMEM(kept.shape, jnp.int32),
            pltpu.VMEM(density.shape, jnp.bfloat16),
            pltpu.VMEM(tensor_blocks.shape, jnp.bfloat16),
            pltpu.SemaphoreType.DMA((4,)),
        ],
        compiler_params=params,
        name="pack",
    )(pairs, kept, density, tensor_blocks)
    packs = [packed]
    for way in range(1, orb):
        packs.append(lax.ppermute(packed, "orb", [(i, send_to(i, way, orb)) for i in range(orb)]))
    codes = jnp.concatenate([pack[size, :slots] for pack in packs]).astype(jnp.int32)

    parts = pl.pallas_call(
        functools.partial(exchange_kernel, orb, slots, aux_width),
        out_shape=jax.ShapeDtypeStruct((BS, full_width), jnp.float32),
        in_specs=[smem] + [vmem] * orb,
        out_specs=vmem,
        scratch_shapes=[
            pltpu.VMEM((orb + 1, BS, full_width), jnp.bfloat16),
            pltpu.VMEM((orb + 1, BS, aux_width * BS), jnp.bfloat16),
            pltpu.VMEM((orb, BS, BS), jnp.float32),
        ],
        compiler_params=params,
        name="exchange",
    )(codes, *packs)

    step = 1
    while step < aux:
        ways = 2 if step == 1 or step * 4 > aux else 4
        terms = [parts]
        for way in range(1, ways):
            terms.append(lax.ppermute(parts, "aux", [(i, i ^ (way * step)) for i in range(aux)]))
        while len(terms) > 1:
            terms = [terms[i] + terms[i + 1] for i in range(0, len(terms), 2)]
        parts = terms[0]
        step *= ways
    return parts


def solution(mesh):
    return jax.shard_map(
        shards,
        mesh=mesh,
        in_specs=(
            P("orb", None),
            P("orb", "aux", None, None, None),
            P("orb", "aux", None),
            P("orb", "aux"),
        ),
        out_specs=P("orb", None),
        check_vma=False,
    )
```

time: 34.4 us -> 30.6 us (0.89)
  starting transfers between devices: 17.1 us -> 9.38 us
  waiting for transfers between devices: 11.4 us -> 15.8 us
  local copies, waits for them, and re-layouts: 2.47 us -> 1.65 us
  Pallas kernels: 1.79 us -> 2.16 us
    ppermute x9 -> x3, starting transfers between devices: 13.5 us -> 5.76 us  [shards(): lax.ppermute(packed, 'orb', [(i, send_to(i, way, orb)) for i in range(orb)])]
    ppermute x9 -> x3, waiting for transfers between devices: 5.43 us -> 10.8 us  [shards(): lax.ppermute(packed, 'orb', [(i, send_to(i, way, orb)) for i in range(orb)])]
    reshape x4 -> x0, local copies, waits for them, and re-layouts: 1.81 us -> none  [shards(): blocks = [b.reshape(slots, aux_width, width, width) for b in blocks]]
    unnamed x6, local copies, waits for them, and re-layouts: 0.66 us -> 1.65 us
    ppermute x4, waiting for transfers between devices: 5.93 us -> 4.97 us  [shards(): lax.ppermute(parts, 'aux', [(i, i ^ way * step) for i in range(aux)])]
  transfers between devices with their start and end apart: 13 -> 7, of which waited for: 6 -> 6; matrix products, arithmetic and copies ran while one was open for 5% -> 0% of each run, Pallas kernels for 2% -> 0%
where the time goes in v4:
time: 30.6 us; the launch traced here: 30.4 us
  waiting for transfers between devices  15.8 us (52%)
  starting transfers between devices  9.38 us (31%)
  Pallas kernels  2.16 us (7%)
  local copies, waits for them, and re-layouts  1.65 us (5%)
  other arithmetic  0.74 us (2%)
  between operations  0.72 us (2%)
    ppermute x3, waiting for transfers between devices, shards(): lax.ppermute(packed, 'orb', [(i, send_to(i, way, orb)) for i in range(orb)])  10.8 us
    ppermute x3, starting transfers between devices, shards(): lax.ppermute(packed, 'orb', [(i, send_to(i, way, orb)) for i in range(orb)])  5.76 us
    ppermute x4, waiting for transfers between devices, shards(): lax.ppermute(parts, 'aux', [(i, i ^ way * step) for i in range(aux)])  4.97 us
    ppermute x4, starting transfers between devices, shards(): lax.ppermute(parts, 'aux', [(i, i ^ way * step) for i in range(aux)])  3.62 us
    unnamed x6, local copies, waits for them, and re-layouts  1.65 us
    pallas_call x1, Pallas kernels, shards(): pl.pallas_call(functools.partial(exchange_kernel, orb, slots, aux_width),...  1.21 us
    pallas_call x1, Pallas kernels, shards(): pl.pallas_call(functools.partial(pack_kernel, orb), out_shape=jax.ShapeDt...  0.95 us
    add x2, other arithmetic, shards(): terms = [terms[i] + terms[i + 1] for i in range(0, len(terms), 2)]  0.66 us
  transfers between devices with their start and end apart: 7, of which 6 were waited for; matrix products, arithmetic and copies ran while one was open for 0% of the time, Pallas kernels for 0%

profile of v4, /device:TPU:0, one launch (start us, length us, event | category | flops | bytes accessed | tf_op | source)
XLA Modules:
  0.0 30.4 jit_solution(9038267124517347410)
XLA Ops:
  0.0 0.0 copy-start.2
  0.7 0.0 copy-done.2
  0.7 0.0 copy-start
  0.7 0.9 %copy-done = bf16[1,1,3,4,4096]{4,3,2,1,0:T(4,128)(2,1)S(1)} copy-done((bf16[1,1,3,4,4096]{4,3,2,1,0:T(4,128)(2,1)S(1)}, bf16[1,1,3,4,4096]{4,3,2,1,0:T(4,128)(2,1)}, u32[]{:S(2)}) %copy-start) | copy-done | bytes 98328
  1.6 0.0 copy-start.1
  1.6 0.8 %copy-done.1 = bf16[64,256]{1,0:T(8,128)(2,1)S(1)} copy-done((bf16[64,256]{1,0:T(8,128)(2,1)S(1)}, bf16[64,256]{1,0:T(8,128)(2,1)}, u32[]{:S(2)}) %copy-start.1) | copy-done | bytes 32792
  2.3 0.9 %pack.1.refs_0_ = bf16[528,128]{1,0:T(8,128)(2,1)S(1)} custom-call(s32[1,1,3]{2,1,0:T(1,128)S(1)} %copy-done.2, s32[1,1]{1,0:T(1,128)S(6)} %copy.5.kept_hbm, bf16[64,256]{1,0:T(8,128)(2,1)S(1)} %copy-done.1, bf16[1,1,3,4,4096]{4,3,2,1,0:T(4,128)(2,1)S(1)} %copy-done), custom_call_target="tpu_custom_call" | custom-call | tf_op jit(solution)/shard_map/pack/pallas_call | solution.py:107
  3.3 5.1 %collective-permute-start.2 = (bf16[528,128]{1,0:T(8,128)(2,1)S(1)}, bf16[528,128]{1,0:T(8,128)(2,1)S(1)}, u32[]{:S(2)}, u32[]{:S(2)}) collective-permute-start(bf16[528,128]{1,0:T(8,128)(2,1)S(1)} %pack.1.refs_0_), channel_id=1, source_target_pairs={{0,3},{1,2},{2,1},{3,0},{4,7},{5,6},{6,5},{7,4},{8,11},{9,10},{10,... | collective-permute-start | bytes 405512 | tf_op jit(solution)/shard_map/ppermute | solution.py:124
  8.4 0.0 collective-permute-start.1
  8.4 0.6 %collective-permute-start = (bf16[528,128]{1,0:T(8,128)(2,1)S(1)}, bf16[528,128]{1,0:T(8,128)(2,1)S(1)}, u32[]{:S(2)}, u32[]{:S(2)}) collective-permute-start(bf16[528,128]{1,0:T(8,128)(2,1)S(1)} %pack.1.refs_0_), channel_id=1, source_target_pairs={{0,1},{1,0},{2,3},{3,2},{4,5},{5,4},{6,7},{7,6},{8,9},{9,8},{10,11... | collective-permute-start | bytes 405512 | tf_op jit(solution)/shard_map/ppermute | solution.py:124
  9.0 3.9 %collective-permute-done.2.refs_3_ = bf16[528,128]{1,0:T(8,128)(2,1)S(1)} collective-permute-done((bf16[528,128]{1,0:T(8,128)(2,1)S(1)}, bf16[528,128]{1,0:T(8,128)(2,1)S(1)}, u32[]{:S(2)}, u32[]{:S(2)}) %collective-permute-start.2) | collective-permute-done | bytes 135200 | tf_op jit(solution)/shard_map/ppermute | solution.py:124
  12.9 6.9 %collective-permute-done.1.refs_2_ = bf16[528,128]{1,0:T(8,128)(2,1)S(1)} collective-permute-done((bf16[528,128]{1,0:T(8,128)(2,1)S(1)}, bf16[528,128]{1,0:T(8,128)(2,1)S(1)}, u32[]{:S(2)}, u32[]{:S(2)}) %collective-permute-start.1) | collective-permute-done | bytes 135200 | tf_op jit(solution)/shard_map/ppermute | solution.py:124
  19.8 0.0 collective-permute-done.refs_1_
  19.8 0.1 maximum_convert_fusion.meta_ref
  19.9 1.2 %exchange.1 = f32[64,256]{1,0:T(8,128)S(1)} custom-call(s32[12]{0:T(128)S(1)} %maximum_convert_fusion.meta_ref, bf16[528,128]{1,0:T(8,128)(2,1)S(1)} %pack.1.refs_0_, bf16[528,128]{1,0:T(8,128)(2,1)S(1)} %collective-permute-done.refs_1_, bf16[528,128]{1,0:T(8,128)(2,1)S(1)} %collective-permute-done.1.refs_2_, bf16[528,128]{1,0:T(8,128)(2,1)S(1)} %collective-permute-done.2.refs_3_), custom_call_target="tpu_custom_call" | custom-call | tf_op jit(solution)/shard_map/exchange/pallas_call | solution.py:127
  21.1 0.1 collective-permute-start.3
  21.2 1.2 %collective-permute-done.3 = f32[64,256]{1,0:T(8,128)S(1)} collective-permute-done((f32[64,256]{1,0:T(8,128)S(1)}, f32[64,256]{1,0:T(8,128)S(1)}, u32[]{:S(2)}, u32[]{:S(2)}) %collective-permute-start.3) | collective-permute-done | bytes 65568 | tf_op jit(solution)/shard_map/ppermute | solution.py:146
  22.5 2.5 %collective-permute-start.6 = (f32[64,256]{1,0:T(8,128)S(1)}, f32[64,256]{1,0:T(8,128)S(1)}, u32[]{:S(2)}, u32[]{:S(2)}) collective-permute-start(f32[64,256]{1,0:T(8,128)S(1)} %add.12), channel_id=1, source_target_pairs={{0,24},{4,28},{8,16},{12,20},{16,8},{20,12},{24,0},{28,4},{1,25},{... | collective-permute-start | bytes 196616 | tf_op jit(solution)/shard_map/ppermute | solution.py:146
  25.0 0.5 %collective-permute-start.5 = (f32[64,256]{1,0:T(8,128)S(1)}, f32[64,256]{1,0:T(8,128)S(1)}, u32[]{:S(2)}, u32[]{:S(2)}) collective-permute-start(f32[64,256]{1,0:T(8,128)S(1)} %add.12), channel_id=1, source_target_pairs={{0,16},{4,20},{8,24},{12,28},{16,0},{20,4},{24,8},{28,12},{1,17},{... | collective-permute-start | bytes 196616 | tf_op jit(solution)/shard_map/ppermute | solution.py:146
  25.5 0.5 %collective-permute-start.4 = (f32[64,256]{1,0:T(8,128)S(1)}, f32[64,256]{1,0:T(8,128)S(1)}, u32[]{:S(2)}, u32[]{:S(2)}) collective-permute-start(f32[64,256]{1,0:T(8,128)S(1)} %add.12), channel_id=1, source_target_pairs={{0,8},{4,12},{8,0},{12,4},{16,24},{20,28},{24,16},{28,20},{1,9},{5... | collective-permute-start | bytes 196616 | tf_op jit(solution)/shard_map/ppermute | solution.py:146
  26.0 1.7 %collective-permute-done.6 = f32[64,256]{1,0:T(8,128)S(1)} collective-permute-done((f32[64,256]{1,0:T(8,128)S(1)}, f32[64,256]{1,0:T(8,128)S(1)}, u32[]{:S(2)}, u32[]{:S(2)}) %collective-permute-start.6) | collective-permute-done | bytes 65568 | tf_op jit(solution)/shard_map/ppermute | solution.py:146
  27.7 1.5 %collective-permute-done.5 = f32[64,256]{1,0:T(8,128)S(1)} collective-permute-done((f32[64,256]{1,0:T(8,128)S(1)}, f32[64,256]{1,0:T(8,128)S(1)}, u32[]{:S(2)}, u32[]{:S(2)}) %collective-permute-start.5) | collective-permute-done | bytes 65568 | tf_op jit(solution)/shard_map/ppermute | solution.py:146
  29.2 0.5 %collective-permute-done.4 = f32[64,256]{1,0:T(8,128)S(1)} collective-permute-done((f32[64,256]{1,0:T(8,128)S(1)}, f32[64,256]{1,0:T(8,128)S(1)}, u32[]{:S(2)}, u32[]{:S(2)}) %collective-permute-start.4) | collective-permute-done | bytes 65568 | tf_op jit(solution)/shard_map/ppermute | solution.py:146
  29.8 0.6 %add_add_fusion = f32[64,256]{1,0:T(8,128)} fusion(f32[64,256]{1,0:T(8,128)S(1)} %collective-permute-done.5, f32[64,256]{1,0:T(8,128)S(1)} %collective-permute-done.6, f32[64,256]{1,0:T(8,128)S(1)} %add.12, f32[64,256]{1,0:T(8,128)S(1)} %collective-permute-done.4), kind=kLoop, calls=%fused_computation | loop fusion | flops 49152 | bytes 327680 | tf_op jit(solution)/shard_map/add | solution.py:148
  (5 shorter events, 0.0 us)
Async XLA Ops:
  0.0 0.7 %copy-start.2 = (s32[1,1,3]{2,1,0:T(1,128)S(1)}, s32[1,1,3]{2,1,0:T(1,128)}, u32[]{:S(2)}) copy-start(s32[1,1,3]{2,1,0:T(1,128)} %pairs_hbm.1) | copy-start | bytes 40
  0.7 0.9 %copy-start = (bf16[1,1,3,4,4096]{4,3,2,1,0:T(4,128)(2,1)S(1)}, bf16[1,1,3,4,4096]{4,3,2,1,0:T(4,128)(2,1)}, u32[]{:S(2)}) copy-start(bf16[1,1,3,4,4096]{4,3,2,1,0:T(4,128)(2,1)} %blocks_hbm.1) | copy-start | bytes 294916
  1.6 0.8 %copy-start.1 = (bf16[64,256]{1,0:T(8,128)(2,1)S(1)}, bf16[64,256]{1,0:T(8,128)(2,1)}, u32[]{:S(2)}) copy-start(bf16[64,256]{1,0:T(8,128)(2,1)} %density_hbm.1) | copy-start | bytes 98308
  3.3 9.6 %collective-permute-start.2 = (bf16[528,128]{1,0:T(8,128)(2,1)S(1)}, bf16[528,128]{1,0:T(8,128)(2,1)S(1)}, u32[]{:S(2)}, u32[]{:S(2)}) collective-permute-start(bf16[528,128]{1,0:T(8,128)(2,1)S(1)} %pack.1.refs_0_), channel_id=1, source_target_pairs={{0,3},{1,2},{2,1},{3,0},{4,7},{5,6},{6,5},{7,4},{8,11},{9,10},{10,... | collective-permute-start | bytes 405512 | tf_op jit(solution)/shard_map/ppermute | solution.py:124
  8.4 11.4 %collective-permute-start.1 = (bf16[528,128]{1,0:T(8,128)(2,1)S(1)}, bf16[528,128]{1,0:T(8,128)(2,1)S(1)}, u32[]{:S(2)}, u32[]{:S(2)}) collective-permute-start(bf16[528,128]{1,0:T(8,128)(2,1)S(1)} %pack.1.refs_0_), channel_id=1, source_target_pairs={{0,2},{1,3},{2,0},{3,1},{4,6},{5,7},{6,4},{7,5},{8,10},{9,11},{10,... | collective-permute-start | bytes 405512 | tf_op jit(solution)/shard_map/ppermute | solution.py:124
  8.4 11.4 %collective-permute-start = (bf16[528,128]{1,0:T(8,128)(2,1)S(1)}, bf16[528,128]{1,0:T(8,128)(2,1)S(1)}, u32[]{:S(2)}, u32[]{:S(2)}) collective-permute-start(bf16[528,128]{1,0:T(8,128)(2,1)S(1)} %pack.1.refs_0_), channel_id=1, source_target_pairs={{0,1},{1,0},{2,3},{3,2},{4,5},{5,4},{6,7},{7,6},{8,9},{9,8},{10,11... | collective-permute-start | bytes 405512 | tf_op jit(solution)/shard_map/ppermute | solution.py:124
  21.1 1.3 %collective-permute-start.3 = (f32[64,256]{1,0:T(8,128)S(1)}, f32[64,256]{1,0:T(8,128)S(1)}, u32[]{:S(2)}, u32[]{:S(2)}) collective-permute-start(f32[64,256]{1,0:T(8,128)S(1)} %exchange.1), channel_id=1, source_target_pairs={{0,4},{4,0},{8,12},{12,8},{16,20},{20,16},{24,28},{28,24},{1,5},{5... | collective-permute-start | bytes 196616 | tf_op jit(solution)/shard_map/ppermute | solution.py:146
  22.5 5.3 %collective-permute-start.6 = (f32[64,256]{1,0:T(8,128)S(1)}, f32[64,256]{1,0:T(8,128)S(1)}, u32[]{:S(2)}, u32[]{:S(2)}) collective-permute-start(f32[64,256]{1,0:T(8,128)S(1)} %add.12), channel_id=1, source_target_pairs={{0,24},{4,28},{8,16},{12,20},{16,8},{20,12},{24,0},{28,4},{1,25},{... | collective-permute-start | bytes 196616 | tf_op jit(solution)/shard_map/ppermute | solution.py:146
  25.0 4.3 %collective-permute-start.5 = (f32[64,256]{1,0:T(8,128)S(1)}, f32[64,256]{1,0:T(8,128)S(1)}, u32[]{:S(2)}, u32[]{:S(2)}) collective-permute-start(f32[64,256]{1,0:T(8,128)S(1)} %add.12), channel_id=1, source_target_pairs={{0,16},{4,20},{8,24},{12,28},{16,0},{20,4},{24,8},{28,12},{1,17},{... | collective-permute-start | bytes 196616 | tf_op jit(solution)/shard_map/ppermute | solution.py:146
  25.5 4.3 %collective-permute-start.4 = (f32[64,256]{1,0:T(8,128)S(1)}, f32[64,256]{1,0:T(8,128)S(1)}, u32[]{:S(2)}, u32[]{:S(2)}) collective-permute-start(f32[64,256]{1,0:T(8,128)S(1)} %add.12), channel_id=1, source_target_pairs={{0,8},{4,12},{8,0},{12,4},{16,24},{20,28},{24,16},{28,20},{1,9},{5... | collective-permute-start | bytes 196616 | tf_op jit(solution)/shard_map/ppermute | solution.py:146

commit v5 on v4

--- a/solution.py
+++ b/solution.py
@@ -12,22 +12,12 @@
 NOTE = 16
 
 
-def send_to(i, way, count):
-    return i ^ way if count & (count - 1) == 0 else (i + way) % count
-
-
-def source_of(i, way, count):
-    return i ^ way if count & (count - 1) == 0 else lax.rem(i - way + count, count)
-
-
-def pack_kernel(
-    orb, pairs_hbm, kept_hbm, density_hbm, blocks_hbm, out_ref, pairs, kept, rows, blocks, sems
-):
-    sources = (blocks_hbm, density_hbm, pairs_hbm, kept_hbm)
-    targets = (blocks, rows, pairs, kept)
+def pack_kernel(orb, kept, pairs_hbm, density_hbm, blocks_hbm, out_ref, pairs, rows, blocks, sems):
     copies = [
         pltpu.make_async_copy(src, dst, sems.at[i])
-        for i, (src, dst) in enumerate(zip(sources, targets))
+        for i, (src, dst) in enumerate(
+            ((blocks_hbm, blocks), (density_hbm, rows), (pairs_hbm, pairs))
+        )
     ]
     for copy in copies:
         copy.start()
@@ -61,7 +51,7 @@
         return [packs[way][t * BS : (t + 1) * BS] for t in range(first, first + count)]
 
     for way in range(orb):
-        owner = source_of(me, way, orb)
+        owner = lax.rem(me - way + orb, orb)
         for t, part in enumerate(tiles(way, slots * per_slot, full_width // LANES)):
             rows[owner, :, t * LANES : (t + 1) * LANES] = part
     rows[orb] = jnp.zeros_like(rows[orb])
@@ -89,7 +79,7 @@
                 preferred_element_type=jnp.float32,
             )
             total = term if total is None else total + term
-        held[source_of(me, way, orb)] = total
+        held[lax.rem(me - way + orb, orb)] = total
     out_ref[...] = jnp.concatenate([held[n] for n in range(orb)], axis=1)
 
 
@@ -107,21 +97,20 @@
     packed = pl.pallas_call(
         functools.partial(pack_kernel, orb),
         out_shape=jax.ShapeDtypeStruct((size + NOTE, LANES), jnp.bfloat16),
-        in_specs=[pl.BlockSpec(memory_space=pltpu.HBM)] * 4,
+        in_specs=[smem] + [pl.BlockSpec(memory_space=pltpu.HBM)] * 3,
         out_specs=vmem,
         scratch_shapes=[
             pltpu.SMEM(pairs.shape, jnp.int32),
-            pltpu.SMEM(kept.shape, jnp.int32),
             pltpu.VMEM(density.shape, jnp.bfloat16),
             pltpu.VMEM(tensor_blocks.shape, jnp.bfloat16),
-            pltpu.SemaphoreType.DMA((4,)),
+            pltpu.SemaphoreType.DMA((3,)),
         ],
         compiler_params=params,
         name="pack",
-    )(pairs, kept, density, tensor_blocks)
+    )(kept, *(pltpu.with_memory_space_constraint(a, pltpu.HBM) for a in (pairs, density, tensor_blocks)))
     packs = [packed]
     for way in range(1, orb):
-        packs.append(lax.ppermute(packed, "orb", [(i, send_to(i, way, orb)) for i in range(orb)]))
+        packs.append(lax.ppermute(packed, "orb", [(i, (i + way) % orb) for i in range(orb)]))
     codes = jnp.concatenate([pack[size, :slots] for pack in packs]).astype(jnp.int32)
 
     parts = pl.pallas_call(

time: 30.6 us -> 29.2 us (0.954)
  local copies, waits for them, and re-layouts: 1.65 us -> 0.01 us
  starting transfers between devices: 9.38 us -> 9.74 us
    unnamed x6 -> x0, local copies, waits for them, and re-layouts: 1.65 us -> none
    ppermute x3, starting transfers between devices: 5.76 us -> 6.11 us  [shards(): lax.ppermute(packed, 'orb', [(i, (i + way) % orb) for i in range(orb)])]
where the time goes in v5:
time: 29.2 us; the launch traced here: 29 us
  waiting for transfers between devices  15.5 us (53%)
  starting transfers between devices  9.74 us (33%)
  Pallas kernels  2.36 us (8%)
  other arithmetic  0.74 us (3%)
  between operations  0.69 us (2%)
    ppermute x3, waiting for transfers between devices, shards(): lax.ppermute(packed, 'orb', [(i, (i + way) % orb) for i in range(orb)])  10.5 us
    ppermute x3, starting transfers between devices, shards(): lax.ppermute(packed, 'orb', [(i, (i + way) % orb) for i in range(orb)])  6.11 us
    ppermute x4, waiting for transfers between devices, shards(): lax.ppermute(parts, 'aux', [(i, i ^ way * step) for i in range(aux)])  4.97 us
    ppermute x4, starting transfers between devices, shards(): lax.ppermute(parts, 'aux', [(i, i ^ way * step) for i in range(aux)])  3.62 us
    pallas_call x1, Pallas kernels, shards(): pl.pallas_call(functools.partial(exchange_kernel, orb, slots, aux_width),...  1.21 us
    pallas_call x1, Pallas kernels, shards(): pl.pallas_call(functools.partial(pack_kernel, orb), out_shape=jax.ShapeDt...  1.15 us
    add x2, other arithmetic, shards(): terms = [terms[i] + terms[i + 1] for i in range(0, len(terms), 2)]  0.66 us
  transfers between devices with their start and end apart: 7, of which 6 were waited for; matrix products, arithmetic and copies ran while one was open for 0% of the time, Pallas kernels for 0%

profile of v5, /device:TPU:0, one launch (start us, length us, event | category | flops | bytes accessed | tf_op | source)
XLA Modules:
  0.0 29.0 jit_solution(16386894783885066365)
XLA Ops:
  0.7 1.2 %pack.1.refs_0_ = bf16[528,128]{1,0:T(8,128)(2,1)S(1)} custom-call(s32[1,1]{1,0:T(1,128)S(6)} %copy.5.kept, s32[1,1,3]{2,1,0:T(1,128)} %pairs_hbm.1, bf16[64,256]{1,0:T(8,128)(2,1)} %density_hbm.1, bf16[1,1,3,4,4096]{4,3,2,1,0:T(4,128)(2,1)} %blocks_hbm.1), custom_call_target="tpu_custom_call" | custom-call | tf_op jit(solution)/shard_map/pack/pallas_call | solution.py:97
  1.8 5.1 %collective-permute-start.2 = (bf16[528,128]{1,0:T(8,128)(2,1)S(1)}, bf16[528,128]{1,0:T(8,128)(2,1)S(1)}, u32[]{:S(2)}, u32[]{:S(2)}) collective-permute-start(bf16[528,128]{1,0:T(8,128)(2,1)S(1)} %pack.1.refs_0_), channel_id=1, source_target_pairs={{0,3},{1,0},{2,1},{3,2},{4,7},{5,4},{6,5},{7,6},{8,11},{9,8},{10,9... | collective-permute-start | bytes 405512 | tf_op jit(solution)/shard_map/ppermute | solution.py:113
  6.9 0.0 collective-permute-start.1
  6.9 1.0 %collective-permute-start = (bf16[528,128]{1,0:T(8,128)(2,1)S(1)}, bf16[528,128]{1,0:T(8,128)(2,1)S(1)}, u32[]{:S(2)}, u32[]{:S(2)}) collective-permute-start(bf16[528,128]{1,0:T(8,128)(2,1)S(1)} %pack.1.refs_0_), channel_id=1, source_target_pairs={{0,1},{1,2},{2,3},{3,0},{4,5},{5,6},{6,7},{7,4},{8,9},{9,10},{10,1... | collective-permute-start | bytes 405512 | tf_op jit(solution)/shard_map/ppermute | solution.py:113
  7.9 3.0 %collective-permute-done.2.refs_3_ = bf16[528,128]{1,0:T(8,128)(2,1)S(1)} collective-permute-done((bf16[528,128]{1,0:T(8,128)(2,1)S(1)}, bf16[528,128]{1,0:T(8,128)(2,1)S(1)}, u32[]{:S(2)}, u32[]{:S(2)}) %collective-permute-start.2) | collective-permute-done | bytes 135200 | tf_op jit(solution)/shard_map/ppermute | solution.py:113
  10.9 7.5 %collective-permute-done.1.refs_2_ = bf16[528,128]{1,0:T(8,128)(2,1)S(1)} collective-permute-done((bf16[528,128]{1,0:T(8,128)(2,1)S(1)}, bf16[528,128]{1,0:T(8,128)(2,1)S(1)}, u32[]{:S(2)}, u32[]{:S(2)}) %collective-permute-start.1) | collective-permute-done | bytes 135200 | tf_op jit(solution)/shard_map/ppermute | solution.py:113
  18.4 0.0 collective-permute-done.refs_1_
  18.4 0.1 maximum_convert_fusion.meta_ref
  18.5 1.2 %exchange.1 = f32[64,256]{1,0:T(8,128)S(1)} custom-call(s32[12]{0:T(128)S(1)} %maximum_convert_fusion.meta_ref, bf16[528,128]{1,0:T(8,128)(2,1)S(1)} %pack.1.refs_0_, bf16[528,128]{1,0:T(8,128)(2,1)S(1)} %collective-permute-done.refs_1_, bf16[528,128]{1,0:T(8,128)(2,1)S(1)} %collective-permute-done.1.refs_2_, bf16[528,128]{1,0:T(8,128)(2,1)S(1)} %collective-permute-done.2.refs_3_), custom_call_target="tpu_custom_call" | custom-call | tf_op jit(solution)/shard_map/exchange/pallas_call | solution.py:116
  19.7 0.1 collective-permute-start.3
  19.8 1.2 %collective-permute-done.3 = f32[64,256]{1,0:T(8,128)S(1)} collective-permute-done((f32[64,256]{1,0:T(8,128)S(1)}, f32[64,256]{1,0:T(8,128)S(1)}, u32[]{:S(2)}, u32[]{:S(2)}) %collective-permute-start.3) | collective-permute-done | bytes 65568 | tf_op jit(solution)/shard_map/ppermute | solution.py:135
  21.1 2.5 %collective-permute-start.6 = (f32[64,256]{1,0:T(8,128)S(1)}, f32[64,256]{1,0:T(8,128)S(1)}, u32[]{:S(2)}, u32[]{:S(2)}) collective-permute-start(f32[64,256]{1,0:T(8,128)S(1)} %add.12), channel_id=1, source_target_pairs={{0,24},{4,28},{8,16},{12,20},{16,8},{20,12},{24,0},{28,4},{1,25},{... | collective-permute-start | bytes 196616 | tf_op jit(solution)/shard_map/ppermute | solution.py:135
  23.6 0.5 %collective-permute-start.5 = (f32[64,256]{1,0:T(8,128)S(1)}, f32[64,256]{1,0:T(8,128)S(1)}, u32[]{:S(2)}, u32[]{:S(2)}) collective-permute-start(f32[64,256]{1,0:T(8,128)S(1)} %add.12), channel_id=1, source_target_pairs={{0,16},{4,20},{8,24},{12,28},{16,0},{20,4},{24,8},{28,12},{1,17},{... | collective-permute-start | bytes 196616 | tf_op jit(solution)/shard_map/ppermute | solution.py:135
  24.1 0.5 %collective-permute-start.4 = (f32[64,256]{1,0:T(8,128)S(1)}, f32[64,256]{1,0:T(8,128)S(1)}, u32[]{:S(2)}, u32[]{:S(2)}) collective-permute-start(f32[64,256]{1,0:T(8,128)S(1)} %add.12), channel_id=1, source_target_pairs={{0,8},{4,12},{8,0},{12,4},{16,24},{20,28},{24,16},{28,20},{1,9},{5... | collective-permute-start | bytes 196616 | tf_op jit(solution)/shard_map/ppermute | solution.py:135
  24.6 1.7 %collective-permute-done.6 = f32[64,256]{1,0:T(8,128)S(1)} collective-permute-done((f32[64,256]{1,0:T(8,128)S(1)}, f32[64,256]{1,0:T(8,128)S(1)}, u32[]{:S(2)}, u32[]{:S(2)}) %collective-permute-start.6) | collective-permute-done | bytes 65568 | tf_op jit(solution)/shard_map/ppermute | solution.py:135
  26.3 1.5 %collective-permute-done.5 = f32[64,256]{1,0:T(8,128)S(1)} collective-permute-done((f32[64,256]{1,0:T(8,128)S(1)}, f32[64,256]{1,0:T(8,128)S(1)}, u32[]{:S(2)}, u32[]{:S(2)}) %collective-permute-start.5) | collective-permute-done | bytes 65568 | tf_op jit(solution)/shard_map/ppermute | solution.py:135
  27.8 0.5 %collective-permute-done.4 = f32[64,256]{1,0:T(8,128)S(1)} collective-permute-done((f32[64,256]{1,0:T(8,128)S(1)}, f32[64,256]{1,0:T(8,128)S(1)}, u32[]{:S(2)}, u32[]{:S(2)}) %collective-permute-start.4) | collective-permute-done | bytes 65568 | tf_op jit(solution)/shard_map/ppermute | solution.py:135
  28.3 0.6 %add_add_fusion = f32[64,256]{1,0:T(8,128)} fusion(f32[64,256]{1,0:T(8,128)S(1)} %collective-permute-done.5, f32[64,256]{1,0:T(8,128)S(1)} %collective-permute-done.6, f32[64,256]{1,0:T(8,128)S(1)} %add.12, f32[64,256]{1,0:T(8,128)S(1)} %collective-permute-done.4), kind=kLoop, calls=%fused_computation | loop fusion | flops 49152 | bytes 327680 | tf_op jit(solution)/shard_map/add | solution.py:137
  (5 shorter events, 0.0 us)
Async XLA Ops:
  1.8 9.1 %collective-permute-start.2 = (bf16[528,128]{1,0:T(8,128)(2,1)S(1)}, bf16[528,128]{1,0:T(8,128)(2,1)S(1)}, u32[]{:S(2)}, u32[]{:S(2)}) collective-permute-start(bf16[528,128]{1,0:T(8,128)(2,1)S(1)} %pack.1.refs_0_), channel_id=1, source_target_pairs={{0,3},{1,0},{2,1},{3,2},{4,7},{5,4},{6,5},{7,6},{8,11},{9,8},{10,9... | collective-permute-start | bytes 405512 | tf_op jit(solution)/shard_map/ppermute | solution.py:113
  6.9 11.5 %collective-permute-start.1 = (bf16[528,128]{1,0:T(8,128)(2,1)S(1)}, bf16[528,128]{1,0:T(8,128)(2,1)S(1)}, u32[]{:S(2)}, u32[]{:S(2)}) collective-permute-start(bf16[528,128]{1,0:T(8,128)(2,1)S(1)} %pack.1.refs_0_), channel_id=1, source_target_pairs={{0,2},{1,3},{2,0},{3,1},{4,6},{5,7},{6,4},{7,5},{8,10},{9,11},{10,... | collective-permute-start | bytes 405512 | tf_op jit(solution)/shard_map/ppermute | solution.py:113
  6.9 11.5 %collective-permute-start = (bf16[528,128]{1,0:T(8,128)(2,1)S(1)}, bf16[528,128]{1,0:T(8,128)(2,1)S(1)}, u32[]{:S(2)}, u32[]{:S(2)}) collective-permute-start(bf16[528,128]{1,0:T(8,128)(2,1)S(1)} %pack.1.refs_0_), channel_id=1, source_target_pairs={{0,1},{1,2},{2,3},{3,0},{4,5},{5,6},{6,7},{7,4},{8,9},{9,10},{10,1... | collective-permute-start | bytes 405512 | tf_op jit(solution)/shard_map/ppermute | solution.py:113
  19.7 1.3 %collective-permute-start.3 = (f32[64,256]{1,0:T(8,128)S(1)}, f32[64,256]{1,0:T(8,128)S(1)}, u32[]{:S(2)}, u32[]{:S(2)}) collective-permute-start(f32[64,256]{1,0:T(8,128)S(1)} %exchange.1), channel_id=1, source_target_pairs={{0,4},{4,0},{8,12},{12,8},{16,20},{20,16},{24,28},{28,24},{1,5},{5... | collective-permute-start | bytes 196616 | tf_op jit(solution)/shard_map/ppermute | solution.py:135
  21.1 5.3 %collective-permute-start.6 = (f32[64,256]{1,0:T(8,128)S(1)}, f32[64,256]{1,0:T(8,128)S(1)}, u32[]{:S(2)}, u32[]{:S(2)}) collective-permute-start(f32[64,256]{1,0:T(8,128)S(1)} %add.12), channel_id=1, source_target_pairs={{0,24},{4,28},{8,16},{12,20},{16,8},{20,12},{24,0},{28,4},{1,25},{... | collective-permute-start | bytes 196616 | tf_op jit(solution)/shard_map/ppermute | solution.py:135
  23.6 4.3 %collective-permute-start.5 = (f32[64,256]{1,0:T(8,128)S(1)}, f32[64,256]{1,0:T(8,128)S(1)}, u32[]{:S(2)}, u32[]{:S(2)}) collective-permute-start(f32[64,256]{1,0:T(8,128)S(1)} %add.12), channel_id=1, source_target_pairs={{0,16},{4,20},{8,24},{12,28},{16,0},{20,4},{24,8},{28,12},{1,17},{... | collective-permute-start | bytes 196616 | tf_op jit(solution)/shard_map/ppermute | solution.py:135
  24.1 4.3 %collective-permute-start.4 = (f32[64,256]{1,0:T(8,128)S(1)}, f32[64,256]{1,0:T(8,128)S(1)}, u32[]{:S(2)}, u32[]{:S(2)}) collective-permute-start(f32[64,256]{1,0:T(8,128)S(1)} %add.12), channel_id=1, source_target_pairs={{0,8},{4,12},{8,0},{12,4},{16,24},{20,28},{24,16},{28,20},{1,9},{5... | collective-permute-start | bytes 196616 | tf_op jit(solution)/shard_map/ppermute | solution.py:135

commit v6 on v5

--- a/solution.py
+++ b/solution.py
@@ -41,22 +41,22 @@
     out_ref[tile * BS :] = note.astype(jnp.float32).astype(jnp.bfloat16)
 
 
-def exchange_kernel(orb, slots, aux_width, meta_ref, *refs):
-    packs, (out_ref, rows, half_ref, held) = refs[:orb], refs[orb:]
+def exchange_kernel(slots, aux_width, meta_ref, packs, out_ref, rows, half_ref):
+    orb = packs.shape[0]
     me = lax.axis_index("orb")
     full_width = out_ref.shape[1]
     per_slot = aux_width * BS // LANES
 
-    def tiles(way, first, count):
-        return [packs[way][t * BS : (t + 1) * BS] for t in range(first, first + count)]
+    def tiles(owner, first, count):
+        return [packs[owner, t * BS : (t + 1) * BS] for t in range(first, first + count)]
 
-    for way in range(orb):
-        owner = lax.rem(me - way + orb, orb)
-        for t, part in enumerate(tiles(way, slots * per_slot, full_width // LANES)):
+    for owner in range(orb):
+        for t, part in enumerate(tiles(owner, slots * per_slot, full_width // LANES)):
             rows[owner, :, t * LANES : (t + 1) * LANES] = part
     rows[orb] = jnp.zeros_like(rows[orb])
-    selected = jnp.concatenate([rows[meta_ref[j]] for j in range(slots)], axis=0)
-    own = jnp.concatenate(tiles(0, 0, slots * per_slot), axis=1)
+    selected = [rows[meta_ref[me * slots + j]] for j in range(slots)]
+    selected = jnp.concatenate(selected, axis=0)
+    own = jnp.concatenate(tiles(me, 0, slots * per_slot), axis=1)
     left = []
     for p in range(aux_width):
         cuts = [(j * aux_width + p) * BS for j in range(slots)]
@@ -69,18 +69,19 @@
             axis=1,
         )
     half_ref[orb] = jnp.zeros_like(half_ref[orb])
-    for way in range(orb):
+    columns = []
+    for owner in range(orb):
         total = None
         for j in range(slots):
             term = lax.dot_general(
-                half_ref[meta_ref[way * slots + j]],
-                jnp.concatenate(tiles(way, j * per_slot, per_slot), axis=1),
+                half_ref[meta_ref[owner * slots + j]],
+                jnp.concatenate(tiles(owner, j * per_slot, per_slot), axis=1),
                 (((1,), (1,)), ((), ())),
                 preferred_element_type=jnp.float32,
             )
             total = term if total is None else total + term
-        held[lax.rem(me - way + orb, orb)] = total
-    out_ref[...] = jnp.concatenate([held[n] for n in range(orb)], axis=1)
+        columns.append(total)
+    out_ref[...] = jnp.concatenate(columns, axis=1)
 
 
 def shards(density, tensor_blocks, pairs, kept):
@@ -108,24 +109,22 @@
         compiler_params=params,
         name="pack",
     )(kept, *(pltpu.with_memory_space_constraint(a, pltpu.HBM) for a in (pairs, density, tensor_blocks)))
-    packs = [packed]
-    for way in range(1, orb):
-        packs.append(lax.ppermute(packed, "orb", [(i, (i + way) % orb) for i in range(orb)]))
-    codes = jnp.concatenate([pack[size, :slots] for pack in packs]).astype(jnp.int32)
+    copies = jnp.broadcast_to(packed, (orb, *packed.shape))
+    packs = lax.all_to_all(copies, "orb", 0, 0)
+    codes = packs[:, size, :slots].astype(jnp.int32).reshape(orb * slots)
 
     parts = pl.pallas_call(
-        functools.partial(exchange_kernel, orb, slots, aux_width),
+        functools.partial(exchange_kernel, slots, aux_width),
         out_shape=jax.ShapeDtypeStruct((BS, full_width), jnp.float32),
-        in_specs=[smem] + [vmem] * orb,
+        in_specs=[smem, vmem],
         out_specs=vmem,
         scratch_shapes=[
             pltpu.VMEM((orb + 1, BS, full_width), jnp.bfloat16),
             pltpu.VMEM((orb + 1, BS, aux_width * BS), jnp.bfloat16),
-            pltpu.VMEM((orb, BS, BS), jnp.float32),
         ],
         compiler_params=params,
         name="exchange",
-    )(codes, *packs)
+    )(codes, packs)
 
     step = 1
     while step < aux:

time: 29.2 us -> 33.6 us (1.15)
  blocking collectives: 0 us -> 21 us
  waiting for transfers between devices: 15.5 us -> 4.97 us
  starting transfers between devices: 9.74 us -> 3.62 us
    all_to_all x0 -> x1, blocking collectives: none -> 21 us  [shards(): packs = lax.all_to_all(copies, 'orb', 0, 0)]
    ppermute x3 -> x0, waiting for transfers between devices: 10.5 us -> none  [shards(): lax.ppermute(packed, 'orb', [(i, (i + way) % orb) for i in range(orb)])]
    ppermute x3 -> x0, starting transfers between devices: 6.11 us -> none  [shards(): lax.ppermute(packed, 'orb', [(i, (i + way) % orb) for i in range(orb)])]
  transfers between devices with their start and end apart: 7 -> 4, of which waited for: 6 -> 4; matrix products, arithmetic and copies ran while one was open for 0% -> 0% of each run, Pallas kernels for 0% -> 0%
where the time goes in v6:
time: 33.6 us; the launch traced here: 33.4 us
  blocking collectives  21 us (62%)
  waiting for transfers between devices  4.97 us (15%)
  starting transfers between devices  3.62 us (11%)
  Pallas kernels  2.36 us (7%)
  between operations  0.69 us (2%)
  other arithmetic  0.68 us (2%)
    all_to_all x1, blocking collectives, shards(): packs = lax.all_to_all(copies, 'orb', 0, 0)  21 us
    ppermute x4, waiting for transfers between devices, shards(): lax.ppermute(parts, 'aux', [(i, i ^ way * step) for i in range(aux)])  4.97 us
    ppermute x4, starting transfers between devices, shards(): lax.ppermute(parts, 'aux', [(i, i ^ way * step) for i in range(aux)])  3.62 us
    pallas_call x1, Pallas kernels, shards(): pl.pallas_call(functools.partial(exchange_kernel, slots, aux_width), out_...  1.21 us
    pallas_call x1, Pallas kernels, shards(): pl.pallas_call(functools.partial(pack_kernel, orb), out_shape=jax.ShapeDt...  1.15 us
  transfers between devices with their start and end apart: 4, of which 4 were waited for; matrix products, arithmetic and copies ran while one was open for 0% of the time, Pallas kernels for 0%

profile of v6, /device:TPU:0, one launch (start us, length us, event | category | flops | bytes accessed | tf_op | source)
XLA Modules:
  0.0 33.4 jit_solution(6077495126422142900)
XLA Ops:
  0.7 1.2 %pack.1 = bf16[528,128]{1,0:T(8,128)(2,1)S(1)} custom-call(s32[1,1]{1,0:T(1,128)S(6)} %copy.5.kept, s32[1,1,3]{2,1,0:T(1,128)} %pairs_hbm.1, bf16[64,256]{1,0:T(8,128)(2,1)} %density_hbm.1, bf16[1,1,3,4,4096]{4,3,2,1,0:T(4,128)(2,1)} %blocks_hbm.1), custom_call_target="tpu_custom_call" | custom-call | tf_op jit(solution)/shard_map/pack/pallas_call | solution.py:98
  1.8 0.1 broadcast_in_dim.3
  1.9 21.0 %all_to_all.5.packs = bf16[4,528,128]{2,1,0:T(8,128)(2,1)S(1)} all-to-all(bf16[4,528,128]{2,1,0:T(8,128)(2,1)S(1)} %broadcast_in_dim.3), channel_id=1, replica_groups=mesh['aux'=8,'orb'=4] {'orb'}, dimensions={0} | all-to-all | bytes 1081344 | tf_op jit(solution)/shard_map/all_to_all | solution.py:113
  22.9 0.1 reshape.4.meta_ref
  23.0 1.2 %exchange.1 = f32[64,256]{1,0:T(8,128)S(1)} custom-call(s32[12]{0:T(128)S(1)} %reshape.4.meta_ref, bf16[4,528,128]{2,1,0:T(8,128)(2,1)S(1)} %all_to_all.5.packs), custom_call_target="tpu_custom_call" | custom-call | tf_op jit(solution)/shard_map/exchange/pallas_call | solution.py:116
  24.2 0.1 collective-permute-start
  24.3 1.2 %collective-permute-done = f32[64,256]{1,0:T(8,128)S(1)} collective-permute-done((f32[64,256]{1,0:T(8,128)S(1)}, f32[64,256]{1,0:T(8,128)S(1)}, u32[]{:S(2)}, u32[]{:S(2)}) %collective-permute-start) | collective-permute-done | bytes 65568 | tf_op jit(solution)/shard_map/ppermute | solution.py:134
  25.5 2.5 %collective-permute-start.3 = (f32[64,256]{1,0:T(8,128)S(1)}, f32[64,256]{1,0:T(8,128)S(1)}, u32[]{:S(2)}, u32[]{:S(2)}) collective-permute-start(f32[64,256]{1,0:T(8,128)S(1)} %add.12), channel_id=1, source_target_pairs={{0,24},{4,28},{8,16},{12,20},{16,8},{20,12},{24,0},{28,4},{1,25},{... | collective-permute-start | bytes 196616 | tf_op jit(solution)/shard_map/ppermute | solution.py:134
  28.0 0.5 %collective-permute-start.2 = (f32[64,256]{1,0:T(8,128)S(1)}, f32[64,256]{1,0:T(8,128)S(1)}, u32[]{:S(2)}, u32[]{:S(2)}) collective-permute-start(f32[64,256]{1,0:T(8,128)S(1)} %add.12), channel_id=1, source_target_pairs={{0,16},{4,20},{8,24},{12,28},{16,0},{20,4},{24,8},{28,12},{1,17},{... | collective-permute-start | bytes 196616 | tf_op jit(solution)/shard_map/ppermute | solution.py:134
  28.5 0.5 %collective-permute-start.1 = (f32[64,256]{1,0:T(8,128)S(1)}, f32[64,256]{1,0:T(8,128)S(1)}, u32[]{:S(2)}, u32[]{:S(2)}) collective-permute-start(f32[64,256]{1,0:T(8,128)S(1)} %add.12), channel_id=1, source_target_pairs={{0,8},{4,12},{8,0},{12,4},{16,24},{20,28},{24,16},{28,20},{1,9},{5... | collective-permute-start | bytes 196616 | tf_op jit(solution)/shard_map/ppermute | solution.py:134
  29.1 1.7 %collective-permute-done.3 = f32[64,256]{1,0:T(8,128)S(1)} collective-permute-done((f32[64,256]{1,0:T(8,128)S(1)}, f32[64,256]{1,0:T(8,128)S(1)}, u32[]{:S(2)}, u32[]{:S(2)}) %collective-permute-start.3) | collective-permute-done | bytes 65568 | tf_op jit(solution)/shard_map/ppermute | solution.py:134
  30.8 1.5 %collective-permute-done.2 = f32[64,256]{1,0:T(8,128)S(1)} collective-permute-done((f32[64,256]{1,0:T(8,128)S(1)}, f32[64,256]{1,0:T(8,128)S(1)}, u32[]{:S(2)}, u32[]{:S(2)}) %collective-permute-start.2) | collective-permute-done | bytes 65568 | tf_op jit(solution)/shard_map/ppermute | solution.py:134
  32.3 0.5 %collective-permute-done.1 = f32[64,256]{1,0:T(8,128)S(1)} collective-permute-done((f32[64,256]{1,0:T(8,128)S(1)}, f32[64,256]{1,0:T(8,128)S(1)}, u32[]{:S(2)}, u32[]{:S(2)}) %collective-permute-start.1) | collective-permute-done | bytes 65568 | tf_op jit(solution)/shard_map/ppermute | solution.py:134
  32.8 0.6 %add_add_fusion = f32[64,256]{1,0:T(8,128)} fusion(f32[64,256]{1,0:T(8,128)S(1)} %collective-permute-done.2, f32[64,256]{1,0:T(8,128)S(1)} %collective-permute-done.3, f32[64,256]{1,0:T(8,128)S(1)} %add.12, f32[64,256]{1,0:T(8,128)S(1)} %collective-permute-done.1), kind=kLoop, calls=%fused_computation | loop fusion | flops 49152 | bytes 327680 | tf_op jit(solution)/shard_map/add | solution.py:136
  (2 shorter events, 0.0 us)
Async XLA Ops:
  24.2 1.3 %collective-permute-start = (f32[64,256]{1,0:T(8,128)S(1)}, f32[64,256]{1,0:T(8,128)S(1)}, u32[]{:S(2)}, u32[]{:S(2)}) collective-permute-start(f32[64,256]{1,0:T(8,128)S(1)} %exchange.1), channel_id=1, source_target_pairs={{0,4},{4,0},{8,12},{12,8},{16,20},{20,16},{24,28},{28,24},{1,5},{5... | collective-permute-start | bytes 196616 | tf_op jit(solution)/shard_map/ppermute | solution.py:134
  25.5 5.3 %collective-permute-start.3 = (f32[64,256]{1,0:T(8,128)S(1)}, f32[64,256]{1,0:T(8,128)S(1)}, u32[]{:S(2)}, u32[]{:S(2)}) collective-permute-start(f32[64,256]{1,0:T(8,128)S(1)} %add.12), channel_id=1, source_target_pairs={{0,24},{4,28},{8,16},{12,20},{16,8},{20,12},{24,0},{28,4},{1,25},{... | collective-permute-start | bytes 196616 | tf_op jit(solution)/shard_map/ppermute | solution.py:134
  28.0 4.3 %collective-permute-start.2 = (f32[64,256]{1,0:T(8,128)S(1)}, f32[64,256]{1,0:T(8,128)S(1)}, u32[]{:S(2)}, u32[]{:S(2)}) collective-permute-start(f32[64,256]{1,0:T(8,128)S(1)} %add.12), channel_id=1, source_target_pairs={{0,16},{4,20},{8,24},{12,28},{16,0},{20,4},{24,8},{28,12},{1,17},{... | collective-permute-start | bytes 196616 | tf_op jit(solution)/shard_map/ppermute | solution.py:134
  28.5 4.3 %collective-permute-start.1 = (f32[64,256]{1,0:T(8,128)S(1)}, f32[64,256]{1,0:T(8,128)S(1)}, u32[]{:S(2)}, u32[]{:S(2)}) collective-permute-start(f32[64,256]{1,0:T(8,128)S(1)} %add.12), channel_id=1, source_target_pairs={{0,8},{4,12},{8,0},{12,4},{16,24},{20,28},{24,16},{28,20},{1,9},{5... | collective-permute-start | bytes 196616 | tf_op jit(solution)/shard_map/ppermute | solution.py:134

commit v7 on v5

--- a/solution.py
+++ b/solution.py
@@ -130,9 +130,12 @@
     step = 1
     while step < aux:
         ways = 2 if step == 1 or step * 4 > aux else 4
+        if step == 2:
+            parts = parts.astype(jnp.bfloat16)
         terms = [parts]
         for way in range(1, ways):
             terms.append(lax.ppermute(parts, "aux", [(i, i ^ (way * step)) for i in range(aux)]))
+        terms = [term.astype(jnp.float32) for term in terms]
         while len(terms) > 1:
             terms = [terms[i] + terms[i + 1] for i in range(0, len(terms), 2)]
         parts = terms[0]

time: 29.2 us -> 28.8 us (0.986)
  waiting for transfers between devices: 15.5 us -> 15.1 us
    ppermute x4, waiting for transfers between devices: 4.97 us -> 4.62 us  [shards(): lax.ppermute(parts, 'aux', [(i, i ^ way * step) for i in range(aux)])]
    add x2 -> x1, other arithmetic: 0.66 us -> 0.65 us  [shards(): terms = [terms[i] + terms[i + 1] for i in range(0, len(terms), 2)]]
where the time goes in v7:
time: 28.8 us; the launch traced here: 28.6 us
  waiting for transfers between devices  15.1 us (52%)
  starting transfers between devices  9.74 us (34%)
  Pallas kernels  2.36 us (8%)
  other arithmetic  0.74 us (3%)
  between operations  0.69 us (2%)
    ppermute x3, waiting for transfers between devices, shards(): lax.ppermute(packed, 'orb', [(i, (i + way) % orb) for i in range(orb)])  10.5 us
    ppermute x3, starting transfers between devices, shards(): lax.ppermute(packed, 'orb', [(i, (i + way) % orb) for i in range(orb)])  6.11 us
    ppermute x4, waiting for transfers between devices, shards(): lax.ppermute(parts, 'aux', [(i, i ^ way * step) for i in range(aux)])  4.62 us
    ppermute x4, starting transfers between devices, shards(): lax.ppermute(parts, 'aux', [(i, i ^ way * step) for i in range(aux)])  3.62 us
    pallas_call x1, Pallas kernels, shards(): pl.pallas_call(functools.partial(exchange_kernel, orb, slots, aux_width),...  1.21 us
    pallas_call x1, Pallas kernels, shards(): pl.pallas_call(functools.partial(pack_kernel, orb), out_shape=jax.ShapeDt...  1.15 us
    add x1, other arithmetic, shards(): terms = [terms[i] + terms[i + 1] for i in range(0, len(terms), 2)]  0.65 us
  transfers between devices with their start and end apart: 7, of which 6 were waited for; matrix products, arithmetic and copies ran while one was open for 0% of the time, Pallas kernels for 0%

profile of v7, /device:TPU:0, one launch (start us, length us, event | category | flops | bytes accessed | tf_op | source)
XLA Modules:
  0.0 28.6 jit_solution(11133434791974140759)
XLA Ops:
  0.7 1.2 %pack.1.refs_0_ = bf16[528,128]{1,0:T(8,128)(2,1)S(1)} custom-call(s32[1,1]{1,0:T(1,128)S(6)} %copy.5.kept, s32[1,1,3]{2,1,0:T(1,128)} %pairs_hbm.1, bf16[64,256]{1,0:T(8,128)(2,1)} %density_hbm.1, bf16[1,1,3,4,4096]{4,3,2,1,0:T(4,128)(2,1)} %blocks_hbm.1), custom_call_target="tpu_custom_call" | custom-call | tf_op jit(solution)/shard_map/pack/pallas_call | solution.py:97
  1.8 5.1 %collective-permute-start.2 = (bf16[528,128]{1,0:T(8,128)(2,1)S(1)}, bf16[528,128]{1,0:T(8,128)(2,1)S(1)}, u32[]{:S(2)}, u32[]{:S(2)}) collective-permute-start(bf16[528,128]{1,0:T(8,128)(2,1)S(1)} %pack.1.refs_0_), channel_id=1, source_target_pairs={{0,3},{1,0},{2,1},{3,2},{4,7},{5,4},{6,5},{7,6},{8,11},{9,8},{10,9... | collective-permute-start | bytes 405512 | tf_op jit(solution)/shard_map/ppermute | solution.py:113
  6.9 0.0 collective-permute-start.1
  6.9 1.0 %collective-permute-start = (bf16[528,128]{1,0:T(8,128)(2,1)S(1)}, bf16[528,128]{1,0:T(8,128)(2,1)S(1)}, u32[]{:S(2)}, u32[]{:S(2)}) collective-permute-start(bf16[528,128]{1,0:T(8,128)(2,1)S(1)} %pack.1.refs_0_), channel_id=1, source_target_pairs={{0,1},{1,2},{2,3},{3,0},{4,5},{5,6},{6,7},{7,4},{8,9},{9,10},{10,1... | collective-permute-start | bytes 405512 | tf_op jit(solution)/shard_map/ppermute | solution.py:113
  7.9 3.0 %collective-permute-done.2.refs_3_ = bf16[528,128]{1,0:T(8,128)(2,1)S(1)} collective-permute-done((bf16[528,128]{1,0:T(8,128)(2,1)S(1)}, bf16[528,128]{1,0:T(8,128)(2,1)S(1)}, u32[]{:S(2)}, u32[]{:S(2)}) %collective-permute-start.2) | collective-permute-done | bytes 135200 | tf_op jit(solution)/shard_map/ppermute | solution.py:113
  10.9 7.5 %collective-permute-done.1.refs_2_ = bf16[528,128]{1,0:T(8,128)(2,1)S(1)} collective-permute-done((bf16[528,128]{1,0:T(8,128)(2,1)S(1)}, bf16[528,128]{1,0:T(8,128)(2,1)S(1)}, u32[]{:S(2)}, u32[]{:S(2)}) %collective-permute-start.1) | collective-permute-done | bytes 135200 | tf_op jit(solution)/shard_map/ppermute | solution.py:113
  18.4 0.0 collective-permute-done.refs_1_
  18.4 0.1 maximum_convert_fusion.meta_ref
  18.5 1.2 %exchange.1 = f32[64,256]{1,0:T(8,128)S(1)} custom-call(s32[12]{0:T(128)S(1)} %maximum_convert_fusion.meta_ref, bf16[528,128]{1,0:T(8,128)(2,1)S(1)} %pack.1.refs_0_, bf16[528,128]{1,0:T(8,128)(2,1)S(1)} %collective-permute-done.refs_1_, bf16[528,128]{1,0:T(8,128)(2,1)S(1)} %collective-permute-done.1.refs_2_, bf16[528,128]{1,0:T(8,128)(2,1)S(1)} %collective-permute-done.2.refs_3_), custom_call_target="tpu_custom_call" | custom-call | tf_op jit(solution)/shard_map/exchange/pallas_call | solution.py:116
  19.7 0.1 collective-permute-start.3
  19.8 1.2 %collective-permute-done.3 = f32[64,256]{1,0:T(8,128)S(1)} collective-permute-done((f32[64,256]{1,0:T(8,128)S(1)}, f32[64,256]{1,0:T(8,128)S(1)}, u32[]{:S(2)}, u32[]{:S(2)}) %collective-permute-start.3) | collective-permute-done | bytes 65568 | tf_op jit(solution)/shard_map/ppermute | solution.py:137
  21.1 2.5 %collective-permute-start.6 = (bf16[64,256]{1,0:T(8,128)(2,1)S(1)}, bf16[64,256]{1,0:T(8,128)(2,1)S(1)}, u32[]{:S(2)}, u32[]{:S(2)}) collective-permute-start(bf16[64,256]{1,0:T(8,128)(2,1)S(1)} %add_convert_fusion), channel_id=1, source_target_pairs={{0,24},{4,28},{8,16},{12,20},{16,8},{20,12},{24,0},{28,4},{1,25},{... | collective-permute-start | bytes 98312 | tf_op jit(solution)/shard_map/ppermute | solution.py:137
  23.6 0.5 %collective-permute-start.5 = (bf16[64,256]{1,0:T(8,128)(2,1)S(1)}, bf16[64,256]{1,0:T(8,128)(2,1)S(1)}, u32[]{:S(2)}, u32[]{:S(2)}) collective-permute-start(bf16[64,256]{1,0:T(8,128)(2,1)S(1)} %add_convert_fusion), channel_id=1, source_target_pairs={{0,16},{4,20},{8,24},{12,28},{16,0},{20,4},{24,8},{28,12},{1,17},{... | collective-permute-start | bytes 98312 | tf_op jit(solution)/shard_map/ppermute | solution.py:137
  24.1 0.5 %collective-permute-start.4 = (bf16[64,256]{1,0:T(8,128)(2,1)S(1)}, bf16[64,256]{1,0:T(8,128)(2,1)S(1)}, u32[]{:S(2)}, u32[]{:S(2)}) collective-permute-start(bf16[64,256]{1,0:T(8,128)(2,1)S(1)} %add_convert_fusion), channel_id=1, source_target_pairs={{0,8},{4,12},{8,0},{12,4},{16,24},{20,28},{24,16},{28,20},{1,9},{5... | collective-permute-start | bytes 98312 | tf_op jit(solution)/shard_map/ppermute | solution.py:137
  24.6 1.3 %collective-permute-done.6 = bf16[64,256]{1,0:T(8,128)(2,1)S(1)} collective-permute-done((bf16[64,256]{1,0:T(8,128)(2,1)S(1)}, bf16[64,256]{1,0:T(8,128)(2,1)S(1)}, u32[]{:S(2)}, u32[]{:S(2)}) %collective-permute-start.6) | collective-permute-done | bytes 32800 | tf_op jit(solution)/shard_map/ppermute | solution.py:137
  25.9 1.5 %collective-permute-done.5 = bf16[64,256]{1,0:T(8,128)(2,1)S(1)} collective-permute-done((bf16[64,256]{1,0:T(8,128)(2,1)S(1)}, bf16[64,256]{1,0:T(8,128)(2,1)S(1)}, u32[]{:S(2)}, u32[]{:S(2)}) %collective-permute-start.5) | collective-permute-done | bytes 32800 | tf_op jit(solution)/shard_map/ppermute | solution.py:137
  27.5 0.5 %collective-permute-done.4 = bf16[64,256]{1,0:T(8,128)(2,1)S(1)} collective-permute-done((bf16[64,256]{1,0:T(8,128)(2,1)S(1)}, bf16[64,256]{1,0:T(8,128)(2,1)S(1)}, u32[]{:S(2)}, u32[]{:S(2)}) %collective-permute-start.4) | collective-permute-done | bytes 32800 | tf_op jit(solution)/shard_map/ppermute | solution.py:137
  28.0 0.6 %add_add_fusion = f32[64,256]{1,0:T(8,128)} fusion(bf16[64,256]{1,0:T(8,128)(2,1)S(1)} %collective-permute-done.6, bf16[64,256]{1,0:T(8,128)(2,1)S(1)} %collective-permute-done.5, bf16[64,256]{1,0:T(8,128)(2,1)S(1)} %collective-permute-done.4, bf16[64,256]{1,0:T(8,128)(2,1)S(1)} %add_convert_fusion), kind=kLoop, calls=%fused_computation | loop fusion | flops 114688 | bytes 196608 | tf_op jit(solution)/shard_map/add | solution.py:140
  (5 shorter events, 0.0 us)
Async XLA Ops:
  1.8 9.1 %collective-permute-start.2 = (bf16[528,128]{1,0:T(8,128)(2,1)S(1)}, bf16[528,128]{1,0:T(8,128)(2,1)S(1)}, u32[]{:S(2)}, u32[]{:S(2)}) collective-permute-start(bf16[528,128]{1,0:T(8,128)(2,1)S(1)} %pack.1.refs_0_), channel_id=1, source_target_pairs={{0,3},{1,0},{2,1},{3,2},{4,7},{5,4},{6,5},{7,6},{8,11},{9,8},{10,9... | collective-permute-start | bytes 405512 | tf_op jit(solution)/shard_map/ppermute | solution.py:113
  6.9 11.5 %collective-permute-start.1 = (bf16[528,128]{1,0:T(8,128)(2,1)S(1)}, bf16[528,128]{1,0:T(8,128)(2,1)S(1)}, u32[]{:S(2)}, u32[]{:S(2)}) collective-permute-start(bf16[528,128]{1,0:T(8,128)(2,1)S(1)} %pack.1.refs_0_), channel_id=1, source_target_pairs={{0,2},{1,3},{2,0},{3,1},{4,6},{5,7},{6,4},{7,5},{8,10},{9,11},{10,... | collective-permute-start | bytes 405512 | tf_op jit(solution)/shard_map/ppermute | solution.py:113
  6.9 11.5 %collective-permute-start = (bf16[528,128]{1,0:T(8,128)(2,1)S(1)}, bf16[528,128]{1,0:T(8,128)(2,1)S(1)}, u32[]{:S(2)}, u32[]{:S(2)}) collective-permute-start(bf16[528,128]{1,0:T(8,128)(2,1)S(1)} %pack.1.refs_0_), channel_id=1, source_target_pairs={{0,1},{1,2},{2,3},{3,0},{4,5},{5,6},{6,7},{7,4},{8,9},{9,10},{10,1... | collective-permute-start | bytes 405512 | tf_op jit(solution)/shard_map/ppermute | solution.py:113
  19.7 1.3 %collective-permute-start.3 = (f32[64,256]{1,0:T(8,128)S(1)}, f32[64,256]{1,0:T(8,128)S(1)}, u32[]{:S(2)}, u32[]{:S(2)}) collective-permute-start(f32[64,256]{1,0:T(8,128)S(1)} %exchange.1), channel_id=1, source_target_pairs={{0,4},{4,0},{8,12},{12,8},{16,20},{20,16},{24,28},{28,24},{1,5},{5... | collective-permute-start | bytes 196616 | tf_op jit(solution)/shard_map/ppermute | solution.py:137
  21.1 4.9 %collective-permute-start.6 = (bf16[64,256]{1,0:T(8,128)(2,1)S(1)}, bf16[64,256]{1,0:T(8,128)(2,1)S(1)}, u32[]{:S(2)}, u32[]{:S(2)}) collective-permute-start(bf16[64,256]{1,0:T(8,128)(2,1)S(1)} %add_convert_fusion), channel_id=1, source_target_pairs={{0,24},{4,28},{8,16},{12,20},{16,8},{20,12},{24,0},{28,4},{1,25},{... | collective-permute-start | bytes 98312 | tf_op jit(solution)/shard_map/ppermute | solution.py:137
  23.6 3.9 %collective-permute-start.5 = (bf16[64,256]{1,0:T(8,128)(2,1)S(1)}, bf16[64,256]{1,0:T(8,128)(2,1)S(1)}, u32[]{:S(2)}, u32[]{:S(2)}) collective-permute-start(bf16[64,256]{1,0:T(8,128)(2,1)S(1)} %add_convert_fusion), channel_id=1, source_target_pairs={{0,16},{4,20},{8,24},{12,28},{16,0},{20,4},{24,8},{28,12},{1,17},{... | collective-permute-start | bytes 98312 | tf_op jit(solution)/shard_map/ppermute | solution.py:137
  24.1 3.9 %collective-permute-start.4 = (bf16[64,256]{1,0:T(8,128)(2,1)S(1)}, bf16[64,256]{1,0:T(8,128)(2,1)S(1)}, u32[]{:S(2)}, u32[]{:S(2)}) collective-permute-start(bf16[64,256]{1,0:T(8,128)(2,1)S(1)} %add_convert_fusion), channel_id=1, source_target_pairs={{0,8},{4,12},{8,0},{12,4},{16,24},{20,28},{24,16},{28,20},{1,9},{5... | collective-permute-start | bytes 98312 | tf_op jit(solution)/shard_map/ppermute | solution.py:137

commit v8 on v5

--- a/solution.py
+++ b/solution.py
@@ -12,7 +12,18 @@
 NOTE = 16
 
 
-def pack_kernel(orb, kept, pairs_hbm, density_hbm, blocks_hbm, out_ref, pairs, rows, blocks, sems):
+def lay_blocks(raw, out_ref):
+    slots, aux_width = raw.shape[:2]
+    square = raw.reshape(slots * aux_width, BS, BS)
+    for tile in range(slots * aux_width // 2):
+        both = jnp.concatenate([square[2 * tile], square[2 * tile + 1]], axis=1)
+        out_ref[tile * BS : (tile + 1) * BS] = both
+    return slots * aux_width // 2
+
+
+def pack_kernel(
+    orb, kept, pairs_hbm, density_hbm, blocks_hbm, out_ref, tail_ref, pairs, rows, blocks, sems
+):
     copies = [
         pltpu.make_async_copy(src, dst, sems.at[i])
         for i, (src, dst) in enumerate(
@@ -23,37 +34,44 @@
         copy.start()
     for copy in copies:
         copy.wait()
-    slots, aux_width = blocks.shape[2:4]
-    square = blocks[0, 0].reshape(slots * aux_width, BS, BS)
-    tile = 0
-    for pair in range(0, slots * aux_width, 2):
-        both = jnp.concatenate([square[pair], square[pair + 1]], axis=1)
-        out_ref[tile * BS : (tile + 1) * BS] = both
-        tile += 1
+    slots = blocks.shape[2]
+    tile = lay_blocks(blocks[0, 0], out_ref)
     for at in range(0, rows.shape[1], LANES):
-        out_ref[tile * BS : (tile + 1) * BS] = rows[:, at : at + LANES]
+        part = rows[:, at : at + LANES]
+        out_ref[tile * BS : (tile + 1) * BS] = part
+        tail_ref[at // LANES * BS : (at // LANES + 1) * BS] = part
         tile += 1
     shape = (NOTE, LANES)
     lane = lax.broadcasted_iota(jnp.int32, shape, 1)
     note = jnp.zeros(shape, jnp.int32)
     for j in range(slots):
         note = jnp.where(lane == j, jnp.where(j < kept[0, 0], pairs[0, 0, j], orb), note)
-    out_ref[tile * BS :] = note.astype(jnp.float32).astype(jnp.bfloat16)
+    note = note.astype(jnp.float32).astype(jnp.bfloat16)
+    out_ref[tile * BS :] = note
+    tail_ref[rows.shape[1] // LANES * BS :] = note
+
+
+def relay_kernel(blocks, out_ref):
+    lay_blocks(blocks[0, 0], out_ref)
 
 
 def exchange_kernel(orb, slots, aux_width, meta_ref, *refs):
-    packs, (out_ref, rows, half_ref, held) = refs[:orb], refs[orb:]
+    packs, tails, (out_ref, rows, half_ref, held) = refs[:orb], refs[orb : 2 * orb], refs[2 * orb :]
     me = lax.axis_index("orb")
     full_width = out_ref.shape[1]
     per_slot = aux_width * BS // LANES
+    count = full_width // LANES
 
     def tiles(way, first, count):
         return [packs[way][t * BS : (t + 1) * BS] for t in range(first, first + count)]
 
     for way in range(orb):
         owner = lax.rem(me - way + orb, orb)
-        for t, part in enumerate(tiles(way, slots * per_slot, full_width // LANES)):
-            rows[owner, :, t * LANES : (t + 1) * LANES] = part
+        first = tails[way].shape[0] - NOTE - count * BS
+        for t in range(count):
+            rows[owner, :, t * LANES : (t + 1) * LANES] = tails[way][
+                first + t * BS : first + (t + 1) * BS
+            ]
     rows[orb] = jnp.zeros_like(rows[orb])
     selected = jnp.concatenate([rows[meta_ref[j]] for j in range(slots)], axis=0)
     own = jnp.concatenate(tiles(0, 0, slots * per_slot), axis=1)
@@ -94,11 +112,14 @@
     smem = pl.BlockSpec(memory_space=pltpu.SMEM)
     params = pltpu.CompilerParams(vmem_limit_bytes=32 * 1024 * 1024)
 
-    packed = pl.pallas_call(
+    packed, tail = pl.pallas_call(
         functools.partial(pack_kernel, orb),
-        out_shape=jax.ShapeDtypeStruct((size + NOTE, LANES), jnp.bfloat16),
+        out_shape=[
+            jax.ShapeDtypeStruct((rows + NOTE, LANES), jnp.bfloat16)
+            for rows in (size, full_width // LANES * BS)
+        ],
         in_specs=[smem] + [pl.BlockSpec(memory_space=pltpu.HBM)] * 3,
-        out_specs=vmem,
+        out_specs=[vmem, vmem],
         scratch_shapes=[
             pltpu.SMEM(pairs.shape, jnp.int32),
             pltpu.VMEM(density.shape, jnp.bfloat16),
@@ -108,15 +129,33 @@
         compiler_params=params,
         name="pack",
     )(kept, *(pltpu.with_memory_space_constraint(a, pltpu.HBM) for a in (pairs, density, tensor_blocks)))
-    packs = [packed]
+    packs, tails = [packed], [packed]
     for way in range(1, orb):
-        packs.append(lax.ppermute(packed, "orb", [(i, (i + way) % orb) for i in range(orb)]))
-    codes = jnp.concatenate([pack[size, :slots] for pack in packs]).astype(jnp.int32)
+        perm = [(i, (i + way) % orb) for i in range(orb)]
+        if way == orb // 2:
+            raw = lax.ppermute(tensor_blocks, "orb", perm)
+            packs.append(
+                pl.pallas_call(
+                    relay_kernel,
+                    out_shape=jax.ShapeDtypeStruct(
+                        (slots * aux_width * BS * BS // LANES, LANES), jnp.bfloat16
+                    ),
+                    in_specs=[vmem],
+                    out_specs=vmem,
+                    compiler_params=params,
+                    name="relay",
+                )(raw)
+            )
+            tails.append(lax.ppermute(tail, "orb", perm))
+        else:
+            packs.append(lax.ppermute(packed, "orb", perm))
+            tails.append(packs[-1])
+    codes = jnp.concatenate([pack[-NOTE, :slots] for pack in tails]).astype(jnp.int32)
 
     parts = pl.pallas_call(
         functools.partial(exchange_kernel, orb, slots, aux_width),
         out_shape=jax.ShapeDtypeStruct((BS, full_width), jnp.float32),
-        in_specs=[smem] + [vmem] * orb,
+        in_specs=[smem] + [vmem] * (2 * orb),
         out_specs=vmem,
         scratch_shapes=[
             pltpu.VMEM((orb + 1, BS, full_width), jnp.bfloat16),
@@ -125,7 +164,7 @@
         ],
         compiler_params=params,
         name="exchange",
-    )(codes, *packs)
+    )(codes, *packs, *tails)
 
     step = 1
     while step < aux:

time: 29.2 us -> 27.6 us (0.945)
  waiting for transfers between devices: 15.5 us -> 12.6 us
  starting transfers between devices: 9.74 us -> 10.8 us
    ppermute x3 -> x4, waiting for transfers between devices: 10.5 us -> 7.58 us  [the longest x1 7.57 us: shards(): tails.append(lax.ppermute(tail, 'orb', perm))]
    ppermute x3 -> x4, starting transfers between devices: 6.11 us -> 7.13 us  [the longest x1 4.04 us: shards(): raw = lax.ppermute(tensor_blocks, 'orb', perm)]
    pallas_call x1 -> x2, Pallas kernels: 1.15 us -> 1.38 us  [the longest x1 1.15 us: shards(): pl.pallas_call(functools.partial(pack_kernel, orb), out_shape=[jax.ShapeD...]
  transfers between devices with their start and end apart: 7 -> 8, of which waited for: 6 -> 5; matrix products, arithmetic and copies ran while one was open for 0% -> 0% of each run, Pallas kernels for 0% -> 5%
where the time goes in v8:
time: 27.6 us; the launch traced here: 27.4 us
  waiting for transfers between devices  12.6 us (46%)
  starting transfers between devices  10.8 us (39%)
  Pallas kernels  2.59 us (9%)
  other arithmetic  0.74 us (3%)
  between operations  0.72 us (3%)
    ppermute x1, waiting for transfers between devices, shards(): tails.append(lax.ppermute(tail, 'orb', perm))  7.57 us
    ppermute x4, waiting for transfers between devices, shards(): lax.ppermute(parts, 'aux', [(i, i ^ way * step) for i in range(aux)])  5.02 us
    ppermute x1, starting transfers between devices, shards(): raw = lax.ppermute(tensor_blocks, 'orb', perm)  4.04 us
    ppermute x4, starting transfers between devices, shards(): lax.ppermute(parts, 'aux', [(i, i ^ way * step) for i in range(aux)])  3.62 us
    ppermute x2, starting transfers between devices, shards(): packs.append(lax.ppermute(packed, 'orb', perm))  2.08 us
    pallas_call x1, Pallas kernels, shards(): pl.pallas_call(functools.partial(exchange_kernel, orb, slots, aux_width),...  1.2 us
    pallas_call x1, Pallas kernels, shards(): pl.pallas_call(functools.partial(pack_kernel, orb), out_shape=[jax.ShapeD...  1.15 us
    ppermute x1, starting transfers between devices, shards(): tails.append(lax.ppermute(tail, 'orb', perm))  1.02 us
  transfers between devices with their start and end apart: 8, of which 5 were waited for; matrix products, arithmetic and copies ran while one was open for 0% of the time, Pallas kernels for 5%

profile of v8, /device:TPU:0, one launch (start us, length us, event | category | flops | bytes accessed | tf_op | source)
XLA Modules:
  0.0 27.4 jit_solution(16858146745067182929)
XLA Ops:
  0.0 4.0 %collective-permute-start.3 = (bf16[1,1,3,4,4096]{4,3,2,1,0:T(4,128)(2,1)}, bf16[1,1,3,4,4096]{4,3,2,1,0:T(4,128)(2,1)S(1)}, u32[]{:S(2)}, u32[]{:S(2)}) collective-permute-start(bf16[1,1,3,4,4096]{4,3,2,1,0:T(4,128)(2,1)} %blocks_hbm.1), channel_id=1, source_target_pairs={{0,2},{1,3},{2,0},{3,1},{4,6},{5,7},{6,4},{7,5},{8,10},{9,11},{10,... | collective-permute-start | bytes 294920 | tf_op jit(solution)/shard_map/ppermute | solution.py:136
  4.7 1.2 %pack.1 = (bf16[528,128]{1,0:T(8,128)(2,1)S(1)}, bf16[144,128]{1,0:T(8,128)(2,1)S(1)}) custom-call(s32[1,1]{1,0:T(1,128)S(6)} %copy.5.kept, s32[1,1,3]{2,1,0:T(1,128)} %pairs_hbm.1, bf16[64,256]{1,0:T(8,128)(2,1)} %density_hbm.1, bf16[1,1,3,4,4096]{4,3,2,1,0:T(4,128)(2,1)} %blocks_hbm.1), custom_call_target="tpu_custom_call" | custom-call | tf_op jit(solution)/shard_map/pack/pallas_call | solution.py:115
  5.9 1.4 %collective-permute-start.2 = (bf16[528,128]{1,0:T(8,128)(2,1)S(1)}, bf16[528,128]{1,0:T(8,128)(2,1)S(1)}, u32[]{:S(2)}, u32[]{:S(2)}) collective-permute-start(bf16[528,128]{1,0:T(8,128)(2,1)S(1)} %get-tuple-element.7.refs_0_.refs_4_), channel_id=1, source_target_pairs={{0,3},{1,0},{2,1},{3,2},{4,7},{5,4},{6,5},{7,6},{8,11},{9,8},{10,9... | collective-permute-start | bytes 405512 | tf_op jit(solution)/shard_map/ppermute | solution.py:151
  7.3 0.7 %collective-permute-start = (bf16[528,128]{1,0:T(8,128)(2,1)S(1)}, bf16[528,128]{1,0:T(8,128)(2,1)S(1)}, u32[]{:S(2)}, u32[]{:S(2)}) collective-permute-start(bf16[528,128]{1,0:T(8,128)(2,1)S(1)} %get-tuple-element.7.refs_0_.refs_4_), channel_id=1, source_target_pairs={{0,1},{1,2},{2,3},{3,0},{4,5},{5,6},{6,7},{7,4},{8,9},{9,10},{10,1... | collective-permute-start | bytes 405512 | tf_op jit(solution)/shard_map/ppermute | solution.py:151
  7.9 1.0 %collective-permute-start.1 = (bf16[144,128]{1,0:T(8,128)(2,1)S(1)}, bf16[144,128]{1,0:T(8,128)(2,1)S(1)}, u32[]{:S(2)}, u32[]{:S(2)}) collective-permute-start(bf16[144,128]{1,0:T(8,128)(2,1)S(1)} %get-tuple-element.8), channel_id=1, source_target_pairs={{0,2},{1,3},{2,0},{3,1},{4,6},{5,7},{6,4},{7,5},{8,10},{9,11},{10,... | collective-permute-start | bytes 110600 | tf_op jit(solution)/shard_map/ppermute | solution.py:149
  8.9 7.6 %collective-permute-done.1.refs_6_ = bf16[144,128]{1,0:T(8,128)(2,1)S(1)} collective-permute-done((bf16[144,128]{1,0:T(8,128)(2,1)S(1)}, bf16[144,128]{1,0:T(8,128)(2,1)S(1)}, u32[]{:S(2)}, u32[]{:S(2)}) %collective-permute-start.1) | collective-permute-done | bytes 36896 | tf_op jit(solution)/shard_map/ppermute | solution.py:149
  16.5 0.0 collective-permute-done.3.blocks
  16.5 0.2 relay.1.refs_2_
  16.8 0.0 collective-permute-done.2.refs_3_.refs_7_
  16.8 0.0 collective-permute-done.refs_1_.refs_5_
  16.8 0.1 maximum_convert_fusion.meta_ref
  16.9 1.2 %exchange.1 = f32[64,256]{1,0:T(8,128)S(1)} custom-call(s32[12]{0:T(128)S(1)} %maximum_convert_fusion.meta_ref, bf16[528,128]{1,0:T(8,128)(2,1)S(1)} %get-tuple-element.7.refs_0_.refs_4_, bf16[528,128]{1,0:T(8,128)(2,1)S(1)} %collective-permute-done.refs_1_.refs_5_, bf16[384,128]{1,0:T(8,128)(2,1)S(1)} %relay.1.refs_2_, ...), custom_call_target="tpu_custom_call" | custom-call | tf_op jit(solution)/shard_map/exchange/pallas_call | solution.py:155
  18.1 0.1 collective-permute-start.4
  18.2 1.2 %collective-permute-done.4 = f32[64,256]{1,0:T(8,128)S(1)} collective-permute-done((f32[64,256]{1,0:T(8,128)S(1)}, f32[64,256]{1,0:T(8,128)S(1)}, u32[]{:S(2)}, u32[]{:S(2)}) %collective-permute-start.4) | collective-permute-done | bytes 65568 | tf_op jit(solution)/shard_map/ppermute | solution.py:174
  19.4 2.6 %collective-permute-start.7 = (f32[64,256]{1,0:T(8,128)S(1)}, f32[64,256]{1,0:T(8,128)S(1)}, u32[]{:S(2)}, u32[]{:S(2)}) collective-permute-start(f32[64,256]{1,0:T(8,128)S(1)} %add.12), channel_id=1, source_target_pairs={{0,24},{4,28},{8,16},{12,20},{16,8},{20,12},{24,0},{28,4},{1,25},{... | collective-permute-start | bytes 196616 | tf_op jit(solution)/shard_map/ppermute | solution.py:174
  22.0 0.5 %collective-permute-start.6 = (f32[64,256]{1,0:T(8,128)S(1)}, f32[64,256]{1,0:T(8,128)S(1)}, u32[]{:S(2)}, u32[]{:S(2)}) collective-permute-start(f32[64,256]{1,0:T(8,128)S(1)} %add.12), channel_id=1, source_target_pairs={{0,16},{4,20},{8,24},{12,28},{16,0},{20,4},{24,8},{28,12},{1,17},{... | collective-permute-start | bytes 196616 | tf_op jit(solution)/shard_map/ppermute | solution.py:174
  22.5 0.5 %collective-permute-start.5 = (f32[64,256]{1,0:T(8,128)S(1)}, f32[64,256]{1,0:T(8,128)S(1)}, u32[]{:S(2)}, u32[]{:S(2)}) collective-permute-start(f32[64,256]{1,0:T(8,128)S(1)} %add.12), channel_id=1, source_target_pairs={{0,8},{4,12},{8,0},{12,4},{16,24},{20,28},{24,16},{28,20},{1,9},{5... | collective-permute-start | bytes 196616 | tf_op jit(solution)/shard_map/ppermute | solution.py:174
  23.0 1.7 %collective-permute-done.7 = f32[64,256]{1,0:T(8,128)S(1)} collective-permute-done((f32[64,256]{1,0:T(8,128)S(1)}, f32[64,256]{1,0:T(8,128)S(1)}, u32[]{:S(2)}, u32[]{:S(2)}) %collective-permute-start.7) | collective-permute-done | bytes 65568 | tf_op jit(solution)/shard_map/ppermute | solution.py:174
  24.7 1.6 %collective-permute-done.6 = f32[64,256]{1,0:T(8,128)S(1)} collective-permute-done((f32[64,256]{1,0:T(8,128)S(1)}, f32[64,256]{1,0:T(8,128)S(1)}, u32[]{:S(2)}, u32[]{:S(2)}) %collective-permute-start.6) | collective-permute-done | bytes 65568 | tf_op jit(solution)/shard_map/ppermute | solution.py:174
  26.3 0.5 %collective-permute-done.5 = f32[64,256]{1,0:T(8,128)S(1)} collective-permute-done((f32[64,256]{1,0:T(8,128)S(1)}, f32[64,256]{1,0:T(8,128)S(1)}, u32[]{:S(2)}, u32[]{:S(2)}) %collective-permute-start.5) | collective-permute-done | bytes 65568 | tf_op jit(solution)/shard_map/ppermute | solution.py:174
  26.8 0.6 %add_add_fusion = f32[64,256]{1,0:T(8,128)} fusion(f32[64,256]{1,0:T(8,128)S(1)} %collective-permute-done.6, f32[64,256]{1,0:T(8,128)S(1)} %collective-permute-done.7, f32[64,256]{1,0:T(8,128)S(1)} %add.12, f32[64,256]{1,0:T(8,128)S(1)} %collective-permute-done.5), kind=kLoop, calls=%fused_computation | loop fusion | flops 49152 | bytes 327680 | tf_op jit(solution)/shard_map/add | solution.py:176
  (5 shorter events, 0.0 us)
Async XLA Ops:
  0.0 16.5 %collective-permute-start.3 = (bf16[1,1,3,4,4096]{4,3,2,1,0:T(4,128)(2,1)}, bf16[1,1,3,4,4096]{4,3,2,1,0:T(4,128)(2,1)S(1)}, u32[]{:S(2)}, u32[]{:S(2)}) collective-permute-start(bf16[1,1,3,4,4096]{4,3,2,1,0:T(4,128)(2,1)} %blocks_hbm.1), channel_id=1, source_target_pairs={{0,2},{1,3},{2,0},{3,1},{4,6},{5,7},{6,4},{7,5},{8,10},{9,11},{10,... | collective-permute-start | bytes 294920 | tf_op jit(solution)/shard_map/ppermute | solution.py:136
  5.9 10.9 %collective-permute-start.2 = (bf16[528,128]{1,0:T(8,128)(2,1)S(1)}, bf16[528,128]{1,0:T(8,128)(2,1)S(1)}, u32[]{:S(2)}, u32[]{:S(2)}) collective-permute-start(bf16[528,128]{1,0:T(8,128)(2,1)S(1)} %get-tuple-element.7.refs_0_.refs_4_), channel_id=1, source_target_pairs={{0,3},{1,0},{2,1},{3,2},{4,7},{5,4},{6,5},{7,6},{8,11},{9,8},{10,9... | collective-permute-start | bytes 405512 | tf_op jit(solution)/shard_map/ppermute | solution.py:151
  7.3 9.5 %collective-permute-start = (bf16[528,128]{1,0:T(8,128)(2,1)S(1)}, bf16[528,128]{1,0:T(8,128)(2,1)S(1)}, u32[]{:S(2)}, u32[]{:S(2)}) collective-permute-start(bf16[528,128]{1,0:T(8,128)(2,1)S(1)} %get-tuple-element.7.refs_0_.refs_4_), channel_id=1, source_target_pairs={{0,1},{1,2},{2,3},{3,0},{4,5},{5,6},{6,7},{7,4},{8,9},{9,10},{10,1... | collective-permute-start | bytes 405512 | tf_op jit(solution)/shard_map/ppermute | solution.py:151
  7.9 8.6 %collective-permute-start.1 = (bf16[144,128]{1,0:T(8,128)(2,1)S(1)}, bf16[144,128]{1,0:T(8,128)(2,1)S(1)}, u32[]{:S(2)}, u32[]{:S(2)}) collective-permute-start(bf16[144,128]{1,0:T(8,128)(2,1)S(1)} %get-tuple-element.8), channel_id=1, source_target_pairs={{0,2},{1,3},{2,0},{3,1},{4,6},{5,7},{6,4},{7,5},{8,10},{9,11},{10,... | collective-permute-start | bytes 110600 | tf_op jit(solution)/shard_map/ppermute | solution.py:149
  18.1 1.3 %collective-permute-start.4 = (f32[64,256]{1,0:T(8,128)S(1)}, f32[64,256]{1,0:T(8,128)S(1)}, u32[]{:S(2)}, u32[]{:S(2)}) collective-permute-start(f32[64,256]{1,0:T(8,128)S(1)} %exchange.1), channel_id=1, source_target_pairs={{0,4},{4,0},{8,12},{12,8},{16,20},{20,16},{24,28},{28,24},{1,5},{5... | collective-permute-start | bytes 196616 | tf_op jit(solution)/shard_map/ppermute | solution.py:174
  19.4 5.2 %collective-permute-start.7 = (f32[64,256]{1,0:T(8,128)S(1)}, f32[64,256]{1,0:T(8,128)S(1)}, u32[]{:S(2)}, u32[]{:S(2)}) collective-permute-start(f32[64,256]{1,0:T(8,128)S(1)} %add.12), channel_id=1, source_target_pairs={{0,24},{4,28},{8,16},{12,20},{16,8},{20,12},{24,0},{28,4},{1,25},{... | collective-permute-start | bytes 196616 | tf_op jit(solution)/shard_map/ppermute | solution.py:174
  22.0 4.3 %collective-permute-start.6 = (f32[64,256]{1,0:T(8,128)S(1)}, f32[64,256]{1,0:T(8,128)S(1)}, u32[]{:S(2)}, u32[]{:S(2)}) collective-permute-start(f32[64,256]{1,0:T(8,128)S(1)} %add.12), channel_id=1, source_target_pairs={{0,16},{4,20},{8,24},{12,28},{16,0},{20,4},{24,8},{28,12},{1,17},{... | collective-permute-start | bytes 196616 | tf_op jit(solution)/shard_map/ppermute | solution.py:174
  22.5 4.3 %collective-permute-start.5 = (f32[64,256]{1,0:T(8,128)S(1)}, f32[64,256]{1,0:T(8,128)S(1)}, u32[]{:S(2)}, u32[]{:S(2)}) collective-permute-start(f32[64,256]{1,0:T(8,128)S(1)} %add.12), channel_id=1, source_target_pairs={{0,8},{4,12},{8,0},{12,4},{16,24},{20,28},{24,16},{28,20},{1,9},{5... | collective-permute-start | bytes 196616 | tf_op jit(solution)/shard_map/ppermute | solution.py:174

commit v9 on v8

--- a/solution.py
+++ b/solution.py
@@ -10,6 +10,22 @@
 BS = 64
 LANES = 128
 NOTE = 16
+
+
+def routes(orb):
+    if orb == 4:
+        return [(0, 1, 2, 3), (1, 3, 0, 2), (2, 0, 3, 1), (3, 2, 1, 0)]
+    return [tuple((i + way) % orb for i in range(orb)) for way in range(orb)]
+
+
+def owner_of(me, way, orb):
+    if orb == 4:
+        route = routes(orb)[way]
+        owner = jnp.int32(route.index(0))
+        for i in range(1, orb):
+            owner = jnp.where(me == i, route.index(i), owner)
+        return owner
+    return lax.rem(me - way + orb, orb)
 
 
 def lay_blocks(raw, out_ref):
@@ -66,7 +82,7 @@
         return [packs[way][t * BS : (t + 1) * BS] for t in range(first, first + count)]
 
     for way in range(orb):
-        owner = lax.rem(me - way + orb, orb)
+        owner = owner_of(me, way, orb)
         first = tails[way].shape[0] - NOTE - count * BS
         for t in range(count):
             rows[owner, :, t * LANES : (t + 1) * LANES] = tails[way][
@@ -97,7 +113,7 @@
                 preferred_element_type=jnp.float32,
             )
             total = term if total is None else total + term
-        held[lax.rem(me - way + orb, orb)] = total
+        held[owner_of(me, way, orb)] = total
     out_ref[...] = jnp.concatenate([held[n] for n in range(orb)], axis=1)
 
 
@@ -131,8 +147,8 @@
     )(kept, *(pltpu.with_memory_space_constraint(a, pltpu.HBM) for a in (pairs, density, tensor_blocks)))
     packs, tails = [packed], [packed]
     for way in range(1, orb):
-        perm = [(i, (i + way) % orb) for i in range(orb)]
-        if way == orb // 2:
+        perm = list(enumerate(routes(orb)[way]))
+        if way == 1:
             raw = lax.ppermute(tensor_blocks, "orb", perm)
             packs.append(
                 pl.pallas_call(

time: 27.6 us -> 29.3 us (1.062)
  waiting for transfers between devices: 12.6 us -> 13.9 us
  starting transfers between devices: 10.8 us -> 11.2 us
    ppermute x2, starting transfers between devices: 2.08 us -> 4.12 us  [shards(): packs.append(lax.ppermute(packed, 'orb', perm))]
    ppermute x1, waiting for transfers between devices: 7.57 us -> 8.92 us  [shards(): tails.append(lax.ppermute(tail, 'orb', perm))]
    ppermute x1, starting transfers between devices: 4.04 us -> 3.02 us  [shards(): raw = lax.ppermute(tensor_blocks, 'orb', perm)]
    ppermute x1, starting transfers between devices: 1.02 us -> 0.45 us  [shards(): tails.append(lax.ppermute(tail, 'orb', perm))]
where the time goes in v9:
time: 29.3 us; the launch traced here: 29.2 us
  waiting for transfers between devices  13.9 us (47%)
  starting transfers between devices  11.2 us (38%)
  Pallas kernels  2.59 us (9%)
  other arithmetic  0.74 us (3%)
  between operations  0.71 us (2%)
    ppermute x1, waiting for transfers between devices, shards(): tails.append(lax.ppermute(tail, 'orb', perm))  8.92 us
    ppermute x4, waiting for transfers between devices, shards(): lax.ppermute(parts, 'aux', [(i, i ^ way * step) for i in range(aux)])  4.97 us
    ppermute x2, starting transfers between devices, shards(): packs.append(lax.ppermute(packed, 'orb', perm))  4.12 us
    ppermute x4, starting transfers between devices, shards(): lax.ppermute(parts, 'aux', [(i, i ^ way * step) for i in range(aux)])  3.63 us
    ppermute x1, starting transfers between devices, shards(): raw = lax.ppermute(tensor_blocks, 'orb', perm)  3.02 us
    pallas_call x1, Pallas kernels, shards(): pl.pallas_call(functools.partial(exchange_kernel, orb, slots, aux_width),...  1.21 us
    pallas_call x1, Pallas kernels, shards(): pl.pallas_call(functools.partial(pack_kernel, orb), out_shape=[jax.ShapeD...  1.15 us
    add x2, other arithmetic, shards(): terms = [terms[i] + terms[i + 1] for i in range(0, len(terms), 2)]  0.66 us
  transfers between devices with their start and end apart: 8, of which 5 were waited for; matrix products, arithmetic and copies ran while one was open for 0% of the time, Pallas kernels for 5%

profile of v9, /device:TPU:0, one launch (start us, length us, event | category | flops | bytes accessed | tf_op | source)
XLA Modules:
  0.0 29.2 jit_solution(4056150521838472499)
XLA Ops:
  0.0 3.0 %collective-permute-start.3 = (bf16[1,1,3,4,4096]{4,3,2,1,0:T(4,128)(2,1)}, bf16[1,1,3,4,4096]{4,3,2,1,0:T(4,128)(2,1)S(1)}, u32[]{:S(2)}, u32[]{:S(2)}) collective-permute-start(bf16[1,1,3,4,4096]{4,3,2,1,0:T(4,128)(2,1)} %blocks_hbm.1), channel_id=1, source_target_pairs={{0,1},{1,3},{2,0},{3,2},{4,5},{5,7},{6,4},{7,6},{8,9},{9,11},{10,8... | collective-permute-start | bytes 294920 | tf_op jit(solution)/shard_map/ppermute | solution.py:152
  3.7 1.2 %pack.1 = (bf16[528,128]{1,0:T(8,128)(2,1)S(1)}, bf16[144,128]{1,0:T(8,128)(2,1)S(1)}) custom-call(s32[1,1]{1,0:T(1,128)S(6)} %copy.5.kept, s32[1,1,3]{2,1,0:T(1,128)} %pairs_hbm.1, bf16[64,256]{1,0:T(8,128)(2,1)} %density_hbm.1, bf16[1,1,3,4,4096]{4,3,2,1,0:T(4,128)(2,1)} %blocks_hbm.1), custom_call_target="tpu_custom_call" | custom-call | tf_op jit(solution)/shard_map/pack/pallas_call | solution.py:131
  4.8 2.5 %collective-permute-start.2 = (bf16[528,128]{1,0:T(8,128)(2,1)S(1)}, bf16[528,128]{1,0:T(8,128)(2,1)S(1)}, u32[]{:S(2)}, u32[]{:S(2)}) collective-permute-start(bf16[528,128]{1,0:T(8,128)(2,1)S(1)} %get-tuple-element.7.refs_0_.refs_4_), channel_id=1, source_target_pairs={{0,3},{1,2},{2,1},{3,0},{4,7},{5,6},{6,5},{7,4},{8,11},{9,10},{10,... | collective-permute-start | bytes 405512 | tf_op jit(solution)/shard_map/ppermute | solution.py:167
  7.4 1.6 %collective-permute-start.1 = (bf16[528,128]{1,0:T(8,128)(2,1)S(1)}, bf16[528,128]{1,0:T(8,128)(2,1)S(1)}, u32[]{:S(2)}, u32[]{:S(2)}) collective-permute-start(bf16[528,128]{1,0:T(8,128)(2,1)S(1)} %get-tuple-element.7.refs_0_.refs_4_), channel_id=1, source_target_pairs={{0,2},{1,0},{2,3},{3,1},{4,6},{5,4},{6,7},{7,5},{8,10},{9,8},{10,1... | collective-permute-start | bytes 405512 | tf_op jit(solution)/shard_map/ppermute | solution.py:167
  9.0 0.4 %collective-permute-start = (bf16[144,128]{1,0:T(8,128)(2,1)S(1)}, bf16[144,128]{1,0:T(8,128)(2,1)S(1)}, u32[]{:S(2)}, u32[]{:S(2)}) collective-permute-start(bf16[144,128]{1,0:T(8,128)(2,1)S(1)} %get-tuple-element.8), channel_id=1, source_target_pairs={{0,1},{1,3},{2,0},{3,2},{4,5},{5,7},{6,4},{7,6},{8,9},{9,11},{10,8... | collective-permute-start | bytes 110600 | tf_op jit(solution)/shard_map/ppermute | solution.py:165
  9.4 8.9 %collective-permute-done.refs_5_ = bf16[144,128]{1,0:T(8,128)(2,1)S(1)} collective-permute-done((bf16[144,128]{1,0:T(8,128)(2,1)S(1)}, bf16[144,128]{1,0:T(8,128)(2,1)S(1)}, u32[]{:S(2)}, u32[]{:S(2)}) %collective-permute-start) | collective-permute-done | bytes 36896 | tf_op jit(solution)/shard_map/ppermute | solution.py:165
  18.3 0.0 collective-permute-done.3.blocks
  18.3 0.2 relay.1.refs_1_
  18.6 0.0 collective-permute-done.2.refs_3_.refs_7_
  18.6 0.0 collective-permute-done.1.refs_2_.refs_6_
  18.6 0.1 maximum_convert_fusion.meta_ref
  18.7 1.2 %exchange.1 = f32[64,256]{1,0:T(8,128)S(1)} custom-call(s32[12]{0:T(128)S(1)} %maximum_convert_fusion.meta_ref, bf16[528,128]{1,0:T(8,128)(2,1)S(1)} %get-tuple-element.7.refs_0_.refs_4_, bf16[384,128]{1,0:T(8,128)(2,1)S(1)} %relay.1.refs_1_, bf16[528,128]{1,0:T(8,128)(2,1)S(1)} %collective-permute-done.1.refs_2_.refs_6_, ...), custom_call_target="tpu_custom_call" | custom-call | tf_op jit(solution)/shard_map/exchange/pallas_call | solution.py:171
  19.9 0.1 collective-permute-start.4
  20.0 1.2 %collective-permute-done.4 = f32[64,256]{1,0:T(8,128)S(1)} collective-permute-done((f32[64,256]{1,0:T(8,128)S(1)}, f32[64,256]{1,0:T(8,128)S(1)}, u32[]{:S(2)}, u32[]{:S(2)}) %collective-permute-start.4) | collective-permute-done | bytes 65568 | tf_op jit(solution)/shard_map/ppermute | solution.py:190
  21.2 2.5 %collective-permute-start.7 = (f32[64,256]{1,0:T(8,128)S(1)}, f32[64,256]{1,0:T(8,128)S(1)}, u32[]{:S(2)}, u32[]{:S(2)}) collective-permute-start(f32[64,256]{1,0:T(8,128)S(1)} %add.12), channel_id=1, source_target_pairs={{0,24},{4,28},{8,16},{12,20},{16,8},{20,12},{24,0},{28,4},{1,25},{... | collective-permute-start | bytes 196616 | tf_op jit(solution)/shard_map/ppermute | solution.py:190
  23.7 0.5 %collective-permute-start.6 = (f32[64,256]{1,0:T(8,128)S(1)}, f32[64,256]{1,0:T(8,128)S(1)}, u32[]{:S(2)}, u32[]{:S(2)}) collective-permute-start(f32[64,256]{1,0:T(8,128)S(1)} %add.12), channel_id=1, source_target_pairs={{0,16},{4,20},{8,24},{12,28},{16,0},{20,4},{24,8},{28,12},{1,17},{... | collective-permute-start | bytes 196616 | tf_op jit(solution)/shard_map/ppermute | solution.py:190
  24.3 0.5 %collective-permute-start.5 = (f32[64,256]{1,0:T(8,128)S(1)}, f32[64,256]{1,0:T(8,128)S(1)}, u32[]{:S(2)}, u32[]{:S(2)}) collective-permute-start(f32[64,256]{1,0:T(8,128)S(1)} %add.12), channel_id=1, source_target_pairs={{0,8},{4,12},{8,0},{12,4},{16,24},{20,28},{24,16},{28,20},{1,9},{5... | collective-permute-start | bytes 196616 | tf_op jit(solution)/shard_map/ppermute | solution.py:190
  24.8 1.7 %collective-permute-done.7 = f32[64,256]{1,0:T(8,128)S(1)} collective-permute-done((f32[64,256]{1,0:T(8,128)S(1)}, f32[64,256]{1,0:T(8,128)S(1)}, u32[]{:S(2)}, u32[]{:S(2)}) %collective-permute-start.7) | collective-permute-done | bytes 65568 | tf_op jit(solution)/shard_map/ppermute | solution.py:190
  26.5 1.5 %collective-permute-done.6 = f32[64,256]{1,0:T(8,128)S(1)} collective-permute-done((f32[64,256]{1,0:T(8,128)S(1)}, f32[64,256]{1,0:T(8,128)S(1)}, u32[]{:S(2)}, u32[]{:S(2)}) %collective-permute-start.6) | collective-permute-done | bytes 65568 | tf_op jit(solution)/shard_map/ppermute | solution.py:190
  28.0 0.5 %collective-permute-done.5 = f32[64,256]{1,0:T(8,128)S(1)} collective-permute-done((f32[64,256]{1,0:T(8,128)S(1)}, f32[64,256]{1,0:T(8,128)S(1)}, u32[]{:S(2)}, u32[]{:S(2)}) %collective-permute-start.5) | collective-permute-done | bytes 65568 | tf_op jit(solution)/shard_map/ppermute | solution.py:190
  28.5 0.6 %add_add_fusion = f32[64,256]{1,0:T(8,128)} fusion(f32[64,256]{1,0:T(8,128)S(1)} %collective-permute-done.6, f32[64,256]{1,0:T(8,128)S(1)} %collective-permute-done.7, f32[64,256]{1,0:T(8,128)S(1)} %add.12, f32[64,256]{1,0:T(8,128)S(1)} %collective-permute-done.5), kind=kLoop, calls=%fused_computation | loop fusion | flops 49152 | bytes 327680 | tf_op jit(solution)/shard_map/add | solution.py:192
  (5 shorter events, 0.0 us)
Async XLA Ops:
  0.0 18.3 %collective-permute-start.3 = (bf16[1,1,3,4,4096]{4,3,2,1,0:T(4,128)(2,1)}, bf16[1,1,3,4,4096]{4,3,2,1,0:T(4,128)(2,1)S(1)}, u32[]{:S(2)}, u32[]{:S(2)}) collective-permute-start(bf16[1,1,3,4,4096]{4,3,2,1,0:T(4,128)(2,1)} %blocks_hbm.1), channel_id=1, source_target_pairs={{0,1},{1,3},{2,0},{3,2},{4,5},{5,7},{6,4},{7,6},{8,9},{9,11},{10,8... | collective-permute-start | bytes 294920 | tf_op jit(solution)/shard_map/ppermute | solution.py:152
  4.8 13.7 %collective-permute-start.2 = (bf16[528,128]{1,0:T(8,128)(2,1)S(1)}, bf16[528,128]{1,0:T(8,128)(2,1)S(1)}, u32[]{:S(2)}, u32[]{:S(2)}) collective-permute-start(bf16[528,128]{1,0:T(8,128)(2,1)S(1)} %get-tuple-element.7.refs_0_.refs_4_), channel_id=1, source_target_pairs={{0,3},{1,2},{2,1},{3,0},{4,7},{5,6},{6,5},{7,4},{8,11},{9,10},{10,... | collective-permute-start | bytes 405512 | tf_op jit(solution)/shard_map/ppermute | solution.py:167
  7.4 11.2 %collective-permute-start.1 = (bf16[528,128]{1,0:T(8,128)(2,1)S(1)}, bf16[528,128]{1,0:T(8,128)(2,1)S(1)}, u32[]{:S(2)}, u32[]{:S(2)}) collective-permute-start(bf16[528,128]{1,0:T(8,128)(2,1)S(1)} %get-tuple-element.7.refs_0_.refs_4_), channel_id=1, source_target_pairs={{0,2},{1,0},{2,3},{3,1},{4,6},{5,4},{6,7},{7,5},{8,10},{9,8},{10,1... | collective-permute-start | bytes 405512 | tf_op jit(solution)/shard_map/ppermute | solution.py:167
  9.0 9.4 %collective-permute-start = (bf16[144,128]{1,0:T(8,128)(2,1)S(1)}, bf16[144,128]{1,0:T(8,128)(2,1)S(1)}, u32[]{:S(2)}, u32[]{:S(2)}) collective-permute-start(bf16[144,128]{1,0:T(8,128)(2,1)S(1)} %get-tuple-element.8), channel_id=1, source_target_pairs={{0,1},{1,3},{2,0},{3,2},{4,5},{5,7},{6,4},{7,6},{8,9},{9,11},{10,8... | collective-permute-start | bytes 110600 | tf_op jit(solution)/shard_map/ppermute | solution.py:165
  19.9 1.3 %collective-permute-start.4 = (f32[64,256]{1,0:T(8,128)S(1)}, f32[64,256]{1,0:T(8,128)S(1)}, u32[]{:S(2)}, u32[]{:S(2)}) collective-permute-start(f32[64,256]{1,0:T(8,128)S(1)} %exchange.1), channel_id=1, source_target_pairs={{0,4},{4,0},{8,12},{12,8},{16,20},{20,16},{24,28},{28,24},{1,5},{5... | collective-permute-start | bytes 196616 | tf_op jit(solution)/shard_map/ppermute | solution.py:190
  21.2 5.3 %collective-permute-start.7 = (f32[64,256]{1,0:T(8,128)S(1)}, f32[64,256]{1,0:T(8,128)S(1)}, u32[]{:S(2)}, u32[]{:S(2)}) collective-permute-start(f32[64,256]{1,0:T(8,128)S(1)} %add.12), channel_id=1, source_target_pairs={{0,24},{4,28},{8,16},{12,20},{16,8},{20,12},{24,0},{28,4},{1,25},{... | collective-permute-start | bytes 196616 | tf_op jit(solution)/shard_map/ppermute | solution.py:190
  23.7 4.3 %collective-permute-start.6 = (f32[64,256]{1,0:T(8,128)S(1)}, f32[64,256]{1,0:T(8,128)S(1)}, u32[]{:S(2)}, u32[]{:S(2)}) collective-permute-start(f32[64,256]{1,0:T(8,128)S(1)} %add.12), channel_id=1, source_target_pairs={{0,16},{4,20},{8,24},{12,28},{16,0},{20,4},{24,8},{28,12},{1,17},{... | collective-permute-start | bytes 196616 | tf_op jit(solution)/shard_map/ppermute | solution.py:190
  24.3 4.3 %collective-permute-start.5 = (f32[64,256]{1,0:T(8,128)S(1)}, f32[64,256]{1,0:T(8,128)S(1)}, u32[]{:S(2)}, u32[]{:S(2)}) collective-permute-start(f32[64,256]{1,0:T(8,128)S(1)} %add.12), channel_id=1, source_target_pairs={{0,8},{4,12},{8,0},{12,4},{16,24},{20,28},{24,16},{28,20},{1,9},{5... | collective-permute-start | bytes 196616 | tf_op jit(solution)/shard_map/ppermute | solution.py:190

commit v10 on v8

v10 whole, which is shorter than its diff:
```python
import functools

import jax
import jax.numpy as jnp
from jax import lax
from jax.experimental import pallas as pl
from jax.experimental.pallas import tpu as pltpu
from jax.sharding import PartitionSpec as P

BS = 64
LANES = 128
NOTE = 16


def lay_blocks(raw, out_ref):
    slots, aux_width = raw.shape[:2]
    square = raw.reshape(slots * aux_width, BS, BS)
    for tile in range(slots * aux_width // 2):
        both = jnp.concatenate([square[2 * tile], square[2 * tile + 1]], axis=1)
        out_ref[tile * BS : (tile + 1) * BS] = both
    return slots * aux_width // 2


def pack_kernel(
    orb, kept, pairs_hbm, density_hbm, raw_hbm, out_ref, note_ref, pairs, rows, raw, sems
):
    height = rows.shape[0]
    first = pl.multiple_of(lax.rem(lax.axis_index("aux"), 2) * height, height)
    copies = [
        pltpu.make_async_copy(src, dst, sems.at[i])
        for i, (src, dst) in enumerate(
            (
                (raw_hbm, raw),
                (density_hbm.at[pl.ds(first, height)], rows),
                (pairs_hbm, pairs),
            )
        )
    ]
    for copy in copies:
        copy.start()
    for copy in copies:
        copy.wait()
    lay_blocks(raw[0, 0], out_ref)
    tiles = rows.shape[1] // LANES
    for t in range(tiles):
        note_ref[t * height : (t + 1) * height] = rows[:, t * LANES : (t + 1) * LANES]
    shape = (NOTE, LANES)
    lane = lax.broadcasted_iota(jnp.int32, shape, 1)
    note = jnp.zeros(shape, jnp.int32)
    for j in range(pairs.shape[2]):
        note = jnp.where(lane == j, jnp.where(j < kept[0, 0], pairs[0, 0, j], orb), note)
    note_ref[tiles * height :] = note.astype(jnp.float32).astype(jnp.bfloat16)


def merge_kernel(*refs):
    notes, (parts_ref, codes_ref) = refs[:-2], refs[-2:]
    part = notes[0].shape[0] - NOTE
    codes_ref[0] = notes[0][part:][:8].astype(jnp.float32).astype(jnp.int32)
    for i, note in enumerate(notes[1:]):
        parts_ref[i * part : (i + 1) * part] = note[:part]
        codes_ref[i + 1] = note[part:][:8].astype(jnp.float32).astype(jnp.int32)


def relay_kernel(raw, out_ref):
    lay_blocks(raw[0, 0], out_ref)


def half_kernel(orb, slots, aux_width, meta_ref, density_ref, blocks_ref, *refs):
    own_parts, swapped, half_ref, rows = refs[: orb - 1], refs[orb - 1], refs[orb], refs[orb + 1]
    me = lax.axis_index("orb")
    parity = lax.rem(lax.axis_index("aux"), 2)
    height = BS // 2
    count = density_ref.shape[1] // LANES
    near = pl.multiple_of(parity * height, height)
    far = pl.multiple_of((1 - parity) * height, height)
    rows[me] = density_ref[...]
    for way in range(1, orb):
        owner = lax.rem(me - way + orb, orb)
        for t in range(count):
            lanes = slice(t * LANES, (t + 1) * LANES)
            at = (way - 1) * count + t
            rows[owner, pl.ds(near, height), lanes] = own_parts[way - 1][
                t * height : (t + 1) * height
            ]
            rows[owner, pl.ds(far, height), lanes] = swapped[at * height : (at + 1) * height]
    rows[orb] = jnp.zeros_like(rows[orb])
    selected = jnp.concatenate([rows[meta_ref[j]] for j in range(slots)], axis=0)
    tiles = blocks_ref.shape[0] // BS
    own = jnp.concatenate([blocks_ref[t * BS : (t + 1) * BS] for t in range(tiles)], axis=1)
    left = []
    for p in range(aux_width):
        cuts = [(j * aux_width + p) * BS for j in range(slots)]
        left.append(jnp.concatenate([own[:, cut : cut + BS] for cut in cuts], axis=1))
    left = jnp.concatenate(left, axis=0)
    half = jnp.dot(left, selected, preferred_element_type=jnp.float32).astype(jnp.bfloat16)
    for k in range(orb):
        half_ref[k] = jnp.concatenate(
            [half[p * BS : (p + 1) * BS, k * BS : (k + 1) * BS] for p in range(aux_width)],
            axis=1,
        )
    half_ref[orb] = jnp.zeros_like(half_ref[orb])


def exchange_kernel(orb, slots, aux_width, meta_ref, half_ref, *refs):
    packs, (out_ref, held) = refs[:orb], refs[orb:]
    me = lax.axis_index("orb")
    per_slot = aux_width * BS // LANES
    for way in range(orb):
        total = None
        for j in range(slots):
            tiles = [
                packs[way][t * BS : (t + 1) * BS] for t in range(j * per_slot, (j + 1) * per_slot)
            ]
            term = lax.dot_general(
                half_ref[meta_ref[way * slots + j]],
                jnp.concatenate(tiles, axis=1),
                (((1,), (1,)), ((), ())),
                preferred_element_type=jnp.float32,
            )
            total = term if total is None else total + term
        held[lax.rem(me - way + orb, orb)] = total
    out_ref[...] = jnp.concatenate([held[n] for n in range(orb)], axis=1)


def shards(density, tensor_blocks, pairs, kept):
    full_width = density.shape[1]
    slots = tensor_blocks.shape[2]
    aux_width = tensor_blocks.shape[3]
    orb = lax.axis_size("orb")
    aux = lax.axis_size("aux")
    height = BS // 2
    part = height * full_width // LANES
    size = slots * aux_width * BS // LANES * BS
    vmem = pl.BlockSpec(memory_space=pltpu.VMEM)
    smem = pl.BlockSpec(memory_space=pltpu.SMEM)
    hbm = pl.BlockSpec(memory_space=pltpu.HBM)
    params = pltpu.CompilerParams(vmem_limit_bytes=32 * 1024 * 1024)
    laid = jax.ShapeDtypeStruct((size, LANES), jnp.bfloat16)
    perms = [[(i, (i + way) % orb) for i in range(orb)] for way in range(orb)]

    own, note = pl.pallas_call(
        functools.partial(pack_kernel, orb),
        out_shape=[laid, jax.ShapeDtypeStruct((part + NOTE, LANES), jnp.bfloat16)],
        in_specs=[smem, hbm, hbm, hbm],
        out_specs=[vmem, vmem],
        scratch_shapes=[
            pltpu.SMEM(pairs.shape, jnp.int32),
            pltpu.VMEM((height, full_width), jnp.bfloat16),
            pltpu.VMEM(tensor_blocks.shape, jnp.bfloat16),
            pltpu.SemaphoreType.DMA((3,)),
        ],
        compiler_params=params,
        name="pack",
    )(
        kept,
        *(pltpu.with_memory_space_constraint(a, pltpu.HBM) for a in (pairs, density, tensor_blocks)),
    )
    notes = [note] + [lax.ppermute(note, "orb", perms[way]) for way in range(1, orb)]
    raw = lax.ppermute(tensor_blocks, "orb", perms[orb // 2])
    notes, raw = lax.optimization_barrier((notes, raw))
    packs = [own]
    for way in range(1, orb):
        if way == orb // 2:
            packs.append(
                pl.pallas_call(
                    relay_kernel,
                    out_shape=laid,
                    in_specs=[vmem],
                    out_specs=vmem,
                    compiler_params=params,
                    name="relay",
                )(raw)
            )
        else:
            packs.append(lax.ppermute(own, "orb", perms[way]))
    parts, codes = pl.pallas_call(
        merge_kernel,
        out_shape=[
            jax.ShapeDtypeStruct(((orb - 1) * part, LANES), jnp.bfloat16),
            jax.ShapeDtypeStruct((orb, 8, LANES), jnp.int32),
        ],
        in_specs=[vmem] * orb,
        out_specs=[vmem, vmem],
        compiler_params=params,
        name="merge",
    )(*notes)
    codes = codes[:, 0, :slots].reshape(orb * slots)
    swapped = lax.ppermute(parts, "aux", [(i, i ^ 1) for i in range(aux)])
    half = pl.pallas_call(
        functools.partial(half_kernel, orb, slots, aux_width),
        out_shape=jax.ShapeDtypeStruct((orb + 1, BS, aux_width * BS), jnp.bfloat16),
        in_specs=[smem] + [vmem] * (orb + 2),
        out_specs=vmem,
        scratch_shapes=[pltpu.VMEM((orb + 1, BS, full_width), jnp.bfloat16)],
        compiler_params=params,
        name="half",
    )(codes, density, own, *notes[1:], swapped)
    parts = pl.pallas_call(
        functools.partial(exchange_kernel, orb, slots, aux_width),
        out_shape=jax.ShapeDtypeStruct((BS, full_width), jnp.float32),
        in_specs=[smem] + [vmem] * (orb + 1),
        out_specs=vmem,
        scratch_shapes=[pltpu.VMEM((orb, BS, BS), jnp.float32)],
        compiler_params=params,
        name="exchange",
    )(codes, half, *packs)

    step = 1
    while step < aux:
        ways = 2 if step == 1 or step * 4 > aux else 4
        terms = [parts]
        for way in range(1, ways):
            terms.append(lax.ppermute(parts, "aux", [(i, i ^ (way * step)) for i in range(aux)]))
        while len(terms) > 1:
            terms = [terms[i] + terms[i + 1] for i in range(0, len(terms), 2)]
        parts = terms[0]
        step *= ways
    return parts


def solution(mesh):
    return jax.shard_map(
        shards,
        mesh=mesh,
        in_specs=(
            P("orb", None),
            P("orb", "aux", None, None, None),
            P("orb", "aux", None),
            P("orb", "aux"),
        ),
        out_specs=P("orb", None),
        check_vma=False,
    )
```

time: 27.6 us -> 29.5 us (1.069)
  starting transfers between devices: 10.8 us -> 14.6 us
  waiting for transfers between devices: 12.6 us -> 10.1 us
  Pallas kernels: 2.59 us -> 3.1 us
    ppermute x4 -> x7, starting transfers between devices: 7.13 us -> 11 us  [the longest x1 4.04 us: shards(): raw = lax.ppermute(tensor_blocks, 'orb', perms[orb // 2])]
    ppermute x4 -> x7, waiting for transfers between devices: 7.58 us -> 5.13 us  [the longest x2 2.39 us: shards(): packs.append(lax.ppermute(own, 'orb', perms[way]))]
    pallas_call x2 -> x4, Pallas kernels: 1.38 us -> 2.23 us  [the longest x1 1.16 us: shards(): pl.pallas_call(functools.partial(pack_kernel, orb), out_shape=[laid, jax....]
    pallas_call x1, Pallas kernels: 1.2 us -> 0.87 us  [shards(): pl.pallas_call(functools.partial(exchange_kernel, orb, slots, aux_width),...]
  transfers between devices with their start and end apart: 8 -> 11, of which waited for: 5 -> 7; matrix products, arithmetic and copies ran while one was open for 0% -> 0% of each run, Pallas kernels for 5% -> 8%
where the time goes in v10:
time: 29.5 us; the launch traced here: 29.3 us
  starting transfers between devices  14.6 us (49%)
  waiting for transfers between devices  10.1 us (34%)
  Pallas kernels  3.1 us (11%)
  between operations  0.72 us (2%)
  other arithmetic  0.66 us (2%)
    ppermute x4, waiting for transfers between devices, shards(): lax.ppermute(parts, 'aux', [(i, i ^ way * step) for i in range(aux)])  4.97 us
    ppermute x1, starting transfers between devices, shards(): raw = lax.ppermute(tensor_blocks, 'orb', perms[orb // 2])  4.04 us
    ppermute x2, starting transfers between devices, shards(): packs.append(lax.ppermute(own, 'orb', perms[way]))  3.82 us
    ppermute x4, starting transfers between devices, shards(): lax.ppermute(parts, 'aux', [(i, i ^ way * step) for i in range(aux)])  3.62 us
    ppermute x3, starting transfers between devices, shards(): lax.ppermute(note, 'orb', perms[way])  3.09 us
    ppermute x2, waiting for transfers between devices, shards(): packs.append(lax.ppermute(own, 'orb', perms[way]))  2.39 us
    ppermute x3, waiting for transfers between devices, shards(): lax.ppermute(note, 'orb', perms[way])  1.86 us
    pallas_call x1, Pallas kernels, shards(): pl.pallas_call(functools.partial(pack_kernel, orb), out_shape=[laid, jax....  1.16 us
  transfers between devices with their start and end apart: 11, of which 7 were waited for; matrix products, arithmetic and copies ran while one was open for 0% of the time, Pallas kernels for 8%

profile of v10, /device:TPU:0, one launch (start us, length us, event | category | flops | bytes accessed | tf_op | source)
XLA Modules:
  0.0 29.3 jit_solution(5472544912240884826)
XLA Ops:
  0.0 4.0 %collective-permute-start.3 = (bf16[1,1,3,4,4096]{4,3,2,1,0:T(4,128)(2,1)}, bf16[1,1,3,4,4096]{4,3,2,1,0:T(4,128)(2,1)S(1)}, u32[]{:S(2)}, u32[]{:S(2)}) collective-permute-start(bf16[1,1,3,4,4096]{4,3,2,1,0:T(4,128)(2,1)} %raw_hbm.1), channel_id=1, source_target_pairs={{0,2},{1,3},{2,0},{3,1},{4,6},{5,7},{6,4},{7,5},{8,10},{9,11},{10,... | collective-permute-start | bytes 294920 | tf_op jit(solution)/shard_map/ppermute | solution.py:159
  4.7 1.2 %pack.1 = (bf16[384,128]{1,0:T(8,128)(2,1)S(1)}, bf16[80,128]{1,0:T(8,128)(2,1)S(1)}) custom-call(s32[1,1]{1,0:T(1,128)S(6)} %copy.5.kept, s32[1,1,3]{2,1,0:T(1,128)} %pairs_hbm.1, bf16[64,256]{1,0:T(8,128)(2,1)} %density_ref.1, bf16[1,1,3,4,4096]{4,3,2,1,0:T(4,128)(2,1)} %raw_hbm.1), custom_call_target="tpu_custom_call" | custom-call | tf_op jit(solution)/shard_map/pack/pallas_call | solution.py:141
  5.9 1.4 %collective-permute-start.2 = (bf16[80,128]{1,0:T(8,128)(2,1)S(1)}, bf16[80,128]{1,0:T(8,128)(2,1)S(1)}, u32[]{:S(2)}, u32[]{:S(2)}) collective-permute-start(bf16[80,128]{1,0:T(8,128)(2,1)S(1)} %get-tuple-element.15.refs_0_), channel_id=1, source_target_pairs={{0,3},{1,0},{2,1},{3,2},{4,7},{5,4},{6,5},{7,6},{8,11},{9,8},{10,9... | collective-permute-start | bytes 61448 | tf_op jit(solution)/shard_map/ppermute | solution.py:158
  7.3 1.7 %collective-permute-start.1 = (bf16[80,128]{1,0:T(8,128)(2,1)S(1)}, bf16[80,128]{1,0:T(8,128)(2,1)S(1)}, u32[]{:S(2)}, u32[]{:S(2)}) collective-permute-start(bf16[80,128]{1,0:T(8,128)(2,1)S(1)} %get-tuple-element.15.refs_0_), channel_id=1, source_target_pairs={{0,2},{1,3},{2,0},{3,1},{4,6},{5,7},{6,4},{7,5},{8,10},{9,11},{10,... | collective-permute-start | bytes 61448 | tf_op jit(solution)/shard_map/ppermute | solution.py:158
  8.9 0.0 collective-permute-start
  8.9 3.8 %collective-permute-start.6 = (bf16[384,128]{1,0:T(8,128)(2,1)S(1)}, bf16[384,128]{1,0:T(8,128)(2,1)S(1)}, u32[]{:S(2)}, u32[]{:S(2)}) collective-permute-start(bf16[384,128]{1,0:T(8,128)(2,1)S(1)} %get-tuple-element.20.blocks_ref.refs_0_), channel_id=1, source_target_pairs={{0,3},{1,0},{2,1},{3,2},{4,7},{5,4},{6,5},{7,6},{8,11},{9,8},{10,9... | collective-permute-start | bytes 294920 | tf_op jit(solution)/shard_map/ppermute | solution.py:175
  12.8 0.0 collective-permute-done.2.refs_3_.refs_2_
  12.8 0.0 collective-permute-start.5
  12.8 0.0 collective-permute-done.1.refs_2_.refs_1_
  12.8 1.9 %collective-permute-done.refs_1_.refs_0_ = bf16[80,128]{1,0:T(8,128)(2,1)S(1)} collective-permute-done((bf16[80,128]{1,0:T(8,128)(2,1)S(1)}, bf16[80,128]{1,0:T(8,128)(2,1)S(1)}, u32[]{:S(2)}, u32[]{:S(2)}) %collective-permute-start) | collective-permute-done | bytes 20512 | tf_op jit(solution)/shard_map/ppermute | solution.py:158
  14.6 0.0 collective-permute-done.3.raw
  14.6 0.1 collective-permute-start.4
  14.7 0.1 reshape_squeeze.3.meta_ref
  14.8 0.0 copy-start
  14.8 0.2 relay.1.refs_2_
  15.1 0.9 %collective-permute-done.4.refs_3_ = bf16[192,128]{1,0:T(8,128)(2,1)S(1)} collective-permute-done((bf16[192,128]{1,0:T(8,128)(2,1)S(1)}, bf16[192,128]{1,0:T(8,128)(2,1)S(1)}, u32[]{:S(2)}, u32[]{:S(2)}) %collective-permute-start.4) | collective-permute-done | bytes 49184 | tf_op jit(solution)/shard_map/ppermute | solution.py:188
  15.9 0.0 copy-done
  15.9 0.8 %half.1.half_ref = bf16[5,64,256]{2,1,0:T(8,128)(2,1)S(1)} custom-call(s32[12]{0:T(128)S(1)} %reshape_squeeze.3.meta_ref, bf16[64,256]{1,0:T(8,128)(2,1)S(1)} %copy-done, bf16[384,128]{1,0:T(8,128)(2,1)S(1)} %get-tuple-element.20.blocks_ref.refs_0_, bf16[80,128]{1,0:T(8,128)(2,1)S(1)} %collective-permute-done.refs_1_.refs_0_, ...), custom_call_target="tpu_custom_call" | custom-call | tf_op jit(solution)/shard_map/half/pallas_call | solution.py:189
  16.8 0.0 collective-permute-done.6.refs_3_
  16.8 2.4 %collective-permute-done.5.refs_1_ = bf16[384,128]{1,0:T(8,128)(2,1)S(1)} collective-permute-done((bf16[384,128]{1,0:T(8,128)(2,1)S(1)}, bf16[384,128]{1,0:T(8,128)(2,1)S(1)}, u32[]{:S(2)}, u32[]{:S(2)}) %collective-permute-start.5) | collective-permute-done | bytes 98336 | tf_op jit(solution)/shard_map/ppermute | solution.py:175
  19.2 0.9 %exchange.1 = f32[64,256]{1,0:T(8,128)S(1)} custom-call(s32[12]{0:T(128)S(1)} %reshape_squeeze.3.meta_ref, bf16[5,64,256]{2,1,0:T(8,128)(2,1)S(1)} %half.1.half_ref, bf16[384,128]{1,0:T(8,128)(2,1)S(1)} %get-tuple-element.20.blocks_ref.refs_0_, bf16[384,128]{1,0:T(8,128)(2,1)S(1)} %collective-permute-done.5.refs_1_, bf16[384,128]{1,0:T(8,128)(2,1)S(1)} %relay.1.refs_2_, ...), custom_call_target="tpu_custom_call" | custom-call | tf_op jit(solution)/shard_map/exchange/pallas_call | solution.py:198
  20.1 0.1 collective-permute-start.7
  20.1 1.2 %collective-permute-done.7 = f32[64,256]{1,0:T(8,128)S(1)} collective-permute-done((f32[64,256]{1,0:T(8,128)S(1)}, f32[64,256]{1,0:T(8,128)S(1)}, u32[]{:S(2)}, u32[]{:S(2)}) %collective-permute-start.7) | collective-permute-done | bytes 65568 | tf_op jit(solution)/shard_map/ppermute | solution.py:213
  21.4 2.5 %collective-permute-start.10 = (f32[64,256]{1,0:T(8,128)S(1)}, f32[64,256]{1,0:T(8,128)S(1)}, u32[]{:S(2)}, u32[]{:S(2)}) collective-permute-start(f32[64,256]{1,0:T(8,128)S(1)} %add.12), channel_id=1, source_target_pairs={{0,24},{4,28},{8,16},{12,20},{16,8},{20,12},{24,0},{28,4},{1,25},{... | collective-permute-start | bytes 196616 | tf_op jit(solution)/shard_map/ppermute | solution.py:213
  23.9 0.5 %collective-permute-start.9 = (f32[64,256]{1,0:T(8,128)S(1)}, f32[64,256]{1,0:T(8,128)S(1)}, u32[]{:S(2)}, u32[]{:S(2)}) collective-permute-start(f32[64,256]{1,0:T(8,128)S(1)} %add.12), channel_id=1, source_target_pairs={{0,16},{4,20},{8,24},{12,28},{16,0},{20,4},{24,8},{28,12},{1,17},{... | collective-permute-start | bytes 196616 | tf_op jit(solution)/shard_map/ppermute | solution.py:213
  24.4 0.5 %collective-permute-start.8 = (f32[64,256]{1,0:T(8,128)S(1)}, f32[64,256]{1,0:T(8,128)S(1)}, u32[]{:S(2)}, u32[]{:S(2)}) collective-permute-start(f32[64,256]{1,0:T(8,128)S(1)} %add.12), channel_id=1, source_target_pairs={{0,8},{4,12},{8,0},{12,4},{16,24},{20,28},{24,16},{28,20},{1,9},{5... | collective-permute-start | bytes 196616 | tf_op jit(solution)/shard_map/ppermute | solution.py:213
  25.0 1.7 %collective-permute-done.10 = f32[64,256]{1,0:T(8,128)S(1)} collective-permute-done((f32[64,256]{1,0:T(8,128)S(1)}, f32[64,256]{1,0:T(8,128)S(1)}, u32[]{:S(2)}, u32[]{:S(2)}) %collective-permute-start.10) | collective-permute-done | bytes 65568 | tf_op jit(solution)/shard_map/ppermute | solution.py:213
  26.7 1.5 %collective-permute-done.9 = f32[64,256]{1,0:T(8,128)S(1)} collective-permute-done((f32[64,256]{1,0:T(8,128)S(1)}, f32[64,256]{1,0:T(8,128)S(1)}, u32[]{:S(2)}, u32[]{:S(2)}) %collective-permute-start.9) | collective-permute-done | bytes 65568 | tf_op jit(solution)/shard_map/ppermute | solution.py:213
  28.2 0.5 %collective-permute-done.8 = f32[64,256]{1,0:T(8,128)S(1)} collective-permute-done((f32[64,256]{1,0:T(8,128)S(1)}, f32[64,256]{1,0:T(8,128)S(1)}, u32[]{:S(2)}, u32[]{:S(2)}) %collective-permute-start.8) | collective-permute-done | bytes 65568 | tf_op jit(solution)/shard_map/ppermute | solution.py:213
  28.7 0.6 %add_add_fusion = f32[64,256]{1,0:T(8,128)} fusion(f32[64,256]{1,0:T(8,128)S(1)} %collective-permute-done.9, f32[64,256]{1,0:T(8,128)S(1)} %collective-permute-done.10, f32[64,256]{1,0:T(8,128)S(1)} %add.12, f32[64,256]{1,0:T(8,128)S(1)} %collective-permute-done.8), kind=kLoop, calls=%fused_computation | loop fusion | flops 49152 | bytes 327680 | tf_op jit(solution)/shard_map/add | solution.py:215
  (3 shorter events, 0.0 us)
Async XLA Ops:
  0.0 14.6 %collective-permute-start.3 = (bf16[1,1,3,4,4096]{4,3,2,1,0:T(4,128)(2,1)}, bf16[1,1,3,4,4096]{4,3,2,1,0:T(4,128)(2,1)S(1)}, u32[]{:S(2)}, u32[]{:S(2)}) collective-permute-start(bf16[1,1,3,4,4096]{4,3,2,1,0:T(4,128)(2,1)} %raw_hbm.1), channel_id=1, source_target_pairs={{0,2},{1,3},{2,0},{3,1},{4,6},{5,7},{6,4},{7,5},{8,10},{9,11},{10,... | collective-permute-start | bytes 294920 | tf_op jit(solution)/shard_map/ppermute | solution.py:159
  5.9 6.9 %collective-permute-start.2 = (bf16[80,128]{1,0:T(8,128)(2,1)S(1)}, bf16[80,128]{1,0:T(8,128)(2,1)S(1)}, u32[]{:S(2)}, u32[]{:S(2)}) collective-permute-start(bf16[80,128]{1,0:T(8,128)(2,1)S(1)} %get-tuple-element.15.refs_0_), channel_id=1, source_target_pairs={{0,3},{1,0},{2,1},{3,2},{4,7},{5,4},{6,5},{7,6},{8,11},{9,8},{10,9... | collective-permute-start | bytes 61448 | tf_op jit(solution)/shard_map/ppermute | solution.py:158
  7.3 5.5 %collective-permute-start.1 = (bf16[80,128]{1,0:T(8,128)(2,1)S(1)}, bf16[80,128]{1,0:T(8,128)(2,1)S(1)}, u32[]{:S(2)}, u32[]{:S(2)}) collective-permute-start(bf16[80,128]{1,0:T(8,128)(2,1)S(1)} %get-tuple-element.15.refs_0_), channel_id=1, source_target_pairs={{0,2},{1,3},{2,0},{3,1},{4,6},{5,7},{6,4},{7,5},{8,10},{9,11},{10,... | collective-permute-start | bytes 61448 | tf_op jit(solution)/shard_map/ppermute | solution.py:158
  8.9 5.7 %collective-permute-start = (bf16[80,128]{1,0:T(8,128)(2,1)S(1)}, bf16[80,128]{1,0:T(8,128)(2,1)S(1)}, u32[]{:S(2)}, u32[]{:S(2)}) collective-permute-start(bf16[80,128]{1,0:T(8,128)(2,1)S(1)} %get-tuple-element.15.refs_0_), channel_id=1, source_target_pairs={{0,1},{1,2},{2,3},{3,0},{4,5},{5,6},{6,7},{7,4},{8,9},{9,10},{10,1... | collective-permute-start | bytes 61448 | tf_op jit(solution)/shard_map/ppermute | solution.py:158
  8.9 7.8 %collective-permute-start.6 = (bf16[384,128]{1,0:T(8,128)(2,1)S(1)}, bf16[384,128]{1,0:T(8,128)(2,1)S(1)}, u32[]{:S(2)}, u32[]{:S(2)}) collective-permute-start(bf16[384,128]{1,0:T(8,128)(2,1)S(1)} %get-tuple-element.20.blocks_ref.refs_0_), channel_id=1, source_target_pairs={{0,3},{1,0},{2,1},{3,2},{4,7},{5,4},{6,5},{7,6},{8,11},{9,8},{10,9... | collective-permute-start | bytes 294920 | tf_op jit(solution)/shard_map/ppermute | solution.py:175
  12.8 6.4 %collective-permute-start.5 = (bf16[384,128]{1,0:T(8,128)(2,1)S(1)}, bf16[384,128]{1,0:T(8,128)(2,1)S(1)}, u32[]{:S(2)}, u32[]{:S(2)}) collective-permute-start(bf16[384,128]{1,0:T(8,128)(2,1)S(1)} %get-tuple-element.20.blocks_ref.refs_0_), channel_id=1, source_target_pairs={{0,1},{1,2},{2,3},{3,0},{4,5},{5,6},{6,7},{7,4},{8,9},{9,10},{10,1... | collective-permute-start | bytes 294920 | tf_op jit(solution)/shard_map/ppermute | solution.py:175
  14.6 1.3 %collective-permute-start.4 = (bf16[192,128]{1,0:T(8,128)(2,1)S(1)}, bf16[192,128]{1,0:T(8,128)(2,1)S(1)}, u32[]{:S(2)}, u32[]{:S(2)}) collective-permute-start(bf16[192,128]{1,0:T(8,128)(2,1)S(1)} %get-tuple-element.21), channel_id=1, source_target_pairs={{0,4},{4,0},{8,12},{12,8},{16,20},{20,16},{24,28},{28,24},{1,5},{5... | collective-permute-start | bytes 147464 | tf_op jit(solution)/shard_map/ppermute | solution.py:188
  14.8 1.1 %copy-start = (bf16[64,256]{1,0:T(8,128)(2,1)S(1)}, bf16[64,256]{1,0:T(8,128)(2,1)}, u32[]{:S(2)}) copy-start(bf16[64,256]{1,0:T(8,128)(2,1)} %density_ref.1) | copy-start | bytes 98308
  20.1 1.3 %collective-permute-start.7 = (f32[64,256]{1,0:T(8,128)S(1)}, f32[64,256]{1,0:T(8,128)S(1)}, u32[]{:S(2)}, u32[]{:S(2)}) collective-permute-start(f32[64,256]{1,0:T(8,128)S(1)} %exchange.1), channel_id=1, source_target_pairs={{0,4},{4,0},{8,12},{12,8},{16,20},{20,16},{24,28},{28,24},{1,5},{5... | collective-permute-start | bytes 196616 | tf_op jit(solution)/shard_map/ppermute | solution.py:213
  21.4 5.3 %collective-permute-start.10 = (f32[64,256]{1,0:T(8,128)S(1)}, f32[64,256]{1,0:T(8,128)S(1)}, u32[]{:S(2)}, u32[]{:S(2)}) collective-permute-start(f32[64,256]{1,0:T(8,128)S(1)} %add.12), channel_id=1, source_target_pairs={{0,24},{4,28},{8,16},{12,20},{16,8},{20,12},{24,0},{28,4},{1,25},{... | collective-permute-start | bytes 196616 | tf_op jit(solution)/shard_map/ppermute | solution.py:213
  23.9 4.3 %collective-permute-start.9 = (f32[64,256]{1,0:T(8,128)S(1)}, f32[64,256]{1,0:T(8,128)S(1)}, u32[]{:S(2)}, u32[]{:S(2)}) collective-permute-start(f32[64,256]{1,0:T(8,128)S(1)} %add.12), channel_id=1, source_target_pairs={{0,16},{4,20},{8,24},{12,28},{16,0},{20,4},{24,8},{28,12},{1,17},{... | collective-permute-start | bytes 196616 | tf_op jit(solution)/shard_map/ppermute | solution.py:213
  24.4 4.3 %collective-permute-start.8 = (f32[64,256]{1,0:T(8,128)S(1)}, f32[64,256]{1,0:T(8,128)S(1)}, u32[]{:S(2)}, u32[]{:S(2)}) collective-permute-start(f32[64,256]{1,0:T(8,128)S(1)} %add.12), channel_id=1, source_target_pairs={{0,8},{4,12},{8,0},{12,4},{16,24},{20,28},{24,16},{28,20},{1,9},{5... | collective-permute-start | bytes 196616 | tf_op jit(solution)/shard_map/ppermute | solution.py:213

commit v11 on v10

v11 whole, which is shorter than its diff:
```python
import functools

import jax
import jax.numpy as jnp
from jax import lax
from jax.experimental import pallas as pl
from jax.experimental.pallas import tpu as pltpu
from jax.sharding import PartitionSpec as P

BS = 64
LANES = 128
NOTE = 16


def lay_blocks(raw, out_ref):
    slots, aux_width = raw.shape[:2]
    square = raw.reshape(slots * aux_width, BS, BS)
    for tile in range(slots * aux_width // 2):
        both = jnp.concatenate([square[2 * tile], square[2 * tile + 1]], axis=1)
        out_ref[tile * BS : (tile + 1) * BS] = both
    return slots * aux_width // 2


def core_parity():
    return lax.rem(lax.axis_index("aux"), 2)


def pack_kernel(
    orb, kept, pairs_hbm, density_hbm, raw_hbm, full_ref, tail_ref, pairs, rows, raw, sems
):
    copies = [
        pltpu.make_async_copy(src, dst, sems.at[i])
        for i, (src, dst) in enumerate(((raw_hbm, raw), (density_hbm, rows), (pairs_hbm, pairs)))
    ]
    for copy in copies:
        copy.start()
    for copy in copies:
        copy.wait()
    size = lay_blocks(raw[0, 0], full_ref) * BS
    height = BS // 2
    near = pl.multiple_of(core_parity() * height, height)
    tiles = rows.shape[1] // LANES
    for t in range(tiles):
        lanes = slice(t * LANES, (t + 1) * LANES)
        full_ref[size + t * BS : size + (t + 1) * BS] = rows[:, lanes]
        tail_ref[t * height : (t + 1) * height] = rows[pl.ds(near, height), lanes]
    shape = (NOTE, LANES)
    lane = lax.broadcasted_iota(jnp.int32, shape, 1)
    note = jnp.zeros(shape, jnp.int32)
    for j in range(pairs.shape[2]):
        note = jnp.where(lane == j, jnp.where(j < kept[0, 0], pairs[0, 0, j], orb), note)
    note = note.astype(jnp.float32).astype(jnp.bfloat16)
    full_ref[size + tiles * BS :] = note
    tail_ref[tiles * height :] = note


def lean_kernel(full_ref, out_ref):
    size = out_ref.shape[0] - NOTE
    out_ref[:size] = full_ref[:size]
    out_ref[size:] = full_ref[full_ref.shape[0] - NOTE :]


def relay_kernel(raw, out_ref):
    lay_blocks(raw[0, 0], out_ref)


def merge_kernel(size, *refs):
    parts, out_ref = refs[:-1], refs[-1]
    at = 0
    for i, part in enumerate(parts):
        first = size if i < len(parts) - 1 else 0
        count = part.shape[0] - NOTE - first
        out_ref[at : at + count] = part[first : first + count]
        at += count


def half_kernel(orb, slots, aux_width, meta_ref, density_ref, own_ref, *refs):
    fulls, (tail, swapped, half_ref, rows) = refs[:-4], refs[-4:]
    me = lax.axis_index("orb")
    parity = core_parity()
    height = BS // 2
    count = density_ref.shape[1] // LANES
    size = slots * aux_width * BS // LANES * BS
    near = pl.multiple_of(parity * height, height)
    far = pl.multiple_of((1 - parity) * height, height)
    rows[me] = density_ref[...]
    for i, full in enumerate(fulls):
        ahead = lax.rem(me + (1 - 2 * parity) * (i + 1) + orb, orb)
        behind = lax.rem(me - (1 - 2 * parity) * (i + 1) + orb, orb)
        for t in range(count):
            lanes = slice(t * LANES, (t + 1) * LANES)
            at = (i * count + t) * BS
            rows[ahead, :, lanes] = full[size + t * BS : size + (t + 1) * BS]
            rows[behind, :, lanes] = swapped[at : at + BS]
    across = lax.rem(me + orb // 2, orb)
    for t in range(count):
        lanes = slice(t * LANES, (t + 1) * LANES)
        at = len(fulls) * count * BS + t * height
        rows[across, pl.ds(near, height), lanes] = tail[t * height : (t + 1) * height]
        rows[across, pl.ds(far, height), lanes] = swapped[at : at + height]
    rows[orb] = jnp.zeros_like(rows[orb])
    selected = jnp.concatenate([rows[meta_ref[j]] for j in range(slots)], axis=0)
    own = jnp.concatenate([own_ref[at : at + BS] for at in range(0, size, BS)], axis=1)
    left = []
    for p in range(aux_width):
        cuts = [(j * aux_width + p) * BS for j in range(slots)]
        left.append(jnp.concatenate([own[:, cut : cut + BS] for cut in cuts], axis=1))
    left = jnp.concatenate(left, axis=0)
    half = jnp.dot(left, selected, preferred_element_type=jnp.float32).astype(jnp.bfloat16)
    for k in range(orb):
        half_ref[k] = jnp.concatenate(
            [half[p * BS : (p + 1) * BS, k * BS : (k + 1) * BS] for p in range(aux_width)],
            axis=1,
        )
    half_ref[orb] = jnp.zeros_like(half_ref[orb])


def exchange_kernel(orb, slots, aux_width, meta_ref, half_ref, *refs):
    packs, (out_ref, held) = refs[:orb], refs[orb:]
    me = lax.axis_index("orb")
    parity = core_parity()
    per_slot = aux_width * BS // LANES
    steps = [0, orb // 2]
    for i in range(1, orb // 2):
        steps += [(1 - 2 * parity) * i, (2 * parity - 1) * i]
    for way in range(orb):
        total = None
        for j in range(slots):
            tiles = [
                packs[way][t * BS : (t + 1) * BS] for t in range(j * per_slot, (j + 1) * per_slot)
            ]
            term = lax.dot_general(
                half_ref[meta_ref[way * slots + j]],
                jnp.concatenate(tiles, axis=1),
                (((1,), (1,)), ((), ())),
                preferred_element_type=jnp.float32,
            )
            total = term if total is None else total + term
        held[lax.rem(me + steps[way] + orb, orb)] = total
    out_ref[...] = jnp.concatenate([held[n] for n in range(orb)], axis=1)


def shards(density, tensor_blocks, pairs, kept):
    full_width = density.shape[1]
    slots = tensor_blocks.shape[2]
    aux_width = tensor_blocks.shape[3]
    orb = lax.axis_size("orb")
    aux = lax.axis_size("aux")
    rows = full_width // LANES * BS
    size = slots * aux_width * BS // LANES * BS
    vmem = pl.BlockSpec(memory_space=pltpu.VMEM)
    smem = pl.BlockSpec(memory_space=pltpu.SMEM)
    hbm = pl.BlockSpec(memory_space=pltpu.HBM)
    params = pltpu.CompilerParams(vmem_limit_bytes=32 * 1024 * 1024)

    def array(height):
        return jax.ShapeDtypeStruct((height, LANES), jnp.bfloat16)

    def shift(x, even, odd):
        steps = (even, odd)
        perm = [
            (a * orb + o, a * orb + (o + steps[a % 2]) % orb)
            for a in range(aux)
            for o in range(orb)
        ]
        return lax.ppermute(x, ("aux", "orb"), perm)

    full, tail = pl.pallas_call(
        functools.partial(pack_kernel, orb),
        out_shape=[array(size + rows + NOTE), array(rows // 2 + NOTE)],
        in_specs=[smem, hbm, hbm, hbm],
        out_specs=[vmem] * 2,
        scratch_shapes=[
            pltpu.SMEM(pairs.shape, jnp.int32),
            pltpu.VMEM(density.shape, jnp.bfloat16),
            pltpu.VMEM(tensor_blocks.shape, jnp.bfloat16),
            pltpu.SemaphoreType.DMA((3,)),
        ],
        compiler_params=params,
        name="pack",
    )(
        kept,
        *(pltpu.with_memory_space_constraint(a, pltpu.HBM) for a in (pairs, density, tensor_blocks)),
    )
    lean = pl.pallas_call(
        lean_kernel,
        out_shape=array(size + NOTE),
        in_specs=[vmem],
        out_specs=vmem,
        compiler_params=params,
        name="lean",
    )(full)
    raw = shift(tensor_blocks, orb // 2, orb // 2)
    tail_in = shift(tail, orb // 2, orb // 2)
    fulls = [shift(full, -i, i) for i in range(1, orb // 2)]
    leans = [shift(lean, i, -i) for i in range(1, orb // 2)]

    tail_in, raw = lax.optimization_barrier((tail_in, raw))
    merged = pl.pallas_call(
        functools.partial(merge_kernel, size),
        out_shape=array(len(fulls) * rows + rows // 2),
        in_specs=[vmem] * (len(fulls) + 1),
        out_specs=vmem,
        compiler_params=params,
        name="merge",
    )(*fulls, tail_in)
    swapped = lax.ppermute(merged, "aux", [(i, i ^ 1) for i in range(aux)])
    across = pl.pallas_call(
        relay_kernel,
        out_shape=array(size),
        in_specs=[vmem],
        out_specs=vmem,
        compiler_params=params,
        name="relay",
    )(raw)
    half = pl.pallas_call(
        functools.partial(half_kernel, orb, slots, aux_width),
        out_shape=jax.ShapeDtypeStruct((orb + 1, BS, aux_width * BS), jnp.bfloat16),
        in_specs=[smem] + [vmem] * (len(fulls) + 4),
        out_specs=vmem,
        scratch_shapes=[pltpu.VMEM((orb + 1, BS, full_width), jnp.bfloat16)],
        compiler_params=params,
        name="half",
    )(tail[-NOTE, :slots].astype(jnp.int32), density, full, *fulls, tail_in, swapped)
    half, leans = lax.optimization_barrier((half, leans))
    packs, notes = [full, across], [tail, tail_in]
    for pair in zip(fulls, leans):
        packs += pair
        notes += pair
    codes = jnp.concatenate([n[-NOTE, :slots] for n in notes]).astype(jnp.int32)
    parts = pl.pallas_call(
        functools.partial(exchange_kernel, orb, slots, aux_width),
        out_shape=jax.ShapeDtypeStruct((BS, full_width), jnp.float32),
        in_specs=[smem] + [vmem] * (orb + 1),
        out_specs=vmem,
        scratch_shapes=[pltpu.VMEM((orb, BS, BS), jnp.float32)],
        compiler_params=params,
        name="exchange",
    )(codes, half, *packs)

    step = 1
    while step < aux:
        ways = 2 if step == 1 or step * 4 > aux else 4
        terms = [parts]
        for way in range(1, ways):
            terms.append(lax.ppermute(parts, "aux", [(i, i ^ (way * step)) for i in range(aux)]))
        while len(terms) > 1:
            terms = [terms[i] + terms[i + 1] for i in range(0, len(terms), 2)]
        parts = terms[0]
        step *= ways
    return parts


def solution(mesh):
    return jax.shard_map(
        shards,
        mesh=mesh,
        in_specs=(
            P("orb", None),
            P("orb", "aux", None, None, None),
            P("orb", "aux", None),
            P("orb", "aux"),
        ),
        out_specs=P("orb", None),
        check_vma=False,
    )
```

time: 29.5 us -> 26.8 us (0.908)
  starting transfers between devices: 14.6 us -> 11.7 us
    ppermute x7 -> x5, starting transfers between devices: 11 us -> 8.09 us  [the longest x4 8.09 us: shift(): return lax.ppermute(x, ('aux', 'orb'), perm)]
    ppermute x7 -> x5, waiting for transfers between devices: 5.13 us -> 5.31 us  [the longest x4 4.1 us: shift(): return lax.ppermute(x, ('aux', 'orb'), perm)]
    pallas_call x3 -> x4, Pallas kernels: 1.39 us -> 1.39 us  [the longest x1 1.16 us: shards(): pl.pallas_call(functools.partial(pack_kernel, orb), out_shape=[array(size...]
  transfers between devices with their start and end apart: 11 -> 9, of which waited for: 7 -> 8; matrix products, arithmetic and copies ran while one was open for 0% -> 0% of each run, Pallas kernels for 8% -> 8%
where the time goes in v11:
time: 26.8 us; the launch traced here: 26.6 us
  starting transfers between devices  11.7 us (44%)
  waiting for transfers between devices  10.3 us (38%)
  Pallas kernels  3.1 us (12%)
  between operations  0.75 us (3%)
  other arithmetic  0.74 us (3%)
    ppermute x4, starting transfers between devices, shift(): return lax.ppermute(x, ('aux', 'orb'), perm)  8.09 us
    ppermute x4, waiting for transfers between devices, shards(): lax.ppermute(parts, 'aux', [(i, i ^ way * step) for i in range(aux)])  4.97 us
    ppermute x4, waiting for transfers between devices, shift(): return lax.ppermute(x, ('aux', 'orb'), perm)  4.1 us
    ppermute x4, starting transfers between devices, shards(): lax.ppermute(parts, 'aux', [(i, i ^ way * step) for i in range(aux)])  3.62 us
    ppermute x1, waiting for transfers between devices, shards(): swapped = lax.ppermute(merged, 'aux', [(i, i ^ 1) for i in range(aux)])  1.21 us
    pallas_call x1, Pallas kernels, shards(): pl.pallas_call(functools.partial(pack_kernel, orb), out_shape=[array(size...  1.16 us
    pallas_call x1, Pallas kernels, shards(): pl.pallas_call(functools.partial(exchange_kernel, orb, slots, aux_width),...  0.87 us
    pallas_call x1, Pallas kernels, shards(): pl.pallas_call(functools.partial(half_kernel, orb, slots, aux_width), out...  0.84 us
  transfers between devices with their start and end apart: 9, of which 8 were waited for; matrix products, arithmetic and copies ran while one was open for 0% of the time, Pallas kernels for 8%

profile of v11, /device:TPU:0, one launch (start us, length us, event | category | flops | bytes accessed | tf_op | source)
XLA Modules:
  0.0 26.6 jit_solution(4225483088761547525)
XLA Ops:
  0.0 4.0 %collective-permute-start.1 = (bf16[1,1,3,4,4096]{4,3,2,1,0:T(4,128)(2,1)}, bf16[1,1,3,4,4096]{4,3,2,1,0:T(4,128)(2,1)S(1)}, u32[]{:S(2)}, u32[]{:S(2)}) collective-permute-start(bf16[1,1,3,4,4096]{4,3,2,1,0:T(4,128)(2,1)} %raw_hbm.1), channel_id=1, source_target_pairs={{0,2},{1,3},{2,0},{3,1},{4,6},{5,7},{6,4},{7,5},{8,10},{9,11},{10,... | collective-permute-start | bytes 294920 | tf_op jit(solution)/shard_map/ppermute | solution.py:166
  4.7 1.2 %pack.1 = (bf16[528,128]{1,0:T(8,128)(2,1)S(1)}, bf16[80,128]{1,0:T(8,128)(2,1)S(1)}) custom-call(s32[1,1]{1,0:T(1,128)S(6)} %copy.5.kept, s32[1,1,3]{2,1,0:T(1,128)} %pairs_hbm.1, bf16[64,256]{1,0:T(8,128)(2,1)} %density_ref.1, bf16[1,1,3,4,4096]{4,3,2,1,0:T(4,128)(2,1)} %raw_hbm.1), custom_call_target="tpu_custom_call" | custom-call | tf_op jit(solution)/shard_map/pack/pallas_call | solution.py:168
  5.9 0.1 collective-permute-start
  5.9 3.9 %collective-permute-start.2 = (bf16[528,128]{1,0:T(8,128)(2,1)S(1)}, bf16[528,128]{1,0:T(8,128)(2,1)S(1)}, u32[]{:S(2)}, u32[]{:S(2)}) collective-permute-start(bf16[528,128]{1,0:T(8,128)(2,1)S(1)} %get-tuple-element.13.own_ref.full_ref.refs_0_), channel_id=1, source_target_pairs={{0,3},{1,0},{2,1},{3,2},{4,5},{5,6},{6,7},{7,4},{8,11},{9,8},{10,9... | collective-permute-start | bytes 405512 | tf_op jit(solution)/shard_map/ppermute | solution.py:166
  9.9 0.1 collective-permute-start.4
  9.9 2.4 %collective-permute-done.refs_1_ = bf16[80,128]{1,0:T(8,128)(2,1)S(1)} collective-permute-done((bf16[80,128]{1,0:T(8,128)(2,1)S(1)}, bf16[80,128]{1,0:T(8,128)(2,1)S(1)}, u32[]{:S(2)}, u32[]{:S(2)}) %collective-permute-start) | collective-permute-done | bytes 20512 | tf_op jit(solution)/shard_map/ppermute | solution.py:166
  12.3 0.0 collective-permute-done.1.raw
  12.3 0.2 relay.1.refs_1_
  12.5 0.0 copy-start
  12.6 1.1 %collective-permute-done.2.refs_0_.refs_2_ = bf16[528,128]{1,0:T(8,128)(2,1)S(1)} collective-permute-done((bf16[528,128]{1,0:T(8,128)(2,1)S(1)}, bf16[528,128]{1,0:T(8,128)(2,1)S(1)}, u32[]{:S(2)}, u32[]{:S(2)}) %collective-permute-start.2) | collective-permute-done | bytes 135200 | tf_op jit(solution)/shard_map/ppermute | solution.py:166
  13.7 0.0 collective-permute-start.3
  13.7 1.2 %collective-permute-done.3.refs_2_ = bf16[192,128]{1,0:T(8,128)(2,1)S(1)} collective-permute-done((bf16[192,128]{1,0:T(8,128)(2,1)S(1)}, bf16[192,128]{1,0:T(8,128)(2,1)S(1)}, u32[]{:S(2)}, u32[]{:S(2)}) %collective-permute-start.3) | collective-permute-done | bytes 49184 | tf_op jit(solution)/shard_map/ppermute | solution.py:207
  14.9 0.0 copy-done
  14.9 0.8 %half.1.half_ref = bf16[5,64,256]{2,1,0:T(8,128)(2,1)S(1)} custom-call(s32[3]{0:T(128)S(1)} %get-tuple-element.18.meta_ref, bf16[64,256]{1,0:T(8,128)(2,1)S(1)} %copy-done, bf16[528,128]{1,0:T(8,128)(2,1)S(1)} %get-tuple-element.13.own_ref.full_ref.refs_0_, bf16[528,128]{1,0:T(8,128)(2,1)S(1)} %collective-permute-done.2.refs_0_.refs_2_, ...), custom_call_target="tpu_custom_call" | custom-call | tf_op jit(solution)/shard_map/half/pallas_call | solution.py:216
  15.8 0.6 %collective-permute-done.4.refs_3_ = bf16[400,128]{1,0:T(8,128)(2,1)S(1)} collective-permute-done((bf16[400,128]{1,0:T(8,128)(2,1)S(1)}, bf16[400,128]{1,0:T(8,128)(2,1)S(1)}, u32[]{:S(2)}, u32[]{:S(2)}) %collective-permute-start.4) | collective-permute-done | bytes 102432 | tf_op jit(solution)/shard_map/ppermute | solution.py:166
  16.4 0.1 maximum_convert_fusion.meta_ref
  16.5 0.9 %exchange.1 = f32[64,256]{1,0:T(8,128)S(1)} custom-call(s32[12]{0:T(128)S(1)} %maximum_convert_fusion.meta_ref, bf16[5,64,256]{2,1,0:T(8,128)(2,1)S(1)} %half.1.half_ref, bf16[528,128]{1,0:T(8,128)(2,1)S(1)} %get-tuple-element.13.own_ref.full_ref.refs_0_, bf16[384,128]{1,0:T(8,128)(2,1)S(1)} %relay.1.refs_1_, ...), custom_call_target="tpu_custom_call" | custom-call | tf_op jit(solution)/shard_map/exchange/pallas_call | solution.py:231
  17.3 0.1 collective-permute-start.5
  17.4 1.2 %collective-permute-done.5 = f32[64,256]{1,0:T(8,128)S(1)} collective-permute-done((f32[64,256]{1,0:T(8,128)S(1)}, f32[64,256]{1,0:T(8,128)S(1)}, u32[]{:S(2)}, u32[]{:S(2)}) %collective-permute-start.5) | collective-permute-done | bytes 65568 | tf_op jit(solution)/shard_map/ppermute | solution.py:246
  18.7 2.5 %collective-permute-start.8 = (f32[64,256]{1,0:T(8,128)S(1)}, f32[64,256]{1,0:T(8,128)S(1)}, u32[]{:S(2)}, u32[]{:S(2)}) collective-permute-start(f32[64,256]{1,0:T(8,128)S(1)} %add.12), channel_id=1, source_target_pairs={{0,24},{4,28},{8,16},{12,20},{16,8},{20,12},{24,0},{28,4},{1,25},{... | collective-permute-start | bytes 196616 | tf_op jit(solution)/shard_map/ppermute | solution.py:246
  21.2 0.5 %collective-permute-start.7 = (f32[64,256]{1,0:T(8,128)S(1)}, f32[64,256]{1,0:T(8,128)S(1)}, u32[]{:S(2)}, u32[]{:S(2)}) collective-permute-start(f32[64,256]{1,0:T(8,128)S(1)} %add.12), channel_id=1, source_target_pairs={{0,16},{4,20},{8,24},{12,28},{16,0},{20,4},{24,8},{28,12},{1,17},{... | collective-permute-start | bytes 196616 | tf_op jit(solution)/shard_map/ppermute | solution.py:246
  21.7 0.5 %collective-permute-start.6 = (f32[64,256]{1,0:T(8,128)S(1)}, f32[64,256]{1,0:T(8,128)S(1)}, u32[]{:S(2)}, u32[]{:S(2)}) collective-permute-start(f32[64,256]{1,0:T(8,128)S(1)} %add.12), channel_id=1, source_target_pairs={{0,8},{4,12},{8,0},{12,4},{16,24},{20,28},{24,16},{28,20},{1,9},{5... | collective-permute-start | bytes 196616 | tf_op jit(solution)/shard_map/ppermute | solution.py:246
  22.2 1.7 %collective-permute-done.8 = f32[64,256]{1,0:T(8,128)S(1)} collective-permute-done((f32[64,256]{1,0:T(8,128)S(1)}, f32[64,256]{1,0:T(8,128)S(1)}, u32[]{:S(2)}, u32[]{:S(2)}) %collective-permute-start.8) | collective-permute-done | bytes 65568 | tf_op jit(solution)/shard_map/ppermute | solution.py:246
  23.9 1.5 %collective-permute-done.7 = f32[64,256]{1,0:T(8,128)S(1)} collective-permute-done((f32[64,256]{1,0:T(8,128)S(1)}, f32[64,256]{1,0:T(8,128)S(1)}, u32[]{:S(2)}, u32[]{:S(2)}) %collective-permute-start.7) | collective-permute-done | bytes 65568 | tf_op jit(solution)/shard_map/ppermute | solution.py:246
  25.5 0.5 %collective-permute-done.6 = f32[64,256]{1,0:T(8,128)S(1)} collective-permute-done((f32[64,256]{1,0:T(8,128)S(1)}, f32[64,256]{1,0:T(8,128)S(1)}, u32[]{:S(2)}, u32[]{:S(2)}) %collective-permute-start.6) | collective-permute-done | bytes 65568 | tf_op jit(solution)/shard_map/ppermute | solution.py:246
  26.0 0.6 %add_add_fusion = f32[64,256]{1,0:T(8,128)} fusion(f32[64,256]{1,0:T(8,128)S(1)} %collective-permute-done.7, f32[64,256]{1,0:T(8,128)S(1)} %collective-permute-done.8, f32[64,256]{1,0:T(8,128)S(1)} %add.12, f32[64,256]{1,0:T(8,128)S(1)} %collective-permute-done.6), kind=kLoop, calls=%fused_computation | loop fusion | flops 49152 | bytes 327680 | tf_op jit(solution)/shard_map/add | solution.py:248
  (7 shorter events, 0.0 us)
Async XLA Ops:
  0.0 12.3 %collective-permute-start.1 = (bf16[1,1,3,4,4096]{4,3,2,1,0:T(4,128)(2,1)}, bf16[1,1,3,4,4096]{4,3,2,1,0:T(4,128)(2,1)S(1)}, u32[]{:S(2)}, u32[]{:S(2)}) collective-permute-start(bf16[1,1,3,4,4096]{4,3,2,1,0:T(4,128)(2,1)} %raw_hbm.1), channel_id=1, source_target_pairs={{0,2},{1,3},{2,0},{3,1},{4,6},{5,7},{6,4},{7,5},{8,10},{9,11},{10,... | collective-permute-start | bytes 294920 | tf_op jit(solution)/shard_map/ppermute | solution.py:166
  5.9 6.4 %collective-permute-start = (bf16[80,128]{1,0:T(8,128)(2,1)S(1)}, bf16[80,128]{1,0:T(8,128)(2,1)S(1)}, u32[]{:S(2)}, u32[]{:S(2)}) collective-permute-start(bf16[80,128]{1,0:T(8,128)(2,1)S(1)} %get-tuple-element.11), channel_id=1, source_target_pairs={{0,2},{1,3},{2,0},{3,1},{4,6},{5,7},{6,4},{7,5},{8,10},{9,11},{10,... | collective-permute-start | bytes 61448 | tf_op jit(solution)/shard_map/ppermute | solution.py:166
  5.9 7.8 %collective-permute-start.2 = (bf16[528,128]{1,0:T(8,128)(2,1)S(1)}, bf16[528,128]{1,0:T(8,128)(2,1)S(1)}, u32[]{:S(2)}, u32[]{:S(2)}) collective-permute-start(bf16[528,128]{1,0:T(8,128)(2,1)S(1)} %get-tuple-element.13.own_ref.full_ref.refs_0_), channel_id=1, source_target_pairs={{0,3},{1,0},{2,1},{3,2},{4,5},{5,6},{6,7},{7,4},{8,11},{9,8},{10,9... | collective-permute-start | bytes 405512 | tf_op jit(solution)/shard_map/ppermute | solution.py:166
  9.9 6.5 %collective-permute-start.4 = (bf16[400,128]{1,0:T(8,128)(2,1)S(1)}, bf16[400,128]{1,0:T(8,128)(2,1)S(1)}, u32[]{:S(2)}, u32[]{:S(2)}) collective-permute-start(bf16[400,128]{1,0:T(8,128)(2,1)S(1)} %lean.1), channel_id=1, source_target_pairs={{0,1},{1,2},{2,3},{3,0},{4,7},{5,4},{6,5},{7,6},{8,9},{9,10},{10,1... | collective-permute-start | bytes 307208 | tf_op jit(solution)/shard_map/ppermute | solution.py:166
  12.5 2.4 %copy-start = (bf16[64,256]{1,0:T(8,128)(2,1)S(1)}, bf16[64,256]{1,0:T(8,128)(2,1)}, u32[]{:S(2)}) copy-start(bf16[64,256]{1,0:T(8,128)(2,1)} %density_ref.1) | copy-start | bytes 98308
  13.7 1.2 %collective-permute-start.3 = (bf16[192,128]{1,0:T(8,128)(2,1)S(1)}, bf16[192,128]{1,0:T(8,128)(2,1)S(1)}, u32[]{:S(2)}, u32[]{:S(2)}) collective-permute-start(bf16[192,128]{1,0:T(8,128)(2,1)S(1)} %merge.1), channel_id=1, source_target_pairs={{0,4},{4,0},{8,12},{12,8},{16,20},{20,16},{24,28},{28,24},{1,5},{5... | collective-permute-start | bytes 147464 | tf_op jit(solution)/shard_map/ppermute | solution.py:207
  17.3 1.3 %collective-permute-start.5 = (f32[64,256]{1,0:T(8,128)S(1)}, f32[64,256]{1,0:T(8,128)S(1)}, u32[]{:S(2)}, u32[]{:S(2)}) collective-permute-start(f32[64,256]{1,0:T(8,128)S(1)} %exchange.1), channel_id=1, source_target_pairs={{0,4},{4,0},{8,12},{12,8},{16,20},{20,16},{24,28},{28,24},{1,5},{5... | collective-permute-start | bytes 196616 | tf_op jit(solution)/shard_map/ppermute | solution.py:246
  18.7 5.3 %collective-permute-start.8 = (f32[64,256]{1,0:T(8,128)S(1)}, f32[64,256]{1,0:T(8,128)S(1)}, u32[]{:S(2)}, u32[]{:S(2)}) collective-permute-start(f32[64,256]{1,0:T(8,128)S(1)} %add.12), channel_id=1, source_target_pairs={{0,24},{4,28},{8,16},{12,20},{16,8},{20,12},{24,0},{28,4},{1,25},{... | collective-permute-start | bytes 196616 | tf_op jit(solution)/shard_map/ppermute | solution.py:246
  21.2 4.3 %collective-permute-start.7 = (f32[64,256]{1,0:T(8,128)S(1)}, f32[64,256]{1,0:T(8,128)S(1)}, u32[]{:S(2)}, u32[]{:S(2)}) collective-permute-start(f32[64,256]{1,0:T(8,128)S(1)} %add.12), channel_id=1, source_target_pairs={{0,16},{4,20},{8,24},{12,28},{16,0},{20,4},{24,8},{28,12},{1,17},{... | collective-permute-start | bytes 196616 | tf_op jit(solution)/shard_map/ppermute | solution.py:246
  21.7 4.3 %collective-permute-start.6 = (f32[64,256]{1,0:T(8,128)S(1)}, f32[64,256]{1,0:T(8,128)S(1)}, u32[]{:S(2)}, u32[]{:S(2)}) collective-permute-start(f32[64,256]{1,0:T(8,128)S(1)} %add.12), channel_id=1, source_target_pairs={{0,8},{4,12},{8,0},{12,4},{16,24},{20,28},{24,16},{28,20},{1,9},{5... | collective-permute-start | bytes 196616 | tf_op jit(solution)/shard_map/ppermute | solution.py:246

commit v12 on v11

--- a/solution.py
+++ b/solution.py
@@ -19,6 +19,18 @@
         both = jnp.concatenate([square[2 * tile], square[2 * tile + 1]], axis=1)
         out_ref[tile * BS : (tile + 1) * BS] = both
     return slots * aux_width // 2
+
+
+def partner(i, step, sign, orb):
+    if orb == 4:
+        return i ^ (2 - sign)
+    return (i + sign * step) % orb
+
+
+def owner_of(me, step, sign, orb):
+    if orb == 4:
+        return me ^ (2 - sign)
+    return lax.rem(me - sign * step + orb, orb)
 
 
 def core_parity():
@@ -85,8 +97,9 @@
     far = pl.multiple_of((1 - parity) * height, height)
     rows[me] = density_ref[...]
     for i, full in enumerate(fulls):
-        ahead = lax.rem(me + (1 - 2 * parity) * (i + 1) + orb, orb)
-        behind = lax.rem(me - (1 - 2 * parity) * (i + 1) + orb, orb)
+        sign = 1 - 2 * parity
+        ahead = owner_of(me, i + 1, sign, orb)
+        behind = owner_of(me, i + 1, -sign, orb)
         for t in range(count):
             lanes = slice(t * LANES, (t + 1) * LANES)
             at = (i * count + t) * BS
@@ -120,9 +133,10 @@
     me = lax.axis_index("orb")
     parity = core_parity()
     per_slot = aux_width * BS // LANES
-    steps = [0, orb // 2]
+    sign = 1 - 2 * parity
+    owners = [me, lax.rem(me + orb // 2, orb)]
     for i in range(1, orb // 2):
-        steps += [(1 - 2 * parity) * i, (2 * parity - 1) * i]
+        owners += [owner_of(me, i, sign, orb), owner_of(me, i, -sign, orb)]
     for way in range(orb):
         total = None
         for j in range(slots):
@@ -136,7 +150,7 @@
                 preferred_element_type=jnp.float32,
             )
             total = term if total is None else total + term
-        held[lax.rem(me + steps[way] + orb, orb)] = total
+        held[owners[way]] = total
     out_ref[...] = jnp.concatenate([held[n] for n in range(orb)], axis=1)
 
 
@@ -156,10 +170,9 @@
     def array(height):
         return jax.ShapeDtypeStruct((height, LANES), jnp.bfloat16)
 
-    def shift(x, even, odd):
-        steps = (even, odd)
+    def shift(x, step, sign):
         perm = [
-            (a * orb + o, a * orb + (o + steps[a % 2]) % orb)
+            (a * orb + o, a * orb + partner(o, step, sign * (1 - 2 * (a % 2)), orb))
             for a in range(aux)
             for o in range(orb)
         ]
@@ -190,10 +203,11 @@
         compiler_params=params,
         name="lean",
     )(full)
-    raw = shift(tensor_blocks, orb // 2, orb // 2)
-    tail_in = shift(tail, orb // 2, orb // 2)
-    fulls = [shift(full, -i, i) for i in range(1, orb // 2)]
-    leans = [shift(lean, i, -i) for i in range(1, orb // 2)]
+    across = [(i, (i + orb // 2) % orb) for i in range(orb)]
+    raw = lax.ppermute(tensor_blocks, "orb", across)
+    tail_in = lax.ppermute(tail, "orb", across)
+    fulls = [shift(full, i, 1) for i in range(1, orb // 2)]
+    leans = [shift(lean, i, -1) for i in range(1, orb // 2)]
 
     tail_in, raw = lax.optimization_barrier((tail_in, raw))
     merged = pl.pallas_call(

time: 26.8 us -> 26.2 us (0.978)
  waiting for transfers between devices: 10.3 us -> 9.3 us
  starting transfers between devices: 11.7 us -> 12.2 us
    ppermute x0 -> x2, starting transfers between devices: none -> 4.11 us  [the longest x1 4.04 us: shards(): raw = lax.ppermute(tensor_blocks, 'orb', across)]
    ppermute x4 -> x2, starting transfers between devices: 8.09 us -> 4.44 us  [shift(): return lax.ppermute(x, ('aux', 'orb'), perm)]
    ppermute x4 -> x2, waiting for transfers between devices: 4.1 us -> 0.76 us  [shift(): return lax.ppermute(x, ('aux', 'orb'), perm)]
    ppermute x0 -> x2, waiting for transfers between devices: none -> 2.07 us  [the longest x1 2.07 us: shards(): tail_in = lax.ppermute(tail, 'orb', across)]
    ppermute x4, waiting for transfers between devices: 4.97 us -> 5.25 us  [shards(): lax.ppermute(parts, 'aux', [(i, i ^ way * step) for i in range(aux)])]
  transfers between devices with their start and end apart: 9 -> 9, of which waited for: 8 -> 8; matrix products, arithmetic and copies ran while one was open for 0% -> 0% of each run, Pallas kernels for 8% -> 9%
where the time goes in v12:
time: 26.2 us; the launch traced here: 26.1 us
  starting transfers between devices  12.2 us (47%)
  waiting for transfers between devices  9.3 us (35%)
  Pallas kernels  3.1 us (12%)
  other arithmetic  0.74 us (3%)
  between operations  0.74 us (3%)
    ppermute x4, waiting for transfers between devices, shards(): lax.ppermute(parts, 'aux', [(i, i ^ way * step) for i in range(aux)])  5.25 us
    ppermute x2, starting transfers between devices, shift(): return lax.ppermute(x, ('aux', 'orb'), perm)  4.44 us
    ppermute x1, starting transfers between devices, shards(): raw = lax.ppermute(tensor_blocks, 'orb', across)  4.04 us
    ppermute x4, starting transfers between devices, shards(): lax.ppermute(parts, 'aux', [(i, i ^ way * step) for i in range(aux)])  3.62 us
    ppermute x1, waiting for transfers between devices, shards(): tail_in = lax.ppermute(tail, 'orb', across)  2.07 us
    ppermute x1, waiting for transfers between devices, shards(): swapped = lax.ppermute(merged, 'aux', [(i, i ^ 1) for i in range(aux)])  1.21 us
    pallas_call x1, Pallas kernels, shards(): pl.pallas_call(functools.partial(pack_kernel, orb), out_shape=[array(size...  1.16 us
    pallas_call x1, Pallas kernels, shards(): pl.pallas_call(functools.partial(exchange_kernel, orb, slots, aux_width),...  0.87 us
  transfers between devices with their start and end apart: 9, of which 8 were waited for; matrix products, arithmetic and copies ran while one was open for 0% of the time, Pallas kernels for 9%

profile of v12, /device:TPU:0, one launch (start us, length us, event | category | flops | bytes accessed | tf_op | source)
XLA Modules:
  0.0 26.1 jit_solution(14153571579080350029)
XLA Ops:
  0.0 4.0 %collective-permute-start.1 = (bf16[1,1,3,4,4096]{4,3,2,1,0:T(4,128)(2,1)}, bf16[1,1,3,4,4096]{4,3,2,1,0:T(4,128)(2,1)S(1)}, u32[]{:S(2)}, u32[]{:S(2)}) collective-permute-start(bf16[1,1,3,4,4096]{4,3,2,1,0:T(4,128)(2,1)} %raw_hbm.1), channel_id=1, source_target_pairs={{0,2},{1,3},{2,0},{3,1},{4,6},{5,7},{6,4},{7,5},{8,10},{9,11},{10,... | collective-permute-start | bytes 294920 | tf_op jit(solution)/shard_map/ppermute | solution.py:207
  4.7 1.2 %pack.1 = (bf16[528,128]{1,0:T(8,128)(2,1)S(1)}, bf16[80,128]{1,0:T(8,128)(2,1)S(1)}) custom-call(s32[1,1]{1,0:T(1,128)S(6)} %copy.5.kept, s32[1,1,3]{2,1,0:T(1,128)} %pairs_hbm.1, bf16[64,256]{1,0:T(8,128)(2,1)} %density_ref.1, bf16[1,1,3,4,4096]{4,3,2,1,0:T(4,128)(2,1)} %raw_hbm.1), custom_call_target="tpu_custom_call" | custom-call | tf_op jit(solution)/shard_map/pack/pallas_call | solution.py:181
  5.9 0.1 collective-permute-start
  5.9 1.9 %collective-permute-start.2 = (bf16[528,128]{1,0:T(8,128)(2,1)S(1)}, bf16[528,128]{1,0:T(8,128)(2,1)S(1)}, u32[]{:S(2)}, u32[]{:S(2)}) collective-permute-start(bf16[528,128]{1,0:T(8,128)(2,1)S(1)} %get-tuple-element.13.own_ref.full_ref.refs_0_), channel_id=1, source_target_pairs={{0,1},{1,0},{2,3},{3,2},{4,7},{5,6},{6,5},{7,4},{8,9},{9,8},{10,11... | collective-permute-start | bytes 405512 | tf_op jit(solution)/shard_map/ppermute | solution.py:179
  7.8 2.5 %collective-permute-start.4 = (bf16[400,128]{1,0:T(8,128)(2,1)S(1)}, bf16[400,128]{1,0:T(8,128)(2,1)S(1)}, u32[]{:S(2)}, u32[]{:S(2)}) collective-permute-start(bf16[400,128]{1,0:T(8,128)(2,1)S(1)} %lean.1), channel_id=1, source_target_pairs={{0,3},{1,2},{2,1},{3,0},{4,5},{5,4},{6,7},{7,6},{8,11},{9,10},{10,... | collective-permute-start | bytes 307208 | tf_op jit(solution)/shard_map/ppermute | solution.py:179
  10.4 2.1 %collective-permute-done.refs_1_ = bf16[80,128]{1,0:T(8,128)(2,1)S(1)} collective-permute-done((bf16[80,128]{1,0:T(8,128)(2,1)S(1)}, bf16[80,128]{1,0:T(8,128)(2,1)S(1)}, u32[]{:S(2)}, u32[]{:S(2)}) %collective-permute-start) | collective-permute-done | bytes 20512 | tf_op jit(solution)/shard_map/ppermute | solution.py:208
  12.5 0.0 collective-permute-done.1.raw
  12.5 0.2 relay.1.refs_1_
  12.7 0.0 copy-start
  12.7 0.5 %collective-permute-done.2.refs_0_.refs_2_ = bf16[528,128]{1,0:T(8,128)(2,1)S(1)} collective-permute-done((bf16[528,128]{1,0:T(8,128)(2,1)S(1)}, bf16[528,128]{1,0:T(8,128)(2,1)S(1)}, u32[]{:S(2)}, u32[]{:S(2)}) %collective-permute-start.2) | collective-permute-done | bytes 135200 | tf_op jit(solution)/shard_map/ppermute | solution.py:179
  13.2 0.0 collective-permute-start.3
  13.2 1.2 %collective-permute-done.3.refs_2_ = bf16[192,128]{1,0:T(8,128)(2,1)S(1)} collective-permute-done((bf16[192,128]{1,0:T(8,128)(2,1)S(1)}, bf16[192,128]{1,0:T(8,128)(2,1)S(1)}, u32[]{:S(2)}, u32[]{:S(2)}) %collective-permute-start.3) | collective-permute-done | bytes 49184 | tf_op jit(solution)/shard_map/ppermute | solution.py:221
  14.5 0.0 copy-done
  14.5 0.8 %half.1.half_ref = bf16[5,64,256]{2,1,0:T(8,128)(2,1)S(1)} custom-call(s32[3]{0:T(128)S(1)} %get-tuple-element.18.meta_ref, bf16[64,256]{1,0:T(8,128)(2,1)S(1)} %copy-done, bf16[528,128]{1,0:T(8,128)(2,1)S(1)} %get-tuple-element.13.own_ref.full_ref.refs_0_, bf16[528,128]{1,0:T(8,128)(2,1)S(1)} %collective-permute-done.2.refs_0_.refs_2_, ...), custom_call_target="tpu_custom_call" | custom-call | tf_op jit(solution)/shard_map/half/pallas_call | solution.py:230
  15.3 0.3 collective-permute-done.4.refs_3_
  15.6 0.1 maximum_convert_fusion.meta_ref
  15.6 0.9 %exchange.1 = f32[64,256]{1,0:T(8,128)S(1)} custom-call(s32[12]{0:T(128)S(1)} %maximum_convert_fusion.meta_ref, bf16[5,64,256]{2,1,0:T(8,128)(2,1)S(1)} %half.1.half_ref, bf16[528,128]{1,0:T(8,128)(2,1)S(1)} %get-tuple-element.13.own_ref.full_ref.refs_0_, bf16[384,128]{1,0:T(8,128)(2,1)S(1)} %relay.1.refs_1_, ...), custom_call_target="tpu_custom_call" | custom-call | tf_op jit(solution)/shard_map/exchange/pallas_call | solution.py:245
  16.5 0.1 collective-permute-start.5
  16.6 1.2 %collective-permute-done.5 = f32[64,256]{1,0:T(8,128)S(1)} collective-permute-done((f32[64,256]{1,0:T(8,128)S(1)}, f32[64,256]{1,0:T(8,128)S(1)}, u32[]{:S(2)}, u32[]{:S(2)}) %collective-permute-start.5) | collective-permute-done | bytes 65568 | tf_op jit(solution)/shard_map/ppermute | solution.py:260
  17.9 2.8 %collective-permute-start.8 = (f32[64,256]{1,0:T(8,128)S(1)}, f32[64,256]{1,0:T(8,128)S(1)}, u32[]{:S(2)}, u32[]{:S(2)}) collective-permute-start(f32[64,256]{1,0:T(8,128)S(1)} %add.12), channel_id=1, source_target_pairs={{0,24},{4,28},{8,16},{12,20},{16,8},{20,12},{24,0},{28,4},{1,25},{... | collective-permute-start | bytes 196616 | tf_op jit(solution)/shard_map/ppermute | solution.py:260
  20.6 0.5 %collective-permute-start.7 = (f32[64,256]{1,0:T(8,128)S(1)}, f32[64,256]{1,0:T(8,128)S(1)}, u32[]{:S(2)}, u32[]{:S(2)}) collective-permute-start(f32[64,256]{1,0:T(8,128)S(1)} %add.12), channel_id=1, source_target_pairs={{0,16},{4,20},{8,24},{12,28},{16,0},{20,4},{24,8},{28,12},{1,17},{... | collective-permute-start | bytes 196616 | tf_op jit(solution)/shard_map/ppermute | solution.py:260
  21.2 0.3 collective-permute-start.6
  21.4 1.7 %collective-permute-done.8 = f32[64,256]{1,0:T(8,128)S(1)} collective-permute-done((f32[64,256]{1,0:T(8,128)S(1)}, f32[64,256]{1,0:T(8,128)S(1)}, u32[]{:S(2)}, u32[]{:S(2)}) %collective-permute-start.8) | collective-permute-done | bytes 65568 | tf_op jit(solution)/shard_map/ppermute | solution.py:260
  23.1 1.8 %collective-permute-done.7 = f32[64,256]{1,0:T(8,128)S(1)} collective-permute-done((f32[64,256]{1,0:T(8,128)S(1)}, f32[64,256]{1,0:T(8,128)S(1)}, u32[]{:S(2)}, u32[]{:S(2)}) %collective-permute-start.7) | collective-permute-done | bytes 65568 | tf_op jit(solution)/shard_map/ppermute | solution.py:260
  24.9 0.5 %collective-permute-done.6 = f32[64,256]{1,0:T(8,128)S(1)} collective-permute-done((f32[64,256]{1,0:T(8,128)S(1)}, f32[64,256]{1,0:T(8,128)S(1)}, u32[]{:S(2)}, u32[]{:S(2)}) %collective-permute-start.6) | collective-permute-done | bytes 65568 | tf_op jit(solution)/shard_map/ppermute | solution.py:260
  25.4 0.6 %add_add_fusion = f32[64,256]{1,0:T(8,128)} fusion(f32[64,256]{1,0:T(8,128)S(1)} %collective-permute-done.7, f32[64,256]{1,0:T(8,128)S(1)} %collective-permute-done.8, f32[64,256]{1,0:T(8,128)S(1)} %add.12, f32[64,256]{1,0:T(8,128)S(1)} %collective-permute-done.6), kind=kLoop, calls=%fused_computation | loop fusion | flops 49152 | bytes 327680 | tf_op jit(solution)/shard_map/add | solution.py:262
  (7 shorter events, 0.0 us)
Async XLA Ops:
  0.0 12.5 %collective-permute-start.1 = (bf16[1,1,3,4,4096]{4,3,2,1,0:T(4,128)(2,1)}, bf16[1,1,3,4,4096]{4,3,2,1,0:T(4,128)(2,1)S(1)}, u32[]{:S(2)}, u32[]{:S(2)}) collective-permute-start(bf16[1,1,3,4,4096]{4,3,2,1,0:T(4,128)(2,1)} %raw_hbm.1), channel_id=1, source_target_pairs={{0,2},{1,3},{2,0},{3,1},{4,6},{5,7},{6,4},{7,5},{8,10},{9,11},{10,... | collective-permute-start | bytes 294920 | tf_op jit(solution)/shard_map/ppermute | solution.py:207
  5.9 6.6 %collective-permute-start = (bf16[80,128]{1,0:T(8,128)(2,1)S(1)}, bf16[80,128]{1,0:T(8,128)(2,1)S(1)}, u32[]{:S(2)}, u32[]{:S(2)}) collective-permute-start(bf16[80,128]{1,0:T(8,128)(2,1)S(1)} %get-tuple-element.11), channel_id=1, source_target_pairs={{0,2},{1,3},{2,0},{3,1},{4,6},{5,7},{6,4},{7,5},{8,10},{9,11},{10,... | collective-permute-start | bytes 61448 | tf_op jit(solution)/shard_map/ppermute | solution.py:208
  5.9 7.3 %collective-permute-start.2 = (bf16[528,128]{1,0:T(8,128)(2,1)S(1)}, bf16[528,128]{1,0:T(8,128)(2,1)S(1)}, u32[]{:S(2)}, u32[]{:S(2)}) collective-permute-start(bf16[528,128]{1,0:T(8,128)(2,1)S(1)} %get-tuple-element.13.own_ref.full_ref.refs_0_), channel_id=1, source_target_pairs={{0,1},{1,0},{2,3},{3,2},{4,7},{5,6},{6,5},{7,4},{8,9},{9,8},{10,11... | collective-permute-start | bytes 405512 | tf_op jit(solution)/shard_map/ppermute | solution.py:179
  7.8 7.7 %collective-permute-start.4 = (bf16[400,128]{1,0:T(8,128)(2,1)S(1)}, bf16[400,128]{1,0:T(8,128)(2,1)S(1)}, u32[]{:S(2)}, u32[]{:S(2)}) collective-permute-start(bf16[400,128]{1,0:T(8,128)(2,1)S(1)} %lean.1), channel_id=1, source_target_pairs={{0,3},{1,2},{2,1},{3,0},{4,5},{5,4},{6,7},{7,6},{8,11},{9,10},{10,... | collective-permute-start | bytes 307208 | tf_op jit(solution)/shard_map/ppermute | solution.py:179
  12.7 1.8 %copy-start = (bf16[64,256]{1,0:T(8,128)(2,1)S(1)}, bf16[64,256]{1,0:T(8,128)(2,1)}, u32[]{:S(2)}) copy-start(bf16[64,256]{1,0:T(8,128)(2,1)} %density_ref.1) | copy-start | bytes 98308
  13.2 1.2 %collective-permute-start.3 = (bf16[192,128]{1,0:T(8,128)(2,1)S(1)}, bf16[192,128]{1,0:T(8,128)(2,1)S(1)}, u32[]{:S(2)}, u32[]{:S(2)}) collective-permute-start(bf16[192,128]{1,0:T(8,128)(2,1)S(1)} %merge.1), channel_id=1, source_target_pairs={{0,4},{4,0},{8,12},{12,8},{16,20},{20,16},{24,28},{28,24},{1,5},{5... | collective-permute-start | bytes 147464 | tf_op jit(solution)/shard_map/ppermute | solution.py:221
  16.5 1.3 %collective-permute-start.5 = (f32[64,256]{1,0:T(8,128)S(1)}, f32[64,256]{1,0:T(8,128)S(1)}, u32[]{:S(2)}, u32[]{:S(2)}) collective-permute-start(f32[64,256]{1,0:T(8,128)S(1)} %exchange.1), channel_id=1, source_target_pairs={{0,4},{4,0},{8,12},{12,8},{16,20},{20,16},{24,28},{28,24},{1,5},{5... | collective-permute-start | bytes 196616 | tf_op jit(solution)/shard_map/ppermute | solution.py:260
  17.9 5.2 %collective-permute-start.8 = (f32[64,256]{1,0:T(8,128)S(1)}, f32[64,256]{1,0:T(8,128)S(1)}, u32[]{:S(2)}, u32[]{:S(2)}) collective-permute-start(f32[64,256]{1,0:T(8,128)S(1)} %add.12), channel_id=1, source_target_pairs={{0,24},{4,28},{8,16},{12,20},{16,8},{20,12},{24,0},{28,4},{1,25},{... | collective-permute-start | bytes 196616 | tf_op jit(solution)/shard_map/ppermute | solution.py:260
  20.6 4.3 %collective-permute-start.7 = (f32[64,256]{1,0:T(8,128)S(1)}, f32[64,256]{1,0:T(8,128)S(1)}, u32[]{:S(2)}, u32[]{:S(2)}) collective-permute-start(f32[64,256]{1,0:T(8,128)S(1)} %add.12), channel_id=1, source_target_pairs={{0,16},{4,20},{8,24},{12,28},{16,0},{20,4},{24,8},{28,12},{1,17},{... | collective-permute-start | bytes 196616 | tf_op jit(solution)/shard_map/ppermute | solution.py:260
  21.2 4.3 %collective-permute-start.6 = (f32[64,256]{1,0:T(8,128)S(1)}, f32[64,256]{1,0:T(8,128)S(1)}, u32[]{:S(2)}, u32[]{:S(2)}) collective-permute-start(f32[64,256]{1,0:T(8,128)S(1)} %add.12), channel_id=1, source_target_pairs={{0,8},{4,12},{8,0},{12,4},{16,24},{20,28},{24,16},{28,20},{1,9},{5... | collective-permute-start | bytes 196616 | tf_op jit(solution)/shard_map/ppermute | solution.py:260

commit v13 on v12

--- a/solution.py
+++ b/solution.py
@@ -38,7 +38,7 @@
 
 
 def pack_kernel(
-    orb, kept, pairs_hbm, density_hbm, raw_hbm, full_ref, tail_ref, pairs, rows, raw, sems
+    orb, kept, pairs_hbm, density_hbm, raw_hbm, own_ref, near_ref, tail_ref, pairs, rows, raw, sems
 ):
     copies = [
         pltpu.make_async_copy(src, dst, sems.at[i])
@@ -48,13 +48,13 @@
         copy.start()
     for copy in copies:
         copy.wait()
-    size = lay_blocks(raw[0, 0], full_ref) * BS
+    lay_blocks(raw[0, 0], own_ref)
     height = BS // 2
     near = pl.multiple_of(core_parity() * height, height)
     tiles = rows.shape[1] // LANES
     for t in range(tiles):
         lanes = slice(t * LANES, (t + 1) * LANES)
-        full_ref[size + t * BS : size + (t + 1) * BS] = rows[:, lanes]
+        near_ref[t * BS : (t + 1) * BS] = rows[:, lanes]
         tail_ref[t * height : (t + 1) * height] = rows[pl.ds(near, height), lanes]
     shape = (NOTE, LANES)
     lane = lax.broadcasted_iota(jnp.int32, shape, 1)
@@ -62,55 +62,54 @@
     for j in range(pairs.shape[2]):
         note = jnp.where(lane == j, jnp.where(j < kept[0, 0], pairs[0, 0, j], orb), note)
     note = note.astype(jnp.float32).astype(jnp.bfloat16)
-    full_ref[size + tiles * BS :] = note
+    near_ref[tiles * BS :] = note
     tail_ref[tiles * height :] = note
 
 
-def lean_kernel(full_ref, out_ref):
-    size = out_ref.shape[0] - NOTE
-    out_ref[:size] = full_ref[:size]
-    out_ref[size:] = full_ref[full_ref.shape[0] - NOTE :]
+def lean_kernel(own_ref, near_ref, mark_ref, out_ref):
+    size = own_ref.shape[0]
+    out_ref[:size] = own_ref[...]
+    out_ref[size:] = near_ref[near_ref.shape[0] - NOTE :]
 
 
 def relay_kernel(raw, out_ref):
     lay_blocks(raw[0, 0], out_ref)
 
 
-def merge_kernel(size, *refs):
+def merge_kernel(*refs):
     parts, out_ref = refs[:-1], refs[-1]
     at = 0
-    for i, part in enumerate(parts):
-        first = size if i < len(parts) - 1 else 0
-        count = part.shape[0] - NOTE - first
-        out_ref[at : at + count] = part[first : first + count]
+    for part in parts:
+        count = part.shape[0] - NOTE
+        out_ref[at : at + count] = part[:count]
         at += count
 
 
 def half_kernel(orb, slots, aux_width, meta_ref, density_ref, own_ref, *refs):
-    fulls, (tail, swapped, half_ref, rows) = refs[:-4], refs[-4:]
+    nears, (tail, swapped, half_ref, rows) = refs[:-4], refs[-4:]
     me = lax.axis_index("orb")
     parity = core_parity()
     height = BS // 2
     count = density_ref.shape[1] // LANES
     size = slots * aux_width * BS // LANES * BS
-    near = pl.multiple_of(parity * height, height)
-    far = pl.multiple_of((1 - parity) * height, height)
+    mine = pl.multiple_of(parity * height, height)
+    other = pl.multiple_of((1 - parity) * height, height)
     rows[me] = density_ref[...]
-    for i, full in enumerate(fulls):
+    for i, near in enumerate(nears):
         sign = 1 - 2 * parity
         ahead = owner_of(me, i + 1, sign, orb)
         behind = owner_of(me, i + 1, -sign, orb)
         for t in range(count):
             lanes = slice(t * LANES, (t + 1) * LANES)
             at = (i * count + t) * BS
-            rows[ahead, :, lanes] = full[size + t * BS : size + (t + 1) * BS]
+            rows[ahead, :, lanes] = near[t * BS : (t + 1) * BS]
             rows[behind, :, lanes] = swapped[at : at + BS]
     across = lax.rem(me + orb // 2, orb)
     for t in range(count):
         lanes = slice(t * LANES, (t + 1) * LANES)
-        at = len(fulls) * count * BS + t * height
-        rows[across, pl.ds(near, height), lanes] = tail[t * height : (t + 1) * height]
-        rows[across, pl.ds(far, height), lanes] = swapped[at : at + height]
+        at = len(nears) * count * BS + t * height
+        rows[across, pl.ds(mine, height), lanes] = tail[t * height : (t + 1) * height]
+        rows[across, pl.ds(other, height), lanes] = swapped[at : at + height]
     rows[orb] = jnp.zeros_like(rows[orb])
     selected = jnp.concatenate([rows[meta_ref[j]] for j in range(slots)], axis=0)
     own = jnp.concatenate([own_ref[at : at + BS] for at in range(0, size, BS)], axis=1)
@@ -131,12 +130,10 @@
 def exchange_kernel(orb, slots, aux_width, meta_ref, half_ref, *refs):
     packs, (out_ref, held) = refs[:orb], refs[orb:]
     me = lax.axis_index("orb")
-    parity = core_parity()
     per_slot = aux_width * BS // LANES
-    sign = 1 - 2 * parity
     owners = [me, lax.rem(me + orb // 2, orb)]
     for i in range(1, orb // 2):
-        owners += [owner_of(me, i, sign, orb), owner_of(me, i, -sign, orb)]
+        owners += [owner_of(me, i, sign, orb) for sign in (1, -1)]
     for way in range(orb):
         total = None
         for j in range(slots):
@@ -170,19 +167,11 @@
     def array(height):
         return jax.ShapeDtypeStruct((height, LANES), jnp.bfloat16)
 
-    def shift(x, step, sign):
-        perm = [
-            (a * orb + o, a * orb + partner(o, step, sign * (1 - 2 * (a % 2)), orb))
-            for a in range(aux)
-            for o in range(orb)
-        ]
-        return lax.ppermute(x, ("aux", "orb"), perm)
-
-    full, tail = pl.pallas_call(
+    own, near, tail = pl.pallas_call(
         functools.partial(pack_kernel, orb),
-        out_shape=[array(size + rows + NOTE), array(rows // 2 + NOTE)],
+        out_shape=[array(size), array(rows + NOTE), array(rows // 2 + NOTE)],
         in_specs=[smem, hbm, hbm, hbm],
-        out_specs=[vmem] * 2,
+        out_specs=[vmem] * 3,
         scratch_shapes=[
             pltpu.SMEM(pairs.shape, jnp.int32),
             pltpu.VMEM(density.shape, jnp.bfloat16),
@@ -195,29 +184,39 @@
         kept,
         *(pltpu.with_memory_space_constraint(a, pltpu.HBM) for a in (pairs, density, tensor_blocks)),
     )
+    mark = lax.ppermute(tail, "aux", [(i, i ^ 1) for i in range(aux)])
     lean = pl.pallas_call(
         lean_kernel,
         out_shape=array(size + NOTE),
-        in_specs=[vmem],
+        in_specs=[vmem] * 3,
         out_specs=vmem,
         compiler_params=params,
         name="lean",
-    )(full)
+    )(own, near, mark)
     across = [(i, (i + orb // 2) % orb) for i in range(orb)]
     raw = lax.ppermute(tensor_blocks, "orb", across)
     tail_in = lax.ppermute(tail, "orb", across)
-    fulls = [shift(full, i, 1) for i in range(1, orb // 2)]
-    leans = [shift(lean, i, -1) for i in range(1, orb // 2)]
+    nears, leans = [], []
+    for i in range(1, orb // 2):
+        perm = [
+            (a * orb + o, a * orb + partner(o, i, 1 - 2 * (a % 2), orb))
+            for a in range(aux)
+            for o in range(orb)
+        ]
+        nears.append(lax.ppermute(near, ("aux", "orb"), perm))
+        for sign in (1, -1):
+            perm = [(o, partner(o, i, sign, orb)) for o in range(orb)]
+            leans.append(lax.ppermute(lean, "orb", perm))
 
     tail_in, raw = lax.optimization_barrier((tail_in, raw))
     merged = pl.pallas_call(
-        functools.partial(merge_kernel, size),
-        out_shape=array(len(fulls) * rows + rows // 2),
-        in_specs=[vmem] * (len(fulls) + 1),
+        merge_kernel,
+        out_shape=array(len(nears) * rows + rows // 2),
+        in_specs=[vmem] * (len(nears) + 1),
         out_specs=vmem,
         compiler_params=params,
         name="merge",
-    )(*fulls, tail_in)
+    )(*nears, tail_in)
     swapped = lax.ppermute(merged, "aux", [(i, i ^ 1) for i in range(aux)])
     across = pl.pallas_call(
         relay_kernel,
@@ -230,17 +229,14 @@
     half = pl.pallas_call(
         functools.partial(half_kernel, orb, slots, aux_width),
         out_shape=jax.ShapeDtypeStruct((orb + 1, BS, aux_width * BS), jnp.bfloat16),
-        in_specs=[smem] + [vmem] * (len(fulls) + 4),
+        in_specs=[smem] + [vmem] * (len(nears) + 4),
         out_specs=vmem,
         scratch_shapes=[pltpu.VMEM((orb + 1, BS, full_width), jnp.bfloat16)],
         compiler_params=params,
         name="half",
-    )(tail[-NOTE, :slots].astype(jnp.int32), density, full, *fulls, tail_in, swapped)
+    )(tail[-NOTE, :slots].astype(jnp.int32), density, own, *nears, tail_in, swapped)
     half, leans = lax.optimization_barrier((half, leans))
-    packs, notes = [full, across], [tail, tail_in]
-    for pair in zip(fulls, leans):
-        packs += pair
-        notes += pair
+    packs, notes = [own, across, *leans], [tail, tail_in, *leans]
     codes = jnp.concatenate([n[-NOTE, :slots] for n in notes]).astype(jnp.int32)
     parts = pl.pallas_call(
         functools.partial(exchange_kernel, orb, slots, aux_width),

time: 26.2 us -> 27.4 us (1.046)
  starting transfers between devices: 12.2 us -> 13.3 us
    ppermute x2 -> x4, waiting for transfers between devices: 0.76 us -> 3.65 us  [the longest x2 3.65 us: shards(): leans.append(lax.ppermute(lean, 'orb', perm))]
    ppermute x1, waiting for transfers between devices: 2.07 us -> 0.01 us  [shards(): tail_in = lax.ppermute(tail, 'orb', across)]
    ppermute x2 -> x4, starting transfers between devices: 4.44 us -> 5.19 us  [the longest x2 3.22 us: shards(): leans.append(lax.ppermute(lean, 'orb', perm))]
    ppermute x1, waiting for transfers between devices: 1.21 us -> 0.67 us  [shards(): swapped = lax.ppermute(merged, 'aux', [(i, i ^ 1) for i in range(aux)])]
    ppermute x1, starting transfers between devices: 0.01 us -> 0.39 us  [shards(): swapped = lax.ppermute(merged, 'aux', [(i, i ^ 1) for i in range(aux)])]
    ppermute x4, waiting for transfers between devices: 5.25 us -> 4.97 us  [shards(): lax.ppermute(parts, 'aux', [(i, i ^ way * step) for i in range(aux)])]
  transfers between devices with their start and end apart: 9 -> 11, of which waited for: 8 -> 7; matrix products, arithmetic and copies ran while one was open for 0% -> 0% of each run, Pallas kernels for 9% -> 8%
where the time goes in v13:
time: 27.4 us; the launch traced here: 27.2 us
  starting transfers between devices  13.3 us (49%)
  waiting for transfers between devices  9.3 us (34%)
  Pallas kernels  3.11 us (11%)
  other arithmetic  0.74 us (3%)
  between operations  0.73 us (3%)
    ppermute x4, waiting for transfers between devices, shards(): lax.ppermute(parts, 'aux', [(i, i ^ way * step) for i in range(aux)])  4.97 us
    ppermute x1, starting transfers between devices, shards(): raw = lax.ppermute(tensor_blocks, 'orb', across)  4.04 us
    ppermute x2, waiting for transfers between devices, shards(): leans.append(lax.ppermute(lean, 'orb', perm))  3.65 us
    ppermute x4, starting transfers between devices, shards(): lax.ppermute(parts, 'aux', [(i, i ^ way * step) for i in range(aux)])  3.62 us
    ppermute x2, starting transfers between devices, shards(): leans.append(lax.ppermute(lean, 'orb', perm))  3.22 us
    ppermute x1, starting transfers between devices, shards(): nears.append(lax.ppermute(near, ('aux', 'orb'), perm))  1.9 us
    pallas_call x1, Pallas kernels, shards(): pl.pallas_call(functools.partial(pack_kernel, orb), out_shape=[array(size...  1.16 us
    pallas_call x1, Pallas kernels, shards(): pl.pallas_call(functools.partial(exchange_kernel, orb, slots, aux_width),...  0.87 us
  transfers between devices with their start and end apart: 11, of which 7 were waited for; matrix products, arithmetic and copies ran while one was open for 0% of the time, Pallas kernels for 8%

profile of v13, /device:TPU:0, one launch (start us, length us, event | category | flops | bytes accessed | tf_op | source)
XLA Modules:
  0.0 27.2 jit_solution(17096446649939327082)
XLA Ops:
  0.0 4.0 %collective-permute-start.1 = (bf16[1,1,3,4,4096]{4,3,2,1,0:T(4,128)(2,1)}, bf16[1,1,3,4,4096]{4,3,2,1,0:T(4,128)(2,1)S(1)}, u32[]{:S(2)}, u32[]{:S(2)}) collective-permute-start(bf16[1,1,3,4,4096]{4,3,2,1,0:T(4,128)(2,1)} %raw_hbm.1), channel_id=1, source_target_pairs={{0,2},{1,3},{2,0},{3,1},{4,6},{5,7},{6,4},{7,5},{8,10},{9,11},{10,... | collective-permute-start | bytes 294920 | tf_op jit(solution)/shard_map/ppermute | solution.py:197
  4.7 1.2 %pack.1 = (bf16[384,128]{1,0:T(8,128)(2,1)S(1)}, bf16[144,128]{1,0:T(8,128)(2,1)S(1)}, bf16[80,128]{1,0:T(8,128)(2,1)S(1)}) custom-call(s32[1,1]{1,0:T(1,128)S(6)} %copy.5.kept, s32[1,1,3]{2,1,0:T(1,128)} %pairs_hbm.1, bf16[64,256]{1,0:T(8,128)(2,1)} %density_ref.1, bf16[1,1,3,4,4096]{4,3,2,1,0:T(4,128)(2,1)} %raw_hbm.1), custom_call_target="tpu_custom_call" | custom-call | tf_op jit(solution)/shard_map/pack/pallas_call | solution.py:170
  5.9 0.1 collective-permute-start.4
  5.9 0.1 collective-permute-start
  6.0 1.9 %collective-permute-start.2 = (bf16[144,128]{1,0:T(8,128)(2,1)S(1)}, bf16[144,128]{1,0:T(8,128)(2,1)S(1)}, u32[]{:S(2)}, u32[]{:S(2)}) collective-permute-start(bf16[144,128]{1,0:T(8,128)(2,1)S(1)} %get-tuple-element.16.near_ref), channel_id=1, source_target_pairs={{0,1},{1,0},{2,3},{3,2},{4,7},{5,6},{6,5},{7,4},{8,9},{9,8},{10,11... | collective-permute-start | bytes 110600 | tf_op jit(solution)/shard_map/ppermute | solution.py:206
  7.9 0.0 collective-permute-done.4.mark_ref
  7.9 2.5 %collective-permute-start.6 = (bf16[400,128]{1,0:T(8,128)(2,1)S(1)}, bf16[400,128]{1,0:T(8,128)(2,1)S(1)}, u32[]{:S(2)}, u32[]{:S(2)}) collective-permute-start(bf16[400,128]{1,0:T(8,128)(2,1)S(1)} %lean.1), channel_id=1, source_target_pairs={{0,3},{1,2},{2,1},{3,0},{4,7},{5,6},{6,5},{7,4},{8,11},{9,10},{10,... | collective-permute-start | bytes 307208 | tf_op jit(solution)/shard_map/ppermute | solution.py:209
  10.5 0.7 %collective-permute-start.5 = (bf16[400,128]{1,0:T(8,128)(2,1)S(1)}, bf16[400,128]{1,0:T(8,128)(2,1)S(1)}, u32[]{:S(2)}, u32[]{:S(2)}) collective-permute-start(bf16[400,128]{1,0:T(8,128)(2,1)S(1)} %lean.1), channel_id=1, source_target_pairs={{0,1},{1,0},{2,3},{3,2},{4,5},{5,4},{6,7},{7,6},{8,9},{9,8},{10,11... | collective-permute-start | bytes 307208 | tf_op jit(solution)/shard_map/ppermute | solution.py:209
  11.1 0.0 collective-permute-done.refs_1_
  11.2 0.0 collective-permute-done.1.raw
  11.2 0.0 collective-permute-done.2.refs_0_
  11.2 0.4 %collective-permute-start.3 = (bf16[192,128]{1,0:T(8,128)(2,1)S(1)}, bf16[192,128]{1,0:T(8,128)(2,1)S(1)}, u32[]{:S(2)}, u32[]{:S(2)}) collective-permute-start(bf16[192,128]{1,0:T(8,128)(2,1)S(1)} %merge.1), channel_id=1, source_target_pairs={{0,4},{4,0},{8,12},{12,8},{16,20},{20,16},{24,28},{28,24},{1,5},{5... | collective-permute-start | bytes 147464 | tf_op jit(solution)/shard_map/ppermute | solution.py:220
  11.6 0.0 copy-start
  11.6 0.2 relay.1.refs_1_
  11.8 0.7 %collective-permute-done.3.refs_2_ = bf16[192,128]{1,0:T(8,128)(2,1)S(1)} collective-permute-done((bf16[192,128]{1,0:T(8,128)(2,1)S(1)}, bf16[192,128]{1,0:T(8,128)(2,1)S(1)}, u32[]{:S(2)}, u32[]{:S(2)}) %collective-permute-start.3) | collective-permute-done | bytes 49184 | tf_op jit(solution)/shard_map/ppermute | solution.py:220
  12.5 0.0 copy-done
  12.5 0.8 %half.1.half_ref = bf16[5,64,256]{2,1,0:T(8,128)(2,1)S(1)} custom-call(s32[3]{0:T(128)S(1)} %get-tuple-element.22.meta_ref, bf16[64,256]{1,0:T(8,128)(2,1)S(1)} %copy-done, bf16[384,128]{1,0:T(8,128)(2,1)S(1)} %get-tuple-element.15.own_ref.refs_0_, bf16[144,128]{1,0:T(8,128)(2,1)S(1)} %collective-permute-done.2.refs_0_, ...), custom_call_target="tpu_custom_call" | custom-call | tf_op jit(solution)/shard_map/half/pallas_call | solution.py:229
  13.3 1.5 %collective-permute-done.6.refs_3_ = bf16[400,128]{1,0:T(8,128)(2,1)S(1)} collective-permute-done((bf16[400,128]{1,0:T(8,128)(2,1)S(1)}, bf16[400,128]{1,0:T(8,128)(2,1)S(1)}, u32[]{:S(2)}, u32[]{:S(2)}) %collective-permute-start.6) | collective-permute-done | bytes 102432 | tf_op jit(solution)/shard_map/ppermute | solution.py:209
  14.8 2.2 %collective-permute-done.5.refs_2_ = bf16[400,128]{1,0:T(8,128)(2,1)S(1)} collective-permute-done((bf16[400,128]{1,0:T(8,128)(2,1)S(1)}, bf16[400,128]{1,0:T(8,128)(2,1)S(1)}, u32[]{:S(2)}, u32[]{:S(2)}) %collective-permute-start.5) | collective-permute-done | bytes 102432 | tf_op jit(solution)/shard_map/ppermute | solution.py:209
  17.0 0.1 maximum_convert_fusion.meta_ref
  17.1 0.9 %exchange.1 = f32[64,256]{1,0:T(8,128)S(1)} custom-call(s32[12]{0:T(128)S(1)} %maximum_convert_fusion.meta_ref, bf16[5,64,256]{2,1,0:T(8,128)(2,1)S(1)} %half.1.half_ref, bf16[384,128]{1,0:T(8,128)(2,1)S(1)} %get-tuple-element.15.own_ref.refs_0_, bf16[384,128]{1,0:T(8,128)(2,1)S(1)} %relay.1.refs_1_, bf16[400,128]{1,0:T(8,128)(2,1)S(1)} %collective-permute-done.5.refs_2_, ...), custom_call_target="tpu_custom_call" | custom-call | tf_op jit(solution)/shard_map/exchange/pallas_call | solution.py:241
  17.9 0.1 collective-permute-start.7
  18.0 1.2 %collective-permute-done.7 = f32[64,256]{1,0:T(8,128)S(1)} collective-permute-done((f32[64,256]{1,0:T(8,128)S(1)}, f32[64,256]{1,0:T(8,128)S(1)}, u32[]{:S(2)}, u32[]{:S(2)}) %collective-permute-start.7) | collective-permute-done | bytes 65568 | tf_op jit(solution)/shard_map/ppermute | solution.py:256
  19.3 2.5 %collective-permute-start.10 = (f32[64,256]{1,0:T(8,128)S(1)}, f32[64,256]{1,0:T(8,128)S(1)}, u32[]{:S(2)}, u32[]{:S(2)}) collective-permute-start(f32[64,256]{1,0:T(8,128)S(1)} %add.12), channel_id=1, source_target_pairs={{0,24},{4,28},{8,16},{12,20},{16,8},{20,12},{24,0},{28,4},{1,25},{... | collective-permute-start | bytes 196616 | tf_op jit(solution)/shard_map/ppermute | solution.py:256
  21.8 0.5 %collective-permute-start.9 = (f32[64,256]{1,0:T(8,128)S(1)}, f32[64,256]{1,0:T(8,128)S(1)}, u32[]{:S(2)}, u32[]{:S(2)}) collective-permute-start(f32[64,256]{1,0:T(8,128)S(1)} %add.12), channel_id=1, source_target_pairs={{0,16},{4,20},{8,24},{12,28},{16,0},{20,4},{24,8},{28,12},{1,17},{... | collective-permute-start | bytes 196616 | tf_op jit(solution)/shard_map/ppermute | solution.py:256
  22.3 0.5 %collective-permute-start.8 = (f32[64,256]{1,0:T(8,128)S(1)}, f32[64,256]{1,0:T(8,128)S(1)}, u32[]{:S(2)}, u32[]{:S(2)}) collective-permute-start(f32[64,256]{1,0:T(8,128)S(1)} %add.12), channel_id=1, source_target_pairs={{0,8},{4,12},{8,0},{12,4},{16,24},{20,28},{24,16},{28,20},{1,9},{5... | collective-permute-start | bytes 196616 | tf_op jit(solution)/shard_map/ppermute | solution.py:256
  22.8 1.7 %collective-permute-done.10 = f32[64,256]{1,0:T(8,128)S(1)} collective-permute-done((f32[64,256]{1,0:T(8,128)S(1)}, f32[64,256]{1,0:T(8,128)S(1)}, u32[]{:S(2)}, u32[]{:S(2)}) %collective-permute-start.10) | collective-permute-done | bytes 65568 | tf_op jit(solution)/shard_map/ppermute | solution.py:256
  24.5 1.5 %collective-permute-done.9 = f32[64,256]{1,0:T(8,128)S(1)} collective-permute-done((f32[64,256]{1,0:T(8,128)S(1)}, f32[64,256]{1,0:T(8,128)S(1)}, u32[]{:S(2)}, u32[]{:S(2)}) %collective-permute-start.9) | collective-permute-done | bytes 65568 | tf_op jit(solution)/shard_map/ppermute | solution.py:256
  26.0 0.5 %collective-permute-done.8 = f32[64,256]{1,0:T(8,128)S(1)} collective-permute-done((f32[64,256]{1,0:T(8,128)S(1)}, f32[64,256]{1,0:T(8,128)S(1)}, u32[]{:S(2)}, u32[]{:S(2)}) %collective-permute-start.8) | collective-permute-done | bytes 65568 | tf_op jit(solution)/shard_map/ppermute | solution.py:256
  26.6 0.6 %add_add_fusion = f32[64,256]{1,0:T(8,128)} fusion(f32[64,256]{1,0:T(8,128)S(1)} %collective-permute-done.9, f32[64,256]{1,0:T(8,128)S(1)} %collective-permute-done.10, f32[64,256]{1,0:T(8,128)S(1)} %add.12, f32[64,256]{1,0:T(8,128)S(1)} %collective-permute-done.8), kind=kLoop, calls=%fused_computation | loop fusion | flops 49152 | bytes 327680 | tf_op jit(solution)/shard_map/add | solution.py:258
  (6 shorter events, 0.0 us)
Async XLA Ops:
  0.0 11.2 %collective-permute-start.1 = (bf16[1,1,3,4,4096]{4,3,2,1,0:T(4,128)(2,1)}, bf16[1,1,3,4,4096]{4,3,2,1,0:T(4,128)(2,1)S(1)}, u32[]{:S(2)}, u32[]{:S(2)}) collective-permute-start(bf16[1,1,3,4,4096]{4,3,2,1,0:T(4,128)(2,1)} %raw_hbm.1), channel_id=1, source_target_pairs={{0,2},{1,3},{2,0},{3,1},{4,6},{5,7},{6,4},{7,5},{8,10},{9,11},{10,... | collective-permute-start | bytes 294920 | tf_op jit(solution)/shard_map/ppermute | solution.py:197
  5.9 2.1 %collective-permute-start.4 = (bf16[80,128]{1,0:T(8,128)(2,1)S(1)}, bf16[80,128]{1,0:T(8,128)(2,1)S(1)}, u32[]{:S(2)}, u32[]{:S(2)}) collective-permute-start(bf16[80,128]{1,0:T(8,128)(2,1)S(1)} %get-tuple-element.13), channel_id=1, source_target_pairs={{0,4},{4,0},{8,12},{12,8},{16,20},{20,16},{24,28},{28,24},{1,5},{5... | collective-permute-start | bytes 61448 | tf_op jit(solution)/shard_map/ppermute | solution.py:187
  5.9 5.2 %collective-permute-start = (bf16[80,128]{1,0:T(8,128)(2,1)S(1)}, bf16[80,128]{1,0:T(8,128)(2,1)S(1)}, u32[]{:S(2)}, u32[]{:S(2)}) collective-permute-start(bf16[80,128]{1,0:T(8,128)(2,1)S(1)} %get-tuple-element.13), channel_id=1, source_target_pairs={{0,2},{1,3},{2,0},{3,1},{4,6},{5,7},{6,4},{7,5},{8,10},{9,11},{10,... | collective-permute-start | bytes 61448 | tf_op jit(solution)/shard_map/ppermute | solution.py:198
  6.0 5.1 %collective-permute-start.2 = (bf16[144,128]{1,0:T(8,128)(2,1)S(1)}, bf16[144,128]{1,0:T(8,128)(2,1)S(1)}, u32[]{:S(2)}, u32[]{:S(2)}) collective-permute-start(bf16[144,128]{1,0:T(8,128)(2,1)S(1)} %get-tuple-element.16.near_ref), channel_id=1, source_target_pairs={{0,1},{1,0},{2,3},{3,2},{4,7},{5,6},{6,5},{7,4},{8,9},{9,8},{10,11... | collective-permute-start | bytes 110600 | tf_op jit(solution)/shard_map/ppermute | solution.py:206
  7.9 6.8 %collective-permute-start.6 = (bf16[400,128]{1,0:T(8,128)(2,1)S(1)}, bf16[400,128]{1,0:T(8,128)(2,1)S(1)}, u32[]{:S(2)}, u32[]{:S(2)}) collective-permute-start(bf16[400,128]{1,0:T(8,128)(2,1)S(1)} %lean.1), channel_id=1, source_target_pairs={{0,3},{1,2},{2,1},{3,0},{4,7},{5,6},{6,5},{7,4},{8,11},{9,10},{10,... | collective-permute-start | bytes 307208 | tf_op jit(solution)/shard_map/ppermute | solution.py:209
  10.5 6.5 %collective-permute-start.5 = (bf16[400,128]{1,0:T(8,128)(2,1)S(1)}, bf16[400,128]{1,0:T(8,128)(2,1)S(1)}, u32[]{:S(2)}, u32[]{:S(2)}) collective-permute-start(bf16[400,128]{1,0:T(8,128)(2,1)S(1)} %lean.1), channel_id=1, source_target_pairs={{0,1},{1,0},{2,3},{3,2},{4,5},{5,4},{6,7},{7,6},{8,9},{9,8},{10,11... | collective-permute-start | bytes 307208 | tf_op jit(solution)/shard_map/ppermute | solution.py:209
  11.2 1.3 %collective-permute-start.3 = (bf16[192,128]{1,0:T(8,128)(2,1)S(1)}, bf16[192,128]{1,0:T(8,128)(2,1)S(1)}, u32[]{:S(2)}, u32[]{:S(2)}) collective-permute-start(bf16[192,128]{1,0:T(8,128)(2,1)S(1)} %merge.1), channel_id=1, source_target_pairs={{0,4},{4,0},{8,12},{12,8},{16,20},{20,16},{24,28},{28,24},{1,5},{5... | collective-permute-start | bytes 147464 | tf_op jit(solution)/shard_map/ppermute | solution.py:220
  11.6 0.9 %copy-start = (bf16[64,256]{1,0:T(8,128)(2,1)S(1)}, bf16[64,256]{1,0:T(8,128)(2,1)}, u32[]{:S(2)}) copy-start(bf16[64,256]{1,0:T(8,128)(2,1)} %density_ref.1) | copy-start | bytes 98308
  17.9 1.3 %collective-permute-start.7 = (f32[64,256]{1,0:T(8,128)S(1)}, f32[64,256]{1,0:T(8,128)S(1)}, u32[]{:S(2)}, u32[]{:S(2)}) collective-permute-start(f32[64,256]{1,0:T(8,128)S(1)} %exchange.1), channel_id=1, source_target_pairs={{0,4},{4,0},{8,12},{12,8},{16,20},{20,16},{24,28},{28,24},{1,5},{5... | collective-permute-start | bytes 196616 | tf_op jit(solution)/shard_map/ppermute | solution.py:256
  19.3 5.3 %collective-permute-start.10 = (f32[64,256]{1,0:T(8,128)S(1)}, f32[64,256]{1,0:T(8,128)S(1)}, u32[]{:S(2)}, u32[]{:S(2)}) collective-permute-start(f32[64,256]{1,0:T(8,128)S(1)} %add.12), channel_id=1, source_target_pairs={{0,24},{4,28},{8,16},{12,20},{16,8},{20,12},{24,0},{28,4},{1,25},{... | collective-permute-start | bytes 196616 | tf_op jit(solution)/shard_map/ppermute | solution.py:256
  21.8 4.3 %collective-permute-start.9 = (f32[64,256]{1,0:T(8,128)S(1)}, f32[64,256]{1,0:T(8,128)S(1)}, u32[]{:S(2)}, u32[]{:S(2)}) collective-permute-start(f32[64,256]{1,0:T(8,128)S(1)} %add.12), channel_id=1, source_target_pairs={{0,16},{4,20},{8,24},{12,28},{16,0},{20,4},{24,8},{28,12},{1,17},{... | collective-permute-start | bytes 196616 | tf_op jit(solution)/shard_map/ppermute | solution.py:256
  22.3 4.3 %collective-permute-start.8 = (f32[64,256]{1,0:T(8,128)S(1)}, f32[64,256]{1,0:T(8,128)S(1)}, u32[]{:S(2)}, u32[]{:S(2)}) collective-permute-start(f32[64,256]{1,0:T(8,128)S(1)} %add.12), channel_id=1, source_target_pairs={{0,8},{4,12},{8,0},{12,4},{16,24},{20,28},{24,16},{28,20},{1,9},{5... | collective-permute-start | bytes 196616 | tf_op jit(solution)/shard_map/ppermute | solution.py:256

commit v14 on v13

--- a/solution.py
+++ b/solution.py
@@ -130,10 +130,11 @@
 def exchange_kernel(orb, slots, aux_width, meta_ref, half_ref, *refs):
     packs, (out_ref, held) = refs[:orb], refs[orb:]
     me = lax.axis_index("orb")
+    parity = core_parity()
     per_slot = aux_width * BS // LANES
     owners = [me, lax.rem(me + orb // 2, orb)]
     for i in range(1, orb // 2):
-        owners += [owner_of(me, i, sign, orb) for sign in (1, -1)]
+        owners += [owner_of(me, i, sign * (1 - 2 * parity), orb) for sign in (-1, 1)]
     for way in range(orb):
         total = None
         for j in range(slots):
@@ -204,9 +205,13 @@
             for o in range(orb)
         ]
         nears.append(lax.ppermute(near, ("aux", "orb"), perm))
-        for sign in (1, -1):
-            perm = [(o, partner(o, i, sign, orb)) for o in range(orb)]
-            leans.append(lax.ppermute(lean, "orb", perm))
+        for sign in (-1, 1):
+            perm = [
+                (a * orb + o, a * orb + partner(o, i, sign * (1 - 2 * (a % 2)), orb))
+                for a in range(aux)
+                for o in range(orb)
+            ]
+            leans.append(lax.ppermute(lean, ("aux", "orb"), perm))
 
     tail_in, raw = lax.optimization_barrier((tail_in, raw))
     merged = pl.pallas_call(

time: 27.4 us -> 27.7 us (1.011)
  starting transfers between devices: 13.3 us -> 13.9 us
  waiting for transfers between devices: 9.3 us -> 9.02 us
    ppermute x2, starting transfers between devices: 3.22 us -> 4.12 us  [shards(): leans.append(lax.ppermute(lean, ('aux', 'orb'), perm))]
    ppermute x2, waiting for transfers between devices: 3.65 us -> 3.07 us  [shards(): leans.append(lax.ppermute(lean, ('aux', 'orb'), perm))]
    ppermute x1, starting transfers between devices: 0.39 us -> 0.07 us  [shards(): swapped = lax.ppermute(merged, 'aux', [(i, i ^ 1) for i in range(aux)])]
    ppermute x1, waiting for transfers between devices: 0.67 us -> 0.97 us  [shards(): swapped = lax.ppermute(merged, 'aux', [(i, i ^ 1) for i in range(aux)])]
  transfers between devices with their start and end apart: 11 -> 11, of which waited for: 7 -> 6; matrix products, arithmetic and copies ran while one was open for 0% -> 0% of each run, Pallas kernels for 8% -> 8%
where the time goes in v14:
time: 27.7 us; the launch traced here: 27.5 us
  starting transfers between devices  13.9 us (50%)
  waiting for transfers between devices  9.02 us (33%)
  Pallas kernels  3.11 us (11%)
  between operations  0.76 us (3%)
  other arithmetic  0.74 us (3%)
    ppermute x4, waiting for transfers between devices, shards(): lax.ppermute(parts, 'aux', [(i, i ^ way * step) for i in range(aux)])  4.97 us
    ppermute x2, starting transfers between devices, shards(): leans.append(lax.ppermute(lean, ('aux', 'orb'), perm))  4.12 us
    ppermute x1, starting transfers between devices, shards(): raw = lax.ppermute(tensor_blocks, 'orb', across)  4.04 us
    ppermute x4, starting transfers between devices, shards(): lax.ppermute(parts, 'aux', [(i, i ^ way * step) for i in range(aux)])  3.62 us
    ppermute x2, waiting for transfers between devices, shards(): leans.append(lax.ppermute(lean, ('aux', 'orb'), perm))  3.07 us
    ppermute x1, starting transfers between devices, shards(): nears.append(lax.ppermute(near, ('aux', 'orb'), perm))  1.9 us
    pallas_call x1, Pallas kernels, shards(): pl.pallas_call(functools.partial(pack_kernel, orb), out_shape=[array(size...  1.16 us
    ppermute x1, waiting for transfers between devices, shards(): swapped = lax.ppermute(merged, 'aux', [(i, i ^ 1) for i in range(aux)])  0.97 us
  transfers between devices with their start and end apart: 11, of which 6 were waited for; matrix products, arithmetic and copies ran while one was open for 0% of the time, Pallas kernels for 8%

profile of v14, /device:TPU:0, one launch (start us, length us, event | category | flops | bytes accessed | tf_op | source)
XLA Modules:
  0.0 27.5 jit_solution(4939451454171386400)
XLA Ops:
  0.0 4.0 %collective-permute-start.1 = (bf16[1,1,3,4,4096]{4,3,2,1,0:T(4,128)(2,1)}, bf16[1,1,3,4,4096]{4,3,2,1,0:T(4,128)(2,1)S(1)}, u32[]{:S(2)}, u32[]{:S(2)}) collective-permute-start(bf16[1,1,3,4,4096]{4,3,2,1,0:T(4,128)(2,1)} %raw_hbm.1), channel_id=1, source_target_pairs={{0,2},{1,3},{2,0},{3,1},{4,6},{5,7},{6,4},{7,5},{8,10},{9,11},{10,... | collective-permute-start | bytes 294920 | tf_op jit(solution)/shard_map/ppermute | solution.py:198
  4.7 1.2 %pack.1 = (bf16[384,128]{1,0:T(8,128)(2,1)S(1)}, bf16[144,128]{1,0:T(8,128)(2,1)S(1)}, bf16[80,128]{1,0:T(8,128)(2,1)S(1)}) custom-call(s32[1,1]{1,0:T(1,128)S(6)} %copy.5.kept, s32[1,1,3]{2,1,0:T(1,128)} %pairs_hbm.1, bf16[64,256]{1,0:T(8,128)(2,1)} %density_ref.1, bf16[1,1,3,4,4096]{4,3,2,1,0:T(4,128)(2,1)} %raw_hbm.1), custom_call_target="tpu_custom_call" | custom-call | tf_op jit(solution)/shard_map/pack/pallas_call | solution.py:171
  5.9 0.1 collective-permute-start.4
  5.9 0.1 collective-permute-start
  6.0 1.9 %collective-permute-start.2 = (bf16[144,128]{1,0:T(8,128)(2,1)S(1)}, bf16[144,128]{1,0:T(8,128)(2,1)S(1)}, u32[]{:S(2)}, u32[]{:S(2)}) collective-permute-start(bf16[144,128]{1,0:T(8,128)(2,1)S(1)} %get-tuple-element.16.near_ref), channel_id=1, source_target_pairs={{0,1},{1,0},{2,3},{3,2},{4,7},{5,6},{6,5},{7,4},{8,9},{9,8},{10,11... | collective-permute-start | bytes 110600 | tf_op jit(solution)/shard_map/ppermute | solution.py:207
  7.9 0.0 collective-permute-done.4.mark_ref
  7.9 0.8 %collective-permute-start.6 = (bf16[400,128]{1,0:T(8,128)(2,1)S(1)}, bf16[400,128]{1,0:T(8,128)(2,1)S(1)}, u32[]{:S(2)}, u32[]{:S(2)}) collective-permute-start(bf16[400,128]{1,0:T(8,128)(2,1)S(1)} %lean.1), channel_id=1, source_target_pairs={{0,1},{1,0},{2,3},{3,2},{4,7},{5,6},{6,5},{7,4},{8,9},{9,8},{10,11... | collective-permute-start | bytes 307208 | tf_op jit(solution)/shard_map/ppermute | solution.py:214
  8.8 3.3 %collective-permute-start.5 = (bf16[400,128]{1,0:T(8,128)(2,1)S(1)}, bf16[400,128]{1,0:T(8,128)(2,1)S(1)}, u32[]{:S(2)}, u32[]{:S(2)}) collective-permute-start(bf16[400,128]{1,0:T(8,128)(2,1)S(1)} %lean.1), channel_id=1, source_target_pairs={{0,3},{1,2},{2,1},{3,0},{4,5},{5,4},{6,7},{7,6},{8,11},{9,10},{10,... | collective-permute-start | bytes 307208 | tf_op jit(solution)/shard_map/ppermute | solution.py:214
  12.0 0.0 collective-permute-done.refs_1_
  12.1 0.0 collective-permute-done.1.raw
  12.1 0.0 collective-permute-done.2.refs_0_
  12.1 0.1 collective-permute-start.3
  12.2 0.0 copy-start
  12.2 0.2 relay.1.refs_1_
  12.4 1.0 %collective-permute-done.3.refs_2_ = bf16[192,128]{1,0:T(8,128)(2,1)S(1)} collective-permute-done((bf16[192,128]{1,0:T(8,128)(2,1)S(1)}, bf16[192,128]{1,0:T(8,128)(2,1)S(1)}, u32[]{:S(2)}, u32[]{:S(2)}) %collective-permute-start.3) | collective-permute-done | bytes 49184 | tf_op jit(solution)/shard_map/ppermute | solution.py:225
  13.4 0.0 copy-done
  13.4 0.8 %half.1.half_ref = bf16[5,64,256]{2,1,0:T(8,128)(2,1)S(1)} custom-call(s32[3]{0:T(128)S(1)} %get-tuple-element.22.meta_ref, bf16[64,256]{1,0:T(8,128)(2,1)S(1)} %copy-done, bf16[384,128]{1,0:T(8,128)(2,1)S(1)} %get-tuple-element.15.own_ref.refs_0_, bf16[144,128]{1,0:T(8,128)(2,1)S(1)} %collective-permute-done.2.refs_0_, ...), custom_call_target="tpu_custom_call" | custom-call | tf_op jit(solution)/shard_map/half/pallas_call | solution.py:234
  14.2 0.0 collective-permute-done.6.refs_3_
  14.2 3.1 %collective-permute-done.5.refs_2_ = bf16[400,128]{1,0:T(8,128)(2,1)S(1)} collective-permute-done((bf16[400,128]{1,0:T(8,128)(2,1)S(1)}, bf16[400,128]{1,0:T(8,128)(2,1)S(1)}, u32[]{:S(2)}, u32[]{:S(2)}) %collective-permute-start.5) | collective-permute-done | bytes 102432 | tf_op jit(solution)/shard_map/ppermute | solution.py:214
  17.3 0.1 maximum_convert_fusion.meta_ref
  17.4 0.9 %exchange.1 = f32[64,256]{1,0:T(8,128)S(1)} custom-call(s32[12]{0:T(128)S(1)} %maximum_convert_fusion.meta_ref, bf16[5,64,256]{2,1,0:T(8,128)(2,1)S(1)} %half.1.half_ref, bf16[384,128]{1,0:T(8,128)(2,1)S(1)} %get-tuple-element.15.own_ref.refs_0_, bf16[384,128]{1,0:T(8,128)(2,1)S(1)} %relay.1.refs_1_, bf16[400,128]{1,0:T(8,128)(2,1)S(1)} %collective-permute-done.5.refs_2_, ...), custom_call_target="tpu_custom_call" | custom-call | tf_op jit(solution)/shard_map/exchange/pallas_call | solution.py:246
  18.3 0.1 collective-permute-start.7
  18.3 1.2 %collective-permute-done.7 = f32[64,256]{1,0:T(8,128)S(1)} collective-permute-done((f32[64,256]{1,0:T(8,128)S(1)}, f32[64,256]{1,0:T(8,128)S(1)}, u32[]{:S(2)}, u32[]{:S(2)}) %collective-permute-start.7) | collective-permute-done | bytes 65568 | tf_op jit(solution)/shard_map/ppermute | solution.py:261
  19.6 2.5 %collective-permute-start.10 = (f32[64,256]{1,0:T(8,128)S(1)}, f32[64,256]{1,0:T(8,128)S(1)}, u32[]{:S(2)}, u32[]{:S(2)}) collective-permute-start(f32[64,256]{1,0:T(8,128)S(1)} %add.12), channel_id=1, source_target_pairs={{0,24},{4,28},{8,16},{12,20},{16,8},{20,12},{24,0},{28,4},{1,25},{... | collective-permute-start | bytes 196616 | tf_op jit(solution)/shard_map/ppermute | solution.py:261
  22.1 0.5 %collective-permute-start.9 = (f32[64,256]{1,0:T(8,128)S(1)}, f32[64,256]{1,0:T(8,128)S(1)}, u32[]{:S(2)}, u32[]{:S(2)}) collective-permute-start(f32[64,256]{1,0:T(8,128)S(1)} %add.12), channel_id=1, source_target_pairs={{0,16},{4,20},{8,24},{12,28},{16,0},{20,4},{24,8},{28,12},{1,17},{... | collective-permute-start | bytes 196616 | tf_op jit(solution)/shard_map/ppermute | solution.py:261
  22.6 0.5 %collective-permute-start.8 = (f32[64,256]{1,0:T(8,128)S(1)}, f32[64,256]{1,0:T(8,128)S(1)}, u32[]{:S(2)}, u32[]{:S(2)}) collective-permute-start(f32[64,256]{1,0:T(8,128)S(1)} %add.12), channel_id=1, source_target_pairs={{0,8},{4,12},{8,0},{12,4},{16,24},{20,28},{24,16},{28,20},{1,9},{5... | collective-permute-start | bytes 196616 | tf_op jit(solution)/shard_map/ppermute | solution.py:261
  23.2 1.7 %collective-permute-done.10 = f32[64,256]{1,0:T(8,128)S(1)} collective-permute-done((f32[64,256]{1,0:T(8,128)S(1)}, f32[64,256]{1,0:T(8,128)S(1)}, u32[]{:S(2)}, u32[]{:S(2)}) %collective-permute-start.10) | collective-permute-done | bytes 65568 | tf_op jit(solution)/shard_map/ppermute | solution.py:261
  24.9 1.5 %collective-permute-done.9 = f32[64,256]{1,0:T(8,128)S(1)} collective-permute-done((f32[64,256]{1,0:T(8,128)S(1)}, f32[64,256]{1,0:T(8,128)S(1)}, u32[]{:S(2)}, u32[]{:S(2)}) %collective-permute-start.9) | collective-permute-done | bytes 65568 | tf_op jit(solution)/shard_map/ppermute | solution.py:261
  26.4 0.5 %collective-permute-done.8 = f32[64,256]{1,0:T(8,128)S(1)} collective-permute-done((f32[64,256]{1,0:T(8,128)S(1)}, f32[64,256]{1,0:T(8,128)S(1)}, u32[]{:S(2)}, u32[]{:S(2)}) %collective-permute-start.8) | collective-permute-done | bytes 65568 | tf_op jit(solution)/shard_map/ppermute | solution.py:261
  26.9 0.6 %add_add_fusion = f32[64,256]{1,0:T(8,128)} fusion(f32[64,256]{1,0:T(8,128)S(1)} %collective-permute-done.9, f32[64,256]{1,0:T(8,128)S(1)} %collective-permute-done.10, f32[64,256]{1,0:T(8,128)S(1)} %add.12, f32[64,256]{1,0:T(8,128)S(1)} %collective-permute-done.8), kind=kLoop, calls=%fused_computation | loop fusion | flops 49152 | bytes 327680 | tf_op jit(solution)/shard_map/add | solution.py:263
  (6 shorter events, 0.0 us)
Async XLA Ops:
  0.0 12.1 %collective-permute-start.1 = (bf16[1,1,3,4,4096]{4,3,2,1,0:T(4,128)(2,1)}, bf16[1,1,3,4,4096]{4,3,2,1,0:T(4,128)(2,1)S(1)}, u32[]{:S(2)}, u32[]{:S(2)}) collective-permute-start(bf16[1,1,3,4,4096]{4,3,2,1,0:T(4,128)(2,1)} %raw_hbm.1), channel_id=1, source_target_pairs={{0,2},{1,3},{2,0},{3,1},{4,6},{5,7},{6,4},{7,5},{8,10},{9,11},{10,... | collective-permute-start | bytes 294920 | tf_op jit(solution)/shard_map/ppermute | solution.py:198
  5.9 2.1 %collective-permute-start.4 = (bf16[80,128]{1,0:T(8,128)(2,1)S(1)}, bf16[80,128]{1,0:T(8,128)(2,1)S(1)}, u32[]{:S(2)}, u32[]{:S(2)}) collective-permute-start(bf16[80,128]{1,0:T(8,128)(2,1)S(1)} %get-tuple-element.13), channel_id=1, source_target_pairs={{0,4},{4,0},{8,12},{12,8},{16,20},{20,16},{24,28},{28,24},{1,5},{5... | collective-permute-start | bytes 61448 | tf_op jit(solution)/shard_map/ppermute | solution.py:188
  5.9 6.1 %collective-permute-start = (bf16[80,128]{1,0:T(8,128)(2,1)S(1)}, bf16[80,128]{1,0:T(8,128)(2,1)S(1)}, u32[]{:S(2)}, u32[]{:S(2)}) collective-permute-start(bf16[80,128]{1,0:T(8,128)(2,1)S(1)} %get-tuple-element.13), channel_id=1, source_target_pairs={{0,2},{1,3},{2,0},{3,1},{4,6},{5,7},{6,4},{7,5},{8,10},{9,11},{10,... | collective-permute-start | bytes 61448 | tf_op jit(solution)/shard_map/ppermute | solution.py:199
  6.0 6.0 %collective-permute-start.2 = (bf16[144,128]{1,0:T(8,128)(2,1)S(1)}, bf16[144,128]{1,0:T(8,128)(2,1)S(1)}, u32[]{:S(2)}, u32[]{:S(2)}) collective-permute-start(bf16[144,128]{1,0:T(8,128)(2,1)S(1)} %get-tuple-element.16.near_ref), channel_id=1, source_target_pairs={{0,1},{1,0},{2,3},{3,2},{4,7},{5,6},{6,5},{7,4},{8,9},{9,8},{10,11... | collective-permute-start | bytes 110600 | tf_op jit(solution)/shard_map/ppermute | solution.py:207
  7.9 6.3 %collective-permute-start.6 = (bf16[400,128]{1,0:T(8,128)(2,1)S(1)}, bf16[400,128]{1,0:T(8,128)(2,1)S(1)}, u32[]{:S(2)}, u32[]{:S(2)}) collective-permute-start(bf16[400,128]{1,0:T(8,128)(2,1)S(1)} %lean.1), channel_id=1, source_target_pairs={{0,1},{1,0},{2,3},{3,2},{4,7},{5,6},{6,5},{7,4},{8,9},{9,8},{10,11... | collective-permute-start | bytes 307208 | tf_op jit(solution)/shard_map/ppermute | solution.py:214
  8.8 8.5 %collective-permute-start.5 = (bf16[400,128]{1,0:T(8,128)(2,1)S(1)}, bf16[400,128]{1,0:T(8,128)(2,1)S(1)}, u32[]{:S(2)}, u32[]{:S(2)}) collective-permute-start(bf16[400,128]{1,0:T(8,128)(2,1)S(1)} %lean.1), channel_id=1, source_target_pairs={{0,3},{1,2},{2,1},{3,0},{4,5},{5,4},{6,7},{7,6},{8,11},{9,10},{10,... | collective-permute-start | bytes 307208 | tf_op jit(solution)/shard_map/ppermute | solution.py:214
  12.1 1.3 %collective-permute-start.3 = (bf16[192,128]{1,0:T(8,128)(2,1)S(1)}, bf16[192,128]{1,0:T(8,128)(2,1)S(1)}, u32[]{:S(2)}, u32[]{:S(2)}) collective-permute-start(bf16[192,128]{1,0:T(8,128)(2,1)S(1)} %merge.1), channel_id=1, source_target_pairs={{0,4},{4,0},{8,12},{12,8},{16,20},{20,16},{24,28},{28,24},{1,5},{5... | collective-permute-start | bytes 147464 | tf_op jit(solution)/shard_map/ppermute | solution.py:225
  12.2 1.2 %copy-start = (bf16[64,256]{1,0:T(8,128)(2,1)S(1)}, bf16[64,256]{1,0:T(8,128)(2,1)}, u32[]{:S(2)}) copy-start(bf16[64,256]{1,0:T(8,128)(2,1)} %density_ref.1) | copy-start | bytes 98308
  18.3 1.3 %collective-permute-start.7 = (f32[64,256]{1,0:T(8,128)S(1)}, f32[64,256]{1,0:T(8,128)S(1)}, u32[]{:S(2)}, u32[]{:S(2)}) collective-permute-start(f32[64,256]{1,0:T(8,128)S(1)} %exchange.1), channel_id=1, source_target_pairs={{0,4},{4,0},{8,12},{12,8},{16,20},{20,16},{24,28},{28,24},{1,5},{5... | collective-permute-start | bytes 196616 | tf_op jit(solution)/shard_map/ppermute | solution.py:261
  19.6 5.3 %collective-permute-start.10 = (f32[64,256]{1,0:T(8,128)S(1)}, f32[64,256]{1,0:T(8,128)S(1)}, u32[]{:S(2)}, u32[]{:S(2)}) collective-permute-start(f32[64,256]{1,0:T(8,128)S(1)} %add.12), channel_id=1, source_target_pairs={{0,24},{4,28},{8,16},{12,20},{16,8},{20,12},{24,0},{28,4},{1,25},{... | collective-permute-start | bytes 196616 | tf_op jit(solution)/shard_map/ppermute | solution.py:261
  22.1 4.3 %collective-permute-start.9 = (f32[64,256]{1,0:T(8,128)S(1)}, f32[64,256]{1,0:T(8,128)S(1)}, u32[]{:S(2)}, u32[]{:S(2)}) collective-permute-start(f32[64,256]{1,0:T(8,128)S(1)} %add.12), channel_id=1, source_target_pairs={{0,16},{4,20},{8,24},{12,28},{16,0},{20,4},{24,8},{28,12},{1,17},{... | collective-permute-start | bytes 196616 | tf_op jit(solution)/shard_map/ppermute | solution.py:261
  22.6 4.3 %collective-permute-start.8 = (f32[64,256]{1,0:T(8,128)S(1)}, f32[64,256]{1,0:T(8,128)S(1)}, u32[]{:S(2)}, u32[]{:S(2)}) collective-permute-start(f32[64,256]{1,0:T(8,128)S(1)} %add.12), channel_id=1, source_target_pairs={{0,8},{4,12},{8,0},{12,4},{16,24},{20,28},{24,16},{28,20},{1,9},{5... | collective-permute-start | bytes 196616 | tf_op jit(solution)/shard_map/ppermute | solution.py:261

commit v15 on v14

--- a/solution.py
+++ b/solution.py
@@ -185,7 +185,7 @@
         kept,
         *(pltpu.with_memory_space_constraint(a, pltpu.HBM) for a in (pairs, density, tensor_blocks)),
     )
-    mark = lax.ppermute(tail, "aux", [(i, i ^ 1) for i in range(aux)])
+    mark = lax.ppermute(near, "aux", [(i, i ^ 1) for i in range(aux)])
     lean = pl.pallas_call(
         lean_kernel,
         out_shape=array(size + NOTE),

time: 27.7 us -> 28.2 us (1.018)
  waiting for transfers between devices: 9.02 us -> 9.5 us
    ppermute x1, waiting for transfers between devices: 0.01 us -> 0.42 us  [shards(): tail_in = lax.ppermute(tail, 'orb', across)]
  transfers between devices with their start and end apart: 11 -> 11, of which waited for: 6 -> 7; matrix products, arithmetic and copies ran while one was open for 0% -> 0% of each run, Pallas kernels for 8% -> 8%
where the time goes in v15:
time: 28.2 us; the launch traced here: 28 us
  starting transfers between devices  13.9 us (49%)
  waiting for transfers between devices  9.5 us (34%)
  Pallas kernels  3.11 us (11%)
  between operations  0.75 us (3%)
  other arithmetic  0.74 us (3%)
    ppermute x4, waiting for transfers between devices, shards(): lax.ppermute(parts, 'aux', [(i, i ^ way * step) for i in range(aux)])  4.97 us
    ppermute x2, starting transfers between devices, shards(): leans.append(lax.ppermute(lean, ('aux', 'orb'), perm))  4.12 us
    ppermute x1, starting transfers between devices, shards(): raw = lax.ppermute(tensor_blocks, 'orb', across)  4.04 us
    ppermute x4, starting transfers between devices, shards(): lax.ppermute(parts, 'aux', [(i, i ^ way * step) for i in range(aux)])  3.62 us
    ppermute x2, waiting for transfers between devices, shards(): leans.append(lax.ppermute(lean, ('aux', 'orb'), perm))  3.14 us
    ppermute x1, starting transfers between devices, shards(): nears.append(lax.ppermute(near, ('aux', 'orb'), perm))  1.64 us
    pallas_call x1, Pallas kernels, shards(): pl.pallas_call(functools.partial(pack_kernel, orb), out_shape=[array(size...  1.16 us
    ppermute x1, waiting for transfers between devices, shards(): swapped = lax.ppermute(merged, 'aux', [(i, i ^ 1) for i in range(aux)])  0.97 us
  transfers between devices with their start and end apart: 11, of which 7 were waited for; matrix products, arithmetic and copies ran while one was open for 0% of the time, Pallas kernels for 8%

profile of v15, /device:TPU:0, one launch (start us, length us, event | category | flops | bytes accessed | tf_op | source)
XLA Modules:
  0.0 28.0 jit_solution(5410140321167146237)
XLA Ops:
  0.0 4.0 %collective-permute-start.1 = (bf16[1,1,3,4,4096]{4,3,2,1,0:T(4,128)(2,1)}, bf16[1,1,3,4,4096]{4,3,2,1,0:T(4,128)(2,1)S(1)}, u32[]{:S(2)}, u32[]{:S(2)}) collective-permute-start(bf16[1,1,3,4,4096]{4,3,2,1,0:T(4,128)(2,1)} %raw_hbm.1), channel_id=1, source_target_pairs={{0,2},{1,3},{2,0},{3,1},{4,6},{5,7},{6,4},{7,5},{8,10},{9,11},{10,... | collective-permute-start | bytes 294920 | tf_op jit(solution)/shard_map/ppermute | solution.py:198
  4.7 1.2 %pack.1 = (bf16[384,128]{1,0:T(8,128)(2,1)S(1)}, bf16[144,128]{1,0:T(8,128)(2,1)S(1)}, bf16[80,128]{1,0:T(8,128)(2,1)S(1)}) custom-call(s32[1,1]{1,0:T(1,128)S(6)} %copy.5.kept, s32[1,1,3]{2,1,0:T(1,128)} %pairs_hbm.1, bf16[64,256]{1,0:T(8,128)(2,1)} %density_ref.1, bf16[1,1,3,4,4096]{4,3,2,1,0:T(4,128)(2,1)} %raw_hbm.1), custom_call_target="tpu_custom_call" | custom-call | tf_op jit(solution)/shard_map/pack/pallas_call | solution.py:171
  5.9 0.1 collective-permute-start.4
  5.9 1.6 %collective-permute-start.2 = (bf16[144,128]{1,0:T(8,128)(2,1)S(1)}, bf16[144,128]{1,0:T(8,128)(2,1)S(1)}, u32[]{:S(2)}, u32[]{:S(2)}) collective-permute-start(bf16[144,128]{1,0:T(8,128)(2,1)S(1)} %get-tuple-element.16.near_ref), channel_id=1, source_target_pairs={{0,1},{1,0},{2,3},{3,2},{4,7},{5,6},{6,5},{7,4},{8,9},{9,8},{10,11... | collective-permute-start | bytes 110600 | tf_op jit(solution)/shard_map/ppermute | solution.py:207
  7.6 0.3 %collective-permute-start = (bf16[80,128]{1,0:T(8,128)(2,1)S(1)}, bf16[80,128]{1,0:T(8,128)(2,1)S(1)}, u32[]{:S(2)}, u32[]{:S(2)}) collective-permute-start(bf16[80,128]{1,0:T(8,128)(2,1)S(1)} %get-tuple-element.13), channel_id=1, source_target_pairs={{0,2},{1,3},{2,0},{3,1},{4,6},{5,7},{6,4},{7,5},{8,10},{9,11},{10,... | collective-permute-start | bytes 61448 | tf_op jit(solution)/shard_map/ppermute | solution.py:199
  7.9 0.0 collective-permute-done.4.mark_ref
  7.9 0.9 %collective-permute-start.6 = (bf16[400,128]{1,0:T(8,128)(2,1)S(1)}, bf16[400,128]{1,0:T(8,128)(2,1)S(1)}, u32[]{:S(2)}, u32[]{:S(2)}) collective-permute-start(bf16[400,128]{1,0:T(8,128)(2,1)S(1)} %lean.1), channel_id=1, source_target_pairs={{0,1},{1,0},{2,3},{3,2},{4,7},{5,6},{6,5},{7,4},{8,9},{9,8},{10,11... | collective-permute-start | bytes 307208 | tf_op jit(solution)/shard_map/ppermute | solution.py:214
  8.8 3.3 %collective-permute-start.5 = (bf16[400,128]{1,0:T(8,128)(2,1)S(1)}, bf16[400,128]{1,0:T(8,128)(2,1)S(1)}, u32[]{:S(2)}, u32[]{:S(2)}) collective-permute-start(bf16[400,128]{1,0:T(8,128)(2,1)S(1)} %lean.1), channel_id=1, source_target_pairs={{0,3},{1,2},{2,1},{3,0},{4,5},{5,4},{6,7},{7,6},{8,11},{9,10},{10,... | collective-permute-start | bytes 307208 | tf_op jit(solution)/shard_map/ppermute | solution.py:214
  12.0 0.4 %collective-permute-done.refs_1_ = bf16[80,128]{1,0:T(8,128)(2,1)S(1)} collective-permute-done((bf16[80,128]{1,0:T(8,128)(2,1)S(1)}, bf16[80,128]{1,0:T(8,128)(2,1)S(1)}, u32[]{:S(2)}, u32[]{:S(2)}) %collective-permute-start) | collective-permute-done | bytes 20512 | tf_op jit(solution)/shard_map/ppermute | solution.py:199
  12.5 0.0 collective-permute-done.1.raw
  12.5 0.0 collective-permute-done.2.refs_0_
  12.5 0.1 collective-permute-start.3
  12.6 0.0 copy-start
  12.6 0.2 relay.1.refs_1_
  12.8 1.0 %collective-permute-done.3.refs_2_ = bf16[192,128]{1,0:T(8,128)(2,1)S(1)} collective-permute-done((bf16[192,128]{1,0:T(8,128)(2,1)S(1)}, bf16[192,128]{1,0:T(8,128)(2,1)S(1)}, u32[]{:S(2)}, u32[]{:S(2)}) %collective-permute-start.3) | collective-permute-done | bytes 49184 | tf_op jit(solution)/shard_map/ppermute | solution.py:225
  13.8 0.0 copy-done
  13.8 0.8 %half.1.half_ref = bf16[5,64,256]{2,1,0:T(8,128)(2,1)S(1)} custom-call(s32[3]{0:T(128)S(1)} %get-tuple-element.22.meta_ref, bf16[64,256]{1,0:T(8,128)(2,1)S(1)} %copy-done, bf16[384,128]{1,0:T(8,128)(2,1)S(1)} %get-tuple-element.15.own_ref.refs_0_, bf16[144,128]{1,0:T(8,128)(2,1)S(1)} %collective-permute-done.2.refs_0_, ...), custom_call_target="tpu_custom_call" | custom-call | tf_op jit(solution)/shard_map/half/pallas_call | solution.py:234
  14.6 0.0 collective-permute-done.6.refs_3_
  14.6 3.1 %collective-permute-done.5.refs_2_ = bf16[400,128]{1,0:T(8,128)(2,1)S(1)} collective-permute-done((bf16[400,128]{1,0:T(8,128)(2,1)S(1)}, bf16[400,128]{1,0:T(8,128)(2,1)S(1)}, u32[]{:S(2)}, u32[]{:S(2)}) %collective-permute-start.5) | collective-permute-done | bytes 102432 | tf_op jit(solution)/shard_map/ppermute | solution.py:214
  17.8 0.1 maximum_convert_fusion.meta_ref
  17.9 0.9 %exchange.1 = f32[64,256]{1,0:T(8,128)S(1)} custom-call(s32[12]{0:T(128)S(1)} %maximum_convert_fusion.meta_ref, bf16[5,64,256]{2,1,0:T(8,128)(2,1)S(1)} %half.1.half_ref, bf16[384,128]{1,0:T(8,128)(2,1)S(1)} %get-tuple-element.15.own_ref.refs_0_, bf16[384,128]{1,0:T(8,128)(2,1)S(1)} %relay.1.refs_1_, bf16[400,128]{1,0:T(8,128)(2,1)S(1)} %collective-permute-done.5.refs_2_, ...), custom_call_target="tpu_custom_call" | custom-call | tf_op jit(solution)/shard_map/exchange/pallas_call | solution.py:246
  18.7 0.1 collective-permute-start.7
  18.8 1.2 %collective-permute-done.7 = f32[64,256]{1,0:T(8,128)S(1)} collective-permute-done((f32[64,256]{1,0:T(8,128)S(1)}, f32[64,256]{1,0:T(8,128)S(1)}, u32[]{:S(2)}, u32[]{:S(2)}) %collective-permute-start.7) | collective-permute-done | bytes 65568 | tf_op jit(solution)/shard_map/ppermute | solution.py:261
  20.1 2.5 %collective-permute-start.10 = (f32[64,256]{1,0:T(8,128)S(1)}, f32[64,256]{1,0:T(8,128)S(1)}, u32[]{:S(2)}, u32[]{:S(2)}) collective-permute-start(f32[64,256]{1,0:T(8,128)S(1)} %add.12), channel_id=1, source_target_pairs={{0,24},{4,28},{8,16},{12,20},{16,8},{20,12},{24,0},{28,4},{1,25},{... | collective-permute-start | bytes 196616 | tf_op jit(solution)/shard_map/ppermute | solution.py:261
  22.6 0.5 %collective-permute-start.9 = (f32[64,256]{1,0:T(8,128)S(1)}, f32[64,256]{1,0:T(8,128)S(1)}, u32[]{:S(2)}, u32[]{:S(2)}) collective-permute-start(f32[64,256]{1,0:T(8,128)S(1)} %add.12), channel_id=1, source_target_pairs={{0,16},{4,20},{8,24},{12,28},{16,0},{20,4},{24,8},{28,12},{1,17},{... | collective-permute-start | bytes 196616 | tf_op jit(solution)/shard_map/ppermute | solution.py:261
  23.1 0.5 %collective-permute-start.8 = (f32[64,256]{1,0:T(8,128)S(1)}, f32[64,256]{1,0:T(8,128)S(1)}, u32[]{:S(2)}, u32[]{:S(2)}) collective-permute-start(f32[64,256]{1,0:T(8,128)S(1)} %add.12), channel_id=1, source_target_pairs={{0,8},{4,12},{8,0},{12,4},{16,24},{20,28},{24,16},{28,20},{1,9},{5... | collective-permute-start | bytes 196616 | tf_op jit(solution)/shard_map/ppermute | solution.py:261
  23.6 1.7 %collective-permute-done.10 = f32[64,256]{1,0:T(8,128)S(1)} collective-permute-done((f32[64,256]{1,0:T(8,128)S(1)}, f32[64,256]{1,0:T(8,128)S(1)}, u32[]{:S(2)}, u32[]{:S(2)}) %collective-permute-start.10) | collective-permute-done | bytes 65568 | tf_op jit(solution)/shard_map/ppermute | solution.py:261
  25.3 1.5 %collective-permute-done.9 = f32[64,256]{1,0:T(8,128)S(1)} collective-permute-done((f32[64,256]{1,0:T(8,128)S(1)}, f32[64,256]{1,0:T(8,128)S(1)}, u32[]{:S(2)}, u32[]{:S(2)}) %collective-permute-start.9) | collective-permute-done | bytes 65568 | tf_op jit(solution)/shard_map/ppermute | solution.py:261
  26.9 0.5 %collective-permute-done.8 = f32[64,256]{1,0:T(8,128)S(1)} collective-permute-done((f32[64,256]{1,0:T(8,128)S(1)}, f32[64,256]{1,0:T(8,128)S(1)}, u32[]{:S(2)}, u32[]{:S(2)}) %collective-permute-start.8) | collective-permute-done | bytes 65568 | tf_op jit(solution)/shard_map/ppermute | solution.py:261
  27.4 0.6 %add_add_fusion = f32[64,256]{1,0:T(8,128)} fusion(f32[64,256]{1,0:T(8,128)S(1)} %collective-permute-done.9, f32[64,256]{1,0:T(8,128)S(1)} %collective-permute-done.10, f32[64,256]{1,0:T(8,128)S(1)} %add.12, f32[64,256]{1,0:T(8,128)S(1)} %collective-permute-done.8), kind=kLoop, calls=%fused_computation | loop fusion | flops 49152 | bytes 327680 | tf_op jit(solution)/shard_map/add | solution.py:263
  (6 shorter events, 0.0 us)
Async XLA Ops:
  0.0 12.5 %collective-permute-start.1 = (bf16[1,1,3,4,4096]{4,3,2,1,0:T(4,128)(2,1)}, bf16[1,1,3,4,4096]{4,3,2,1,0:T(4,128)(2,1)S(1)}, u32[]{:S(2)}, u32[]{:S(2)}) collective-permute-start(bf16[1,1,3,4,4096]{4,3,2,1,0:T(4,128)(2,1)} %raw_hbm.1), channel_id=1, source_target_pairs={{0,2},{1,3},{2,0},{3,1},{4,6},{5,7},{6,4},{7,5},{8,10},{9,11},{10,... | collective-permute-start | bytes 294920 | tf_op jit(solution)/shard_map/ppermute | solution.py:198
  5.9 2.1 %collective-permute-start.4 = (bf16[144,128]{1,0:T(8,128)(2,1)S(1)}, bf16[144,128]{1,0:T(8,128)(2,1)S(1)}, u32[]{:S(2)}, u32[]{:S(2)}) collective-permute-start(bf16[144,128]{1,0:T(8,128)(2,1)S(1)} %get-tuple-element.16.near_ref), channel_id=1, source_target_pairs={{0,4},{4,0},{8,12},{12,8},{16,20},{20,16},{24,28},{28,24},{1,5},{5... | collective-permute-start | bytes 110600 | tf_op jit(solution)/shard_map/ppermute | solution.py:188
  5.9 6.5 %collective-permute-start.2 = (bf16[144,128]{1,0:T(8,128)(2,1)S(1)}, bf16[144,128]{1,0:T(8,128)(2,1)S(1)}, u32[]{:S(2)}, u32[]{:S(2)}) collective-permute-start(bf16[144,128]{1,0:T(8,128)(2,1)S(1)} %get-tuple-element.16.near_ref), channel_id=1, source_target_pairs={{0,1},{1,0},{2,3},{3,2},{4,7},{5,6},{6,5},{7,4},{8,9},{9,8},{10,11... | collective-permute-start | bytes 110600 | tf_op jit(solution)/shard_map/ppermute | solution.py:207
  7.6 4.9 %collective-permute-start = (bf16[80,128]{1,0:T(8,128)(2,1)S(1)}, bf16[80,128]{1,0:T(8,128)(2,1)S(1)}, u32[]{:S(2)}, u32[]{:S(2)}) collective-permute-start(bf16[80,128]{1,0:T(8,128)(2,1)S(1)} %get-tuple-element.13), channel_id=1, source_target_pairs={{0,2},{1,3},{2,0},{3,1},{4,6},{5,7},{6,4},{7,5},{8,10},{9,11},{10,... | collective-permute-start | bytes 61448 | tf_op jit(solution)/shard_map/ppermute | solution.py:199
  7.9 6.7 %collective-permute-start.6 = (bf16[400,128]{1,0:T(8,128)(2,1)S(1)}, bf16[400,128]{1,0:T(8,128)(2,1)S(1)}, u32[]{:S(2)}, u32[]{:S(2)}) collective-permute-start(bf16[400,128]{1,0:T(8,128)(2,1)S(1)} %lean.1), channel_id=1, source_target_pairs={{0,1},{1,0},{2,3},{3,2},{4,7},{5,6},{6,5},{7,4},{8,9},{9,8},{10,11... | collective-permute-start | bytes 307208 | tf_op jit(solution)/shard_map/ppermute | solution.py:214
  8.8 9.0 %collective-permute-start.5 = (bf16[400,128]{1,0:T(8,128)(2,1)S(1)}, bf16[400,128]{1,0:T(8,128)(2,1)S(1)}, u32[]{:S(2)}, u32[]{:S(2)}) collective-permute-start(bf16[400,128]{1,0:T(8,128)(2,1)S(1)} %lean.1), channel_id=1, source_target_pairs={{0,3},{1,2},{2,1},{3,0},{4,5},{5,4},{6,7},{7,6},{8,11},{9,10},{10,... | collective-permute-start | bytes 307208 | tf_op jit(solution)/shard_map/ppermute | solution.py:214
  12.5 1.3 %collective-permute-start.3 = (bf16[192,128]{1,0:T(8,128)(2,1)S(1)}, bf16[192,128]{1,0:T(8,128)(2,1)S(1)}, u32[]{:S(2)}, u32[]{:S(2)}) collective-permute-start(bf16[192,128]{1,0:T(8,128)(2,1)S(1)} %merge.1), channel_id=1, source_target_pairs={{0,4},{4,0},{8,12},{12,8},{16,20},{20,16},{24,28},{28,24},{1,5},{5... | collective-permute-start | bytes 147464 | tf_op jit(solution)/shard_map/ppermute | solution.py:225
  12.6 1.2 %copy-start = (bf16[64,256]{1,0:T(8,128)(2,1)S(1)}, bf16[64,256]{1,0:T(8,128)(2,1)}, u32[]{:S(2)}) copy-start(bf16[64,256]{1,0:T(8,128)(2,1)} %density_ref.1) | copy-start | bytes 98308
  18.7 1.3 %collective-permute-start.7 = (f32[64,256]{1,0:T(8,128)S(1)}, f32[64,256]{1,0:T(8,128)S(1)}, u32[]{:S(2)}, u32[]{:S(2)}) collective-permute-start(f32[64,256]{1,0:T(8,128)S(1)} %exchange.1), channel_id=1, source_target_pairs={{0,4},{4,0},{8,12},{12,8},{16,20},{20,16},{24,28},{28,24},{1,5},{5... | collective-permute-start | bytes 196616 | tf_op jit(solution)/shard_map/ppermute | solution.py:261
  20.1 5.3 %collective-permute-start.10 = (f32[64,256]{1,0:T(8,128)S(1)}, f32[64,256]{1,0:T(8,128)S(1)}, u32[]{:S(2)}, u32[]{:S(2)}) collective-permute-start(f32[64,256]{1,0:T(8,128)S(1)} %add.12), channel_id=1, source_target_pairs={{0,24},{4,28},{8,16},{12,20},{16,8},{20,12},{24,0},{28,4},{1,25},{... | collective-permute-start | bytes 196616 | tf_op jit(solution)/shard_map/ppermute | solution.py:261
  22.6 4.3 %collective-permute-start.9 = (f32[64,256]{1,0:T(8,128)S(1)}, f32[64,256]{1,0:T(8,128)S(1)}, u32[]{:S(2)}, u32[]{:S(2)}) collective-permute-start(f32[64,256]{1,0:T(8,128)S(1)} %add.12), channel_id=1, source_target_pairs={{0,16},{4,20},{8,24},{12,28},{16,0},{20,4},{24,8},{28,12},{1,17},{... | collective-permute-start | bytes 196616 | tf_op jit(solution)/shard_map/ppermute | solution.py:261
  23.1 4.3 %collective-permute-start.8 = (f32[64,256]{1,0:T(8,128)S(1)}, f32[64,256]{1,0:T(8,128)S(1)}, u32[]{:S(2)}, u32[]{:S(2)}) collective-permute-start(f32[64,256]{1,0:T(8,128)S(1)} %add.12), channel_id=1, source_target_pairs={{0,8},{4,12},{8,0},{12,4},{16,24},{20,28},{24,16},{28,20},{1,9},{5... | collective-permute-start | bytes 196616 | tf_op jit(solution)/shard_map/ppermute | solution.py:261

commit v16 on v15

--- a/solution.py
+++ b/solution.py
@@ -23,14 +23,18 @@
 
 def partner(i, step, sign, orb):
     if orb == 4:
-        return i ^ (2 - sign)
+        return i ^ (3 - sign) // 2
     return (i + sign * step) % orb
 
 
 def owner_of(me, step, sign, orb):
     if orb == 4:
-        return me ^ (2 - sign)
+        return me ^ jnp.where(sign > 0, 1, 2)
     return lax.rem(me - sign * step + orb, orb)
+
+
+def opposite(i, orb):
+    return i ^ 3 if orb == 4 else (i + orb // 2) % orb
 
 
 def core_parity():
@@ -104,7 +108,7 @@
             at = (i * count + t) * BS
             rows[ahead, :, lanes] = near[t * BS : (t + 1) * BS]
             rows[behind, :, lanes] = swapped[at : at + BS]
-    across = lax.rem(me + orb // 2, orb)
+    across = opposite(me, orb)
     for t in range(count):
         lanes = slice(t * LANES, (t + 1) * LANES)
         at = len(nears) * count * BS + t * height
@@ -132,7 +136,7 @@
     me = lax.axis_index("orb")
     parity = core_parity()
     per_slot = aux_width * BS // LANES
-    owners = [me, lax.rem(me + orb // 2, orb)]
+    owners = [me, opposite(me, orb)]
     for i in range(1, orb // 2):
         owners += [owner_of(me, i, sign * (1 - 2 * parity), orb) for sign in (-1, 1)]
     for way in range(orb):
@@ -194,7 +198,7 @@
         compiler_params=params,
         name="lean",
     )(own, near, mark)
-    across = [(i, (i + orb // 2) % orb) for i in range(orb)]
+    across = [(i, opposite(i, orb)) for i in range(orb)]
     raw = lax.ppermute(tensor_blocks, "orb", across)
     tail_in = lax.ppermute(tail, "orb", across)
     nears, leans = [], []

time: 28.2 us -> 26.7 us (0.947)
  waiting for transfers between devices: 9.5 us -> 8.58 us
  starting transfers between devices: 13.9 us -> 13.3 us
    ppermute x2, waiting for transfers between devices: 3.14 us -> 1.4 us  [shards(): leans.append(lax.ppermute(lean, ('aux', 'orb'), perm))]
    ppermute x1, starting transfers between devices: 1.64 us -> 0.07 us  [shards(): nears.append(lax.ppermute(near, ('aux', 'orb'), perm))]
    ppermute x1, starting transfers between devices: 4.04 us -> 5.05 us  [shards(): raw = lax.ppermute(tensor_blocks, 'orb', across)]
    ppermute x1, waiting for transfers between devices: 0.42 us -> 1.15 us  [shards(): tail_in = lax.ppermute(tail, 'orb', across)]
    ppermute x2, starting transfers between devices: 4.12 us -> 3.41 us  [shards(): leans.append(lax.ppermute(lean, ('aux', 'orb'), perm))]
    ppermute x1, starting transfers between devices: 0.34 us -> 0.89 us  [shards(): tail_in = lax.ppermute(tail, 'orb', across)]
  transfers between devices with their start and end apart: 11 -> 11, of which waited for: 7 -> 8; matrix products, arithmetic and copies ran while one was open for 0% -> 0% of each run, Pallas kernels for 8% -> 8%
where the time goes in v16:
time: 26.7 us; the launch traced here: 26.5 us
  starting transfers between devices  13.3 us (50%)
  waiting for transfers between devices  8.58 us (32%)
  Pallas kernels  3.11 us (12%)
  other arithmetic  0.74 us (3%)
  between operations  0.74 us (3%)
    ppermute x1, starting transfers between devices, shards(): raw = lax.ppermute(tensor_blocks, 'orb', across)  5.05 us
    ppermute x4, waiting for transfers between devices, shards(): lax.ppermute(parts, 'aux', [(i, i ^ way * step) for i in range(aux)])  4.83 us
    ppermute x4, starting transfers between devices, shards(): lax.ppermute(parts, 'aux', [(i, i ^ way * step) for i in range(aux)])  3.77 us
    ppermute x2, starting transfers between devices, shards(): leans.append(lax.ppermute(lean, ('aux', 'orb'), perm))  3.41 us
    ppermute x2, waiting for transfers between devices, shards(): leans.append(lax.ppermute(lean, ('aux', 'orb'), perm))  1.4 us
    pallas_call x1, Pallas kernels, shards(): pl.pallas_call(functools.partial(pack_kernel, orb), out_shape=[array(size...  1.16 us
    ppermute x1, waiting for transfers between devices, shards(): tail_in = lax.ppermute(tail, 'orb', across)  1.15 us
    ppermute x1, waiting for transfers between devices, shards(): swapped = lax.ppermute(merged, 'aux', [(i, i ^ 1) for i in range(aux)])  0.97 us
  transfers between devices with their start and end apart: 11, of which 8 were waited for; matrix products, arithmetic and copies ran while one was open for 0% of the time, Pallas kernels for 8%

profile of v16, /device:TPU:0, one launch (start us, length us, event | category | flops | bytes accessed | tf_op | source)
XLA Modules:
  0.0 26.5 jit_solution(1882751926076859708)
XLA Ops:
  0.0 5.0 %collective-permute-start.1 = (bf16[1,1,3,4,4096]{4,3,2,1,0:T(4,128)(2,1)}, bf16[1,1,3,4,4096]{4,3,2,1,0:T(4,128)(2,1)S(1)}, u32[]{:S(2)}, u32[]{:S(2)}) collective-permute-start(bf16[1,1,3,4,4096]{4,3,2,1,0:T(4,128)(2,1)} %raw_hbm.1), channel_id=1, source_target_pairs={{0,3},{1,2},{2,1},{3,0},{4,7},{5,6},{6,5},{7,4},{8,11},{9,10},{10,... | collective-permute-start | bytes 294920 | tf_op jit(solution)/shard_map/ppermute | solution.py:202
  5.7 1.2 %pack.1 = (bf16[384,128]{1,0:T(8,128)(2,1)S(1)}, bf16[144,128]{1,0:T(8,128)(2,1)S(1)}, bf16[80,128]{1,0:T(8,128)(2,1)S(1)}) custom-call(s32[1,1]{1,0:T(1,128)S(6)} %copy.5.kept, s32[1,1,3]{2,1,0:T(1,128)} %pairs_hbm.1, bf16[64,256]{1,0:T(8,128)(2,1)} %density_ref.1, bf16[1,1,3,4,4096]{4,3,2,1,0:T(4,128)(2,1)} %raw_hbm.1), custom_call_target="tpu_custom_call" | custom-call | tf_op jit(solution)/shard_map/pack/pallas_call | solution.py:175
  6.9 0.1 collective-permute-start.4
  6.9 0.1 collective-permute-start.2
  7.0 0.9 %collective-permute-start = (bf16[80,128]{1,0:T(8,128)(2,1)S(1)}, bf16[80,128]{1,0:T(8,128)(2,1)S(1)}, u32[]{:S(2)}, u32[]{:S(2)}) collective-permute-start(bf16[80,128]{1,0:T(8,128)(2,1)S(1)} %get-tuple-element.13), channel_id=1, source_target_pairs={{0,3},{1,2},{2,1},{3,0},{4,7},{5,6},{6,5},{7,4},{8,11},{9,10},{10,... | collective-permute-start | bytes 61448 | tf_op jit(solution)/shard_map/ppermute | solution.py:203
  7.9 0.2 collective-permute-done.4.mark_ref
  8.2 1.0 %collective-permute-start.6 = (bf16[400,128]{1,0:T(8,128)(2,1)S(1)}, bf16[400,128]{1,0:T(8,128)(2,1)S(1)}, u32[]{:S(2)}, u32[]{:S(2)}) collective-permute-start(bf16[400,128]{1,0:T(8,128)(2,1)S(1)} %lean.1), channel_id=1, source_target_pairs={{0,1},{1,0},{2,3},{3,2},{4,6},{5,7},{6,4},{7,5},{8,9},{9,8},{10,11... | collective-permute-start | bytes 307208 | tf_op jit(solution)/shard_map/ppermute | solution.py:218
  9.1 2.4 %collective-permute-start.5 = (bf16[400,128]{1,0:T(8,128)(2,1)S(1)}, bf16[400,128]{1,0:T(8,128)(2,1)S(1)}, u32[]{:S(2)}, u32[]{:S(2)}) collective-permute-start(bf16[400,128]{1,0:T(8,128)(2,1)S(1)} %lean.1), channel_id=1, source_target_pairs={{0,2},{1,3},{2,0},{3,1},{4,5},{5,4},{6,7},{7,6},{8,10},{9,11},{10,... | collective-permute-start | bytes 307208 | tf_op jit(solution)/shard_map/ppermute | solution.py:218
  11.6 1.1 %collective-permute-done.refs_1_ = bf16[80,128]{1,0:T(8,128)(2,1)S(1)} collective-permute-done((bf16[80,128]{1,0:T(8,128)(2,1)S(1)}, bf16[80,128]{1,0:T(8,128)(2,1)S(1)}, u32[]{:S(2)}, u32[]{:S(2)}) %collective-permute-start) | collective-permute-done | bytes 20512 | tf_op jit(solution)/shard_map/ppermute | solution.py:203
  12.7 0.0 collective-permute-done.1.raw
  12.7 0.0 collective-permute-done.2.refs_0_
  12.7 0.1 collective-permute-start.3
  12.8 0.0 copy-start
  12.8 0.2 relay.1.refs_1_
  13.1 1.0 %collective-permute-done.3.refs_2_ = bf16[192,128]{1,0:T(8,128)(2,1)S(1)} collective-permute-done((bf16[192,128]{1,0:T(8,128)(2,1)S(1)}, bf16[192,128]{1,0:T(8,128)(2,1)S(1)}, u32[]{:S(2)}, u32[]{:S(2)}) %collective-permute-start.3) | collective-permute-done | bytes 49184 | tf_op jit(solution)/shard_map/ppermute | solution.py:229
  14.0 0.0 copy-done
  14.0 0.8 %half.1.half_ref = bf16[5,64,256]{2,1,0:T(8,128)(2,1)S(1)} custom-call(s32[3]{0:T(128)S(1)} %get-tuple-element.22.meta_ref, bf16[64,256]{1,0:T(8,128)(2,1)S(1)} %copy-done, bf16[384,128]{1,0:T(8,128)(2,1)S(1)} %get-tuple-element.15.own_ref.refs_0_, bf16[144,128]{1,0:T(8,128)(2,1)S(1)} %collective-permute-done.2.refs_0_, ...), custom_call_target="tpu_custom_call" | custom-call | tf_op jit(solution)/shard_map/half/pallas_call | solution.py:238
  14.9 1.4 %collective-permute-done.6.refs_3_ = bf16[400,128]{1,0:T(8,128)(2,1)S(1)} collective-permute-done((bf16[400,128]{1,0:T(8,128)(2,1)S(1)}, bf16[400,128]{1,0:T(8,128)(2,1)S(1)}, u32[]{:S(2)}, u32[]{:S(2)}) %collective-permute-start.6) | collective-permute-done | bytes 102432 | tf_op jit(solution)/shard_map/ppermute | solution.py:218
  16.3 0.0 collective-permute-done.5.refs_2_
  16.3 0.1 maximum_convert_fusion.meta_ref
  16.4 0.9 %exchange.1 = f32[64,256]{1,0:T(8,128)S(1)} custom-call(s32[12]{0:T(128)S(1)} %maximum_convert_fusion.meta_ref, bf16[5,64,256]{2,1,0:T(8,128)(2,1)S(1)} %half.1.half_ref, bf16[384,128]{1,0:T(8,128)(2,1)S(1)} %get-tuple-element.15.own_ref.refs_0_, bf16[384,128]{1,0:T(8,128)(2,1)S(1)} %relay.1.refs_1_, bf16[400,128]{1,0:T(8,128)(2,1)S(1)} %collective-permute-done.5.refs_2_, ...), custom_call_target="tpu_custom_call" | custom-call | tf_op jit(solution)/shard_map/exchange/pallas_call | solution.py:250
  17.2 0.2 collective-permute-start.7
  17.5 1.1 %collective-permute-done.7 = f32[64,256]{1,0:T(8,128)S(1)} collective-permute-done((f32[64,256]{1,0:T(8,128)S(1)}, f32[64,256]{1,0:T(8,128)S(1)}, u32[]{:S(2)}, u32[]{:S(2)}) %collective-permute-start.7) | collective-permute-done | bytes 65568 | tf_op jit(solution)/shard_map/ppermute | solution.py:265
  18.6 2.5 %collective-permute-start.10 = (f32[64,256]{1,0:T(8,128)S(1)}, f32[64,256]{1,0:T(8,128)S(1)}, u32[]{:S(2)}, u32[]{:S(2)}) collective-permute-start(f32[64,256]{1,0:T(8,128)S(1)} %add.12), channel_id=1, source_target_pairs={{0,24},{4,28},{8,16},{12,20},{16,8},{20,12},{24,0},{28,4},{1,25},{... | collective-permute-start | bytes 196616 | tf_op jit(solution)/shard_map/ppermute | solution.py:265
  21.1 0.5 %collective-permute-start.9 = (f32[64,256]{1,0:T(8,128)S(1)}, f32[64,256]{1,0:T(8,128)S(1)}, u32[]{:S(2)}, u32[]{:S(2)}) collective-permute-start(f32[64,256]{1,0:T(8,128)S(1)} %add.12), channel_id=1, source_target_pairs={{0,16},{4,20},{8,24},{12,28},{16,0},{20,4},{24,8},{28,12},{1,17},{... | collective-permute-start | bytes 196616 | tf_op jit(solution)/shard_map/ppermute | solution.py:265
  21.6 0.5 %collective-permute-start.8 = (f32[64,256]{1,0:T(8,128)S(1)}, f32[64,256]{1,0:T(8,128)S(1)}, u32[]{:S(2)}, u32[]{:S(2)}) collective-permute-start(f32[64,256]{1,0:T(8,128)S(1)} %add.12), channel_id=1, source_target_pairs={{0,8},{4,12},{8,0},{12,4},{16,24},{20,28},{24,16},{28,20},{1,9},{5... | collective-permute-start | bytes 196616 | tf_op jit(solution)/shard_map/ppermute | solution.py:265
  22.1 1.7 %collective-permute-done.10 = f32[64,256]{1,0:T(8,128)S(1)} collective-permute-done((f32[64,256]{1,0:T(8,128)S(1)}, f32[64,256]{1,0:T(8,128)S(1)}, u32[]{:S(2)}, u32[]{:S(2)}) %collective-permute-start.10) | collective-permute-done | bytes 65568 | tf_op jit(solution)/shard_map/ppermute | solution.py:265
  23.8 1.5 %collective-permute-done.9 = f32[64,256]{1,0:T(8,128)S(1)} collective-permute-done((f32[64,256]{1,0:T(8,128)S(1)}, f32[64,256]{1,0:T(8,128)S(1)}, u32[]{:S(2)}, u32[]{:S(2)}) %collective-permute-start.9) | collective-permute-done | bytes 65568 | tf_op jit(solution)/shard_map/ppermute | solution.py:265
  25.4 0.5 %collective-permute-done.8 = f32[64,256]{1,0:T(8,128)S(1)} collective-permute-done((f32[64,256]{1,0:T(8,128)S(1)}, f32[64,256]{1,0:T(8,128)S(1)}, u32[]{:S(2)}, u32[]{:S(2)}) %collective-permute-start.8) | collective-permute-done | bytes 65568 | tf_op jit(solution)/shard_map/ppermute | solution.py:265
  25.9 0.6 %add_add_fusion = f32[64,256]{1,0:T(8,128)} fusion(f32[64,256]{1,0:T(8,128)S(1)} %collective-permute-done.9, f32[64,256]{1,0:T(8,128)S(1)} %collective-permute-done.10, f32[64,256]{1,0:T(8,128)S(1)} %add.12, f32[64,256]{1,0:T(8,128)S(1)} %collective-permute-done.8), kind=kLoop, calls=%fused_computation | loop fusion | flops 49152 | bytes 327680 | tf_op jit(solution)/shard_map/add | solution.py:267
  (6 shorter events, 0.0 us)
Async XLA Ops:
  0.0 12.7 %collective-permute-start.1 = (bf16[1,1,3,4,4096]{4,3,2,1,0:T(4,128)(2,1)}, bf16[1,1,3,4,4096]{4,3,2,1,0:T(4,128)(2,1)S(1)}, u32[]{:S(2)}, u32[]{:S(2)}) collective-permute-start(bf16[1,1,3,4,4096]{4,3,2,1,0:T(4,128)(2,1)} %raw_hbm.1), channel_id=1, source_target_pairs={{0,3},{1,2},{2,1},{3,0},{4,7},{5,6},{6,5},{7,4},{8,11},{9,10},{10,... | collective-permute-start | bytes 294920 | tf_op jit(solution)/shard_map/ppermute | solution.py:202
  6.9 1.3 %collective-permute-start.4 = (bf16[144,128]{1,0:T(8,128)(2,1)S(1)}, bf16[144,128]{1,0:T(8,128)(2,1)S(1)}, u32[]{:S(2)}, u32[]{:S(2)}) collective-permute-start(bf16[144,128]{1,0:T(8,128)(2,1)S(1)} %get-tuple-element.16.near_ref), channel_id=1, source_target_pairs={{0,4},{4,0},{8,12},{12,8},{16,20},{20,16},{24,28},{28,24},{1,5},{5... | collective-permute-start | bytes 110600 | tf_op jit(solution)/shard_map/ppermute | solution.py:192
  6.9 5.8 %collective-permute-start.2 = (bf16[144,128]{1,0:T(8,128)(2,1)S(1)}, bf16[144,128]{1,0:T(8,128)(2,1)S(1)}, u32[]{:S(2)}, u32[]{:S(2)}) collective-permute-start(bf16[144,128]{1,0:T(8,128)(2,1)S(1)} %get-tuple-element.16.near_ref), channel_id=1, source_target_pairs={{0,1},{1,0},{2,3},{3,2},{4,6},{5,7},{6,4},{7,5},{8,9},{9,8},{10,11... | collective-permute-start | bytes 110600 | tf_op jit(solution)/shard_map/ppermute | solution.py:211
  7.0 5.7 %collective-permute-start = (bf16[80,128]{1,0:T(8,128)(2,1)S(1)}, bf16[80,128]{1,0:T(8,128)(2,1)S(1)}, u32[]{:S(2)}, u32[]{:S(2)}) collective-permute-start(bf16[80,128]{1,0:T(8,128)(2,1)S(1)} %get-tuple-element.13), channel_id=1, source_target_pairs={{0,3},{1,2},{2,1},{3,0},{4,7},{5,6},{6,5},{7,4},{8,11},{9,10},{10,... | collective-permute-start | bytes 61448 | tf_op jit(solution)/shard_map/ppermute | solution.py:203
  8.2 8.1 %collective-permute-start.6 = (bf16[400,128]{1,0:T(8,128)(2,1)S(1)}, bf16[400,128]{1,0:T(8,128)(2,1)S(1)}, u32[]{:S(2)}, u32[]{:S(2)}) collective-permute-start(bf16[400,128]{1,0:T(8,128)(2,1)S(1)} %lean.1), channel_id=1, source_target_pairs={{0,1},{1,0},{2,3},{3,2},{4,6},{5,7},{6,4},{7,5},{8,9},{9,8},{10,11... | collective-permute-start | bytes 307208 | tf_op jit(solution)/shard_map/ppermute | solution.py:218
  9.1 7.1 %collective-permute-start.5 = (bf16[400,128]{1,0:T(8,128)(2,1)S(1)}, bf16[400,128]{1,0:T(8,128)(2,1)S(1)}, u32[]{:S(2)}, u32[]{:S(2)}) collective-permute-start(bf16[400,128]{1,0:T(8,128)(2,1)S(1)} %lean.1), channel_id=1, source_target_pairs={{0,2},{1,3},{2,0},{3,1},{4,5},{5,4},{6,7},{7,6},{8,10},{9,11},{10,... | collective-permute-start | bytes 307208 | tf_op jit(solution)/shard_map/ppermute | solution.py:218
  12.7 1.3 %collective-permute-start.3 = (bf16[192,128]{1,0:T(8,128)(2,1)S(1)}, bf16[192,128]{1,0:T(8,128)(2,1)S(1)}, u32[]{:S(2)}, u32[]{:S(2)}) collective-permute-start(bf16[192,128]{1,0:T(8,128)(2,1)S(1)} %merge.1), channel_id=1, source_target_pairs={{0,4},{4,0},{8,12},{12,8},{16,20},{20,16},{24,28},{28,24},{1,5},{5... | collective-permute-start | bytes 147464 | tf_op jit(solution)/shard_map/ppermute | solution.py:229
  12.8 1.2 %copy-start = (bf16[64,256]{1,0:T(8,128)(2,1)S(1)}, bf16[64,256]{1,0:T(8,128)(2,1)}, u32[]{:S(2)}) copy-start(bf16[64,256]{1,0:T(8,128)(2,1)} %density_ref.1) | copy-start | bytes 98308
  17.2 1.3 %collective-permute-start.7 = (f32[64,256]{1,0:T(8,128)S(1)}, f32[64,256]{1,0:T(8,128)S(1)}, u32[]{:S(2)}, u32[]{:S(2)}) collective-permute-start(f32[64,256]{1,0:T(8,128)S(1)} %exchange.1), channel_id=1, source_target_pairs={{0,4},{4,0},{8,12},{12,8},{16,20},{20,16},{24,28},{28,24},{1,5},{5... | collective-permute-start | bytes 196616 | tf_op jit(solution)/shard_map/ppermute | solution.py:265
  18.6 5.3 %collective-permute-start.10 = (f32[64,256]{1,0:T(8,128)S(1)}, f32[64,256]{1,0:T(8,128)S(1)}, u32[]{:S(2)}, u32[]{:S(2)}) collective-permute-start(f32[64,256]{1,0:T(8,128)S(1)} %add.12), channel_id=1, source_target_pairs={{0,24},{4,28},{8,16},{12,20},{16,8},{20,12},{24,0},{28,4},{1,25},{... | collective-permute-start | bytes 196616 | tf_op jit(solution)/shard_map/ppermute | solution.py:265
  21.1 4.3 %collective-permute-start.9 = (f32[64,256]{1,0:T(8,128)S(1)}, f32[64,256]{1,0:T(8,128)S(1)}, u32[]{:S(2)}, u32[]{:S(2)}) collective-permute-start(f32[64,256]{1,0:T(8,128)S(1)} %add.12), channel_id=1, source_target_pairs={{0,16},{4,20},{8,24},{12,28},{16,0},{20,4},{24,8},{28,12},{1,17},{... | collective-permute-start | bytes 196616 | tf_op jit(solution)/shard_map/ppermute | solution.py:265
  21.6 4.3 %collective-permute-start.8 = (f32[64,256]{1,0:T(8,128)S(1)}, f32[64,256]{1,0:T(8,128)S(1)}, u32[]{:S(2)}, u32[]{:S(2)}) collective-permute-start(f32[64,256]{1,0:T(8,128)S(1)} %add.12), channel_id=1, source_target_pairs={{0,8},{4,12},{8,0},{12,4},{16,24},{20,28},{24,16},{28,20},{1,9},{5... | collective-permute-start | bytes 196616 | tf_op jit(solution)/shard_map/ppermute | solution.py:265

commit v17 on v12

--- a/solution.py
+++ b/solution.py
@@ -252,16 +252,20 @@
         name="exchange",
     )(codes, half, *packs)
 
-    step = 1
+    odd = core_parity() == 1
+    parts = parts + lax.ppermute(parts, "aux", [(i, i ^ 1) for i in range(aux)])
+    step = 2
     while step < aux:
-        ways = 2 if step == 1 or step * 4 > aux else 4
-        terms = [parts]
-        for way in range(1, ways):
-            terms.append(lax.ppermute(parts, "aux", [(i, i ^ (way * step)) for i in range(aux)]))
-        while len(terms) > 1:
-            terms = [terms[i] + terms[i + 1] for i in range(0, len(terms), 2)]
-        parts = terms[0]
-        step *= ways
+        if step * 4 > aux:
+            parts = parts + lax.ppermute(parts, "aux", [(i, i ^ step) for i in range(aux)])
+            break
+        first = [(i, i ^ (2 * step if i % 2 else step)) for i in range(aux)]
+        second = [(i, i ^ (3 * step)) for i in range(aux) if i % 2]
+        one = lax.ppermute(parts, "aux", first)
+        two = lax.ppermute(parts, "aux", second)
+        parts = one + jnp.where(odd, two, parts)
+        parts = parts + lax.ppermute(parts, "aux", [(i, i ^ 1) for i in range(aux)])
+        step *= 4
     return parts
 
 

time: 26.2 us -> 27.6 us (1.053); the launches traced: 26.1 us -> 27.2 us
  starting transfers between devices: 12.2 us -> 13.9 us
  waiting for transfers between devices: 9.3 us -> 8.68 us
    ppermute x4, starting transfers between devices: 3.62 us -> 5.35 us  [the longest x2 2.84 us: shards(): parts = parts + lax.ppermute(parts, 'aux', [(i, i ^ 1) for i in range(aux)])]
    ppermute x4, waiting for transfers between devices: 5.25 us -> 4.63 us  [the longest x1 2.49 us: shards(): one = lax.ppermute(parts, 'aux', first)]
    add x2 -> x3, other arithmetic: 0.66 us -> 0.66 us  [the longest x2 0.65 us: shards(): parts = parts + lax.ppermute(parts, 'aux', [(i, i ^ 1) for i in range(aux)])]
  transfers between devices with their start and end apart: 9 -> 9, of which waited for: 8 -> 7; matrix products, arithmetic and copies ran while one was open for 0% -> 0% of each run, Pallas kernels for 9% -> 8%
where the time goes in v17:
time: 27.6 us; the launch traced here: 27.2 us
  starting transfers between devices  13.9 us (50%)
  waiting for transfers between devices  8.68 us (31%)
  Pallas kernels  3.1 us (11%)
  other arithmetic  0.75 us (3%)
  between operations  0.75 us (3%)
    ppermute x2, starting transfers between devices, shift(): return lax.ppermute(x, ('aux', 'orb'), perm)  4.44 us
    ppermute x1, starting transfers between devices, shards(): raw = lax.ppermute(tensor_blocks, 'orb', across)  4.04 us
    ppermute x2, starting transfers between devices, shards(): parts = parts + lax.ppermute(parts, 'aux', [(i, i ^ 1) for i in range(aux)])  2.84 us
    ppermute x1, waiting for transfers between devices, shards(): one = lax.ppermute(parts, 'aux', first)  2.49 us
    ppermute x2, waiting for transfers between devices, shards(): parts = parts + lax.ppermute(parts, 'aux', [(i, i ^ 1) for i in range(aux)])  2.14 us
    ppermute x1, waiting for transfers between devices, shards(): tail_in = lax.ppermute(tail, 'orb', across)  2.07 us
    ppermute x1, starting transfers between devices, shards(): one = lax.ppermute(parts, 'aux', first)  1.84 us
    ppermute x1, waiting for transfers between devices, shards(): swapped = lax.ppermute(merged, 'aux', [(i, i ^ 1) for i in range(aux)])  1.21 us
  transfers between devices with their start and end apart: 9, of which 7 were waited for; matrix products, arithmetic and copies ran while one was open for 0% of the time, Pallas kernels for 8%

profile of v17, /device:TPU:0, one launch (start us, length us, event | category | flops | bytes accessed | tf_op | source)
XLA Modules:
  0.0 27.2 jit_solution(1035986117953303830)
XLA Ops:
  0.0 4.0 %collective-permute-start.1 = (bf16[1,1,3,4,4096]{4,3,2,1,0:T(4,128)(2,1)}, bf16[1,1,3,4,4096]{4,3,2,1,0:T(4,128)(2,1)S(1)}, u32[]{:S(2)}, u32[]{:S(2)}) collective-permute-start(bf16[1,1,3,4,4096]{4,3,2,1,0:T(4,128)(2,1)} %raw_hbm.1), channel_id=1, source_target_pairs={{0,2},{1,3},{2,0},{3,1},{4,6},{5,7},{6,4},{7,5},{8,10},{9,11},{10,... | collective-permute-start | bytes 294920 | tf_op jit(solution)/shard_map/ppermute | solution.py:207
  4.7 1.2 %pack.1 = (bf16[528,128]{1,0:T(8,128)(2,1)S(1)}, bf16[80,128]{1,0:T(8,128)(2,1)S(1)}) custom-call(s32[1,1]{1,0:T(1,128)S(6)} %copy.5.kept, s32[1,1,3]{2,1,0:T(1,128)} %pairs_hbm.1, bf16[64,256]{1,0:T(8,128)(2,1)} %density_ref.1, bf16[1,1,3,4,4096]{4,3,2,1,0:T(4,128)(2,1)} %raw_hbm.1), custom_call_target="tpu_custom_call" | custom-call | tf_op jit(solution)/shard_map/pack/pallas_call | solution.py:181
  5.9 0.1 collective-permute-start
  5.9 1.9 %collective-permute-start.2 = (bf16[528,128]{1,0:T(8,128)(2,1)S(1)}, bf16[528,128]{1,0:T(8,128)(2,1)S(1)}, u32[]{:S(2)}, u32[]{:S(2)}) collective-permute-start(bf16[528,128]{1,0:T(8,128)(2,1)S(1)} %get-tuple-element.13.own_ref.full_ref.refs_0_), channel_id=1, source_target_pairs={{0,1},{1,0},{2,3},{3,2},{4,7},{5,6},{6,5},{7,4},{8,9},{9,8},{10,11... | collective-permute-start | bytes 405512 | tf_op jit(solution)/shard_map/ppermute | solution.py:179
  7.8 2.5 %collective-permute-start.4 = (bf16[400,128]{1,0:T(8,128)(2,1)S(1)}, bf16[400,128]{1,0:T(8,128)(2,1)S(1)}, u32[]{:S(2)}, u32[]{:S(2)}) collective-permute-start(bf16[400,128]{1,0:T(8,128)(2,1)S(1)} %lean.1), channel_id=1, source_target_pairs={{0,3},{1,2},{2,1},{3,0},{4,5},{5,4},{6,7},{7,6},{8,11},{9,10},{10,... | collective-permute-start | bytes 307208 | tf_op jit(solution)/shard_map/ppermute | solution.py:179
  10.4 2.1 %collective-permute-done.refs_1_ = bf16[80,128]{1,0:T(8,128)(2,1)S(1)} collective-permute-done((bf16[80,128]{1,0:T(8,128)(2,1)S(1)}, bf16[80,128]{1,0:T(8,128)(2,1)S(1)}, u32[]{:S(2)}, u32[]{:S(2)}) %collective-permute-start) | collective-permute-done | bytes 20512 | tf_op jit(solution)/shard_map/ppermute | solution.py:208
  12.5 0.0 collective-permute-done.1.raw
  12.5 0.2 relay.1.refs_1_
  12.7 0.0 copy-start
  12.7 0.5 %collective-permute-done.2.refs_0_.refs_2_ = bf16[528,128]{1,0:T(8,128)(2,1)S(1)} collective-permute-done((bf16[528,128]{1,0:T(8,128)(2,1)S(1)}, bf16[528,128]{1,0:T(8,128)(2,1)S(1)}, u32[]{:S(2)}, u32[]{:S(2)}) %collective-permute-start.2) | collective-permute-done | bytes 135200 | tf_op jit(solution)/shard_map/ppermute | solution.py:179
  13.2 0.0 collective-permute-start.3
  13.2 1.2 %collective-permute-done.3.refs_2_ = bf16[192,128]{1,0:T(8,128)(2,1)S(1)} collective-permute-done((bf16[192,128]{1,0:T(8,128)(2,1)S(1)}, bf16[192,128]{1,0:T(8,128)(2,1)S(1)}, u32[]{:S(2)}, u32[]{:S(2)}) %collective-permute-start.3) | collective-permute-done | bytes 49184 | tf_op jit(solution)/shard_map/ppermute | solution.py:221
  14.5 0.0 copy-done
  14.5 0.8 %half.1.half_ref = bf16[5,64,256]{2,1,0:T(8,128)(2,1)S(1)} custom-call(s32[3]{0:T(128)S(1)} %get-tuple-element.18.meta_ref, bf16[64,256]{1,0:T(8,128)(2,1)S(1)} %copy-done, bf16[528,128]{1,0:T(8,128)(2,1)S(1)} %get-tuple-element.13.own_ref.full_ref.refs_0_, bf16[528,128]{1,0:T(8,128)(2,1)S(1)} %collective-permute-done.2.refs_0_.refs_2_, ...), custom_call_target="tpu_custom_call" | custom-call | tf_op jit(solution)/shard_map/half/pallas_call | solution.py:230
  15.3 0.3 collective-permute-done.4.refs_3_
  15.6 0.1 maximum_convert_fusion.meta_ref
  15.6 0.9 %exchange.1 = f32[64,256]{1,0:T(8,128)S(1)} custom-call(s32[12]{0:T(128)S(1)} %maximum_convert_fusion.meta_ref, bf16[5,64,256]{2,1,0:T(8,128)(2,1)S(1)} %half.1.half_ref, bf16[528,128]{1,0:T(8,128)(2,1)S(1)} %get-tuple-element.13.own_ref.full_ref.refs_0_, bf16[384,128]{1,0:T(8,128)(2,1)S(1)} %relay.1.refs_1_, ...), custom_call_target="tpu_custom_call" | custom-call | tf_op jit(solution)/shard_map/exchange/pallas_call | solution.py:245
  16.5 0.1 collective-permute-start.5
  16.6 1.2 %collective-permute-done.5 = f32[64,256]{1,0:T(8,128)S(1)} collective-permute-done((f32[64,256]{1,0:T(8,128)S(1)}, f32[64,256]{1,0:T(8,128)S(1)}, u32[]{:S(2)}, u32[]{:S(2)}) %collective-permute-start.5) | collective-permute-done | bytes 65568 | tf_op jit(solution)/shard_map/ppermute | solution.py:256
  17.9 0.7 %collective-permute-start.7 = (f32[64,256]{1,0:T(8,128)S(1)}, f32[64,256]{1,0:T(8,128)S(1)}, u32[]{:S(2)}, u32[]{:S(2)}) collective-permute-start(f32[64,256]{1,0:T(8,128)S(1)} %add.9), channel_id=1, source_target_pairs={{4,28},{12,20},{20,12},{28,4},{5,29},{13,21},{21,13},{29,5},{6,30}... | collective-permute-start | bytes 196616 | tf_op jit(solution)/shard_map/ppermute | solution.py:265
  18.5 1.8 %collective-permute-start.6 = (f32[64,256]{1,0:T(8,128)S(1)}, f32[64,256]{1,0:T(8,128)S(1)}, u32[]{:S(2)}, u32[]{:S(2)}) collective-permute-start(f32[64,256]{1,0:T(8,128)S(1)} %add.9), channel_id=1, source_target_pairs={{0,8},{4,20},{8,0},{12,28},{16,24},{20,4},{24,16},{28,12},{1,9},{5... | collective-permute-start | bytes 196616 | tf_op jit(solution)/shard_map/ppermute | solution.py:264
  20.4 0.0 collective-permute-done.7
  20.4 2.5 %collective-permute-done.6 = f32[64,256]{1,0:T(8,128)S(1)} collective-permute-done((f32[64,256]{1,0:T(8,128)S(1)}, f32[64,256]{1,0:T(8,128)S(1)}, u32[]{:S(2)}, u32[]{:S(2)}) %collective-permute-start.6) | collective-permute-done | bytes 65568 | tf_op jit(solution)/shard_map/ppermute | solution.py:264
  22.9 2.8 %collective-permute-start.8 = (f32[64,256]{1,0:T(8,128)S(1)}, f32[64,256]{1,0:T(8,128)S(1)}, u32[]{:S(2)}, u32[]{:S(2)}) collective-permute-start(f32[64,256]{1,0:T(8,128)S(1)} %select_add_fusion), channel_id=1, source_target_pairs={{0,4},{4,0},{8,12},{12,8},{16,20},{20,16},{24,28},{28,24},{1,5},{5... | collective-permute-start | bytes 196616 | tf_op jit(solution)/shard_map/ppermute | solution.py:267
  25.6 0.9 %collective-permute-done.8 = f32[64,256]{1,0:T(8,128)S(1)} collective-permute-done((f32[64,256]{1,0:T(8,128)S(1)}, f32[64,256]{1,0:T(8,128)S(1)}, u32[]{:S(2)}, u32[]{:S(2)}) %collective-permute-start.8) | collective-permute-done | bytes 65568 | tf_op jit(solution)/shard_map/ppermute | solution.py:267
  26.5 0.6 %add.11 = f32[64,256]{1,0:T(8,128)} add(f32[64,256]{1,0:T(8,128)S(1)} %select_add_fusion, f32[64,256]{1,0:T(8,128)S(1)} %collective-permute-done.8) | non-fusion elementwise | flops 16384 | bytes 196608 | tf_op jit(solution)/shard_map/add | solution.py:267
  (8 shorter events, 0.0 us)
Async XLA Ops:
  0.0 12.5 %collective-permute-start.1 = (bf16[1,1,3,4,4096]{4,3,2,1,0:T(4,128)(2,1)}, bf16[1,1,3,4,4096]{4,3,2,1,0:T(4,128)(2,1)S(1)}, u32[]{:S(2)}, u32[]{:S(2)}) collective-permute-start(bf16[1,1,3,4,4096]{4,3,2,1,0:T(4,128)(2,1)} %raw_hbm.1), channel_id=1, source_target_pairs={{0,2},{1,3},{2,0},{3,1},{4,6},{5,7},{6,4},{7,5},{8,10},{9,11},{10,... | collective-permute-start | bytes 294920 | tf_op jit(solution)/shard_map/ppermute | solution.py:207
  5.9 6.6 %collective-permute-start = (bf16[80,128]{1,0:T(8,128)(2,1)S(1)}, bf16[80,128]{1,0:T(8,128)(2,1)S(1)}, u32[]{:S(2)}, u32[]{:S(2)}) collective-permute-start(bf16[80,128]{1,0:T(8,128)(2,1)S(1)} %get-tuple-element.11), channel_id=1, source_target_pairs={{0,2},{1,3},{2,0},{3,1},{4,6},{5,7},{6,4},{7,5},{8,10},{9,11},{10,... | collective-permute-start | bytes 61448 | tf_op jit(solution)/shard_map/ppermute | solution.py:208
  5.9 7.3 %collective-permute-start.2 = (bf16[528,128]{1,0:T(8,128)(2,1)S(1)}, bf16[528,128]{1,0:T(8,128)(2,1)S(1)}, u32[]{:S(2)}, u32[]{:S(2)}) collective-permute-start(bf16[528,128]{1,0:T(8,128)(2,1)S(1)} %get-tuple-element.13.own_ref.full_ref.refs_0_), channel_id=1, source_target_pairs={{0,1},{1,0},{2,3},{3,2},{4,7},{5,6},{6,5},{7,4},{8,9},{9,8},{10,11... | collective-permute-start | bytes 405512 | tf_op jit(solution)/shard_map/ppermute | solution.py:179
  7.8 7.7 %collective-permute-start.4 = (bf16[400,128]{1,0:T(8,128)(2,1)S(1)}, bf16[400,128]{1,0:T(8,128)(2,1)S(1)}, u32[]{:S(2)}, u32[]{:S(2)}) collective-permute-start(bf16[400,128]{1,0:T(8,128)(2,1)S(1)} %lean.1), channel_id=1, source_target_pairs={{0,3},{1,2},{2,1},{3,0},{4,5},{5,4},{6,7},{7,6},{8,11},{9,10},{10,... | collective-permute-start | bytes 307208 | tf_op jit(solution)/shard_map/ppermute | solution.py:179
  12.7 1.8 %copy-start = (bf16[64,256]{1,0:T(8,128)(2,1)S(1)}, bf16[64,256]{1,0:T(8,128)(2,1)}, u32[]{:S(2)}) copy-start(bf16[64,256]{1,0:T(8,128)(2,1)} %density_ref.1) | copy-start | bytes 98308
  13.2 1.2 %collective-permute-start.3 = (bf16[192,128]{1,0:T(8,128)(2,1)S(1)}, bf16[192,128]{1,0:T(8,128)(2,1)S(1)}, u32[]{:S(2)}, u32[]{:S(2)}) collective-permute-start(bf16[192,128]{1,0:T(8,128)(2,1)S(1)} %merge.1), channel_id=1, source_target_pairs={{0,4},{4,0},{8,12},{12,8},{16,20},{20,16},{24,28},{28,24},{1,5},{5... | collective-permute-start | bytes 147464 | tf_op jit(solution)/shard_map/ppermute | solution.py:221
  16.5 1.3 %collective-permute-start.5 = (f32[64,256]{1,0:T(8,128)S(1)}, f32[64,256]{1,0:T(8,128)S(1)}, u32[]{:S(2)}, u32[]{:S(2)}) collective-permute-start(f32[64,256]{1,0:T(8,128)S(1)} %exchange.1), channel_id=1, source_target_pairs={{0,4},{4,0},{8,12},{12,8},{16,20},{20,16},{24,28},{28,24},{1,5},{5... | collective-permute-start | bytes 196616 | tf_op jit(solution)/shard_map/ppermute | solution.py:256
  17.9 2.5 %collective-permute-start.7 = (f32[64,256]{1,0:T(8,128)S(1)}, f32[64,256]{1,0:T(8,128)S(1)}, u32[]{:S(2)}, u32[]{:S(2)}) collective-permute-start(f32[64,256]{1,0:T(8,128)S(1)} %add.9), channel_id=1, source_target_pairs={{4,28},{12,20},{20,12},{28,4},{5,29},{13,21},{21,13},{29,5},{6,30}... | collective-permute-start | bytes 196616 | tf_op jit(solution)/shard_map/ppermute | solution.py:265
  18.5 4.3 %collective-permute-start.6 = (f32[64,256]{1,0:T(8,128)S(1)}, f32[64,256]{1,0:T(8,128)S(1)}, u32[]{:S(2)}, u32[]{:S(2)}) collective-permute-start(f32[64,256]{1,0:T(8,128)S(1)} %add.9), channel_id=1, source_target_pairs={{0,8},{4,20},{8,0},{12,28},{16,24},{20,4},{24,16},{28,12},{1,9},{5... | collective-permute-start | bytes 196616 | tf_op jit(solution)/shard_map/ppermute | solution.py:264
  22.9 3.7 %collective-permute-start.8 = (f32[64,256]{1,0:T(8,128)S(1)}, f32[64,256]{1,0:T(8,128)S(1)}, u32[]{:S(2)}, u32[]{:S(2)}) collective-permute-start(f32[64,256]{1,0:T(8,128)S(1)} %select_add_fusion), channel_id=1, source_target_pairs={{0,4},{4,0},{8,12},{12,8},{16,20},{20,16},{24,28},{28,24},{1,5},{5... | collective-permute-start | bytes 196616 | tf_op jit(solution)/shard_map/ppermute | solution.py:267

commit v18 on v5

v18 whole, which is shorter than its diff:
```python
import functools

import jax
import jax.numpy as jnp
from jax import lax
from jax.experimental import pallas as pl
from jax.experimental.pallas import tpu as pltpu
from jax.sharding import PartitionSpec as P

BS = 64
LANES = 128
NOTE = 16


def lay_blocks(raw, out_ref):
    slots, aux_width = raw.shape[:2]
    square = raw.reshape(slots * aux_width, BS, BS)
    for tile in range(slots * aux_width // 2):
        both = jnp.concatenate([square[2 * tile], square[2 * tile + 1]], axis=1)
        out_ref[tile * BS : (tile + 1) * BS] = both
    return slots * aux_width // 2


def partner(i, step, sign, orb):
    if orb == 4:
        return i ^ (3 - sign) // 2
    return (i + sign * step) % orb


def owner_of(me, step, sign, orb):
    if orb == 4:
        return me ^ jnp.where(sign > 0, 1, 2)
    return lax.rem(me - sign * step + orb, orb)


def opposite(i, orb):
    return i ^ 3 if orb == 4 else (i + orb // 2) % orb


def core_parity():
    return lax.rem(lax.axis_index("aux"), 2)


def pack_kernel(
    orb, kept, pairs_hbm, density_hbm, raw_hbm, own_ref, near_ref, pairs, rows, raw, sems
):
    copies = [
        pltpu.make_async_copy(src, dst, sems.at[i])
        for i, (src, dst) in enumerate(((raw_hbm, raw), (density_hbm, rows), (pairs_hbm, pairs)))
    ]
    for copy in copies:
        copy.start()
    for copy in copies:
        copy.wait()
    lay_blocks(raw[0, 0], own_ref)
    tiles = rows.shape[1] // LANES
    for t in range(tiles):
        near_ref[t * BS : (t + 1) * BS] = rows[:, t * LANES : (t + 1) * LANES]
    shape = (NOTE, LANES)
    lane = lax.broadcasted_iota(jnp.int32, shape, 1)
    note = jnp.zeros(shape, jnp.int32)
    for j in range(pairs.shape[2]):
        note = jnp.where(lane == j, jnp.where(j < kept[0, 0], pairs[0, 0, j], orb), note)
    near_ref[tiles * BS :] = note.astype(jnp.float32).astype(jnp.bfloat16)


def relay_kernel(raw, out_ref):
    lay_blocks(raw[0, 0], out_ref)


def join_kernel(own_ref, near_ref, met_ref, out_ref):
    size = own_ref.shape[0]
    out_ref[:size] = own_ref[...]
    out_ref[size : size + NOTE] = near_ref[near_ref.shape[0] - NOTE :]
    out_ref[size + NOTE :] = met_ref[...]


def exchange_kernel(orb, slots, aux_width, meta_ref, density_ref, own_ref, far_ref, last_ref, *refs):
    out_ref, rows, half_ref, held = refs[-4:]
    count = (len(refs) - 4) // 4
    met, swapped, first, second = (refs[i * count : (i + 1) * count] for i in range(4))
    me = lax.axis_index("orb")
    sign = 1 - 2 * core_parity()
    size = own_ref.shape[0]
    tiles = density_ref.shape[1] // LANES
    owners = [me, opposite(me, orb)]
    packs = [own_ref, far_ref]
    rows[me] = density_ref[...]
    parts = [(owners[1], last_ref, last_ref.shape[0] - tiles * BS - NOTE)]
    for i in range(count):
        owners += [owner_of(me, i + 1, sign, orb), owner_of(me, i + 1, -sign, orb)]
        packs += [first[i], second[i]]
        parts += [(owners[-2], met[i], 0), (owners[-1], swapped[i], 0)]
    for owner, part, at in parts:
        for t in range(tiles):
            rows[owner, :, t * LANES : (t + 1) * LANES] = part[at + t * BS : at + (t + 1) * BS]
    rows[orb] = jnp.zeros_like(rows[orb])
    selected = jnp.concatenate([rows[meta_ref[j]] for j in range(slots)], axis=0)
    own = jnp.concatenate([own_ref[at : at + BS] for at in range(0, size, BS)], axis=1)
    left = []
    for p in range(aux_width):
        cuts = [(j * aux_width + p) * BS for j in range(slots)]
        left.append(jnp.concatenate([own[:, cut : cut + BS] for cut in cuts], axis=1))
    left = jnp.concatenate(left, axis=0)
    half = jnp.dot(left, selected, preferred_element_type=jnp.float32).astype(jnp.bfloat16)
    for k in range(orb):
        half_ref[k] = jnp.concatenate(
            [half[p * BS : (p + 1) * BS, k * BS : (k + 1) * BS] for p in range(aux_width)],
            axis=1,
        )
    half_ref[orb] = jnp.zeros_like(half_ref[orb])
    for way in range(orb):
        codes = [meta_ref[way * slots + j] for j in range(slots)]
        held[owners[way]] = lax.dot_general(
            jnp.concatenate([half_ref[code] for code in codes], axis=1),
            jnp.concatenate([packs[way][at : at + BS] for at in range(0, size, BS)], axis=1),
            (((1,), (1,)), ((), ())),
            preferred_element_type=jnp.float32,
        )
    out_ref[...] = jnp.concatenate([held[n] for n in range(orb)], axis=1)


def shards(density, tensor_blocks, pairs, kept):
    full_width = density.shape[1]
    slots = tensor_blocks.shape[2]
    aux_width = tensor_blocks.shape[3]
    orb = lax.axis_size("orb")
    aux = lax.axis_size("aux")
    rows = full_width // LANES * BS
    size = slots * aux_width * BS // LANES * BS
    vmem = pl.BlockSpec(memory_space=pltpu.VMEM)
    smem = pl.BlockSpec(memory_space=pltpu.SMEM)
    hbm = pl.BlockSpec(memory_space=pltpu.HBM)
    params = pltpu.CompilerParams(vmem_limit_bytes=32 * 1024 * 1024)

    def array(height):
        return jax.ShapeDtypeStruct((height, LANES), jnp.bfloat16)

    def shift(x, step, sign):
        perm = [
            (a * orb + o, a * orb + partner(o, step, sign * (1 - 2 * (a % 2)), orb))
            for a in range(aux)
            for o in range(orb)
        ]
        return lax.ppermute(x, ("aux", "orb"), perm)

    own, near = pl.pallas_call(
        functools.partial(pack_kernel, orb),
        out_shape=[array(size), array(rows + NOTE)],
        in_specs=[smem, hbm, hbm, hbm],
        out_specs=[vmem] * 2,
        scratch_shapes=[
            pltpu.SMEM(pairs.shape, jnp.int32),
            pltpu.VMEM(density.shape, jnp.bfloat16),
            pltpu.VMEM(tensor_blocks.shape, jnp.bfloat16),
            pltpu.SemaphoreType.DMA((3,)),
        ],
        compiler_params=params,
        name="pack",
    )(
        kept,
        *(pltpu.with_memory_space_constraint(a, pltpu.HBM) for a in (pairs, density, tensor_blocks)),
    )
    across = [(i, opposite(i, orb)) for i in range(orb)]
    raw = lax.ppermute(tensor_blocks, "orb", across)
    steps = range(1, orb // 2)
    met = [shift(near, i, 1) for i in steps]
    first = [shift(own, i, 1) for i in steps]
    met, raw = lax.optimization_barrier((met, raw))
    second = []
    for i in steps:
        joined = pl.pallas_call(
            join_kernel,
            out_shape=array(size + NOTE + rows + NOTE),
            in_specs=[vmem] * 3,
            out_specs=vmem,
            compiler_params=params,
            name="join",
        )(own, near, met[i - 1])
        second.append(shift(joined, i, -1))
    last = second[0] if orb == 4 else lax.ppermute(near, "orb", across)
    swapped = [lax.ppermute(x, "aux", [(i, i ^ 1) for i in range(aux)]) for x in met]
    far = pl.pallas_call(
        relay_kernel,
        out_shape=array(size),
        in_specs=[vmem],
        out_specs=vmem,
        compiler_params=params,
        name="relay",
    )(raw)
    notes = [near[-NOTE], last[-NOTE]]
    for i in range(len(met)):
        notes += [met[i][-NOTE], second[i][size]]
    codes = jnp.concatenate([note[:slots] for note in notes]).astype(jnp.int32)
    parts = pl.pallas_call(
        functools.partial(exchange_kernel, orb, slots, aux_width),
        out_shape=jax.ShapeDtypeStruct((BS, full_width), jnp.float32),
        in_specs=[smem] + [vmem] * (4 + 4 * len(met)),
        out_specs=vmem,
        scratch_shapes=[
            pltpu.VMEM((orb + 1, BS, full_width), jnp.bfloat16),
            pltpu.VMEM((orb + 1, BS, aux_width * BS), jnp.bfloat16),
            pltpu.VMEM((orb, BS, BS), jnp.float32),
        ],
        compiler_params=params,
        name="exchange",
    )(codes, density, own, far, last, *met, *swapped, *first, *second)

    parts = parts + lax.ppermute(parts, "aux", [(i, i ^ 1) for i in range(aux)])
    step = 2
    while step < aux:
        ways = 2 if step * 4 > aux else 4
        terms = [parts]
        for way in range(1, ways):
            terms.append(lax.ppermute(parts, "aux", [(i, i ^ (way * step)) for i in range(aux)]))
        while len(terms) > 1:
            terms = [terms[i] + terms[i + 1] for i in range(0, len(terms), 2)]
        parts = terms[0]
        step *= ways
    return parts


def solution(mesh):
    return jax.shard_map(
        shards,
        mesh=mesh,
        in_specs=(
            P("orb", None),
            P("orb", "aux", None, None, None),
            P("orb", "aux", None),
            P("orb", "aux"),
        ),
        out_specs=P("orb", None),
        check_vma=False,
    )
```

time: 29.2 us -> 30.1 us (1.031)
  starting transfers between devices: 9.74 us -> 11.2 us
  waiting for transfers between devices: 15.5 us -> 14.6 us
    ppermute x3 -> x6, starting transfers between devices: 6.11 us -> 7.67 us  [the longest x1 5.05 us: shards(): raw = lax.ppermute(tensor_blocks, 'orb', across)]
    ppermute x3 -> x6, waiting for transfers between devices: 10.5 us -> 9.9 us  [the longest x3 8.65 us: shift(): return lax.ppermute(x, ('aux', 'orb'), perm)]
    pallas_call x1 -> x3, Pallas kernels: 1.15 us -> 1.39 us  [the longest x1 1.16 us: shards(): pl.pallas_call(functools.partial(pack_kernel, orb), out_shape=[array(size...]
    ppermute x4 -> x3, waiting for transfers between devices: 4.97 us -> 4.75 us  [shards(): lax.ppermute(parts, 'aux', [(i, i ^ way * step) for i in range(aux)])]
    ppermute x4 -> x3, starting transfers between devices: 3.62 us -> 3.55 us  [shards(): lax.ppermute(parts, 'aux', [(i, i ^ way * step) for i in range(aux)])]
    add x2 -> x1, other arithmetic: 0.66 us -> 0.65 us  [shards(): terms = [terms[i] + terms[i + 1] for i in range(0, len(terms), 2)]]
  transfers between devices with their start and end apart: 7 -> 9, of which waited for: 6 -> 6; matrix products, arithmetic and copies ran while one was open for 0% -> 0% of each run, Pallas kernels for 0% -> 5%
where the time goes in v18:
time: 30.1 us; the launch traced here: 29.9 us
  waiting for transfers between devices  14.6 us (49%)
  starting transfers between devices  11.2 us (37%)
  Pallas kernels  2.61 us (9%)
  other arithmetic  0.74 us (2%)
  between operations  0.73 us (2%)
    ppermute x3, waiting for transfers between devices, shift(): return lax.ppermute(x, ('aux', 'orb'), perm)  8.65 us
    ppermute x1, starting transfers between devices, shards(): raw = lax.ppermute(tensor_blocks, 'orb', across)  5.05 us
    ppermute x3, waiting for transfers between devices, shards(): lax.ppermute(parts, 'aux', [(i, i ^ way * step) for i in range(aux)])  4.75 us
    ppermute x3, starting transfers between devices, shards(): lax.ppermute(parts, 'aux', [(i, i ^ way * step) for i in range(aux)])  3.55 us
    ppermute x3, starting transfers between devices, shift(): return lax.ppermute(x, ('aux', 'orb'), perm)  2.47 us
    ppermute x1, waiting for transfers between devices, shards(): parts = parts + lax.ppermute(parts, 'aux', [(i, i ^ 1) for i in range(aux)])  1.24 us
    pallas_call x1, Pallas kernels, shards(): pl.pallas_call(functools.partial(exchange_kernel, orb, slots, aux_width),...  1.21 us
    pallas_call x1, Pallas kernels, shards(): pl.pallas_call(functools.partial(pack_kernel, orb), out_shape=[array(size...  1.16 us
  transfers between devices with their start and end apart: 9, of which 6 were waited for; matrix products, arithmetic and copies ran while one was open for 0% of the time, Pallas kernels for 5%

profile of v18, /device:TPU:0, one launch (start us, length us, event | category | flops | bytes accessed | tf_op | source)
XLA Modules:
  0.0 29.9 jit_solution(17866610825754269021)
XLA Ops:
  0.0 5.0 %collective-permute-start.1 = (bf16[1,1,3,4,4096]{4,3,2,1,0:T(4,128)(2,1)}, bf16[1,1,3,4,4096]{4,3,2,1,0:T(4,128)(2,1)S(1)}, u32[]{:S(2)}, u32[]{:S(2)}) collective-permute-start(bf16[1,1,3,4,4096]{4,3,2,1,0:T(4,128)(2,1)} %raw_hbm.1), channel_id=1, source_target_pairs={{0,3},{1,2},{2,1},{3,0},{4,7},{5,6},{6,5},{7,4},{8,11},{9,10},{10,... | collective-permute-start | bytes 294920 | tf_op jit(solution)/shard_map/ppermute | solution.py:165
  5.7 1.2 %pack.1 = (bf16[384,128]{1,0:T(8,128)(2,1)S(1)}, bf16[144,128]{1,0:T(8,128)(2,1)S(1)}) custom-call(s32[1,1]{1,0:T(1,128)S(6)} %copy.5.kept, s32[1,1,3]{2,1,0:T(1,128)} %pairs_hbm.1, bf16[64,256]{1,0:T(8,128)(2,1)} %density_ref.1, bf16[1,1,3,4,4096]{4,3,2,1,0:T(4,128)(2,1)} %raw_hbm.1), custom_call_target="tpu_custom_call" | custom-call | tf_op jit(solution)/shard_map/pack/pallas_call | solution.py:147
  6.9 0.1 collective-permute-start
  6.9 2.0 %collective-permute-start.4 = (bf16[384,128]{1,0:T(8,128)(2,1)S(1)}, bf16[384,128]{1,0:T(8,128)(2,1)S(1)}, u32[]{:S(2)}, u32[]{:S(2)}) collective-permute-start(bf16[384,128]{1,0:T(8,128)(2,1)S(1)} %get-tuple-element.10.own_ref), channel_id=1, source_target_pairs={{0,1},{1,0},{2,3},{3,2},{4,6},{5,7},{6,4},{7,5},{8,9},{9,8},{10,11... | collective-permute-start | bytes 294920 | tf_op jit(solution)/shard_map/ppermute | solution.py:145
  9.0 2.2 %collective-permute-done.met_ref.refs_0_ = bf16[144,128]{1,0:T(8,128)(2,1)S(1)} collective-permute-done((bf16[144,128]{1,0:T(8,128)(2,1)S(1)}, bf16[144,128]{1,0:T(8,128)(2,1)S(1)}, u32[]{:S(2)}, u32[]{:S(2)}) %collective-permute-start) | collective-permute-done | bytes 36896 | tf_op jit(solution)/shard_map/ppermute | solution.py:145
  11.1 0.0 collective-permute-done.1.raw
  11.2 0.1 collective-permute-start.3
  11.2 0.4 %collective-permute-start.2 = (bf16[544,128]{1,0:T(8,128)(2,1)S(1)}, bf16[544,128]{1,0:T(8,128)(2,1)S(1)}, u32[]{:S(2)}, u32[]{:S(2)}) collective-permute-start(bf16[544,128]{1,0:T(8,128)(2,1)S(1)} %join.1), channel_id=1, source_target_pairs={{0,2},{1,3},{2,0},{3,1},{4,5},{5,4},{6,7},{7,6},{8,10},{9,11},{10,... | collective-permute-start | bytes 417800 | tf_op jit(solution)/shard_map/ppermute | solution.py:145
  11.6 0.0 copy-start
  11.6 0.2 relay.1.far_ref
  11.9 6.5 %collective-permute-done.2.last_ref.refs_3_ = bf16[544,128]{1,0:T(8,128)(2,1)S(1)} collective-permute-done((bf16[544,128]{1,0:T(8,128)(2,1)S(1)}, bf16[544,128]{1,0:T(8,128)(2,1)S(1)}, u32[]{:S(2)}, u32[]{:S(2)}) %collective-permute-start.2) | collective-permute-done | bytes 139296 | tf_op jit(solution)/shard_map/ppermute | solution.py:145
  18.3 0.1 maximum_convert_fusion.meta_ref
  18.4 0.0 collective-permute-done.4.refs_2_
  18.4 0.0 collective-permute-done.3.refs_1_
  18.4 0.0 copy-done
  18.4 1.2 %exchange.1 = f32[64,256]{1,0:T(8,128)S(1)} custom-call(s32[12]{0:T(128)S(1)} %maximum_convert_fusion.meta_ref, bf16[64,256]{1,0:T(8,128)(2,1)S(1)} %copy-done, bf16[384,128]{1,0:T(8,128)(2,1)S(1)} %get-tuple-element.10.own_ref, bf16[384,128]{1,0:T(8,128)(2,1)S(1)} %relay.1.far_ref, bf16[544,128]{1,0:T(8,128)(2,1)S(1)} %collective-permute-done.2.last_ref.refs_3_, ...), custom_call_target="tpu_custom_call" | custom-call | tf_op jit(solution)/shard_map/exchange/pallas_call | solution.py:195
  19.7 0.1 collective-permute-start.5
  19.7 1.2 %collective-permute-done.5 = f32[64,256]{1,0:T(8,128)S(1)} collective-permute-done((f32[64,256]{1,0:T(8,128)S(1)}, f32[64,256]{1,0:T(8,128)S(1)}, u32[]{:S(2)}, u32[]{:S(2)}) %collective-permute-start.5) | collective-permute-done | bytes 65568 | tf_op jit(solution)/shard_map/ppermute | solution.py:209
  21.0 1.6 %collective-permute-start.6 = (f32[64,256]{1,0:T(8,128)S(1)}, f32[64,256]{1,0:T(8,128)S(1)}, u32[]{:S(2)}, u32[]{:S(2)}) collective-permute-start(f32[64,256]{1,0:T(8,128)S(1)} %add.12), channel_id=1, source_target_pairs={{0,8},{4,12},{8,0},{12,4},{16,24},{20,28},{24,16},{28,20},{1,9},{5... | collective-permute-start | bytes 196616 | tf_op jit(solution)/shard_map/ppermute | solution.py:215
  22.6 1.5 %collective-permute-start.7 = (f32[64,256]{1,0:T(8,128)S(1)}, f32[64,256]{1,0:T(8,128)S(1)}, u32[]{:S(2)}, u32[]{:S(2)}) collective-permute-start(f32[64,256]{1,0:T(8,128)S(1)} %add.12), channel_id=1, source_target_pairs={{0,16},{4,20},{8,24},{12,28},{16,0},{20,4},{24,8},{28,12},{1,17},{... | collective-permute-start | bytes 196616 | tf_op jit(solution)/shard_map/ppermute | solution.py:215
  24.1 0.4 %collective-permute-start.8 = (f32[64,256]{1,0:T(8,128)S(1)}, f32[64,256]{1,0:T(8,128)S(1)}, u32[]{:S(2)}, u32[]{:S(2)}) collective-permute-start(f32[64,256]{1,0:T(8,128)S(1)} %add.12), channel_id=1, source_target_pairs={{0,24},{4,28},{8,16},{12,20},{16,8},{20,12},{24,0},{28,4},{1,25},{... | collective-permute-start | bytes 196616 | tf_op jit(solution)/shard_map/ppermute | solution.py:215
  24.6 0.8 %collective-permute-done.6 = f32[64,256]{1,0:T(8,128)S(1)} collective-permute-done((f32[64,256]{1,0:T(8,128)S(1)}, f32[64,256]{1,0:T(8,128)S(1)}, u32[]{:S(2)}, u32[]{:S(2)}) %collective-permute-start.6) | collective-permute-done | bytes 65568 | tf_op jit(solution)/shard_map/ppermute | solution.py:215
  25.3 1.6 %collective-permute-done.7 = f32[64,256]{1,0:T(8,128)S(1)} collective-permute-done((f32[64,256]{1,0:T(8,128)S(1)}, f32[64,256]{1,0:T(8,128)S(1)}, u32[]{:S(2)}, u32[]{:S(2)}) %collective-permute-start.7) | collective-permute-done | bytes 65568 | tf_op jit(solution)/shard_map/ppermute | solution.py:215
  26.9 2.4 %collective-permute-done.8 = f32[64,256]{1,0:T(8,128)S(1)} collective-permute-done((f32[64,256]{1,0:T(8,128)S(1)}, f32[64,256]{1,0:T(8,128)S(1)}, u32[]{:S(2)}, u32[]{:S(2)}) %collective-permute-start.8) | collective-permute-done | bytes 65568 | tf_op jit(solution)/shard_map/ppermute | solution.py:215
  29.3 0.6 %add_add_fusion = f32[64,256]{1,0:T(8,128)} fusion(f32[64,256]{1,0:T(8,128)S(1)} %collective-permute-done.7, f32[64,256]{1,0:T(8,128)S(1)} %collective-permute-done.8, f32[64,256]{1,0:T(8,128)S(1)} %add.12, f32[64,256]{1,0:T(8,128)S(1)} %collective-permute-done.6), kind=kLoop, calls=%fused_computation | loop fusion | flops 49152 | bytes 327680 | tf_op jit(solution)/shard_map/add | solution.py:217
  (5 shorter events, 0.0 us)
Async XLA Ops:
  0.0 11.1 %collective-permute-start.1 = (bf16[1,1,3,4,4096]{4,3,2,1,0:T(4,128)(2,1)}, bf16[1,1,3,4,4096]{4,3,2,1,0:T(4,128)(2,1)S(1)}, u32[]{:S(2)}, u32[]{:S(2)}) collective-permute-start(bf16[1,1,3,4,4096]{4,3,2,1,0:T(4,128)(2,1)} %raw_hbm.1), channel_id=1, source_target_pairs={{0,3},{1,2},{2,1},{3,0},{4,7},{5,6},{6,5},{7,4},{8,11},{9,10},{10,... | collective-permute-start | bytes 294920 | tf_op jit(solution)/shard_map/ppermute | solution.py:165
  6.9 4.3 %collective-permute-start = (bf16[144,128]{1,0:T(8,128)(2,1)S(1)}, bf16[144,128]{1,0:T(8,128)(2,1)S(1)}, u32[]{:S(2)}, u32[]{:S(2)}) collective-permute-start(bf16[144,128]{1,0:T(8,128)(2,1)S(1)} %get-tuple-element.9.near_ref), channel_id=1, source_target_pairs={{0,1},{1,0},{2,3},{3,2},{4,6},{5,7},{6,4},{7,5},{8,9},{9,8},{10,11... | collective-permute-start | bytes 110600 | tf_op jit(solution)/shard_map/ppermute | solution.py:145
  6.9 11.5 %collective-permute-start.4 = (bf16[384,128]{1,0:T(8,128)(2,1)S(1)}, bf16[384,128]{1,0:T(8,128)(2,1)S(1)}, u32[]{:S(2)}, u32[]{:S(2)}) collective-permute-start(bf16[384,128]{1,0:T(8,128)(2,1)S(1)} %get-tuple-element.10.own_ref), channel_id=1, source_target_pairs={{0,1},{1,0},{2,3},{3,2},{4,6},{5,7},{6,4},{7,5},{8,9},{9,8},{10,11... | collective-permute-start | bytes 294920 | tf_op jit(solution)/shard_map/ppermute | solution.py:145
  11.2 7.3 %collective-permute-start.3 = (bf16[144,128]{1,0:T(8,128)(2,1)S(1)}, bf16[144,128]{1,0:T(8,128)(2,1)S(1)}, u32[]{:S(2)}, u32[]{:S(2)}) collective-permute-start(bf16[144,128]{1,0:T(8,128)(2,1)S(1)} %collective-permute-done.met_ref.refs_0_), channel_id=1, source_target_pairs={{0,4},{4,0},{8,12},{12,8},{16,20},{20,16},{24,28},{28,24},{1,5},{5... | collective-permute-start | bytes 110600 | tf_op jit(solution)/shard_map/ppermute | solution.py:182
  11.2 7.1 %collective-permute-start.2 = (bf16[544,128]{1,0:T(8,128)(2,1)S(1)}, bf16[544,128]{1,0:T(8,128)(2,1)S(1)}, u32[]{:S(2)}, u32[]{:S(2)}) collective-permute-start(bf16[544,128]{1,0:T(8,128)(2,1)S(1)} %join.1), channel_id=1, source_target_pairs={{0,2},{1,3},{2,0},{3,1},{4,5},{5,4},{6,7},{7,6},{8,10},{9,11},{10,... | collective-permute-start | bytes 417800 | tf_op jit(solution)/shard_map/ppermute | solution.py:145
  11.6 6.8 %copy-start = (bf16[64,256]{1,0:T(8,128)(2,1)S(1)}, bf16[64,256]{1,0:T(8,128)(2,1)}, u32[]{:S(2)}) copy-start(bf16[64,256]{1,0:T(8,128)(2,1)} %density_ref.1) | copy-start | bytes 98308
  19.7 1.3 %collective-permute-start.5 = (f32[64,256]{1,0:T(8,128)S(1)}, f32[64,256]{1,0:T(8,128)S(1)}, u32[]{:S(2)}, u32[]{:S(2)}) collective-permute-start(f32[64,256]{1,0:T(8,128)S(1)} %exchange.1), channel_id=1, source_target_pairs={{0,4},{4,0},{8,12},{12,8},{16,20},{20,16},{24,28},{28,24},{1,5},{5... | collective-permute-start | bytes 196616 | tf_op jit(solution)/shard_map/ppermute | solution.py:209
  21.0 4.3 %collective-permute-start.6 = (f32[64,256]{1,0:T(8,128)S(1)}, f32[64,256]{1,0:T(8,128)S(1)}, u32[]{:S(2)}, u32[]{:S(2)}) collective-permute-start(f32[64,256]{1,0:T(8,128)S(1)} %add.12), channel_id=1, source_target_pairs={{0,8},{4,12},{8,0},{12,4},{16,24},{20,28},{24,16},{28,20},{1,9},{5... | collective-permute-start | bytes 196616 | tf_op jit(solution)/shard_map/ppermute | solution.py:215
  22.6 4.3 %collective-permute-start.7 = (f32[64,256]{1,0:T(8,128)S(1)}, f32[64,256]{1,0:T(8,128)S(1)}, u32[]{:S(2)}, u32[]{:S(2)}) collective-permute-start(f32[64,256]{1,0:T(8,128)S(1)} %add.12), channel_id=1, source_target_pairs={{0,16},{4,20},{8,24},{12,28},{16,0},{20,4},{24,8},{28,12},{1,17},{... | collective-permute-start | bytes 196616 | tf_op jit(solution)/shard_map/ppermute | solution.py:215
  24.1 5.2 %collective-permute-start.8 = (f32[64,256]{1,0:T(8,128)S(1)}, f32[64,256]{1,0:T(8,128)S(1)}, u32[]{:S(2)}, u32[]{:S(2)}) collective-permute-start(f32[64,256]{1,0:T(8,128)S(1)} %add.12), channel_id=1, source_target_pairs={{0,24},{4,28},{8,16},{12,20},{16,8},{20,12},{24,0},{28,4},{1,25},{... | collective-permute-start | bytes 196616 | tf_op jit(solution)/shard_map/ppermute | solution.py:215

commit v19 on v12

--- a/solution.py
+++ b/solution.py
@@ -23,14 +23,18 @@
 
 def partner(i, step, sign, orb):
     if orb == 4:
-        return i ^ (2 - sign)
+        return i ^ (3 - sign) // 2
     return (i + sign * step) % orb
 
 
 def owner_of(me, step, sign, orb):
     if orb == 4:
-        return me ^ (2 - sign)
+        return me ^ jnp.where(sign > 0, 1, 2)
     return lax.rem(me - sign * step + orb, orb)
+
+
+def opposite(i, orb):
+    return i ^ 3 if orb == 4 else (i + orb // 2) % orb
 
 
 def core_parity():
@@ -105,7 +109,7 @@
             at = (i * count + t) * BS
             rows[ahead, :, lanes] = full[size + t * BS : size + (t + 1) * BS]
             rows[behind, :, lanes] = swapped[at : at + BS]
-    across = lax.rem(me + orb // 2, orb)
+    across = opposite(me, orb)
     for t in range(count):
         lanes = slice(t * LANES, (t + 1) * LANES)
         at = len(fulls) * count * BS + t * height
@@ -134,7 +138,7 @@
     parity = core_parity()
     per_slot = aux_width * BS // LANES
     sign = 1 - 2 * parity
-    owners = [me, lax.rem(me + orb // 2, orb)]
+    owners = [me, opposite(me, orb)]
     for i in range(1, orb // 2):
         owners += [owner_of(me, i, sign, orb), owner_of(me, i, -sign, orb)]
     for way in range(orb):
@@ -203,7 +207,7 @@
         compiler_params=params,
         name="lean",
     )(full)
-    across = [(i, (i + orb // 2) % orb) for i in range(orb)]
+    across = [(i, opposite(i, orb)) for i in range(orb)]
     raw = lax.ppermute(tensor_blocks, "orb", across)
     tail_in = lax.ppermute(tail, "orb", across)
     fulls = [shift(full, i, 1) for i in range(1, orb // 2)]

time: 26.2 us -> 28.1 us (1.073)
  starting transfers between devices: 12.2 us -> 13.3 us
  waiting for transfers between devices: 9.3 us -> 9.97 us
    ppermute x2, waiting for transfers between devices: 0.76 us -> 2.5 us  [shift(): return lax.ppermute(x, ('aux', 'orb'), perm)]
    ppermute x1, starting transfers between devices: 4.04 us -> 5.05 us  [shards(): raw = lax.ppermute(tensor_blocks, 'orb', across)]
    ppermute x1, waiting for transfers between devices: 2.07 us -> 1.44 us  [shards(): tail_in = lax.ppermute(tail, 'orb', across)]
    ppermute x4, waiting for transfers between devices: 5.25 us -> 4.82 us  [shards(): lax.ppermute(parts, 'aux', [(i, i ^ way * step) for i in range(aux)])]
  transfers between devices with their start and end apart: 9 -> 9, of which waited for: 8 -> 7; matrix products, arithmetic and copies ran while one was open for 0% -> 0% of each run, Pallas kernels for 9% -> 8%
where the time goes in v19:
time: 28.1 us; the launch traced here: 27.9 us
  starting transfers between devices  13.3 us (47%)
  waiting for transfers between devices  9.97 us (35%)
  Pallas kernels  3.11 us (11%)
  between operations  0.76 us (3%)
  other arithmetic  0.74 us (3%)
    ppermute x1, starting transfers between devices, shards(): raw = lax.ppermute(tensor_blocks, 'orb', across)  5.05 us
    ppermute x4, waiting for transfers between devices, shards(): lax.ppermute(parts, 'aux', [(i, i ^ way * step) for i in range(aux)])  4.82 us
    ppermute x2, starting transfers between devices, shift(): return lax.ppermute(x, ('aux', 'orb'), perm)  4.43 us
    ppermute x4, starting transfers between devices, shards(): lax.ppermute(parts, 'aux', [(i, i ^ way * step) for i in range(aux)])  3.78 us
    ppermute x2, waiting for transfers between devices, shift(): return lax.ppermute(x, ('aux', 'orb'), perm)  2.5 us
    ppermute x1, waiting for transfers between devices, shards(): tail_in = lax.ppermute(tail, 'orb', across)  1.44 us
    ppermute x1, waiting for transfers between devices, shards(): swapped = lax.ppermute(merged, 'aux', [(i, i ^ 1) for i in range(aux)])  1.21 us
    pallas_call x1, Pallas kernels, shards(): pl.pallas_call(functools.partial(pack_kernel, orb), out_shape=[array(size...  1.16 us
  transfers between devices with their start and end apart: 9, of which 7 were waited for; matrix products, arithmetic and copies ran while one was open for 0% of the time, Pallas kernels for 8%

profile of v19, /device:TPU:0, one launch (start us, length us, event | category | flops | bytes accessed | tf_op | source)
XLA Modules:
  0.0 27.9 jit_solution(140880915612611216)
XLA Ops:
  0.0 5.0 %collective-permute-start.1 = (bf16[1,1,3,4,4096]{4,3,2,1,0:T(4,128)(2,1)}, bf16[1,1,3,4,4096]{4,3,2,1,0:T(4,128)(2,1)S(1)}, u32[]{:S(2)}, u32[]{:S(2)}) collective-permute-start(bf16[1,1,3,4,4096]{4,3,2,1,0:T(4,128)(2,1)} %raw_hbm.1), channel_id=1, source_target_pairs={{0,3},{1,2},{2,1},{3,0},{4,7},{5,6},{6,5},{7,4},{8,11},{9,10},{10,... | collective-permute-start | bytes 294920 | tf_op jit(solution)/shard_map/ppermute | solution.py:211
  5.7 1.2 %pack.1 = (bf16[528,128]{1,0:T(8,128)(2,1)S(1)}, bf16[80,128]{1,0:T(8,128)(2,1)S(1)}) custom-call(s32[1,1]{1,0:T(1,128)S(6)} %copy.5.kept, s32[1,1,3]{2,1,0:T(1,128)} %pairs_hbm.1, bf16[64,256]{1,0:T(8,128)(2,1)} %density_ref.1, bf16[1,1,3,4,4096]{4,3,2,1,0:T(4,128)(2,1)} %raw_hbm.1), custom_call_target="tpu_custom_call" | custom-call | tf_op jit(solution)/shard_map/pack/pallas_call | solution.py:185
  6.9 0.1 collective-permute-start
  6.9 0.1 collective-permute-start.2
  7.0 4.4 %collective-permute-start.4 = (bf16[400,128]{1,0:T(8,128)(2,1)S(1)}, bf16[400,128]{1,0:T(8,128)(2,1)S(1)}, u32[]{:S(2)}, u32[]{:S(2)}) collective-permute-start(bf16[400,128]{1,0:T(8,128)(2,1)S(1)} %lean.1), channel_id=1, source_target_pairs={{0,2},{1,3},{2,0},{3,1},{4,5},{5,4},{6,7},{7,6},{8,10},{9,11},{10,... | collective-permute-start | bytes 307208 | tf_op jit(solution)/shard_map/ppermute | solution.py:183
  11.4 1.4 %collective-permute-done.refs_1_ = bf16[80,128]{1,0:T(8,128)(2,1)S(1)} collective-permute-done((bf16[80,128]{1,0:T(8,128)(2,1)S(1)}, bf16[80,128]{1,0:T(8,128)(2,1)S(1)}, u32[]{:S(2)}, u32[]{:S(2)}) %collective-permute-start) | collective-permute-done | bytes 20512 | tf_op jit(solution)/shard_map/ppermute | solution.py:212
  12.8 0.0 collective-permute-done.1.raw
  12.8 0.2 relay.1.refs_1_
  13.1 0.0 copy-start
  13.1 2.5 %collective-permute-done.2.refs_0_.refs_2_ = bf16[528,128]{1,0:T(8,128)(2,1)S(1)} collective-permute-done((bf16[528,128]{1,0:T(8,128)(2,1)S(1)}, bf16[528,128]{1,0:T(8,128)(2,1)S(1)}, u32[]{:S(2)}, u32[]{:S(2)}) %collective-permute-start.2) | collective-permute-done | bytes 135200 | tf_op jit(solution)/shard_map/ppermute | solution.py:183
  15.6 0.0 collective-permute-start.3
  15.6 1.2 %collective-permute-done.3.refs_2_ = bf16[192,128]{1,0:T(8,128)(2,1)S(1)} collective-permute-done((bf16[192,128]{1,0:T(8,128)(2,1)S(1)}, bf16[192,128]{1,0:T(8,128)(2,1)S(1)}, u32[]{:S(2)}, u32[]{:S(2)}) %collective-permute-start.3) | collective-permute-done | bytes 49184 | tf_op jit(solution)/shard_map/ppermute | solution.py:225
  16.8 0.0 copy-done
  16.8 0.8 %half.1.half_ref = bf16[5,64,256]{2,1,0:T(8,128)(2,1)S(1)} custom-call(s32[3]{0:T(128)S(1)} %get-tuple-element.18.meta_ref, bf16[64,256]{1,0:T(8,128)(2,1)S(1)} %copy-done, bf16[528,128]{1,0:T(8,128)(2,1)S(1)} %get-tuple-element.13.own_ref.full_ref.refs_0_, bf16[528,128]{1,0:T(8,128)(2,1)S(1)} %collective-permute-done.2.refs_0_.refs_2_, ...), custom_call_target="tpu_custom_call" | custom-call | tf_op jit(solution)/shard_map/half/pallas_call | solution.py:234
  17.7 0.0 collective-permute-done.4.refs_3_
  17.7 0.1 maximum_convert_fusion.meta_ref
  17.8 0.9 %exchange.1 = f32[64,256]{1,0:T(8,128)S(1)} custom-call(s32[12]{0:T(128)S(1)} %maximum_convert_fusion.meta_ref, bf16[5,64,256]{2,1,0:T(8,128)(2,1)S(1)} %half.1.half_ref, bf16[528,128]{1,0:T(8,128)(2,1)S(1)} %get-tuple-element.13.own_ref.full_ref.refs_0_, bf16[384,128]{1,0:T(8,128)(2,1)S(1)} %relay.1.refs_1_, ...), custom_call_target="tpu_custom_call" | custom-call | tf_op jit(solution)/shard_map/exchange/pallas_call | solution.py:249
  18.7 0.2 collective-permute-start.5
  18.9 1.1 %collective-permute-done.5 = f32[64,256]{1,0:T(8,128)S(1)} collective-permute-done((f32[64,256]{1,0:T(8,128)S(1)}, f32[64,256]{1,0:T(8,128)S(1)}, u32[]{:S(2)}, u32[]{:S(2)}) %collective-permute-start.5) | collective-permute-done | bytes 65568 | tf_op jit(solution)/shard_map/ppermute | solution.py:264
  20.0 2.5 %collective-permute-start.8 = (f32[64,256]{1,0:T(8,128)S(1)}, f32[64,256]{1,0:T(8,128)S(1)}, u32[]{:S(2)}, u32[]{:S(2)}) collective-permute-start(f32[64,256]{1,0:T(8,128)S(1)} %add.12), channel_id=1, source_target_pairs={{0,24},{4,28},{8,16},{12,20},{16,8},{20,12},{24,0},{28,4},{1,25},{... | collective-permute-start | bytes 196616 | tf_op jit(solution)/shard_map/ppermute | solution.py:264
  22.5 0.5 %collective-permute-start.7 = (f32[64,256]{1,0:T(8,128)S(1)}, f32[64,256]{1,0:T(8,128)S(1)}, u32[]{:S(2)}, u32[]{:S(2)}) collective-permute-start(f32[64,256]{1,0:T(8,128)S(1)} %add.12), channel_id=1, source_target_pairs={{0,16},{4,20},{8,24},{12,28},{16,0},{20,4},{24,8},{28,12},{1,17},{... | collective-permute-start | bytes 196616 | tf_op jit(solution)/shard_map/ppermute | solution.py:264
  23.0 0.5 %collective-permute-start.6 = (f32[64,256]{1,0:T(8,128)S(1)}, f32[64,256]{1,0:T(8,128)S(1)}, u32[]{:S(2)}, u32[]{:S(2)}) collective-permute-start(f32[64,256]{1,0:T(8,128)S(1)} %add.12), channel_id=1, source_target_pairs={{0,8},{4,12},{8,0},{12,4},{16,24},{20,28},{24,16},{28,20},{1,9},{5... | collective-permute-start | bytes 196616 | tf_op jit(solution)/shard_map/ppermute | solution.py:264
  23.5 1.7 %collective-permute-done.8 = f32[64,256]{1,0:T(8,128)S(1)} collective-permute-done((f32[64,256]{1,0:T(8,128)S(1)}, f32[64,256]{1,0:T(8,128)S(1)}, u32[]{:S(2)}, u32[]{:S(2)}) %collective-permute-start.8) | collective-permute-done | bytes 65568 | tf_op jit(solution)/shard_map/ppermute | solution.py:264
  25.2 1.5 %collective-permute-done.7 = f32[64,256]{1,0:T(8,128)S(1)} collective-permute-done((f32[64,256]{1,0:T(8,128)S(1)}, f32[64,256]{1,0:T(8,128)S(1)}, u32[]{:S(2)}, u32[]{:S(2)}) %collective-permute-start.7) | collective-permute-done | bytes 65568 | tf_op jit(solution)/shard_map/ppermute | solution.py:264
  26.8 0.5 %collective-permute-done.6 = f32[64,256]{1,0:T(8,128)S(1)} collective-permute-done((f32[64,256]{1,0:T(8,128)S(1)}, f32[64,256]{1,0:T(8,128)S(1)}, u32[]{:S(2)}, u32[]{:S(2)}) %collective-permute-start.6) | collective-permute-done | bytes 65568 | tf_op jit(solution)/shard_map/ppermute | solution.py:264
  27.3 0.6 %add_add_fusion = f32[64,256]{1,0:T(8,128)} fusion(f32[64,256]{1,0:T(8,128)S(1)} %collective-permute-done.7, f32[64,256]{1,0:T(8,128)S(1)} %collective-permute-done.8, f32[64,256]{1,0:T(8,128)S(1)} %add.12, f32[64,256]{1,0:T(8,128)S(1)} %collective-permute-done.6), kind=kLoop, calls=%fused_computation | loop fusion | flops 49152 | bytes 327680 | tf_op jit(solution)/shard_map/add | solution.py:266
  (7 shorter events, 0.0 us)
Async XLA Ops:
  0.0 12.8 %collective-permute-start.1 = (bf16[1,1,3,4,4096]{4,3,2,1,0:T(4,128)(2,1)}, bf16[1,1,3,4,4096]{4,3,2,1,0:T(4,128)(2,1)S(1)}, u32[]{:S(2)}, u32[]{:S(2)}) collective-permute-start(bf16[1,1,3,4,4096]{4,3,2,1,0:T(4,128)(2,1)} %raw_hbm.1), channel_id=1, source_target_pairs={{0,3},{1,2},{2,1},{3,0},{4,7},{5,6},{6,5},{7,4},{8,11},{9,10},{10,... | collective-permute-start | bytes 294920 | tf_op jit(solution)/shard_map/ppermute | solution.py:211
  6.9 6.0 %collective-permute-start = (bf16[80,128]{1,0:T(8,128)(2,1)S(1)}, bf16[80,128]{1,0:T(8,128)(2,1)S(1)}, u32[]{:S(2)}, u32[]{:S(2)}) collective-permute-start(bf16[80,128]{1,0:T(8,128)(2,1)S(1)} %get-tuple-element.11), channel_id=1, source_target_pairs={{0,3},{1,2},{2,1},{3,0},{4,7},{5,6},{6,5},{7,4},{8,11},{9,10},{10,... | collective-permute-start | bytes 61448 | tf_op jit(solution)/shard_map/ppermute | solution.py:212
  6.9 8.6 %collective-permute-start.2 = (bf16[528,128]{1,0:T(8,128)(2,1)S(1)}, bf16[528,128]{1,0:T(8,128)(2,1)S(1)}, u32[]{:S(2)}, u32[]{:S(2)}) collective-permute-start(bf16[528,128]{1,0:T(8,128)(2,1)S(1)} %get-tuple-element.13.own_ref.full_ref.refs_0_), channel_id=1, source_target_pairs={{0,1},{1,0},{2,3},{3,2},{4,6},{5,7},{6,4},{7,5},{8,9},{9,8},{10,11... | collective-permute-start | bytes 405512 | tf_op jit(solution)/shard_map/ppermute | solution.py:183
  7.0 10.6 %collective-permute-start.4 = (bf16[400,128]{1,0:T(8,128)(2,1)S(1)}, bf16[400,128]{1,0:T(8,128)(2,1)S(1)}, u32[]{:S(2)}, u32[]{:S(2)}) collective-permute-start(bf16[400,128]{1,0:T(8,128)(2,1)S(1)} %lean.1), channel_id=1, source_target_pairs={{0,2},{1,3},{2,0},{3,1},{4,5},{5,4},{6,7},{7,6},{8,10},{9,11},{10,... | collective-permute-start | bytes 307208 | tf_op jit(solution)/shard_map/ppermute | solution.py:183
  13.1 3.7 %copy-start = (bf16[64,256]{1,0:T(8,128)(2,1)S(1)}, bf16[64,256]{1,0:T(8,128)(2,1)}, u32[]{:S(2)}) copy-start(bf16[64,256]{1,0:T(8,128)(2,1)} %density_ref.1) | copy-start | bytes 98308
  15.6 1.2 %collective-permute-start.3 = (bf16[192,128]{1,0:T(8,128)(2,1)S(1)}, bf16[192,128]{1,0:T(8,128)(2,1)S(1)}, u32[]{:S(2)}, u32[]{:S(2)}) collective-permute-start(bf16[192,128]{1,0:T(8,128)(2,1)S(1)} %merge.1), channel_id=1, source_target_pairs={{0,4},{4,0},{8,12},{12,8},{16,20},{20,16},{24,28},{28,24},{1,5},{5... | collective-permute-start | bytes 147464 | tf_op jit(solution)/shard_map/ppermute | solution.py:225
  18.7 1.3 %collective-permute-start.5 = (f32[64,256]{1,0:T(8,128)S(1)}, f32[64,256]{1,0:T(8,128)S(1)}, u32[]{:S(2)}, u32[]{:S(2)}) collective-permute-start(f32[64,256]{1,0:T(8,128)S(1)} %exchange.1), channel_id=1, source_target_pairs={{0,4},{4,0},{8,12},{12,8},{16,20},{20,16},{24,28},{28,24},{1,5},{5... | collective-permute-start | bytes 196616 | tf_op jit(solution)/shard_map/ppermute | solution.py:264
  20.0 5.3 %collective-permute-start.8 = (f32[64,256]{1,0:T(8,128)S(1)}, f32[64,256]{1,0:T(8,128)S(1)}, u32[]{:S(2)}, u32[]{:S(2)}) collective-permute-start(f32[64,256]{1,0:T(8,128)S(1)} %add.12), channel_id=1, source_target_pairs={{0,24},{4,28},{8,16},{12,20},{16,8},{20,12},{24,0},{28,4},{1,25},{... | collective-permute-start | bytes 196616 | tf_op jit(solution)/shard_map/ppermute | solution.py:264
  22.5 4.3 %collective-permute-start.7 = (f32[64,256]{1,0:T(8,128)S(1)}, f32[64,256]{1,0:T(8,128)S(1)}, u32[]{:S(2)}, u32[]{:S(2)}) collective-permute-start(f32[64,256]{1,0:T(8,128)S(1)} %add.12), channel_id=1, source_target_pairs={{0,16},{4,20},{8,24},{12,28},{16,0},{20,4},{24,8},{28,12},{1,17},{... | collective-permute-start | bytes 196616 | tf_op jit(solution)/shard_map/ppermute | solution.py:264
  23.0 4.3 %collective-permute-start.6 = (f32[64,256]{1,0:T(8,128)S(1)}, f32[64,256]{1,0:T(8,128)S(1)}, u32[]{:S(2)}, u32[]{:S(2)}) collective-permute-start(f32[64,256]{1,0:T(8,128)S(1)} %add.12), channel_id=1, source_target_pairs={{0,8},{4,12},{8,0},{12,4},{16,24},{20,28},{24,16},{28,20},{1,9},{5... | collective-permute-start | bytes 196616 | tf_op jit(solution)/shard_map/ppermute | solution.py:264

commit v20 on v12

--- a/solution.py
+++ b/solution.py
@@ -23,13 +23,13 @@
 
 def partner(i, step, sign, orb):
     if orb == 4:
-        return i ^ (2 - sign)
+        return i ^ (2 + sign)
     return (i + sign * step) % orb
 
 
 def owner_of(me, step, sign, orb):
     if orb == 4:
-        return me ^ (2 - sign)
+        return me ^ (2 + sign)
     return lax.rem(me - sign * step + orb, orb)
 
 

time: 26.2 us -> 27.1 us (1.034)
  waiting for transfers between devices: 9.3 us -> 10.4 us
  starting transfers between devices: 12.2 us -> 11.9 us
    ppermute x2, waiting for transfers between devices: 0.76 us -> 3.55 us  [shift(): return lax.ppermute(x, ('aux', 'orb'), perm)]
    ppermute x1, waiting for transfers between devices: 2.07 us -> 0.86 us  [shards(): tail_in = lax.ppermute(tail, 'orb', across)]
    ppermute x2, starting transfers between devices: 4.44 us -> 4 us  [shift(): return lax.ppermute(x, ('aux', 'orb'), perm)]
    ppermute x4, waiting for transfers between devices: 5.25 us -> 4.83 us  [shards(): lax.ppermute(parts, 'aux', [(i, i ^ way * step) for i in range(aux)])]
  transfers between devices with their start and end apart: 9 -> 9, of which waited for: 8 -> 7; matrix products, arithmetic and copies ran while one was open for 0% -> 0% of each run, Pallas kernels for 9% -> 8%
where the time goes in v20:
time: 27.1 us; the launch traced here: 27 us
  starting transfers between devices  11.9 us (44%)
  waiting for transfers between devices  10.4 us (38%)
  Pallas kernels  3.11 us (11%)
  between operations  0.76 us (3%)
  other arithmetic  0.74 us (3%)
    ppermute x4, waiting for transfers between devices, shards(): lax.ppermute(parts, 'aux', [(i, i ^ way * step) for i in range(aux)])  4.83 us
    ppermute x1, starting transfers between devices, shards(): raw = lax.ppermute(tensor_blocks, 'orb', across)  4.04 us
    ppermute x2, starting transfers between devices, shift(): return lax.ppermute(x, ('aux', 'orb'), perm)  4 us
    ppermute x4, starting transfers between devices, shards(): lax.ppermute(parts, 'aux', [(i, i ^ way * step) for i in range(aux)])  3.77 us
    ppermute x2, waiting for transfers between devices, shift(): return lax.ppermute(x, ('aux', 'orb'), perm)  3.55 us
    ppermute x1, waiting for transfers between devices, shards(): swapped = lax.ppermute(merged, 'aux', [(i, i ^ 1) for i in range(aux)])  1.21 us
    pallas_call x1, Pallas kernels, shards(): pl.pallas_call(functools.partial(pack_kernel, orb), out_shape=[array(size...  1.16 us
    pallas_call x1, Pallas kernels, shards(): pl.pallas_call(functools.partial(exchange_kernel, orb, slots, aux_width),...  0.88 us
  transfers between devices with their start and end apart: 9, of which 7 were waited for; matrix products, arithmetic and copies ran while one was open for 0% of the time, Pallas kernels for 8%

profile of v20, /device:TPU:0, one launch (start us, length us, event | category | flops | bytes accessed | tf_op | source)
XLA Modules:
  0.0 27.0 jit_solution(3110979678141553978)
XLA Ops:
  0.0 4.0 %collective-permute-start.1 = (bf16[1,1,3,4,4096]{4,3,2,1,0:T(4,128)(2,1)}, bf16[1,1,3,4,4096]{4,3,2,1,0:T(4,128)(2,1)S(1)}, u32[]{:S(2)}, u32[]{:S(2)}) collective-permute-start(bf16[1,1,3,4,4096]{4,3,2,1,0:T(4,128)(2,1)} %raw_hbm.1), channel_id=1, source_target_pairs={{0,2},{1,3},{2,0},{3,1},{4,6},{5,7},{6,4},{7,5},{8,10},{9,11},{10,... | collective-permute-start | bytes 294920 | tf_op jit(solution)/shard_map/ppermute | solution.py:207
  4.7 1.2 %pack.1 = (bf16[528,128]{1,0:T(8,128)(2,1)S(1)}, bf16[80,128]{1,0:T(8,128)(2,1)S(1)}) custom-call(s32[1,1]{1,0:T(1,128)S(6)} %copy.5.kept, s32[1,1,3]{2,1,0:T(1,128)} %pairs_hbm.1, bf16[64,256]{1,0:T(8,128)(2,1)} %density_ref.1, bf16[1,1,3,4,4096]{4,3,2,1,0:T(4,128)(2,1)} %raw_hbm.1), custom_call_target="tpu_custom_call" | custom-call | tf_op jit(solution)/shard_map/pack/pallas_call | solution.py:181
  5.9 0.1 collective-permute-start
  5.9 3.9 %collective-permute-start.2 = (bf16[528,128]{1,0:T(8,128)(2,1)S(1)}, bf16[528,128]{1,0:T(8,128)(2,1)S(1)}, u32[]{:S(2)}, u32[]{:S(2)}) collective-permute-start(bf16[528,128]{1,0:T(8,128)(2,1)S(1)} %get-tuple-element.13.own_ref.full_ref.refs_0_), channel_id=1, source_target_pairs={{0,3},{1,2},{2,1},{3,0},{4,5},{5,4},{6,7},{7,6},{8,11},{9,10},{10,... | collective-permute-start | bytes 405512 | tf_op jit(solution)/shard_map/ppermute | solution.py:179
  9.9 0.1 collective-permute-start.4
  10.0 0.9 %collective-permute-done.refs_1_ = bf16[80,128]{1,0:T(8,128)(2,1)S(1)} collective-permute-done((bf16[80,128]{1,0:T(8,128)(2,1)S(1)}, bf16[80,128]{1,0:T(8,128)(2,1)S(1)}, u32[]{:S(2)}, u32[]{:S(2)}) %collective-permute-start) | collective-permute-done | bytes 20512 | tf_op jit(solution)/shard_map/ppermute | solution.py:208
  10.8 0.0 collective-permute-done.1.raw
  10.8 0.2 relay.1.refs_1_
  11.1 0.0 copy-start
  11.1 3.5 %collective-permute-done.2.refs_0_.refs_2_ = bf16[528,128]{1,0:T(8,128)(2,1)S(1)} collective-permute-done((bf16[528,128]{1,0:T(8,128)(2,1)S(1)}, bf16[528,128]{1,0:T(8,128)(2,1)S(1)}, u32[]{:S(2)}, u32[]{:S(2)}) %collective-permute-start.2) | collective-permute-done | bytes 135200 | tf_op jit(solution)/shard_map/ppermute | solution.py:179
  14.6 0.0 collective-permute-start.3
  14.6 1.2 %collective-permute-done.3.refs_2_ = bf16[192,128]{1,0:T(8,128)(2,1)S(1)} collective-permute-done((bf16[192,128]{1,0:T(8,128)(2,1)S(1)}, bf16[192,128]{1,0:T(8,128)(2,1)S(1)}, u32[]{:S(2)}, u32[]{:S(2)}) %collective-permute-start.3) | collective-permute-done | bytes 49184 | tf_op jit(solution)/shard_map/ppermute | solution.py:221
  15.9 0.0 copy-done
  15.9 0.8 %half.1.half_ref = bf16[5,64,256]{2,1,0:T(8,128)(2,1)S(1)} custom-call(s32[3]{0:T(128)S(1)} %get-tuple-element.18.meta_ref, bf16[64,256]{1,0:T(8,128)(2,1)S(1)} %copy-done, bf16[528,128]{1,0:T(8,128)(2,1)S(1)} %get-tuple-element.13.own_ref.full_ref.refs_0_, bf16[528,128]{1,0:T(8,128)(2,1)S(1)} %collective-permute-done.2.refs_0_.refs_2_, ...), custom_call_target="tpu_custom_call" | custom-call | tf_op jit(solution)/shard_map/half/pallas_call | solution.py:230
  16.7 0.0 collective-permute-done.4.refs_3_
  16.7 0.1 maximum_convert_fusion.meta_ref
  16.8 0.9 %exchange.1 = f32[64,256]{1,0:T(8,128)S(1)} custom-call(s32[12]{0:T(128)S(1)} %maximum_convert_fusion.meta_ref, bf16[5,64,256]{2,1,0:T(8,128)(2,1)S(1)} %half.1.half_ref, bf16[528,128]{1,0:T(8,128)(2,1)S(1)} %get-tuple-element.13.own_ref.full_ref.refs_0_, bf16[384,128]{1,0:T(8,128)(2,1)S(1)} %relay.1.refs_1_, ...), custom_call_target="tpu_custom_call" | custom-call | tf_op jit(solution)/shard_map/exchange/pallas_call | solution.py:245
  17.7 0.2 collective-permute-start.5
  17.9 1.1 %collective-permute-done.5 = f32[64,256]{1,0:T(8,128)S(1)} collective-permute-done((f32[64,256]{1,0:T(8,128)S(1)}, f32[64,256]{1,0:T(8,128)S(1)}, u32[]{:S(2)}, u32[]{:S(2)}) %collective-permute-start.5) | collective-permute-done | bytes 65568 | tf_op jit(solution)/shard_map/ppermute | solution.py:260
  19.0 2.5 %collective-permute-start.8 = (f32[64,256]{1,0:T(8,128)S(1)}, f32[64,256]{1,0:T(8,128)S(1)}, u32[]{:S(2)}, u32[]{:S(2)}) collective-permute-start(f32[64,256]{1,0:T(8,128)S(1)} %add.12), channel_id=1, source_target_pairs={{0,24},{4,28},{8,16},{12,20},{16,8},{20,12},{24,0},{28,4},{1,25},{... | collective-permute-start | bytes 196616 | tf_op jit(solution)/shard_map/ppermute | solution.py:260
  21.5 0.5 %collective-permute-start.7 = (f32[64,256]{1,0:T(8,128)S(1)}, f32[64,256]{1,0:T(8,128)S(1)}, u32[]{:S(2)}, u32[]{:S(2)}) collective-permute-start(f32[64,256]{1,0:T(8,128)S(1)} %add.12), channel_id=1, source_target_pairs={{0,16},{4,20},{8,24},{12,28},{16,0},{20,4},{24,8},{28,12},{1,17},{... | collective-permute-start | bytes 196616 | tf_op jit(solution)/shard_map/ppermute | solution.py:260
  22.0 0.5 %collective-permute-start.6 = (f32[64,256]{1,0:T(8,128)S(1)}, f32[64,256]{1,0:T(8,128)S(1)}, u32[]{:S(2)}, u32[]{:S(2)}) collective-permute-start(f32[64,256]{1,0:T(8,128)S(1)} %add.12), channel_id=1, source_target_pairs={{0,8},{4,12},{8,0},{12,4},{16,24},{20,28},{24,16},{28,20},{1,9},{5... | collective-permute-start | bytes 196616 | tf_op jit(solution)/shard_map/ppermute | solution.py:260
  22.6 1.7 %collective-permute-done.8 = f32[64,256]{1,0:T(8,128)S(1)} collective-permute-done((f32[64,256]{1,0:T(8,128)S(1)}, f32[64,256]{1,0:T(8,128)S(1)}, u32[]{:S(2)}, u32[]{:S(2)}) %collective-permute-start.8) | collective-permute-done | bytes 65568 | tf_op jit(solution)/shard_map/ppermute | solution.py:260
  24.3 1.5 %collective-permute-done.7 = f32[64,256]{1,0:T(8,128)S(1)} collective-permute-done((f32[64,256]{1,0:T(8,128)S(1)}, f32[64,256]{1,0:T(8,128)S(1)}, u32[]{:S(2)}, u32[]{:S(2)}) %collective-permute-start.7) | collective-permute-done | bytes 65568 | tf_op jit(solution)/shard_map/ppermute | solution.py:260
  25.8 0.5 %collective-permute-done.6 = f32[64,256]{1,0:T(8,128)S(1)} collective-permute-done((f32[64,256]{1,0:T(8,128)S(1)}, f32[64,256]{1,0:T(8,128)S(1)}, u32[]{:S(2)}, u32[]{:S(2)}) %collective-permute-start.6) | collective-permute-done | bytes 65568 | tf_op jit(solution)/shard_map/ppermute | solution.py:260
  26.3 0.6 %add_add_fusion = f32[64,256]{1,0:T(8,128)} fusion(f32[64,256]{1,0:T(8,128)S(1)} %collective-permute-done.7, f32[64,256]{1,0:T(8,128)S(1)} %collective-permute-done.8, f32[64,256]{1,0:T(8,128)S(1)} %add.12, f32[64,256]{1,0:T(8,128)S(1)} %collective-permute-done.6), kind=kLoop, calls=%fused_computation | loop fusion | flops 49152 | bytes 327680 | tf_op jit(solution)/shard_map/add | solution.py:262
  (7 shorter events, 0.0 us)
Async XLA Ops:
  0.0 10.8 %collective-permute-start.1 = (bf16[1,1,3,4,4096]{4,3,2,1,0:T(4,128)(2,1)}, bf16[1,1,3,4,4096]{4,3,2,1,0:T(4,128)(2,1)S(1)}, u32[]{:S(2)}, u32[]{:S(2)}) collective-permute-start(bf16[1,1,3,4,4096]{4,3,2,1,0:T(4,128)(2,1)} %raw_hbm.1), channel_id=1, source_target_pairs={{0,2},{1,3},{2,0},{3,1},{4,6},{5,7},{6,4},{7,5},{8,10},{9,11},{10,... | collective-permute-start | bytes 294920 | tf_op jit(solution)/shard_map/ppermute | solution.py:207
  5.9 5.0 %collective-permute-start = (bf16[80,128]{1,0:T(8,128)(2,1)S(1)}, bf16[80,128]{1,0:T(8,128)(2,1)S(1)}, u32[]{:S(2)}, u32[]{:S(2)}) collective-permute-start(bf16[80,128]{1,0:T(8,128)(2,1)S(1)} %get-tuple-element.11), channel_id=1, source_target_pairs={{0,2},{1,3},{2,0},{3,1},{4,6},{5,7},{6,4},{7,5},{8,10},{9,11},{10,... | collective-permute-start | bytes 61448 | tf_op jit(solution)/shard_map/ppermute | solution.py:208
  5.9 8.7 %collective-permute-start.2 = (bf16[528,128]{1,0:T(8,128)(2,1)S(1)}, bf16[528,128]{1,0:T(8,128)(2,1)S(1)}, u32[]{:S(2)}, u32[]{:S(2)}) collective-permute-start(bf16[528,128]{1,0:T(8,128)(2,1)S(1)} %get-tuple-element.13.own_ref.full_ref.refs_0_), channel_id=1, source_target_pairs={{0,3},{1,2},{2,1},{3,0},{4,5},{5,4},{6,7},{7,6},{8,11},{9,10},{10,... | collective-permute-start | bytes 405512 | tf_op jit(solution)/shard_map/ppermute | solution.py:179
  9.9 6.8 %collective-permute-start.4 = (bf16[400,128]{1,0:T(8,128)(2,1)S(1)}, bf16[400,128]{1,0:T(8,128)(2,1)S(1)}, u32[]{:S(2)}, u32[]{:S(2)}) collective-permute-start(bf16[400,128]{1,0:T(8,128)(2,1)S(1)} %lean.1), channel_id=1, source_target_pairs={{0,1},{1,0},{2,3},{3,2},{4,7},{5,6},{6,5},{7,4},{8,9},{9,8},{10,11... | collective-permute-start | bytes 307208 | tf_op jit(solution)/shard_map/ppermute | solution.py:179
  11.1 4.8 %copy-start = (bf16[64,256]{1,0:T(8,128)(2,1)S(1)}, bf16[64,256]{1,0:T(8,128)(2,1)}, u32[]{:S(2)}) copy-start(bf16[64,256]{1,0:T(8,128)(2,1)} %density_ref.1) | copy-start | bytes 98308
  14.6 1.2 %collective-permute-start.3 = (bf16[192,128]{1,0:T(8,128)(2,1)S(1)}, bf16[192,128]{1,0:T(8,128)(2,1)S(1)}, u32[]{:S(2)}, u32[]{:S(2)}) collective-permute-start(bf16[192,128]{1,0:T(8,128)(2,1)S(1)} %merge.1), channel_id=1, source_target_pairs={{0,4},{4,0},{8,12},{12,8},{16,20},{20,16},{24,28},{28,24},{1,5},{5... | collective-permute-start | bytes 147464 | tf_op jit(solution)/shard_map/ppermute | solution.py:221
  17.7 1.3 %collective-permute-start.5 = (f32[64,256]{1,0:T(8,128)S(1)}, f32[64,256]{1,0:T(8,128)S(1)}, u32[]{:S(2)}, u32[]{:S(2)}) collective-permute-start(f32[64,256]{1,0:T(8,128)S(1)} %exchange.1), channel_id=1, source_target_pairs={{0,4},{4,0},{8,12},{12,8},{16,20},{20,16},{24,28},{28,24},{1,5},{5... | collective-permute-start | bytes 196616 | tf_op jit(solution)/shard_map/ppermute | solution.py:260
  19.0 5.3 %collective-permute-start.8 = (f32[64,256]{1,0:T(8,128)S(1)}, f32[64,256]{1,0:T(8,128)S(1)}, u32[]{:S(2)}, u32[]{:S(2)}) collective-permute-start(f32[64,256]{1,0:T(8,128)S(1)} %add.12), channel_id=1, source_target_pairs={{0,24},{4,28},{8,16},{12,20},{16,8},{20,12},{24,0},{28,4},{1,25},{... | collective-permute-start | bytes 196616 | tf_op jit(solution)/shard_map/ppermute | solution.py:260
  21.5 4.3 %collective-permute-start.7 = (f32[64,256]{1,0:T(8,128)S(1)}, f32[64,256]{1,0:T(8,128)S(1)}, u32[]{:S(2)}, u32[]{:S(2)}) collective-permute-start(f32[64,256]{1,0:T(8,128)S(1)} %add.12), channel_id=1, source_target_pairs={{0,16},{4,20},{8,24},{12,28},{16,0},{20,4},{24,8},{28,12},{1,17},{... | collective-permute-start | bytes 196616 | tf_op jit(solution)/shard_map/ppermute | solution.py:260
  22.0 4.3 %collective-permute-start.6 = (f32[64,256]{1,0:T(8,128)S(1)}, f32[64,256]{1,0:T(8,128)S(1)}, u32[]{:S(2)}, u32[]{:S(2)}) collective-permute-start(f32[64,256]{1,0:T(8,128)S(1)} %add.12), channel_id=1, source_target_pairs={{0,8},{4,12},{8,0},{12,4},{16,24},{20,28},{24,16},{28,20},{1,9},{5... | collective-permute-start | bytes 196616 | tf_op jit(solution)/shard_map/ppermute | solution.py:260

commit v21 on v12

--- a/solution.py
+++ b/solution.py
@@ -46,12 +46,12 @@
     ]
     for copy in copies:
         copy.start()
-    for copy in copies:
+    for copy in copies[1:]:
         copy.wait()
-    size = lay_blocks(raw[0, 0], full_ref) * BS
     height = BS // 2
     near = pl.multiple_of(core_parity() * height, height)
     tiles = rows.shape[1] // LANES
+    size = full_ref.shape[0] - tiles * BS - NOTE
     for t in range(tiles):
         lanes = slice(t * LANES, (t + 1) * LANES)
         full_ref[size + t * BS : size + (t + 1) * BS] = rows[:, lanes]
@@ -64,6 +64,8 @@
     note = note.astype(jnp.float32).astype(jnp.bfloat16)
     full_ref[size + tiles * BS :] = note
     tail_ref[tiles * height :] = note
+    copies[0].wait()
+    lay_blocks(raw[0, 0], full_ref)
 
 
 def lean_kernel(full_ref, out_ref):
@@ -72,8 +74,15 @@
     out_ref[size:] = full_ref[full_ref.shape[0] - NOTE :]
 
 
-def relay_kernel(raw, out_ref):
+def relay_kernel(slots, aux_width, raw, full_ref, out_ref, left_ref):
     lay_blocks(raw[0, 0], out_ref)
+    size = out_ref.shape[0]
+    own = jnp.concatenate([full_ref[at : at + BS] for at in range(0, size, BS)], axis=1)
+    for p in range(aux_width):
+        cuts = [(j * aux_width + p) * BS for j in range(slots)]
+        left_ref[p * BS : (p + 1) * BS] = jnp.concatenate(
+            [own[:, cut : cut + BS] for cut in cuts], axis=1
+        )
 
 
 def merge_kernel(size, *refs):
@@ -86,26 +95,29 @@
         at += count
 
 
-def half_kernel(orb, slots, aux_width, meta_ref, density_ref, own_ref, *refs):
-    fulls, (tail, swapped, half_ref, rows) = refs[:-4], refs[-4:]
+def exchange_kernel(
+    orb, slots, aux_width, meta_ref, density_ref, left_ref, tail, swapped, *refs
+):
+    packs, (out_ref, rows, half_ref, held) = refs[:orb], refs[orb:]
+    fulls = packs[2::2]
     me = lax.axis_index("orb")
     parity = core_parity()
+    sign = 1 - 2 * parity
     height = BS // 2
     count = density_ref.shape[1] // LANES
     size = slots * aux_width * BS // LANES * BS
     near = pl.multiple_of(parity * height, height)
     far = pl.multiple_of((1 - parity) * height, height)
+    across = lax.rem(me + orb // 2, orb)
+    owners = [me, across]
     rows[me] = density_ref[...]
     for i, full in enumerate(fulls):
-        sign = 1 - 2 * parity
-        ahead = owner_of(me, i + 1, sign, orb)
-        behind = owner_of(me, i + 1, -sign, orb)
+        owners += [owner_of(me, i + 1, sign, orb), owner_of(me, i + 1, -sign, orb)]
         for t in range(count):
             lanes = slice(t * LANES, (t + 1) * LANES)
             at = (i * count + t) * BS
-            rows[ahead, :, lanes] = full[size + t * BS : size + (t + 1) * BS]
-            rows[behind, :, lanes] = swapped[at : at + BS]
-    across = lax.rem(me + orb // 2, orb)
+            rows[owners[-2], :, lanes] = full[size + t * BS : size + (t + 1) * BS]
+            rows[owners[-1], :, lanes] = swapped[at : at + BS]
     for t in range(count):
         lanes = slice(t * LANES, (t + 1) * LANES)
         at = len(fulls) * count * BS + t * height
@@ -113,44 +125,22 @@
         rows[across, pl.ds(far, height), lanes] = swapped[at : at + height]
     rows[orb] = jnp.zeros_like(rows[orb])
     selected = jnp.concatenate([rows[meta_ref[j]] for j in range(slots)], axis=0)
-    own = jnp.concatenate([own_ref[at : at + BS] for at in range(0, size, BS)], axis=1)
-    left = []
-    for p in range(aux_width):
-        cuts = [(j * aux_width + p) * BS for j in range(slots)]
-        left.append(jnp.concatenate([own[:, cut : cut + BS] for cut in cuts], axis=1))
-    left = jnp.concatenate(left, axis=0)
-    half = jnp.dot(left, selected, preferred_element_type=jnp.float32).astype(jnp.bfloat16)
+    half = jnp.dot(left_ref[...], selected, preferred_element_type=jnp.float32)
+    half = half.astype(jnp.bfloat16)
     for k in range(orb):
         half_ref[k] = jnp.concatenate(
             [half[p * BS : (p + 1) * BS, k * BS : (k + 1) * BS] for p in range(aux_width)],
             axis=1,
         )
     half_ref[orb] = jnp.zeros_like(half_ref[orb])
-
-
-def exchange_kernel(orb, slots, aux_width, meta_ref, half_ref, *refs):
-    packs, (out_ref, held) = refs[:orb], refs[orb:]
-    me = lax.axis_index("orb")
-    parity = core_parity()
-    per_slot = aux_width * BS // LANES
-    sign = 1 - 2 * parity
-    owners = [me, lax.rem(me + orb // 2, orb)]
-    for i in range(1, orb // 2):
-        owners += [owner_of(me, i, sign, orb), owner_of(me, i, -sign, orb)]
     for way in range(orb):
-        total = None
-        for j in range(slots):
-            tiles = [
-                packs[way][t * BS : (t + 1) * BS] for t in range(j * per_slot, (j + 1) * per_slot)
-            ]
-            term = lax.dot_general(
-                half_ref[meta_ref[way * slots + j]],
-                jnp.concatenate(tiles, axis=1),
-                (((1,), (1,)), ((), ())),
-                preferred_element_type=jnp.float32,
-            )
-            total = term if total is None else total + term
-        held[owners[way]] = total
+        codes = [meta_ref[way * slots + j] for j in range(slots)]
+        held[owners[way]] = lax.dot_general(
+            jnp.concatenate([half_ref[code] for code in codes], axis=1),
+            jnp.concatenate([packs[way][at : at + BS] for at in range(0, size, BS)], axis=1),
+            (((1,), (1,)), ((), ())),
+            preferred_element_type=jnp.float32,
+        )
     out_ref[...] = jnp.concatenate([held[n] for n in range(orb)], axis=1)
 
 
@@ -219,24 +209,18 @@
         name="merge",
     )(*fulls, tail_in)
     swapped = lax.ppermute(merged, "aux", [(i, i ^ 1) for i in range(aux)])
-    across = pl.pallas_call(
-        relay_kernel,
-        out_shape=array(size),
-        in_specs=[vmem],
-        out_specs=vmem,
+    across, left = pl.pallas_call(
+        functools.partial(relay_kernel, slots, aux_width),
+        out_shape=[
+            array(size),
+            jax.ShapeDtypeStruct((aux_width * BS, slots * BS), jnp.bfloat16),
+        ],
+        in_specs=[vmem] * 2,
+        out_specs=[vmem] * 2,
         compiler_params=params,
         name="relay",
-    )(raw)
-    half = pl.pallas_call(
-        functools.partial(half_kernel, orb, slots, aux_width),
-        out_shape=jax.ShapeDtypeStruct((orb + 1, BS, aux_width * BS), jnp.bfloat16),
-        in_specs=[smem] + [vmem] * (len(fulls) + 4),
-        out_specs=vmem,
-        scratch_shapes=[pltpu.VMEM((orb + 1, BS, full_width), jnp.bfloat16)],
-        compiler_params=params,
-        name="half",
-    )(tail[-NOTE, :slots].astype(jnp.int32), density, full, *fulls, tail_in, swapped)
-    half, leans = lax.optimization_barrier((half, leans))
+    )(raw, full)
+    swapped, leans = lax.optimization_barrier((swapped, leans))
     packs, notes = [full, across], [tail, tail_in]
     for pair in zip(fulls, leans):
         packs += pair
@@ -245,12 +229,16 @@
     parts = pl.pallas_call(
         functools.partial(exchange_kernel, orb, slots, aux_width),
         out_shape=jax.ShapeDtypeStruct((BS, full_width), jnp.float32),
-        in_specs=[smem] + [vmem] * (orb + 1),
+        in_specs=[smem] + [vmem] * (orb + 4),
         out_specs=vmem,
-        scratch_shapes=[pltpu.VMEM((orb, BS, BS), jnp.float32)],
+        scratch_shapes=[
+            pltpu.VMEM((orb + 1, BS, full_width), jnp.bfloat16),
+            pltpu.VMEM((orb + 1, BS, aux_width * BS), jnp.bfloat16),
+            pltpu.VMEM((orb, BS, BS), jnp.float32),
+        ],
         compiler_params=params,
         name="exchange",
-    )(codes, half, *packs)
+    )(codes, density, left, tail_in, swapped, *packs)
 
     step = 1
     while step < aux:

time: 26.2 us -> 26.3 us (level)
  waiting for transfers between devices: 9.3 us -> 9.87 us
  Pallas kernels: 3.1 us -> 2.59 us
    ppermute x2, waiting for transfers between devices: 0.76 us -> 2.82 us  [shift(): return lax.ppermute(x, ('aux', 'orb'), perm)]
    ppermute x1, waiting for transfers between devices: 1.21 us -> 0.01 us  [shards(): swapped = lax.ppermute(merged, 'aux', [(i, i ^ 1) for i in range(aux)])]
    pallas_call x2 -> x1, Pallas kernels: 1.06 us -> 0.23 us  [shards(): pl.pallas_call(functools.partial(relay_kernel, slots, aux_width), out_sha...]
    pallas_call x1, Pallas kernels: 0.87 us -> 1.21 us  [shards(): pl.pallas_call(functools.partial(exchange_kernel, orb, slots, aux_width),...]
    ppermute x4, waiting for transfers between devices: 5.25 us -> 4.97 us  [shards(): lax.ppermute(parts, 'aux', [(i, i ^ way * step) for i in range(aux)])]
  transfers between devices with their start and end apart: 9 -> 9, of which waited for: 8 -> 7; matrix products, arithmetic and copies ran while one was open for 0% -> 0% of each run, Pallas kernels for 9% -> 5%
where the time goes in v21:
time: 26.3 us; the launch traced here: 26.1 us
  starting transfers between devices  12.2 us (46%)
  waiting for transfers between devices  9.87 us (38%)
  Pallas kernels  2.59 us (10%)
  other arithmetic  0.74 us (3%)
  between operations  0.73 us (3%)
    ppermute x4, waiting for transfers between devices, shards(): lax.ppermute(parts, 'aux', [(i, i ^ way * step) for i in range(aux)])  4.97 us
    ppermute x2, starting transfers between devices, shift(): return lax.ppermute(x, ('aux', 'orb'), perm)  4.44 us
    ppermute x1, starting transfers between devices, shards(): raw = lax.ppermute(tensor_blocks, 'orb', across)  4.04 us
    ppermute x4, starting transfers between devices, shards(): lax.ppermute(parts, 'aux', [(i, i ^ way * step) for i in range(aux)])  3.62 us
    ppermute x2, waiting for transfers between devices, shift(): return lax.ppermute(x, ('aux', 'orb'), perm)  2.82 us
    ppermute x1, waiting for transfers between devices, shards(): tail_in = lax.ppermute(tail, 'orb', across)  2.07 us
    pallas_call x1, Pallas kernels, shards(): pl.pallas_call(functools.partial(exchange_kernel, orb, slots, aux_width),...  1.21 us
    pallas_call x1, Pallas kernels, shards(): pl.pallas_call(functools.partial(pack_kernel, orb), out_shape=[array(size...  1.14 us
  transfers between devices with their start and end apart: 9, of which 7 were waited for; matrix products, arithmetic and copies ran while one was open for 0% of the time, Pallas kernels for 5%

profile of v21, /device:TPU:0, one launch (start us, length us, event | category | flops | bytes accessed | tf_op | source)
XLA Modules:
  0.0 26.1 jit_solution(3052236270756098383)
XLA Ops:
  0.0 4.0 %collective-permute-start.1 = (bf16[1,1,3,4,4096]{4,3,2,1,0:T(4,128)(2,1)}, bf16[1,1,3,4,4096]{4,3,2,1,0:T(4,128)(2,1)S(1)}, u32[]{:S(2)}, u32[]{:S(2)}) collective-permute-start(bf16[1,1,3,4,4096]{4,3,2,1,0:T(4,128)(2,1)} %raw_hbm.1), channel_id=1, source_target_pairs={{0,2},{1,3},{2,0},{3,1},{4,6},{5,7},{6,4},{7,5},{8,10},{9,11},{10,... | collective-permute-start | bytes 294920 | tf_op jit(solution)/shard_map/ppermute | solution.py:197
  4.7 1.1 %pack.1 = (bf16[528,128]{1,0:T(8,128)(2,1)S(1)}, bf16[80,128]{1,0:T(8,128)(2,1)S(1)}) custom-call(s32[1,1]{1,0:T(1,128)S(6)} %copy.5.kept, s32[1,1,3]{2,1,0:T(1,128)} %pairs_hbm.1, bf16[64,256]{1,0:T(8,128)(2,1)} %density_ref.1, bf16[1,1,3,4,4096]{4,3,2,1,0:T(4,128)(2,1)} %raw_hbm.1), custom_call_target="tpu_custom_call" | custom-call | tf_op jit(solution)/shard_map/pack/pallas_call | solution.py:171
  5.8 0.1 collective-permute-start
  5.9 1.9 %collective-permute-start.2 = (bf16[528,128]{1,0:T(8,128)(2,1)S(1)}, bf16[528,128]{1,0:T(8,128)(2,1)S(1)}, u32[]{:S(2)}, u32[]{:S(2)}) collective-permute-start(bf16[528,128]{1,0:T(8,128)(2,1)S(1)} %get-tuple-element.15.full_ref.refs_0_), channel_id=1, source_target_pairs={{0,1},{1,0},{2,3},{3,2},{4,7},{5,6},{6,5},{7,4},{8,9},{9,8},{10,11... | collective-permute-start | bytes 405512 | tf_op jit(solution)/shard_map/ppermute | solution.py:169
  7.8 2.5 %collective-permute-start.4 = (bf16[400,128]{1,0:T(8,128)(2,1)S(1)}, bf16[400,128]{1,0:T(8,128)(2,1)S(1)}, u32[]{:S(2)}, u32[]{:S(2)}) collective-permute-start(bf16[400,128]{1,0:T(8,128)(2,1)S(1)} %lean.1), channel_id=1, source_target_pairs={{0,3},{1,2},{2,1},{3,0},{4,5},{5,4},{6,7},{7,6},{8,11},{9,10},{10,... | collective-permute-start | bytes 307208 | tf_op jit(solution)/shard_map/ppermute | solution.py:169
  10.4 2.1 %collective-permute-done.refs_1_.tail = bf16[80,128]{1,0:T(8,128)(2,1)S(1)} collective-permute-done((bf16[80,128]{1,0:T(8,128)(2,1)S(1)}, bf16[80,128]{1,0:T(8,128)(2,1)S(1)}, u32[]{:S(2)}, u32[]{:S(2)}) %collective-permute-start) | collective-permute-done | bytes 20512 | tf_op jit(solution)/shard_map/ppermute | solution.py:198
  12.4 0.0 collective-permute-done.1.raw
  12.4 0.2 relay.1
  12.7 0.5 %collective-permute-done.2.refs_0_.refs_2_ = bf16[528,128]{1,0:T(8,128)(2,1)S(1)} collective-permute-done((bf16[528,128]{1,0:T(8,128)(2,1)S(1)}, bf16[528,128]{1,0:T(8,128)(2,1)S(1)}, u32[]{:S(2)}, u32[]{:S(2)}) %collective-permute-start.2) | collective-permute-done | bytes 135200 | tf_op jit(solution)/shard_map/ppermute | solution.py:169
  13.2 0.0 copy-start
  13.2 0.0 collective-permute-start.3
  13.2 2.3 %collective-permute-done.4.refs_3_ = bf16[400,128]{1,0:T(8,128)(2,1)S(1)} collective-permute-done((bf16[400,128]{1,0:T(8,128)(2,1)S(1)}, bf16[400,128]{1,0:T(8,128)(2,1)S(1)}, u32[]{:S(2)}, u32[]{:S(2)}) %collective-permute-start.4) | collective-permute-done | bytes 102432 | tf_op jit(solution)/shard_map/ppermute | solution.py:169
  15.5 0.0 collective-permute-done.3.swapped
  15.5 0.1 maximum_convert_fusion.meta_ref
  15.6 0.0 copy-done
  15.6 1.2 %exchange.1 = f32[64,256]{1,0:T(8,128)S(1)} custom-call(s32[12]{0:T(128)S(1)} %maximum_convert_fusion.meta_ref, bf16[64,256]{1,0:T(8,128)(2,1)S(1)} %copy-done, bf16[256,192]{1,0:T(8,128)(2,1)S(1)} %get-tuple-element.18.left_ref, bf16[80,128]{1,0:T(8,128)(2,1)S(1)} %collective-permute-done.refs_1_.tail, bf16[192,128]{1,0:T(8,128)(2,1)S(1)} %collective-permute-done.3.swapped, ...), custom_call_target="tpu_custom_call" | custom-call | tf_op jit(solution)/shard_map/exchange/pallas_call | solution.py:229
  16.8 0.1 collective-permute-start.5
  16.9 1.2 %collective-permute-done.5 = f32[64,256]{1,0:T(8,128)S(1)} collective-permute-done((f32[64,256]{1,0:T(8,128)S(1)}, f32[64,256]{1,0:T(8,128)S(1)}, u32[]{:S(2)}, u32[]{:S(2)}) %collective-permute-start.5) | collective-permute-done | bytes 65568 | tf_op jit(solution)/shard_map/ppermute | solution.py:248
  18.2 2.5 %collective-permute-start.8 = (f32[64,256]{1,0:T(8,128)S(1)}, f32[64,256]{1,0:T(8,128)S(1)}, u32[]{:S(2)}, u32[]{:S(2)}) collective-permute-start(f32[64,256]{1,0:T(8,128)S(1)} %add.12), channel_id=1, source_target_pairs={{0,24},{4,28},{8,16},{12,20},{16,8},{20,12},{24,0},{28,4},{1,25},{... | collective-permute-start | bytes 196616 | tf_op jit(solution)/shard_map/ppermute | solution.py:248
  20.7 0.5 %collective-permute-start.7 = (f32[64,256]{1,0:T(8,128)S(1)}, f32[64,256]{1,0:T(8,128)S(1)}, u32[]{:S(2)}, u32[]{:S(2)}) collective-permute-start(f32[64,256]{1,0:T(8,128)S(1)} %add.12), channel_id=1, source_target_pairs={{0,16},{4,20},{8,24},{12,28},{16,0},{20,4},{24,8},{28,12},{1,17},{... | collective-permute-start | bytes 196616 | tf_op jit(solution)/shard_map/ppermute | solution.py:248
  21.2 0.5 %collective-permute-start.6 = (f32[64,256]{1,0:T(8,128)S(1)}, f32[64,256]{1,0:T(8,128)S(1)}, u32[]{:S(2)}, u32[]{:S(2)}) collective-permute-start(f32[64,256]{1,0:T(8,128)S(1)} %add.12), channel_id=1, source_target_pairs={{0,8},{4,12},{8,0},{12,4},{16,24},{20,28},{24,16},{28,20},{1,9},{5... | collective-permute-start | bytes 196616 | tf_op jit(solution)/shard_map/ppermute | solution.py:248
  21.7 1.7 %collective-permute-done.8 = f32[64,256]{1,0:T(8,128)S(1)} collective-permute-done((f32[64,256]{1,0:T(8,128)S(1)}, f32[64,256]{1,0:T(8,128)S(1)}, u32[]{:S(2)}, u32[]{:S(2)}) %collective-permute-start.8) | collective-permute-done | bytes 65568 | tf_op jit(solution)/shard_map/ppermute | solution.py:248
  23.4 1.5 %collective-permute-done.7 = f32[64,256]{1,0:T(8,128)S(1)} collective-permute-done((f32[64,256]{1,0:T(8,128)S(1)}, f32[64,256]{1,0:T(8,128)S(1)}, u32[]{:S(2)}, u32[]{:S(2)}) %collective-permute-start.7) | collective-permute-done | bytes 65568 | tf_op jit(solution)/shard_map/ppermute | solution.py:248
  25.0 0.5 %collective-permute-done.6 = f32[64,256]{1,0:T(8,128)S(1)} collective-permute-done((f32[64,256]{1,0:T(8,128)S(1)}, f32[64,256]{1,0:T(8,128)S(1)}, u32[]{:S(2)}, u32[]{:S(2)}) %collective-permute-start.6) | collective-permute-done | bytes 65568 | tf_op jit(solution)/shard_map/ppermute | solution.py:248
  25.5 0.6 %add_add_fusion = f32[64,256]{1,0:T(8,128)} fusion(f32[64,256]{1,0:T(8,128)S(1)} %collective-permute-done.7, f32[64,256]{1,0:T(8,128)S(1)} %collective-permute-done.8, f32[64,256]{1,0:T(8,128)S(1)} %add.12, f32[64,256]{1,0:T(8,128)S(1)} %collective-permute-done.6), kind=kLoop, calls=%fused_computation | loop fusion | flops 49152 | bytes 327680 | tf_op jit(solution)/shard_map/add | solution.py:250
  (7 shorter events, 0.0 us)
Async XLA Ops:
  0.0 12.4 %collective-permute-start.1 = (bf16[1,1,3,4,4096]{4,3,2,1,0:T(4,128)(2,1)}, bf16[1,1,3,4,4096]{4,3,2,1,0:T(4,128)(2,1)S(1)}, u32[]{:S(2)}, u32[]{:S(2)}) collective-permute-start(bf16[1,1,3,4,4096]{4,3,2,1,0:T(4,128)(2,1)} %raw_hbm.1), channel_id=1, source_target_pairs={{0,2},{1,3},{2,0},{3,1},{4,6},{5,7},{6,4},{7,5},{8,10},{9,11},{10,... | collective-permute-start | bytes 294920 | tf_op jit(solution)/shard_map/ppermute | solution.py:197
  5.8 6.6 %collective-permute-start = (bf16[80,128]{1,0:T(8,128)(2,1)S(1)}, bf16[80,128]{1,0:T(8,128)(2,1)S(1)}, u32[]{:S(2)}, u32[]{:S(2)}) collective-permute-start(bf16[80,128]{1,0:T(8,128)(2,1)S(1)} %get-tuple-element.13), channel_id=1, source_target_pairs={{0,2},{1,3},{2,0},{3,1},{4,6},{5,7},{6,4},{7,5},{8,10},{9,11},{10,... | collective-permute-start | bytes 61448 | tf_op jit(solution)/shard_map/ppermute | solution.py:198
  5.9 7.3 %collective-permute-start.2 = (bf16[528,128]{1,0:T(8,128)(2,1)S(1)}, bf16[528,128]{1,0:T(8,128)(2,1)S(1)}, u32[]{:S(2)}, u32[]{:S(2)}) collective-permute-start(bf16[528,128]{1,0:T(8,128)(2,1)S(1)} %get-tuple-element.15.full_ref.refs_0_), channel_id=1, source_target_pairs={{0,1},{1,0},{2,3},{3,2},{4,7},{5,6},{6,5},{7,4},{8,9},{9,8},{10,11... | collective-permute-start | bytes 405512 | tf_op jit(solution)/shard_map/ppermute | solution.py:169
  7.8 7.7 %collective-permute-start.4 = (bf16[400,128]{1,0:T(8,128)(2,1)S(1)}, bf16[400,128]{1,0:T(8,128)(2,1)S(1)}, u32[]{:S(2)}, u32[]{:S(2)}) collective-permute-start(bf16[400,128]{1,0:T(8,128)(2,1)S(1)} %lean.1), channel_id=1, source_target_pairs={{0,3},{1,2},{2,1},{3,0},{4,5},{5,4},{6,7},{7,6},{8,11},{9,10},{10,... | collective-permute-start | bytes 307208 | tf_op jit(solution)/shard_map/ppermute | solution.py:169
  13.2 2.4 %copy-start = (bf16[64,256]{1,0:T(8,128)(2,1)S(1)}, bf16[64,256]{1,0:T(8,128)(2,1)}, u32[]{:S(2)}) copy-start(bf16[64,256]{1,0:T(8,128)(2,1)} %density_ref.1) | copy-start | bytes 98308
  13.2 2.3 %collective-permute-start.3 = (bf16[192,128]{1,0:T(8,128)(2,1)S(1)}, bf16[192,128]{1,0:T(8,128)(2,1)S(1)}, u32[]{:S(2)}, u32[]{:S(2)}) collective-permute-start(bf16[192,128]{1,0:T(8,128)(2,1)S(1)} %merge.1), channel_id=1, source_target_pairs={{0,4},{4,0},{8,12},{12,8},{16,20},{20,16},{24,28},{28,24},{1,5},{5... | collective-permute-start | bytes 147464 | tf_op jit(solution)/shard_map/ppermute | solution.py:211
  16.8 1.3 %collective-permute-start.5 = (f32[64,256]{1,0:T(8,128)S(1)}, f32[64,256]{1,0:T(8,128)S(1)}, u32[]{:S(2)}, u32[]{:S(2)}) collective-permute-start(f32[64,256]{1,0:T(8,128)S(1)} %exchange.1), channel_id=1, source_target_pairs={{0,4},{4,0},{8,12},{12,8},{16,20},{20,16},{24,28},{28,24},{1,5},{5... | collective-permute-start | bytes 196616 | tf_op jit(solution)/shard_map/ppermute | solution.py:248
  18.2 5.3 %collective-permute-start.8 = (f32[64,256]{1,0:T(8,128)S(1)}, f32[64,256]{1,0:T(8,128)S(1)}, u32[]{:S(2)}, u32[]{:S(2)}) collective-permute-start(f32[64,256]{1,0:T(8,128)S(1)} %add.12), channel_id=1, source_target_pairs={{0,24},{4,28},{8,16},{12,20},{16,8},{20,12},{24,0},{28,4},{1,25},{... | collective-permute-start | bytes 196616 | tf_op jit(solution)/shard_map/ppermute | solution.py:248
  20.7 4.3 %collective-permute-start.7 = (f32[64,256]{1,0:T(8,128)S(1)}, f32[64,256]{1,0:T(8,128)S(1)}, u32[]{:S(2)}, u32[]{:S(2)}) collective-permute-start(f32[64,256]{1,0:T(8,128)S(1)} %add.12), channel_id=1, source_target_pairs={{0,16},{4,20},{8,24},{12,28},{16,0},{20,4},{24,8},{28,12},{1,17},{... | collective-permute-start | bytes 196616 | tf_op jit(solution)/shard_map/ppermute | solution.py:248
  21.2 4.3 %collective-permute-start.6 = (f32[64,256]{1,0:T(8,128)S(1)}, f32[64,256]{1,0:T(8,128)S(1)}, u32[]{:S(2)}, u32[]{:S(2)}) collective-permute-start(f32[64,256]{1,0:T(8,128)S(1)} %add.12), channel_id=1, source_target_pairs={{0,8},{4,12},{8,0},{12,4},{16,24},{20,28},{24,16},{28,20},{1,9},{5... | collective-permute-start | bytes 196616 | tf_op jit(solution)/shard_map/ppermute | solution.py:248

commit v22 on v21

--- a/solution.py
+++ b/solution.py
@@ -9,7 +9,7 @@
 
 BS = 64
 LANES = 128
-NOTE = 16
+NOTE = 8
 
 
 def lay_blocks(raw, out_ref):

time: 26.3 us -> 26.1 us (level)
  no operation moved by 1% of the time
where the time goes in v22:
time: 26.1 us; the launch traced here: 26 us
  starting transfers between devices  12.2 us (47%)
  waiting for transfers between devices  9.74 us (37%)
  Pallas kernels  2.59 us (10%)
  other arithmetic  0.74 us (3%)
  between operations  0.73 us (3%)
    ppermute x4, waiting for transfers between devices, shards(): lax.ppermute(parts, 'aux', [(i, i ^ way * step) for i in range(aux)])  4.97 us
    ppermute x2, starting transfers between devices, shift(): return lax.ppermute(x, ('aux', 'orb'), perm)  4.44 us
    ppermute x1, starting transfers between devices, shards(): raw = lax.ppermute(tensor_blocks, 'orb', across)  4.04 us
    ppermute x4, starting transfers between devices, shards(): lax.ppermute(parts, 'aux', [(i, i ^ way * step) for i in range(aux)])  3.62 us
    ppermute x2, waiting for transfers between devices, shift(): return lax.ppermute(x, ('aux', 'orb'), perm)  2.8 us
    ppermute x1, waiting for transfers between devices, shards(): tail_in = lax.ppermute(tail, 'orb', across)  1.96 us
    pallas_call x1, Pallas kernels, shards(): pl.pallas_call(functools.partial(exchange_kernel, orb, slots, aux_width),...  1.21 us
    pallas_call x1, Pallas kernels, shards(): pl.pallas_call(functools.partial(pack_kernel, orb), out_shape=[array(size...  1.14 us
  transfers between devices with their start and end apart: 9, of which 7 were waited for; matrix products, arithmetic and copies ran while one was open for 0% of the time, Pallas kernels for 5%

profile of v22, /device:TPU:0, one launch (start us, length us, event | category | flops | bytes accessed | tf_op | source)
XLA Modules:
  0.0 26.0 jit_solution(8462580646508147488)
XLA Ops:
  0.0 4.0 %collective-permute-start.1 = (bf16[1,1,3,4,4096]{4,3,2,1,0:T(4,128)(2,1)}, bf16[1,1,3,4,4096]{4,3,2,1,0:T(4,128)(2,1)S(1)}, u32[]{:S(2)}, u32[]{:S(2)}) collective-permute-start(bf16[1,1,3,4,4096]{4,3,2,1,0:T(4,128)(2,1)} %raw_hbm.1), channel_id=1, source_target_pairs={{0,2},{1,3},{2,0},{3,1},{4,6},{5,7},{6,4},{7,5},{8,10},{9,11},{10,... | collective-permute-start | bytes 294920 | tf_op jit(solution)/shard_map/ppermute | solution.py:197
  4.7 1.1 %pack.1 = (bf16[520,128]{1,0:T(8,128)(2,1)S(1)}, bf16[72,128]{1,0:T(8,128)(2,1)S(1)}) custom-call(s32[1,1]{1,0:T(1,128)S(6)} %copy.5.kept, s32[1,1,3]{2,1,0:T(1,128)} %pairs_hbm.1, bf16[64,256]{1,0:T(8,128)(2,1)} %density_ref.1, bf16[1,1,3,4,4096]{4,3,2,1,0:T(4,128)(2,1)} %raw_hbm.1), custom_call_target="tpu_custom_call" | custom-call | tf_op jit(solution)/shard_map/pack/pallas_call | solution.py:171
  5.8 0.1 collective-permute-start
  5.9 1.9 %collective-permute-start.2 = (bf16[520,128]{1,0:T(8,128)(2,1)S(1)}, bf16[520,128]{1,0:T(8,128)(2,1)S(1)}, u32[]{:S(2)}, u32[]{:S(2)}) collective-permute-start(bf16[520,128]{1,0:T(8,128)(2,1)S(1)} %get-tuple-element.15.full_ref.refs_0_), channel_id=1, source_target_pairs={{0,1},{1,0},{2,3},{3,2},{4,7},{5,6},{6,5},{7,4},{8,9},{9,8},{10,11... | collective-permute-start | bytes 399368 | tf_op jit(solution)/shard_map/ppermute | solution.py:169
  7.8 2.5 %collective-permute-start.4 = (bf16[392,128]{1,0:T(8,128)(2,1)S(1)}, bf16[392,128]{1,0:T(8,128)(2,1)S(1)}, u32[]{:S(2)}, u32[]{:S(2)}) collective-permute-start(bf16[392,128]{1,0:T(8,128)(2,1)S(1)} %lean.1), channel_id=1, source_target_pairs={{0,3},{1,2},{2,1},{3,0},{4,5},{5,4},{6,7},{7,6},{8,11},{9,10},{10,... | collective-permute-start | bytes 301064 | tf_op jit(solution)/shard_map/ppermute | solution.py:169
  10.4 2.0 %collective-permute-done.refs_1_.tail = bf16[72,128]{1,0:T(8,128)(2,1)S(1)} collective-permute-done((bf16[72,128]{1,0:T(8,128)(2,1)S(1)}, bf16[72,128]{1,0:T(8,128)(2,1)S(1)}, u32[]{:S(2)}, u32[]{:S(2)}) %collective-permute-start) | collective-permute-done | bytes 18464 | tf_op jit(solution)/shard_map/ppermute | solution.py:198
  12.3 0.0 collective-permute-done.1.raw
  12.3 0.2 relay.1
  12.6 0.6 %collective-permute-done.2.refs_0_.refs_2_ = bf16[520,128]{1,0:T(8,128)(2,1)S(1)} collective-permute-done((bf16[520,128]{1,0:T(8,128)(2,1)S(1)}, bf16[520,128]{1,0:T(8,128)(2,1)S(1)}, u32[]{:S(2)}, u32[]{:S(2)}) %collective-permute-start.2) | collective-permute-done | bytes 133152 | tf_op jit(solution)/shard_map/ppermute | solution.py:169
  13.1 0.0 copy-start
  13.2 0.0 collective-permute-start.3
  13.2 2.2 %collective-permute-done.4.refs_3_ = bf16[392,128]{1,0:T(8,128)(2,1)S(1)} collective-permute-done((bf16[392,128]{1,0:T(8,128)(2,1)S(1)}, bf16[392,128]{1,0:T(8,128)(2,1)S(1)}, u32[]{:S(2)}, u32[]{:S(2)}) %collective-permute-start.4) | collective-permute-done | bytes 100384 | tf_op jit(solution)/shard_map/ppermute | solution.py:169
  15.4 0.0 collective-permute-done.3.swapped
  15.4 0.1 maximum_convert_fusion.meta_ref
  15.5 0.0 copy-done
  15.5 1.2 %exchange.1 = f32[64,256]{1,0:T(8,128)S(1)} custom-call(s32[12]{0:T(128)S(1)} %maximum_convert_fusion.meta_ref, bf16[64,256]{1,0:T(8,128)(2,1)S(1)} %copy-done, bf16[256,192]{1,0:T(8,128)(2,1)S(1)} %get-tuple-element.18.left_ref, bf16[72,128]{1,0:T(8,128)(2,1)S(1)} %collective-permute-done.refs_1_.tail, bf16[192,128]{1,0:T(8,128)(2,1)S(1)} %collective-permute-done.3.swapped, ...), custom_call_target="tpu_custom_call" | custom-call | tf_op jit(solution)/shard_map/exchange/pallas_call | solution.py:229
  16.7 0.1 collective-permute-start.5
  16.8 1.2 %collective-permute-done.5 = f32[64,256]{1,0:T(8,128)S(1)} collective-permute-done((f32[64,256]{1,0:T(8,128)S(1)}, f32[64,256]{1,0:T(8,128)S(1)}, u32[]{:S(2)}, u32[]{:S(2)}) %collective-permute-start.5) | collective-permute-done | bytes 65568 | tf_op jit(solution)/shard_map/ppermute | solution.py:248
  18.0 2.5 %collective-permute-start.8 = (f32[64,256]{1,0:T(8,128)S(1)}, f32[64,256]{1,0:T(8,128)S(1)}, u32[]{:S(2)}, u32[]{:S(2)}) collective-permute-start(f32[64,256]{1,0:T(8,128)S(1)} %add.12), channel_id=1, source_target_pairs={{0,24},{4,28},{8,16},{12,20},{16,8},{20,12},{24,0},{28,4},{1,25},{... | collective-permute-start | bytes 196616 | tf_op jit(solution)/shard_map/ppermute | solution.py:248
  20.6 0.5 %collective-permute-start.7 = (f32[64,256]{1,0:T(8,128)S(1)}, f32[64,256]{1,0:T(8,128)S(1)}, u32[]{:S(2)}, u32[]{:S(2)}) collective-permute-start(f32[64,256]{1,0:T(8,128)S(1)} %add.12), channel_id=1, source_target_pairs={{0,16},{4,20},{8,24},{12,28},{16,0},{20,4},{24,8},{28,12},{1,17},{... | collective-permute-start | bytes 196616 | tf_op jit(solution)/shard_map/ppermute | solution.py:248
  21.1 0.5 %collective-permute-start.6 = (f32[64,256]{1,0:T(8,128)S(1)}, f32[64,256]{1,0:T(8,128)S(1)}, u32[]{:S(2)}, u32[]{:S(2)}) collective-permute-start(f32[64,256]{1,0:T(8,128)S(1)} %add.12), channel_id=1, source_target_pairs={{0,8},{4,12},{8,0},{12,4},{16,24},{20,28},{24,16},{28,20},{1,9},{5... | collective-permute-start | bytes 196616 | tf_op jit(solution)/shard_map/ppermute | solution.py:248
  21.6 1.7 %collective-permute-done.8 = f32[64,256]{1,0:T(8,128)S(1)} collective-permute-done((f32[64,256]{1,0:T(8,128)S(1)}, f32[64,256]{1,0:T(8,128)S(1)}, u32[]{:S(2)}, u32[]{:S(2)}) %collective-permute-start.8) | collective-permute-done | bytes 65568 | tf_op jit(solution)/shard_map/ppermute | solution.py:248
  23.3 1.5 %collective-permute-done.7 = f32[64,256]{1,0:T(8,128)S(1)} collective-permute-done((f32[64,256]{1,0:T(8,128)S(1)}, f32[64,256]{1,0:T(8,128)S(1)}, u32[]{:S(2)}, u32[]{:S(2)}) %collective-permute-start.7) | collective-permute-done | bytes 65568 | tf_op jit(solution)/shard_map/ppermute | solution.py:248
  24.8 0.5 %collective-permute-done.6 = f32[64,256]{1,0:T(8,128)S(1)} collective-permute-done((f32[64,256]{1,0:T(8,128)S(1)}, f32[64,256]{1,0:T(8,128)S(1)}, u32[]{:S(2)}, u32[]{:S(2)}) %collective-permute-start.6) | collective-permute-done | bytes 65568 | tf_op jit(solution)/shard_map/ppermute | solution.py:248
  25.3 0.6 %add_add_fusion = f32[64,256]{1,0:T(8,128)} fusion(f32[64,256]{1,0:T(8,128)S(1)} %collective-permute-done.7, f32[64,256]{1,0:T(8,128)S(1)} %collective-permute-done.8, f32[64,256]{1,0:T(8,128)S(1)} %add.12, f32[64,256]{1,0:T(8,128)S(1)} %collective-permute-done.6), kind=kLoop, calls=%fused_computation | loop fusion | flops 49152 | bytes 327680 | tf_op jit(solution)/shard_map/add | solution.py:250
  (7 shorter events, 0.0 us)
Async XLA Ops:
  0.0 12.3 %collective-permute-start.1 = (bf16[1,1,3,4,4096]{4,3,2,1,0:T(4,128)(2,1)}, bf16[1,1,3,4,4096]{4,3,2,1,0:T(4,128)(2,1)S(1)}, u32[]{:S(2)}, u32[]{:S(2)}) collective-permute-start(bf16[1,1,3,4,4096]{4,3,2,1,0:T(4,128)(2,1)} %raw_hbm.1), channel_id=1, source_target_pairs={{0,2},{1,3},{2,0},{3,1},{4,6},{5,7},{6,4},{7,5},{8,10},{9,11},{10,... | collective-permute-start | bytes 294920 | tf_op jit(solution)/shard_map/ppermute | solution.py:197
  5.8 6.5 %collective-permute-start = (bf16[72,128]{1,0:T(8,128)(2,1)S(1)}, bf16[72,128]{1,0:T(8,128)(2,1)S(1)}, u32[]{:S(2)}, u32[]{:S(2)}) collective-permute-start(bf16[72,128]{1,0:T(8,128)(2,1)S(1)} %get-tuple-element.13), channel_id=1, source_target_pairs={{0,2},{1,3},{2,0},{3,1},{4,6},{5,7},{6,4},{7,5},{8,10},{9,11},{10,... | collective-permute-start | bytes 55304 | tf_op jit(solution)/shard_map/ppermute | solution.py:198
  5.9 7.2 %collective-permute-start.2 = (bf16[520,128]{1,0:T(8,128)(2,1)S(1)}, bf16[520,128]{1,0:T(8,128)(2,1)S(1)}, u32[]{:S(2)}, u32[]{:S(2)}) collective-permute-start(bf16[520,128]{1,0:T(8,128)(2,1)S(1)} %get-tuple-element.15.full_ref.refs_0_), channel_id=1, source_target_pairs={{0,1},{1,0},{2,3},{3,2},{4,7},{5,6},{6,5},{7,4},{8,9},{9,8},{10,11... | collective-permute-start | bytes 399368 | tf_op jit(solution)/shard_map/ppermute | solution.py:169
  7.8 7.6 %collective-permute-start.4 = (bf16[392,128]{1,0:T(8,128)(2,1)S(1)}, bf16[392,128]{1,0:T(8,128)(2,1)S(1)}, u32[]{:S(2)}, u32[]{:S(2)}) collective-permute-start(bf16[392,128]{1,0:T(8,128)(2,1)S(1)} %lean.1), channel_id=1, source_target_pairs={{0,3},{1,2},{2,1},{3,0},{4,5},{5,4},{6,7},{7,6},{8,11},{9,10},{10,... | collective-permute-start | bytes 301064 | tf_op jit(solution)/shard_map/ppermute | solution.py:169
  13.1 2.4 %copy-start = (bf16[64,256]{1,0:T(8,128)(2,1)S(1)}, bf16[64,256]{1,0:T(8,128)(2,1)}, u32[]{:S(2)}) copy-start(bf16[64,256]{1,0:T(8,128)(2,1)} %density_ref.1) | copy-start | bytes 98308
  13.2 2.3 %collective-permute-start.3 = (bf16[192,128]{1,0:T(8,128)(2,1)S(1)}, bf16[192,128]{1,0:T(8,128)(2,1)S(1)}, u32[]{:S(2)}, u32[]{:S(2)}) collective-permute-start(bf16[192,128]{1,0:T(8,128)(2,1)S(1)} %merge.1), channel_id=1, source_target_pairs={{0,4},{4,0},{8,12},{12,8},{16,20},{20,16},{24,28},{28,24},{1,5},{5... | collective-permute-start | bytes 147464 | tf_op jit(solution)/shard_map/ppermute | solution.py:211
  16.7 1.3 %collective-permute-start.5 = (f32[64,256]{1,0:T(8,128)S(1)}, f32[64,256]{1,0:T(8,128)S(1)}, u32[]{:S(2)}, u32[]{:S(2)}) collective-permute-start(f32[64,256]{1,0:T(8,128)S(1)} %exchange.1), channel_id=1, source_target_pairs={{0,4},{4,0},{8,12},{12,8},{16,20},{20,16},{24,28},{28,24},{1,5},{5... | collective-permute-start | bytes 196616 | tf_op jit(solution)/shard_map/ppermute | solution.py:248
  18.0 5.3 %collective-permute-start.8 = (f32[64,256]{1,0:T(8,128)S(1)}, f32[64,256]{1,0:T(8,128)S(1)}, u32[]{:S(2)}, u32[]{:S(2)}) collective-permute-start(f32[64,256]{1,0:T(8,128)S(1)} %add.12), channel_id=1, source_target_pairs={{0,24},{4,28},{8,16},{12,20},{16,8},{20,12},{24,0},{28,4},{1,25},{... | collective-permute-start | bytes 196616 | tf_op jit(solution)/shard_map/ppermute | solution.py:248
  20.6 4.3 %collective-permute-start.7 = (f32[64,256]{1,0:T(8,128)S(1)}, f32[64,256]{1,0:T(8,128)S(1)}, u32[]{:S(2)}, u32[]{:S(2)}) collective-permute-start(f32[64,256]{1,0:T(8,128)S(1)} %add.12), channel_id=1, source_target_pairs={{0,16},{4,20},{8,24},{12,28},{16,0},{20,4},{24,8},{28,12},{1,17},{... | collective-permute-start | bytes 196616 | tf_op jit(solution)/shard_map/ppermute | solution.py:248
  21.1 4.3 %collective-permute-start.6 = (f32[64,256]{1,0:T(8,128)S(1)}, f32[64,256]{1,0:T(8,128)S(1)}, u32[]{:S(2)}, u32[]{:S(2)}) collective-permute-start(f32[64,256]{1,0:T(8,128)S(1)} %add.12), channel_id=1, source_target_pairs={{0,8},{4,12},{8,0},{12,4},{16,24},{20,28},{24,16},{28,20},{1,9},{5... | collective-permute-start | bytes 196616 | tf_op jit(solution)/shard_map/ppermute | solution.py:248

commit v23 on v22

--- a/solution.py
+++ b/solution.py
@@ -38,7 +38,7 @@
 
 
 def pack_kernel(
-    orb, kept, pairs_hbm, density_hbm, raw_hbm, full_ref, tail_ref, pairs, rows, raw, sems
+    orb, kept, pairs_hbm, density_hbm, raw_hbm, full_ref, pairs, rows, raw, sems
 ):
     copies = [
         pltpu.make_async_copy(src, dst, sems.at[i])
@@ -48,30 +48,34 @@
         copy.start()
     for copy in copies[1:]:
         copy.wait()
-    height = BS // 2
-    near = pl.multiple_of(core_parity() * height, height)
     tiles = rows.shape[1] // LANES
     size = full_ref.shape[0] - tiles * BS - NOTE
     for t in range(tiles):
         lanes = slice(t * LANES, (t + 1) * LANES)
         full_ref[size + t * BS : size + (t + 1) * BS] = rows[:, lanes]
-        tail_ref[t * height : (t + 1) * height] = rows[pl.ds(near, height), lanes]
     shape = (NOTE, LANES)
     lane = lax.broadcasted_iota(jnp.int32, shape, 1)
     note = jnp.zeros(shape, jnp.int32)
     for j in range(pairs.shape[2]):
         note = jnp.where(lane == j, jnp.where(j < kept[0, 0], pairs[0, 0, j], orb), note)
-    note = note.astype(jnp.float32).astype(jnp.bfloat16)
-    full_ref[size + tiles * BS :] = note
-    tail_ref[tiles * height :] = note
+    full_ref[size + tiles * BS :] = note.astype(jnp.float32).astype(jnp.bfloat16)
     copies[0].wait()
     lay_blocks(raw[0, 0], full_ref)
 
 
-def lean_kernel(full_ref, out_ref):
+def tail_kernel(size, full_ref, out_ref):
+    height = BS // 2
+    tiles = (out_ref.shape[0] - NOTE) // height
+    for t in range(tiles):
+        first = pl.multiple_of(size + t * BS + core_parity() * height, height)
+        out_ref[t * height : (t + 1) * height] = full_ref[pl.ds(first, height)]
+    out_ref[tiles * height :] = full_ref[full_ref.shape[0] - NOTE :]
+
+
+def lean_kernel(full_ref, tail_ref, out_ref):
     size = out_ref.shape[0] - NOTE
     out_ref[:size] = full_ref[:size]
-    out_ref[size:] = full_ref[full_ref.shape[0] - NOTE :]
+    out_ref[size:] = tail_ref[tail_ref.shape[0] - NOTE :]
 
 
 def relay_kernel(slots, aux_width, raw, full_ref, out_ref, left_ref):
@@ -168,11 +172,11 @@
         ]
         return lax.ppermute(x, ("aux", "orb"), perm)
 
-    full, tail = pl.pallas_call(
+    full = pl.pallas_call(
         functools.partial(pack_kernel, orb),
-        out_shape=[array(size + rows + NOTE), array(rows // 2 + NOTE)],
+        out_shape=array(size + rows + NOTE),
         in_specs=[smem, hbm, hbm, hbm],
-        out_specs=[vmem] * 2,
+        out_specs=vmem,
         scratch_shapes=[
             pltpu.SMEM(pairs.shape, jnp.int32),
             pltpu.VMEM(density.shape, jnp.bfloat16),
@@ -185,14 +189,22 @@
         kept,
         *(pltpu.with_memory_space_constraint(a, pltpu.HBM) for a in (pairs, density, tensor_blocks)),
     )
+    tail = pl.pallas_call(
+        functools.partial(tail_kernel, size),
+        out_shape=array(rows // 2 + NOTE),
+        in_specs=[vmem],
+        out_specs=vmem,
+        compiler_params=params,
+        name="tail",
+    )(full)
     lean = pl.pallas_call(
         lean_kernel,
         out_shape=array(size + NOTE),
-        in_specs=[vmem],
+        in_specs=[vmem] * 2,
         out_specs=vmem,
         compiler_params=params,
         name="lean",
-    )(full)
+    )(full, tail)
     across = [(i, (i + orb // 2) % orb) for i in range(orb)]
     raw = lax.ppermute(tensor_blocks, "orb", across)
     tail_in = lax.ppermute(tail, "orb", across)

time: 26.1 us -> 25.5 us (0.977)
  waiting for transfers between devices: 9.74 us -> 8.98 us
    ppermute x2, waiting for transfers between devices: 2.8 us -> 1.55 us  [shift(): return lax.ppermute(x, ('aux', 'orb'), perm)]
    ppermute x1, waiting for transfers between devices: 1.96 us -> 2.3 us  [shards(): tail_in = lax.ppermute(tail, 'orb', across)]
    ppermute x1, starting transfers between devices: 0.07 us -> 0.34 us  [shards(): tail_in = lax.ppermute(tail, 'orb', across)]
    pallas_call x1 -> x2, Pallas kernels: 1.14 us -> 1.15 us  [the longest x1 1.14 us: shards(): pl.pallas_call(functools.partial(pack_kernel, orb), out_shape=array(size...]
  transfers between devices with their start and end apart: 9 -> 9, of which waited for: 7 -> 8; matrix products, arithmetic and copies ran while one was open for 0% -> 0% of each run, Pallas kernels for 5% -> 5%
where the time goes in v23:
time: 25.5 us; the launch traced here: 25.4 us
  starting transfers between devices  12.3 us (48%)
  waiting for transfers between devices  8.98 us (35%)
  Pallas kernels  2.59 us (10%)
  other arithmetic  0.74 us (3%)
  between operations  0.71 us (3%)
    ppermute x4, waiting for transfers between devices, shards(): lax.ppermute(parts, 'aux', [(i, i ^ way * step) for i in range(aux)])  5.03 us
    ppermute x2, starting transfers between devices, shift(): return lax.ppermute(x, ('aux', 'orb'), perm)  4.18 us
    ppermute x1, starting transfers between devices, shards(): raw = lax.ppermute(tensor_blocks, 'orb', across)  4.04 us
    ppermute x4, starting transfers between devices, shards(): lax.ppermute(parts, 'aux', [(i, i ^ way * step) for i in range(aux)])  3.78 us
    ppermute x1, waiting for transfers between devices, shards(): tail_in = lax.ppermute(tail, 'orb', across)  2.3 us
    ppermute x2, waiting for transfers between devices, shift(): return lax.ppermute(x, ('aux', 'orb'), perm)  1.55 us
    pallas_call x1, Pallas kernels, shards(): pl.pallas_call(functools.partial(exchange_kernel, orb, slots, aux_width),...  1.21 us
    pallas_call x1, Pallas kernels, shards(): pl.pallas_call(functools.partial(pack_kernel, orb), out_shape=array(size...  1.14 us
  transfers between devices with their start and end apart: 9, of which 8 were waited for; matrix products, arithmetic and copies ran while one was open for 0% of the time, Pallas kernels for 5%

profile of v23, /device:TPU:0, one launch (start us, length us, event | category | flops | bytes accessed | tf_op | source)
XLA Modules:
  0.0 25.4 jit_solution(12548786939810231047)
XLA Ops:
  0.0 4.0 %collective-permute-start.1 = (bf16[1,1,3,4,4096]{4,3,2,1,0:T(4,128)(2,1)}, bf16[1,1,3,4,4096]{4,3,2,1,0:T(4,128)(2,1)S(1)}, u32[]{:S(2)}, u32[]{:S(2)}) collective-permute-start(bf16[1,1,3,4,4096]{4,3,2,1,0:T(4,128)(2,1)} %raw_hbm.1), channel_id=1, source_target_pairs={{0,2},{1,3},{2,0},{3,1},{4,6},{5,7},{6,4},{7,5},{8,10},{9,11},{10,... | collective-permute-start | bytes 294920 | tf_op jit(solution)/shard_map/ppermute | solution.py:209
  4.7 1.1 %pack.1.full_ref.refs_0_ = bf16[520,128]{1,0:T(8,128)(2,1)S(1)} custom-call(s32[1,1]{1,0:T(1,128)S(6)} %copy.5.kept, s32[1,1,3]{2,1,0:T(1,128)} %pairs_hbm.1, bf16[64,256]{1,0:T(8,128)(2,1)} %density_ref.1, bf16[1,1,3,4,4096]{4,3,2,1,0:T(4,128)(2,1)} %raw_hbm.1), custom_call_target="tpu_custom_call" | custom-call | tf_op jit(solution)/shard_map/pack/pallas_call | solution.py:175
  5.8 1.6 %collective-permute-start.2 = (bf16[520,128]{1,0:T(8,128)(2,1)S(1)}, bf16[520,128]{1,0:T(8,128)(2,1)S(1)}, u32[]{:S(2)}, u32[]{:S(2)}) collective-permute-start(bf16[520,128]{1,0:T(8,128)(2,1)S(1)} %pack.1.full_ref.refs_0_), channel_id=1, source_target_pairs={{0,1},{1,0},{2,3},{3,2},{4,7},{5,6},{6,5},{7,4},{8,9},{9,8},{10,11... | collective-permute-start | bytes 399368 | tf_op jit(solution)/shard_map/ppermute | solution.py:173
  7.5 0.3 %collective-permute-start = (bf16[72,128]{1,0:T(8,128)(2,1)S(1)}, bf16[72,128]{1,0:T(8,128)(2,1)S(1)}, u32[]{:S(2)}, u32[]{:S(2)}) collective-permute-start(bf16[72,128]{1,0:T(8,128)(2,1)S(1)} %tail.1.tail_ref), channel_id=1, source_target_pairs={{0,2},{1,3},{2,0},{3,1},{4,6},{5,7},{6,4},{7,5},{8,10},{9,11},{10,... | collective-permute-start | bytes 55304 | tf_op jit(solution)/shard_map/ppermute | solution.py:210
  7.8 2.5 %collective-permute-start.4 = (bf16[392,128]{1,0:T(8,128)(2,1)S(1)}, bf16[392,128]{1,0:T(8,128)(2,1)S(1)}, u32[]{:S(2)}, u32[]{:S(2)}) collective-permute-start(bf16[392,128]{1,0:T(8,128)(2,1)S(1)} %lean.1), channel_id=1, source_target_pairs={{0,3},{1,2},{2,1},{3,0},{4,5},{5,4},{6,7},{7,6},{8,11},{9,10},{10,... | collective-permute-start | bytes 301064 | tf_op jit(solution)/shard_map/ppermute | solution.py:173
  10.4 2.3 %collective-permute-done.refs_1_.tail = bf16[72,128]{1,0:T(8,128)(2,1)S(1)} collective-permute-done((bf16[72,128]{1,0:T(8,128)(2,1)S(1)}, bf16[72,128]{1,0:T(8,128)(2,1)S(1)}, u32[]{:S(2)}, u32[]{:S(2)}) %collective-permute-start) | collective-permute-done | bytes 18464 | tf_op jit(solution)/shard_map/ppermute | solution.py:210
  12.7 0.0 collective-permute-done.1.raw
  12.7 0.2 relay.1
  12.9 0.4 %collective-permute-done.2.refs_0_.refs_2_ = bf16[520,128]{1,0:T(8,128)(2,1)S(1)} collective-permute-done((bf16[520,128]{1,0:T(8,128)(2,1)S(1)}, bf16[520,128]{1,0:T(8,128)(2,1)S(1)}, u32[]{:S(2)}, u32[]{:S(2)}) %collective-permute-start.2) | collective-permute-done | bytes 133152 | tf_op jit(solution)/shard_map/ppermute | solution.py:173
  13.4 0.0 copy-start
  13.4 0.0 collective-permute-start.3
  13.4 1.1 %collective-permute-done.4.refs_3_ = bf16[392,128]{1,0:T(8,128)(2,1)S(1)} collective-permute-done((bf16[392,128]{1,0:T(8,128)(2,1)S(1)}, bf16[392,128]{1,0:T(8,128)(2,1)S(1)}, u32[]{:S(2)}, u32[]{:S(2)}) %collective-permute-start.4) | collective-permute-done | bytes 100384 | tf_op jit(solution)/shard_map/ppermute | solution.py:173
  14.5 0.1 collective-permute-done.3.swapped
  14.6 0.1 maximum_convert_fusion.meta_ref
  14.7 0.0 copy-done
  14.7 1.2 %exchange.1 = f32[64,256]{1,0:T(8,128)S(1)} custom-call(s32[12]{0:T(128)S(1)} %maximum_convert_fusion.meta_ref, bf16[64,256]{1,0:T(8,128)(2,1)S(1)} %copy-done, bf16[256,192]{1,0:T(8,128)(2,1)S(1)} %get-tuple-element.14.left_ref, bf16[72,128]{1,0:T(8,128)(2,1)S(1)} %collective-permute-done.refs_1_.tail, bf16[192,128]{1,0:T(8,128)(2,1)S(1)} %collective-permute-done.3.swapped, ...), custom_call_target="tpu_custom_call" | custom-call | tf_op jit(solution)/shard_map/exchange/pallas_call | solution.py:241
  15.9 0.2 collective-permute-start.5
  16.1 1.1 %collective-permute-done.5 = f32[64,256]{1,0:T(8,128)S(1)} collective-permute-done((f32[64,256]{1,0:T(8,128)S(1)}, f32[64,256]{1,0:T(8,128)S(1)}, u32[]{:S(2)}, u32[]{:S(2)}) %collective-permute-start.5) | collective-permute-done | bytes 65568 | tf_op jit(solution)/shard_map/ppermute | solution.py:260
  17.2 2.7 %collective-permute-start.8 = (f32[64,256]{1,0:T(8,128)S(1)}, f32[64,256]{1,0:T(8,128)S(1)}, u32[]{:S(2)}, u32[]{:S(2)}) collective-permute-start(f32[64,256]{1,0:T(8,128)S(1)} %add.12), channel_id=1, source_target_pairs={{0,24},{4,28},{8,16},{12,20},{16,8},{20,12},{24,0},{28,4},{1,25},{... | collective-permute-start | bytes 196616 | tf_op jit(solution)/shard_map/ppermute | solution.py:260
  19.9 0.5 %collective-permute-start.7 = (f32[64,256]{1,0:T(8,128)S(1)}, f32[64,256]{1,0:T(8,128)S(1)}, u32[]{:S(2)}, u32[]{:S(2)}) collective-permute-start(f32[64,256]{1,0:T(8,128)S(1)} %add.12), channel_id=1, source_target_pairs={{0,16},{4,20},{8,24},{12,28},{16,0},{20,4},{24,8},{28,12},{1,17},{... | collective-permute-start | bytes 196616 | tf_op jit(solution)/shard_map/ppermute | solution.py:260
  20.5 0.3 %collective-permute-start.6 = (f32[64,256]{1,0:T(8,128)S(1)}, f32[64,256]{1,0:T(8,128)S(1)}, u32[]{:S(2)}, u32[]{:S(2)}) collective-permute-start(f32[64,256]{1,0:T(8,128)S(1)} %add.12), channel_id=1, source_target_pairs={{0,8},{4,12},{8,0},{12,4},{16,24},{20,28},{24,16},{28,20},{1,9},{5... | collective-permute-start | bytes 196616 | tf_op jit(solution)/shard_map/ppermute | solution.py:260
  20.8 1.7 %collective-permute-done.8 = f32[64,256]{1,0:T(8,128)S(1)} collective-permute-done((f32[64,256]{1,0:T(8,128)S(1)}, f32[64,256]{1,0:T(8,128)S(1)}, u32[]{:S(2)}, u32[]{:S(2)}) %collective-permute-start.8) | collective-permute-done | bytes 65568 | tf_op jit(solution)/shard_map/ppermute | solution.py:260
  22.5 1.8 %collective-permute-done.7 = f32[64,256]{1,0:T(8,128)S(1)} collective-permute-done((f32[64,256]{1,0:T(8,128)S(1)}, f32[64,256]{1,0:T(8,128)S(1)}, u32[]{:S(2)}, u32[]{:S(2)}) %collective-permute-start.7) | collective-permute-done | bytes 65568 | tf_op jit(solution)/shard_map/ppermute | solution.py:260
  24.2 0.5 %collective-permute-done.6 = f32[64,256]{1,0:T(8,128)S(1)} collective-permute-done((f32[64,256]{1,0:T(8,128)S(1)}, f32[64,256]{1,0:T(8,128)S(1)}, u32[]{:S(2)}, u32[]{:S(2)}) %collective-permute-start.6) | collective-permute-done | bytes 65568 | tf_op jit(solution)/shard_map/ppermute | solution.py:260
  24.7 0.6 %add_add_fusion = f32[64,256]{1,0:T(8,128)} fusion(f32[64,256]{1,0:T(8,128)S(1)} %collective-permute-done.7, f32[64,256]{1,0:T(8,128)S(1)} %collective-permute-done.8, f32[64,256]{1,0:T(8,128)S(1)} %add.12, f32[64,256]{1,0:T(8,128)S(1)} %collective-permute-done.6), kind=kLoop, calls=%fused_computation | loop fusion | flops 49152 | bytes 327680 | tf_op jit(solution)/shard_map/add | solution.py:262
  (8 shorter events, 0.0 us)
Async XLA Ops:
  0.0 12.7 %collective-permute-start.1 = (bf16[1,1,3,4,4096]{4,3,2,1,0:T(4,128)(2,1)}, bf16[1,1,3,4,4096]{4,3,2,1,0:T(4,128)(2,1)S(1)}, u32[]{:S(2)}, u32[]{:S(2)}) collective-permute-start(bf16[1,1,3,4,4096]{4,3,2,1,0:T(4,128)(2,1)} %raw_hbm.1), channel_id=1, source_target_pairs={{0,2},{1,3},{2,0},{3,1},{4,6},{5,7},{6,4},{7,5},{8,10},{9,11},{10,... | collective-permute-start | bytes 294920 | tf_op jit(solution)/shard_map/ppermute | solution.py:209
  5.8 7.5 %collective-permute-start.2 = (bf16[520,128]{1,0:T(8,128)(2,1)S(1)}, bf16[520,128]{1,0:T(8,128)(2,1)S(1)}, u32[]{:S(2)}, u32[]{:S(2)}) collective-permute-start(bf16[520,128]{1,0:T(8,128)(2,1)S(1)} %pack.1.full_ref.refs_0_), channel_id=1, source_target_pairs={{0,1},{1,0},{2,3},{3,2},{4,7},{5,6},{6,5},{7,4},{8,9},{9,8},{10,11... | collective-permute-start | bytes 399368 | tf_op jit(solution)/shard_map/ppermute | solution.py:173
  7.5 5.2 %collective-permute-start = (bf16[72,128]{1,0:T(8,128)(2,1)S(1)}, bf16[72,128]{1,0:T(8,128)(2,1)S(1)}, u32[]{:S(2)}, u32[]{:S(2)}) collective-permute-start(bf16[72,128]{1,0:T(8,128)(2,1)S(1)} %tail.1.tail_ref), channel_id=1, source_target_pairs={{0,2},{1,3},{2,0},{3,1},{4,6},{5,7},{6,4},{7,5},{8,10},{9,11},{10,... | collective-permute-start | bytes 55304 | tf_op jit(solution)/shard_map/ppermute | solution.py:210
  7.8 6.7 %collective-permute-start.4 = (bf16[392,128]{1,0:T(8,128)(2,1)S(1)}, bf16[392,128]{1,0:T(8,128)(2,1)S(1)}, u32[]{:S(2)}, u32[]{:S(2)}) collective-permute-start(bf16[392,128]{1,0:T(8,128)(2,1)S(1)} %lean.1), channel_id=1, source_target_pairs={{0,3},{1,2},{2,1},{3,0},{4,5},{5,4},{6,7},{7,6},{8,11},{9,10},{10,... | collective-permute-start | bytes 301064 | tf_op jit(solution)/shard_map/ppermute | solution.py:173
  13.4 1.3 %copy-start = (bf16[64,256]{1,0:T(8,128)(2,1)S(1)}, bf16[64,256]{1,0:T(8,128)(2,1)}, u32[]{:S(2)}) copy-start(bf16[64,256]{1,0:T(8,128)(2,1)} %density_ref.1) | copy-start | bytes 98308
  13.4 1.2 %collective-permute-start.3 = (bf16[192,128]{1,0:T(8,128)(2,1)S(1)}, bf16[192,128]{1,0:T(8,128)(2,1)S(1)}, u32[]{:S(2)}, u32[]{:S(2)}) collective-permute-start(bf16[192,128]{1,0:T(8,128)(2,1)S(1)} %merge.1), channel_id=1, source_target_pairs={{0,4},{4,0},{8,12},{12,8},{16,20},{20,16},{24,28},{28,24},{1,5},{5... | collective-permute-start | bytes 147464 | tf_op jit(solution)/shard_map/ppermute | solution.py:223
  15.9 1.3 %collective-permute-start.5 = (f32[64,256]{1,0:T(8,128)S(1)}, f32[64,256]{1,0:T(8,128)S(1)}, u32[]{:S(2)}, u32[]{:S(2)}) collective-permute-start(f32[64,256]{1,0:T(8,128)S(1)} %exchange.1), channel_id=1, source_target_pairs={{0,4},{4,0},{8,12},{12,8},{16,20},{20,16},{24,28},{28,24},{1,5},{5... | collective-permute-start | bytes 196616 | tf_op jit(solution)/shard_map/ppermute | solution.py:260
  17.2 5.2 %collective-permute-start.8 = (f32[64,256]{1,0:T(8,128)S(1)}, f32[64,256]{1,0:T(8,128)S(1)}, u32[]{:S(2)}, u32[]{:S(2)}) collective-permute-start(f32[64,256]{1,0:T(8,128)S(1)} %add.12), channel_id=1, source_target_pairs={{0,24},{4,28},{8,16},{12,20},{16,8},{20,12},{24,0},{28,4},{1,25},{... | collective-permute-start | bytes 196616 | tf_op jit(solution)/shard_map/ppermute | solution.py:260
  19.9 4.3 %collective-permute-start.7 = (f32[64,256]{1,0:T(8,128)S(1)}, f32[64,256]{1,0:T(8,128)S(1)}, u32[]{:S(2)}, u32[]{:S(2)}) collective-permute-start(f32[64,256]{1,0:T(8,128)S(1)} %add.12), channel_id=1, source_target_pairs={{0,16},{4,20},{8,24},{12,28},{16,0},{20,4},{24,8},{28,12},{1,17},{... | collective-permute-start | bytes 196616 | tf_op jit(solution)/shard_map/ppermute | solution.py:260
  20.5 4.3 %collective-permute-start.6 = (f32[64,256]{1,0:T(8,128)S(1)}, f32[64,256]{1,0:T(8,128)S(1)}, u32[]{:S(2)}, u32[]{:S(2)}) collective-permute-start(f32[64,256]{1,0:T(8,128)S(1)} %add.12), channel_id=1, source_target_pairs={{0,8},{4,12},{8,0},{12,4},{16,24},{20,28},{24,16},{28,20},{1,9},{5... | collective-permute-start | bytes 196616 | tf_op jit(solution)/shard_map/ppermute | solution.py:260

commit v24 on v23

--- a/solution.py
+++ b/solution.py
@@ -63,19 +63,20 @@
     lay_blocks(raw[0, 0], full_ref)
 
 
-def tail_kernel(size, full_ref, out_ref):
+def lean_kernel(full_ref, out_ref):
+    size = out_ref.shape[0] - NOTE
+    out_ref[:size] = full_ref[:size]
+    out_ref[size:] = full_ref[full_ref.shape[0] - NOTE :]
+
+
+def tail_kernel(full_ref, lean_ref, out_ref):
     height = BS // 2
+    size = lean_ref.shape[0] - NOTE
     tiles = (out_ref.shape[0] - NOTE) // height
     for t in range(tiles):
         first = pl.multiple_of(size + t * BS + core_parity() * height, height)
         out_ref[t * height : (t + 1) * height] = full_ref[pl.ds(first, height)]
-    out_ref[tiles * height :] = full_ref[full_ref.shape[0] - NOTE :]
-
-
-def lean_kernel(full_ref, tail_ref, out_ref):
-    size = out_ref.shape[0] - NOTE
-    out_ref[:size] = full_ref[:size]
-    out_ref[size:] = tail_ref[tail_ref.shape[0] - NOTE :]
+    out_ref[tiles * height :] = lean_ref[size:]
 
 
 def relay_kernel(slots, aux_width, raw, full_ref, out_ref, left_ref):
@@ -189,22 +190,22 @@
         kept,
         *(pltpu.with_memory_space_constraint(a, pltpu.HBM) for a in (pairs, density, tensor_blocks)),
     )
-    tail = pl.pallas_call(
-        functools.partial(tail_kernel, size),
-        out_shape=array(rows // 2 + NOTE),
-        in_specs=[vmem],
-        out_specs=vmem,
-        compiler_params=params,
-        name="tail",
-    )(full)
     lean = pl.pallas_call(
         lean_kernel,
         out_shape=array(size + NOTE),
+        in_specs=[vmem],
+        out_specs=vmem,
+        compiler_params=params,
+        name="lean",
+    )(full)
+    tail = pl.pallas_call(
+        tail_kernel,
+        out_shape=array(rows // 2 + NOTE),
         in_specs=[vmem] * 2,
         out_specs=vmem,
         compiler_params=params,
-        name="lean",
-    )(full, tail)
+        name="tail",
+    )(full, lean)
     across = [(i, (i + orb // 2) % orb) for i in range(orb)]
     raw = lax.ppermute(tensor_blocks, "orb", across)
     tail_in = lax.ppermute(tail, "orb", across)

time: 25.5 us -> 27.3 us (1.071)
  waiting for transfers between devices: 8.98 us -> 11.5 us
  starting transfers between devices: 12.3 us -> 11.5 us
    ppermute x1, waiting for transfers between devices: 2.3 us -> 5.46 us  [shards(): tail_in = lax.ppermute(tail, 'orb', across)]
    ppermute x2, starting transfers between devices: 4.18 us -> 1.71 us  [shift(): return lax.ppermute(x, ('aux', 'orb'), perm)]
    ppermute x2, waiting for transfers between devices: 1.55 us -> 0.01 us  [shift(): return lax.ppermute(x, ('aux', 'orb'), perm)]
    ppermute x1, starting transfers between devices: 0.34 us -> 1.88 us  [shards(): tail_in = lax.ppermute(tail, 'orb', across)]
    ppermute x1, waiting for transfers between devices: 0.1 us -> 1.2 us  [shards(): swapped = lax.ppermute(merged, 'aux', [(i, i ^ 1) for i in range(aux)])]
  transfers between devices with their start and end apart: 9 -> 9, of which waited for: 8 -> 6; matrix products, arithmetic and copies ran while one was open for 0% -> 0% of each run, Pallas kernels for 5% -> 5%
where the time goes in v24:
time: 27.3 us; the launch traced here: 27.1 us
  starting transfers between devices  11.5 us (42%)
  waiting for transfers between devices  11.5 us (42%)
  Pallas kernels  2.61 us (10%)
  between operations  0.76 us (3%)
  other arithmetic  0.74 us (3%)
    ppermute x1, waiting for transfers between devices, shards(): tail_in = lax.ppermute(tail, 'orb', across)  5.46 us
    ppermute x4, waiting for transfers between devices, shards(): lax.ppermute(parts, 'aux', [(i, i ^ way * step) for i in range(aux)])  4.87 us
    ppermute x1, starting transfers between devices, shards(): raw = lax.ppermute(tensor_blocks, 'orb', across)  4.04 us
    ppermute x4, starting transfers between devices, shards(): lax.ppermute(parts, 'aux', [(i, i ^ way * step) for i in range(aux)])  3.78 us
    ppermute x1, starting transfers between devices, shards(): tail_in = lax.ppermute(tail, 'orb', across)  1.88 us
    ppermute x2, starting transfers between devices, shift(): return lax.ppermute(x, ('aux', 'orb'), perm)  1.71 us
    pallas_call x1, Pallas kernels, shards(): pl.pallas_call(functools.partial(exchange_kernel, orb, slots, aux_width),...  1.21 us
    ppermute x1, waiting for transfers between devices, shards(): swapped = lax.ppermute(merged, 'aux', [(i, i ^ 1) for i in range(aux)])  1.2 us
  transfers between devices with their start and end apart: 9, of which 6 were waited for; matrix products, arithmetic and copies ran while one was open for 0% of the time, Pallas kernels for 5%

profile of v24, /device:TPU:0, one launch (start us, length us, event | category | flops | bytes accessed | tf_op | source)
XLA Modules:
  0.0 27.1 jit_solution(6091009615970192702)
XLA Ops:
  0.0 4.0 %collective-permute-start.1 = (bf16[1,1,3,4,4096]{4,3,2,1,0:T(4,128)(2,1)}, bf16[1,1,3,4,4096]{4,3,2,1,0:T(4,128)(2,1)S(1)}, u32[]{:S(2)}, u32[]{:S(2)}) collective-permute-start(bf16[1,1,3,4,4096]{4,3,2,1,0:T(4,128)(2,1)} %raw_hbm.1), channel_id=1, source_target_pairs={{0,2},{1,3},{2,0},{3,1},{4,6},{5,7},{6,4},{7,5},{8,10},{9,11},{10,... | collective-permute-start | bytes 294920 | tf_op jit(solution)/shard_map/ppermute | solution.py:210
  4.7 1.1 %pack.1.full_ref.refs_0_ = bf16[520,128]{1,0:T(8,128)(2,1)S(1)} custom-call(s32[1,1]{1,0:T(1,128)S(6)} %copy.5.kept, s32[1,1,3]{2,1,0:T(1,128)} %pairs_hbm.1, bf16[64,256]{1,0:T(8,128)(2,1)} %density_ref.1, bf16[1,1,3,4,4096]{4,3,2,1,0:T(4,128)(2,1)} %raw_hbm.1), custom_call_target="tpu_custom_call" | custom-call | tf_op jit(solution)/shard_map/pack/pallas_call | solution.py:176
  5.8 1.6 %collective-permute-start.2 = (bf16[520,128]{1,0:T(8,128)(2,1)S(1)}, bf16[520,128]{1,0:T(8,128)(2,1)S(1)}, u32[]{:S(2)}, u32[]{:S(2)}) collective-permute-start(bf16[520,128]{1,0:T(8,128)(2,1)S(1)} %pack.1.full_ref.refs_0_), channel_id=1, source_target_pairs={{0,1},{1,0},{2,3},{3,2},{4,7},{5,6},{6,5},{7,4},{8,9},{9,8},{10,11... | collective-permute-start | bytes 399368 | tf_op jit(solution)/shard_map/ppermute | solution.py:174
  7.5 0.1 collective-permute-start.4
  7.6 1.9 %collective-permute-start = (bf16[72,128]{1,0:T(8,128)(2,1)S(1)}, bf16[72,128]{1,0:T(8,128)(2,1)S(1)}, u32[]{:S(2)}, u32[]{:S(2)}) collective-permute-start(bf16[72,128]{1,0:T(8,128)(2,1)S(1)} %tail.1), channel_id=1, source_target_pairs={{0,2},{1,3},{2,0},{3,1},{4,6},{5,7},{6,4},{7,5},{8,10},{9,11},{10,... | collective-permute-start | bytes 55304 | tf_op jit(solution)/shard_map/ppermute | solution.py:211
  9.5 5.5 %collective-permute-done.refs_1_.tail = bf16[72,128]{1,0:T(8,128)(2,1)S(1)} collective-permute-done((bf16[72,128]{1,0:T(8,128)(2,1)S(1)}, bf16[72,128]{1,0:T(8,128)(2,1)S(1)}, u32[]{:S(2)}, u32[]{:S(2)}) %collective-permute-start) | collective-permute-done | bytes 18464 | tf_op jit(solution)/shard_map/ppermute | solution.py:211
  14.9 0.0 collective-permute-done.1.raw
  14.9 0.2 relay.1
  15.2 0.0 collective-permute-done.2.refs_0_.refs_2_
  15.2 0.0 copy-start
  15.2 0.1 collective-permute-start.3
  15.3 0.0 collective-permute-done.4.refs_3_
  15.3 1.2 %collective-permute-done.3.swapped = bf16[192,128]{1,0:T(8,128)(2,1)S(1)} collective-permute-done((bf16[192,128]{1,0:T(8,128)(2,1)S(1)}, bf16[192,128]{1,0:T(8,128)(2,1)S(1)}, u32[]{:S(2)}, u32[]{:S(2)}) %collective-permute-start.3) | collective-permute-done | bytes 49184 | tf_op jit(solution)/shard_map/ppermute | solution.py:224
  16.5 0.1 maximum_convert_fusion.meta_ref
  16.6 0.0 copy-done
  16.6 1.2 %exchange.1 = f32[64,256]{1,0:T(8,128)S(1)} custom-call(s32[12]{0:T(128)S(1)} %maximum_convert_fusion.meta_ref, bf16[64,256]{1,0:T(8,128)(2,1)S(1)} %copy-done, bf16[256,192]{1,0:T(8,128)(2,1)S(1)} %get-tuple-element.14.left_ref, bf16[72,128]{1,0:T(8,128)(2,1)S(1)} %collective-permute-done.refs_1_.tail, bf16[192,128]{1,0:T(8,128)(2,1)S(1)} %collective-permute-done.3.swapped, ...), custom_call_target="tpu_custom_call" | custom-call | tf_op jit(solution)/shard_map/exchange/pallas_call | solution.py:242
  17.8 0.2 collective-permute-start.5
  18.0 1.1 %collective-permute-done.5 = f32[64,256]{1,0:T(8,128)S(1)} collective-permute-done((f32[64,256]{1,0:T(8,128)S(1)}, f32[64,256]{1,0:T(8,128)S(1)}, u32[]{:S(2)}, u32[]{:S(2)}) %collective-permute-start.5) | collective-permute-done | bytes 65568 | tf_op jit(solution)/shard_map/ppermute | solution.py:261
  19.2 2.6 %collective-permute-start.8 = (f32[64,256]{1,0:T(8,128)S(1)}, f32[64,256]{1,0:T(8,128)S(1)}, u32[]{:S(2)}, u32[]{:S(2)}) collective-permute-start(f32[64,256]{1,0:T(8,128)S(1)} %add.12), channel_id=1, source_target_pairs={{0,24},{4,28},{8,16},{12,20},{16,8},{20,12},{24,0},{28,4},{1,25},{... | collective-permute-start | bytes 196616 | tf_op jit(solution)/shard_map/ppermute | solution.py:261
  21.7 0.5 %collective-permute-start.7 = (f32[64,256]{1,0:T(8,128)S(1)}, f32[64,256]{1,0:T(8,128)S(1)}, u32[]{:S(2)}, u32[]{:S(2)}) collective-permute-start(f32[64,256]{1,0:T(8,128)S(1)} %add.12), channel_id=1, source_target_pairs={{0,16},{4,20},{8,24},{12,28},{16,0},{20,4},{24,8},{28,12},{1,17},{... | collective-permute-start | bytes 196616 | tf_op jit(solution)/shard_map/ppermute | solution.py:261
  22.2 0.5 %collective-permute-start.6 = (f32[64,256]{1,0:T(8,128)S(1)}, f32[64,256]{1,0:T(8,128)S(1)}, u32[]{:S(2)}, u32[]{:S(2)}) collective-permute-start(f32[64,256]{1,0:T(8,128)S(1)} %add.12), channel_id=1, source_target_pairs={{0,8},{4,12},{8,0},{12,4},{16,24},{20,28},{24,16},{28,20},{1,9},{5... | collective-permute-start | bytes 196616 | tf_op jit(solution)/shard_map/ppermute | solution.py:261
  22.7 1.7 %collective-permute-done.8 = f32[64,256]{1,0:T(8,128)S(1)} collective-permute-done((f32[64,256]{1,0:T(8,128)S(1)}, f32[64,256]{1,0:T(8,128)S(1)}, u32[]{:S(2)}, u32[]{:S(2)}) %collective-permute-start.8) | collective-permute-done | bytes 65568 | tf_op jit(solution)/shard_map/ppermute | solution.py:261
  24.4 1.6 %collective-permute-done.7 = f32[64,256]{1,0:T(8,128)S(1)} collective-permute-done((f32[64,256]{1,0:T(8,128)S(1)}, f32[64,256]{1,0:T(8,128)S(1)}, u32[]{:S(2)}, u32[]{:S(2)}) %collective-permute-start.7) | collective-permute-done | bytes 65568 | tf_op jit(solution)/shard_map/ppermute | solution.py:261
  26.0 0.5 %collective-permute-done.6 = f32[64,256]{1,0:T(8,128)S(1)} collective-permute-done((f32[64,256]{1,0:T(8,128)S(1)}, f32[64,256]{1,0:T(8,128)S(1)}, u32[]{:S(2)}, u32[]{:S(2)}) %collective-permute-start.6) | collective-permute-done | bytes 65568 | tf_op jit(solution)/shard_map/ppermute | solution.py:261
  26.5 0.6 %add_add_fusion = f32[64,256]{1,0:T(8,128)} fusion(f32[64,256]{1,0:T(8,128)S(1)} %collective-permute-done.7, f32[64,256]{1,0:T(8,128)S(1)} %collective-permute-done.8, f32[64,256]{1,0:T(8,128)S(1)} %add.12, f32[64,256]{1,0:T(8,128)S(1)} %collective-permute-done.6), kind=kLoop, calls=%fused_computation | loop fusion | flops 49152 | bytes 327680 | tf_op jit(solution)/shard_map/add | solution.py:263
  (8 shorter events, 0.0 us)
Async XLA Ops:
  0.0 14.9 %collective-permute-start.1 = (bf16[1,1,3,4,4096]{4,3,2,1,0:T(4,128)(2,1)}, bf16[1,1,3,4,4096]{4,3,2,1,0:T(4,128)(2,1)S(1)}, u32[]{:S(2)}, u32[]{:S(2)}) collective-permute-start(bf16[1,1,3,4,4096]{4,3,2,1,0:T(4,128)(2,1)} %raw_hbm.1), channel_id=1, source_target_pairs={{0,2},{1,3},{2,0},{3,1},{4,6},{5,7},{6,4},{7,5},{8,10},{9,11},{10,... | collective-permute-start | bytes 294920 | tf_op jit(solution)/shard_map/ppermute | solution.py:210
  5.8 9.3 %collective-permute-start.2 = (bf16[520,128]{1,0:T(8,128)(2,1)S(1)}, bf16[520,128]{1,0:T(8,128)(2,1)S(1)}, u32[]{:S(2)}, u32[]{:S(2)}) collective-permute-start(bf16[520,128]{1,0:T(8,128)(2,1)S(1)} %pack.1.full_ref.refs_0_), channel_id=1, source_target_pairs={{0,1},{1,0},{2,3},{3,2},{4,7},{5,6},{6,5},{7,4},{8,9},{9,8},{10,11... | collective-permute-start | bytes 399368 | tf_op jit(solution)/shard_map/ppermute | solution.py:174
  7.5 7.8 %collective-permute-start.4 = (bf16[392,128]{1,0:T(8,128)(2,1)S(1)}, bf16[392,128]{1,0:T(8,128)(2,1)S(1)}, u32[]{:S(2)}, u32[]{:S(2)}) collective-permute-start(bf16[392,128]{1,0:T(8,128)(2,1)S(1)} %lean.1.lean_ref), channel_id=1, source_target_pairs={{0,3},{1,2},{2,1},{3,0},{4,5},{5,4},{6,7},{7,6},{8,11},{9,10},{10,... | collective-permute-start | bytes 301064 | tf_op jit(solution)/shard_map/ppermute | solution.py:174
  7.6 7.3 %collective-permute-start = (bf16[72,128]{1,0:T(8,128)(2,1)S(1)}, bf16[72,128]{1,0:T(8,128)(2,1)S(1)}, u32[]{:S(2)}, u32[]{:S(2)}) collective-permute-start(bf16[72,128]{1,0:T(8,128)(2,1)S(1)} %tail.1), channel_id=1, source_target_pairs={{0,2},{1,3},{2,0},{3,1},{4,6},{5,7},{6,4},{7,5},{8,10},{9,11},{10,... | collective-permute-start | bytes 55304 | tf_op jit(solution)/shard_map/ppermute | solution.py:211
  15.2 1.4 %copy-start = (bf16[64,256]{1,0:T(8,128)(2,1)S(1)}, bf16[64,256]{1,0:T(8,128)(2,1)}, u32[]{:S(2)}) copy-start(bf16[64,256]{1,0:T(8,128)(2,1)} %density_ref.1) | copy-start | bytes 98308
  15.2 1.3 %collective-permute-start.3 = (bf16[192,128]{1,0:T(8,128)(2,1)S(1)}, bf16[192,128]{1,0:T(8,128)(2,1)S(1)}, u32[]{:S(2)}, u32[]{:S(2)}) collective-permute-start(bf16[192,128]{1,0:T(8,128)(2,1)S(1)} %merge.1), channel_id=1, source_target_pairs={{0,4},{4,0},{8,12},{12,8},{16,20},{20,16},{24,28},{28,24},{1,5},{5... | collective-permute-start | bytes 147464 | tf_op jit(solution)/shard_map/ppermute | solution.py:224
  17.8 1.3 %collective-permute-start.5 = (f32[64,256]{1,0:T(8,128)S(1)}, f32[64,256]{1,0:T(8,128)S(1)}, u32[]{:S(2)}, u32[]{:S(2)}) collective-permute-start(f32[64,256]{1,0:T(8,128)S(1)} %exchange.1), channel_id=1, source_target_pairs={{0,4},{4,0},{8,12},{12,8},{16,20},{20,16},{24,28},{28,24},{1,5},{5... | collective-permute-start | bytes 196616 | tf_op jit(solution)/shard_map/ppermute | solution.py:261
  19.2 5.2 %collective-permute-start.8 = (f32[64,256]{1,0:T(8,128)S(1)}, f32[64,256]{1,0:T(8,128)S(1)}, u32[]{:S(2)}, u32[]{:S(2)}) collective-permute-start(f32[64,256]{1,0:T(8,128)S(1)} %add.12), channel_id=1, source_target_pairs={{0,24},{4,28},{8,16},{12,20},{16,8},{20,12},{24,0},{28,4},{1,25},{... | collective-permute-start | bytes 196616 | tf_op jit(solution)/shard_map/ppermute | solution.py:261
  21.7 4.3 %collective-permute-start.7 = (f32[64,256]{1,0:T(8,128)S(1)}, f32[64,256]{1,0:T(8,128)S(1)}, u32[]{:S(2)}, u32[]{:S(2)}) collective-permute-start(f32[64,256]{1,0:T(8,128)S(1)} %add.12), channel_id=1, source_target_pairs={{0,16},{4,20},{8,24},{12,28},{16,0},{20,4},{24,8},{28,12},{1,17},{... | collective-permute-start | bytes 196616 | tf_op jit(solution)/shard_map/ppermute | solution.py:261
  22.2 4.3 %collective-permute-start.6 = (f32[64,256]{1,0:T(8,128)S(1)}, f32[64,256]{1,0:T(8,128)S(1)}, u32[]{:S(2)}, u32[]{:S(2)}) collective-permute-start(f32[64,256]{1,0:T(8,128)S(1)} %add.12), channel_id=1, source_target_pairs={{0,8},{4,12},{8,0},{12,4},{16,24},{20,28},{24,16},{28,20},{1,9},{5... | collective-permute-start | bytes 196616 | tf_op jit(solution)/shard_map/ppermute | solution.py:261

commit v25 on v23

--- a/solution.py
+++ b/solution.py
@@ -104,6 +104,8 @@
 ):
     packs, (out_ref, rows, half_ref, held) = refs[:orb], refs[orb:]
     fulls = packs[2::2]
+    notes = meta_ref[...]
+    meta = [notes[i] for i in range(orb * slots)]
     me = lax.axis_index("orb")
     parity = core_parity()
     sign = 1 - 2 * parity
@@ -128,7 +130,7 @@
         rows[across, pl.ds(near, height), lanes] = tail[t * height : (t + 1) * height]
         rows[across, pl.ds(far, height), lanes] = swapped[at : at + height]
     rows[orb] = jnp.zeros_like(rows[orb])
-    selected = jnp.concatenate([rows[meta_ref[j]] for j in range(slots)], axis=0)
+    selected = jnp.concatenate([rows[meta[j]] for j in range(slots)], axis=0)
     half = jnp.dot(left_ref[...], selected, preferred_element_type=jnp.float32)
     half = half.astype(jnp.bfloat16)
     for k in range(orb):
@@ -138,7 +140,7 @@
         )
     half_ref[orb] = jnp.zeros_like(half_ref[orb])
     for way in range(orb):
-        codes = [meta_ref[way * slots + j] for j in range(slots)]
+        codes = meta[way * slots : (way + 1) * slots]
         held[owners[way]] = lax.dot_general(
             jnp.concatenate([half_ref[code] for code in codes], axis=1),
             jnp.concatenate([packs[way][at : at + BS] for at in range(0, size, BS)], axis=1),
@@ -241,7 +243,7 @@
     parts = pl.pallas_call(
         functools.partial(exchange_kernel, orb, slots, aux_width),
         out_shape=jax.ShapeDtypeStruct((BS, full_width), jnp.float32),
-        in_specs=[smem] + [vmem] * (orb + 4),
+        in_specs=[vmem] * (orb + 5),
         out_specs=vmem,
         scratch_shapes=[
             pltpu.VMEM((orb + 1, BS, full_width), jnp.bfloat16),

time: 25.5 us -> 25 us (0.980)
  Pallas kernels: 2.59 us -> 2.11 us
    pallas_call x1, Pallas kernels: 1.21 us -> 0.73 us  [shards(): pl.pallas_call(functools.partial(exchange_kernel, orb, slots, aux_width),...]
  transfers between devices with their start and end apart: 9 -> 9, of which waited for: 8 -> 8; matrix products, arithmetic and copies ran while one was open for 0% -> 0% of each run, Pallas kernels for 5% -> 6%
where the time goes in v25:
time: 25 us; the launch traced here: 24.9 us
  starting transfers between devices  12.3 us (49%)
  waiting for transfers between devices  8.98 us (36%)
  Pallas kernels  2.11 us (8%)
  other arithmetic  0.74 us (3%)
  between operations  0.71 us (3%)
    ppermute x4, waiting for transfers between devices, shards(): lax.ppermute(parts, 'aux', [(i, i ^ way * step) for i in range(aux)])  5.03 us
    ppermute x2, starting transfers between devices, shift(): return lax.ppermute(x, ('aux', 'orb'), perm)  4.18 us
    ppermute x1, starting transfers between devices, shards(): raw = lax.ppermute(tensor_blocks, 'orb', across)  4.04 us
    ppermute x4, starting transfers between devices, shards(): lax.ppermute(parts, 'aux', [(i, i ^ way * step) for i in range(aux)])  3.78 us
    ppermute x1, waiting for transfers between devices, shards(): tail_in = lax.ppermute(tail, 'orb', across)  2.3 us
    ppermute x2, waiting for transfers between devices, shift(): return lax.ppermute(x, ('aux', 'orb'), perm)  1.55 us
    pallas_call x1, Pallas kernels, shards(): pl.pallas_call(functools.partial(pack_kernel, orb), out_shape=array(size...  1.14 us
    pallas_call x1, Pallas kernels, shards(): pl.pallas_call(functools.partial(exchange_kernel, orb, slots, aux_width),...  0.73 us
  transfers between devices with their start and end apart: 9, of which 8 were waited for; matrix products, arithmetic and copies ran while one was open for 0% of the time, Pallas kernels for 6%

profile of v25, /device:TPU:0, one launch (start us, length us, event | category | flops | bytes accessed | tf_op | source)
XLA Modules:
  0.0 24.9 jit_solution(5685562079347036344)
XLA Ops:
  0.0 4.0 %collective-permute-start.1 = (bf16[1,1,3,4,4096]{4,3,2,1,0:T(4,128)(2,1)}, bf16[1,1,3,4,4096]{4,3,2,1,0:T(4,128)(2,1)S(1)}, u32[]{:S(2)}, u32[]{:S(2)}) collective-permute-start(bf16[1,1,3,4,4096]{4,3,2,1,0:T(4,128)(2,1)} %raw_hbm.1), channel_id=1, source_target_pairs={{0,2},{1,3},{2,0},{3,1},{4,6},{5,7},{6,4},{7,5},{8,10},{9,11},{10,... | collective-permute-start | bytes 294920 | tf_op jit(solution)/shard_map/ppermute | solution.py:211
  4.7 1.1 %pack.1.full_ref.refs_0_ = bf16[520,128]{1,0:T(8,128)(2,1)S(1)} custom-call(s32[1,1]{1,0:T(1,128)S(6)} %copy.5.kept, s32[1,1,3]{2,1,0:T(1,128)} %pairs_hbm.1, bf16[64,256]{1,0:T(8,128)(2,1)} %density_ref.1, bf16[1,1,3,4,4096]{4,3,2,1,0:T(4,128)(2,1)} %raw_hbm.1), custom_call_target="tpu_custom_call" | custom-call | tf_op jit(solution)/shard_map/pack/pallas_call | solution.py:177
  5.8 1.6 %collective-permute-start.2 = (bf16[520,128]{1,0:T(8,128)(2,1)S(1)}, bf16[520,128]{1,0:T(8,128)(2,1)S(1)}, u32[]{:S(2)}, u32[]{:S(2)}) collective-permute-start(bf16[520,128]{1,0:T(8,128)(2,1)S(1)} %pack.1.full_ref.refs_0_), channel_id=1, source_target_pairs={{0,1},{1,0},{2,3},{3,2},{4,7},{5,6},{6,5},{7,4},{8,9},{9,8},{10,11... | collective-permute-start | bytes 399368 | tf_op jit(solution)/shard_map/ppermute | solution.py:175
  7.5 0.3 %collective-permute-start = (bf16[72,128]{1,0:T(8,128)(2,1)S(1)}, bf16[72,128]{1,0:T(8,128)(2,1)S(1)}, u32[]{:S(2)}, u32[]{:S(2)}) collective-permute-start(bf16[72,128]{1,0:T(8,128)(2,1)S(1)} %tail.1.tail_ref), channel_id=1, source_target_pairs={{0,2},{1,3},{2,0},{3,1},{4,6},{5,7},{6,4},{7,5},{8,10},{9,11},{10,... | collective-permute-start | bytes 55304 | tf_op jit(solution)/shard_map/ppermute | solution.py:212
  7.8 2.5 %collective-permute-start.4 = (bf16[392,128]{1,0:T(8,128)(2,1)S(1)}, bf16[392,128]{1,0:T(8,128)(2,1)S(1)}, u32[]{:S(2)}, u32[]{:S(2)}) collective-permute-start(bf16[392,128]{1,0:T(8,128)(2,1)S(1)} %lean.1), channel_id=1, source_target_pairs={{0,3},{1,2},{2,1},{3,0},{4,5},{5,4},{6,7},{7,6},{8,11},{9,10},{10,... | collective-permute-start | bytes 301064 | tf_op jit(solution)/shard_map/ppermute | solution.py:175
  10.4 2.3 %collective-permute-done.refs_1_.tail = bf16[72,128]{1,0:T(8,128)(2,1)S(1)} collective-permute-done((bf16[72,128]{1,0:T(8,128)(2,1)S(1)}, bf16[72,128]{1,0:T(8,128)(2,1)S(1)}, u32[]{:S(2)}, u32[]{:S(2)}) %collective-permute-start) | collective-permute-done | bytes 18464 | tf_op jit(solution)/shard_map/ppermute | solution.py:212
  12.7 0.0 collective-permute-done.1.raw
  12.7 0.2 relay.1
  12.9 0.4 %collective-permute-done.2.refs_0_.refs_2_ = bf16[520,128]{1,0:T(8,128)(2,1)S(1)} collective-permute-done((bf16[520,128]{1,0:T(8,128)(2,1)S(1)}, bf16[520,128]{1,0:T(8,128)(2,1)S(1)}, u32[]{:S(2)}, u32[]{:S(2)}) %collective-permute-start.2) | collective-permute-done | bytes 133152 | tf_op jit(solution)/shard_map/ppermute | solution.py:175
  13.4 0.0 copy-start
  13.4 0.0 collective-permute-start.3
  13.4 1.1 %collective-permute-done.4.refs_3_ = bf16[392,128]{1,0:T(8,128)(2,1)S(1)} collective-permute-done((bf16[392,128]{1,0:T(8,128)(2,1)S(1)}, bf16[392,128]{1,0:T(8,128)(2,1)S(1)}, u32[]{:S(2)}, u32[]{:S(2)}) %collective-permute-start.4) | collective-permute-done | bytes 100384 | tf_op jit(solution)/shard_map/ppermute | solution.py:175
  14.5 0.1 collective-permute-done.3.swapped
  14.6 0.1 maximum_convert_fusion.meta_ref
  14.7 0.0 copy-done
  14.7 0.7 %exchange.1 = f32[64,256]{1,0:T(8,128)S(1)} custom-call(s32[12]{0:T(128)S(1)} %maximum_convert_fusion.meta_ref, bf16[64,256]{1,0:T(8,128)(2,1)S(1)} %copy-done, bf16[256,192]{1,0:T(8,128)(2,1)S(1)} %get-tuple-element.14.left_ref, bf16[72,128]{1,0:T(8,128)(2,1)S(1)} %collective-permute-done.refs_1_.tail, bf16[192,128]{1,0:T(8,128)(2,1)S(1)} %collective-permute-done.3.swapped, ...), custom_call_target="tpu_custom_call" | custom-call | tf_op jit(solution)/shard_map/exchange/pallas_call | solution.py:243
  15.4 0.2 collective-permute-start.5
  15.6 1.1 %collective-permute-done.5 = f32[64,256]{1,0:T(8,128)S(1)} collective-permute-done((f32[64,256]{1,0:T(8,128)S(1)}, f32[64,256]{1,0:T(8,128)S(1)}, u32[]{:S(2)}, u32[]{:S(2)}) %collective-permute-start.5) | collective-permute-done | bytes 65568 | tf_op jit(solution)/shard_map/ppermute | solution.py:262
  16.8 2.7 %collective-permute-start.8 = (f32[64,256]{1,0:T(8,128)S(1)}, f32[64,256]{1,0:T(8,128)S(1)}, u32[]{:S(2)}, u32[]{:S(2)}) collective-permute-start(f32[64,256]{1,0:T(8,128)S(1)} %add.12), channel_id=1, source_target_pairs={{0,24},{4,28},{8,16},{12,20},{16,8},{20,12},{24,0},{28,4},{1,25},{... | collective-permute-start | bytes 196616 | tf_op jit(solution)/shard_map/ppermute | solution.py:262
  19.5 0.5 %collective-permute-start.7 = (f32[64,256]{1,0:T(8,128)S(1)}, f32[64,256]{1,0:T(8,128)S(1)}, u32[]{:S(2)}, u32[]{:S(2)}) collective-permute-start(f32[64,256]{1,0:T(8,128)S(1)} %add.12), channel_id=1, source_target_pairs={{0,16},{4,20},{8,24},{12,28},{16,0},{20,4},{24,8},{28,12},{1,17},{... | collective-permute-start | bytes 196616 | tf_op jit(solution)/shard_map/ppermute | solution.py:262
  20.0 0.3 %collective-permute-start.6 = (f32[64,256]{1,0:T(8,128)S(1)}, f32[64,256]{1,0:T(8,128)S(1)}, u32[]{:S(2)}, u32[]{:S(2)}) collective-permute-start(f32[64,256]{1,0:T(8,128)S(1)} %add.12), channel_id=1, source_target_pairs={{0,8},{4,12},{8,0},{12,4},{16,24},{20,28},{24,16},{28,20},{1,9},{5... | collective-permute-start | bytes 196616 | tf_op jit(solution)/shard_map/ppermute | solution.py:262
  20.3 1.7 %collective-permute-done.8 = f32[64,256]{1,0:T(8,128)S(1)} collective-permute-done((f32[64,256]{1,0:T(8,128)S(1)}, f32[64,256]{1,0:T(8,128)S(1)}, u32[]{:S(2)}, u32[]{:S(2)}) %collective-permute-start.8) | collective-permute-done | bytes 65568 | tf_op jit(solution)/shard_map/ppermute | solution.py:262
  22.0 1.7 %collective-permute-done.7 = f32[64,256]{1,0:T(8,128)S(1)} collective-permute-done((f32[64,256]{1,0:T(8,128)S(1)}, f32[64,256]{1,0:T(8,128)S(1)}, u32[]{:S(2)}, u32[]{:S(2)}) %collective-permute-start.7) | collective-permute-done | bytes 65568 | tf_op jit(solution)/shard_map/ppermute | solution.py:262
  23.7 0.5 %collective-permute-done.6 = f32[64,256]{1,0:T(8,128)S(1)} collective-permute-done((f32[64,256]{1,0:T(8,128)S(1)}, f32[64,256]{1,0:T(8,128)S(1)}, u32[]{:S(2)}, u32[]{:S(2)}) %collective-permute-start.6) | collective-permute-done | bytes 65568 | tf_op jit(solution)/shard_map/ppermute | solution.py:262
  24.2 0.6 %add_add_fusion = f32[64,256]{1,0:T(8,128)} fusion(f32[64,256]{1,0:T(8,128)S(1)} %collective-permute-done.7, f32[64,256]{1,0:T(8,128)S(1)} %collective-permute-done.8, f32[64,256]{1,0:T(8,128)S(1)} %add.12, f32[64,256]{1,0:T(8,128)S(1)} %collective-permute-done.6), kind=kLoop, calls=%fused_computation | loop fusion | flops 49152 | bytes 327680 | tf_op jit(solution)/shard_map/add | solution.py:264
  (8 shorter events, 0.0 us)
Async XLA Ops:
  0.0 12.7 %collective-permute-start.1 = (bf16[1,1,3,4,4096]{4,3,2,1,0:T(4,128)(2,1)}, bf16[1,1,3,4,4096]{4,3,2,1,0:T(4,128)(2,1)S(1)}, u32[]{:S(2)}, u32[]{:S(2)}) collective-permute-start(bf16[1,1,3,4,4096]{4,3,2,1,0:T(4,128)(2,1)} %raw_hbm.1), channel_id=1, source_target_pairs={{0,2},{1,3},{2,0},{3,1},{4,6},{5,7},{6,4},{7,5},{8,10},{9,11},{10,... | collective-permute-start | bytes 294920 | tf_op jit(solution)/shard_map/ppermute | solution.py:211
  5.8 7.5 %collective-permute-start.2 = (bf16[520,128]{1,0:T(8,128)(2,1)S(1)}, bf16[520,128]{1,0:T(8,128)(2,1)S(1)}, u32[]{:S(2)}, u32[]{:S(2)}) collective-permute-start(bf16[520,128]{1,0:T(8,128)(2,1)S(1)} %pack.1.full_ref.refs_0_), channel_id=1, source_target_pairs={{0,1},{1,0},{2,3},{3,2},{4,7},{5,6},{6,5},{7,4},{8,9},{9,8},{10,11... | collective-permute-start | bytes 399368 | tf_op jit(solution)/shard_map/ppermute | solution.py:175
  7.5 5.2 %collective-permute-start = (bf16[72,128]{1,0:T(8,128)(2,1)S(1)}, bf16[72,128]{1,0:T(8,128)(2,1)S(1)}, u32[]{:S(2)}, u32[]{:S(2)}) collective-permute-start(bf16[72,128]{1,0:T(8,128)(2,1)S(1)} %tail.1.tail_ref), channel_id=1, source_target_pairs={{0,2},{1,3},{2,0},{3,1},{4,6},{5,7},{6,4},{7,5},{8,10},{9,11},{10,... | collective-permute-start | bytes 55304 | tf_op jit(solution)/shard_map/ppermute | solution.py:212
  7.8 6.7 %collective-permute-start.4 = (bf16[392,128]{1,0:T(8,128)(2,1)S(1)}, bf16[392,128]{1,0:T(8,128)(2,1)S(1)}, u32[]{:S(2)}, u32[]{:S(2)}) collective-permute-start(bf16[392,128]{1,0:T(8,128)(2,1)S(1)} %lean.1), channel_id=1, source_target_pairs={{0,3},{1,2},{2,1},{3,0},{4,5},{5,4},{6,7},{7,6},{8,11},{9,10},{10,... | collective-permute-start | bytes 301064 | tf_op jit(solution)/shard_map/ppermute | solution.py:175
  13.4 1.3 %copy-start = (bf16[64,256]{1,0:T(8,128)(2,1)S(1)}, bf16[64,256]{1,0:T(8,128)(2,1)}, u32[]{:S(2)}) copy-start(bf16[64,256]{1,0:T(8,128)(2,1)} %density_ref.1) | copy-start | bytes 98308
  13.4 1.2 %collective-permute-start.3 = (bf16[192,128]{1,0:T(8,128)(2,1)S(1)}, bf16[192,128]{1,0:T(8,128)(2,1)S(1)}, u32[]{:S(2)}, u32[]{:S(2)}) collective-permute-start(bf16[192,128]{1,0:T(8,128)(2,1)S(1)} %merge.1), channel_id=1, source_target_pairs={{0,4},{4,0},{8,12},{12,8},{16,20},{20,16},{24,28},{28,24},{1,5},{5... | collective-permute-start | bytes 147464 | tf_op jit(solution)/shard_map/ppermute | solution.py:225
  15.4 1.3 %collective-permute-start.5 = (f32[64,256]{1,0:T(8,128)S(1)}, f32[64,256]{1,0:T(8,128)S(1)}, u32[]{:S(2)}, u32[]{:S(2)}) collective-permute-start(f32[64,256]{1,0:T(8,128)S(1)} %exchange.1), channel_id=1, source_target_pairs={{0,4},{4,0},{8,12},{12,8},{16,20},{20,16},{24,28},{28,24},{1,5},{5... | collective-permute-start | bytes 196616 | tf_op jit(solution)/shard_map/ppermute | solution.py:262
  16.8 5.2 %collective-permute-start.8 = (f32[64,256]{1,0:T(8,128)S(1)}, f32[64,256]{1,0:T(8,128)S(1)}, u32[]{:S(2)}, u32[]{:S(2)}) collective-permute-start(f32[64,256]{1,0:T(8,128)S(1)} %add.12), channel_id=1, source_target_pairs={{0,24},{4,28},{8,16},{12,20},{16,8},{20,12},{24,0},{28,4},{1,25},{... | collective-permute-start | bytes 196616 | tf_op jit(solution)/shard_map/ppermute | solution.py:262
  19.5 4.3 %collective-permute-start.7 = (f32[64,256]{1,0:T(8,128)S(1)}, f32[64,256]{1,0:T(8,128)S(1)}, u32[]{:S(2)}, u32[]{:S(2)}) collective-permute-start(f32[64,256]{1,0:T(8,128)S(1)} %add.12), channel_id=1, source_target_pairs={{0,16},{4,20},{8,24},{12,28},{16,0},{20,4},{24,8},{28,12},{1,17},{... | collective-permute-start | bytes 196616 | tf_op jit(solution)/shard_map/ppermute | solution.py:262
  20.0 4.3 %collective-permute-start.6 = (f32[64,256]{1,0:T(8,128)S(1)}, f32[64,256]{1,0:T(8,128)S(1)}, u32[]{:S(2)}, u32[]{:S(2)}) collective-permute-start(f32[64,256]{1,0:T(8,128)S(1)} %add.12), channel_id=1, source_target_pairs={{0,8},{4,12},{8,0},{12,4},{16,24},{20,28},{24,16},{28,20},{1,9},{5... | collective-permute-start | bytes 196616 | tf_op jit(solution)/shard_map/ppermute | solution.py:262

commit v26 on v25

--- a/solution.py
+++ b/solution.py
@@ -56,8 +56,9 @@
     shape = (NOTE, LANES)
     lane = lax.broadcasted_iota(jnp.int32, shape, 1)
     note = jnp.zeros(shape, jnp.int32)
+    named = pairs[0]
     for j in range(pairs.shape[2]):
-        note = jnp.where(lane == j, jnp.where(j < kept[0, 0], pairs[0, 0, j], orb), note)
+        note = jnp.where(lane == j, jnp.where(j < kept[0, 0], named[0, j], orb), note)
     full_ref[size + tiles * BS :] = note.astype(jnp.float32).astype(jnp.bfloat16)
     copies[0].wait()
     lay_blocks(raw[0, 0], full_ref)
@@ -180,7 +181,7 @@
         in_specs=[smem, hbm, hbm, hbm],
         out_specs=vmem,
         scratch_shapes=[
-            pltpu.SMEM(pairs.shape, jnp.int32),
+            pltpu.VMEM(pairs.shape, jnp.int32),
             pltpu.VMEM(density.shape, jnp.bfloat16),
             pltpu.VMEM(tensor_blocks.shape, jnp.bfloat16),
             pltpu.SemaphoreType.DMA((3,)),

time: 25 us -> 25.1 us (level)
  no operation moved by 1% of the time
where the time goes in v26:
time: 25.1 us; the launch traced here: 24.9 us
  starting transfers between devices  12.3 us (49%)
  waiting for transfers between devices  8.97 us (36%)
  Pallas kernels  2.14 us (9%)
  other arithmetic  0.74 us (3%)
  between operations  0.71 us (3%)
    ppermute x4, waiting for transfers between devices, shards(): lax.ppermute(parts, 'aux', [(i, i ^ way * step) for i in range(aux)])  5.02 us
    ppermute x2, starting transfers between devices, shift(): return lax.ppermute(x, ('aux', 'orb'), perm)  4.18 us
    ppermute x1, starting transfers between devices, shards(): raw = lax.ppermute(tensor_blocks, 'orb', across)  4.04 us
    ppermute x4, starting transfers between devices, shards(): lax.ppermute(parts, 'aux', [(i, i ^ way * step) for i in range(aux)])  3.78 us
    ppermute x1, waiting for transfers between devices, shards(): tail_in = lax.ppermute(tail, 'orb', across)  2.31 us
    ppermute x2, waiting for transfers between devices, shift(): return lax.ppermute(x, ('aux', 'orb'), perm)  1.54 us
    pallas_call x1, Pallas kernels, shards(): pl.pallas_call(functools.partial(pack_kernel, orb), out_shape=array(size...  1.17 us
    pallas_call x1, Pallas kernels, shards(): pl.pallas_call(functools.partial(exchange_kernel, orb, slots, aux_width),...  0.73 us
  transfers between devices with their start and end apart: 9, of which 8 were waited for; matrix products, arithmetic and copies ran while one was open for 0% of the time, Pallas kernels for 6%

profile of v26, /device:TPU:0, one launch (start us, length us, event | category | flops | bytes accessed | tf_op | source)
XLA Modules:
  0.0 24.9 jit_solution(4441546662615124321)
XLA Ops:
  0.0 4.0 %collective-permute-start.1 = (bf16[1,1,3,4,4096]{4,3,2,1,0:T(4,128)(2,1)}, bf16[1,1,3,4,4096]{4,3,2,1,0:T(4,128)(2,1)S(1)}, u32[]{:S(2)}, u32[]{:S(2)}) collective-permute-start(bf16[1,1,3,4,4096]{4,3,2,1,0:T(4,128)(2,1)} %raw_hbm.1), channel_id=1, source_target_pairs={{0,2},{1,3},{2,0},{3,1},{4,6},{5,7},{6,4},{7,5},{8,10},{9,11},{10,... | collective-permute-start | bytes 294920 | tf_op jit(solution)/shard_map/ppermute | solution.py:212
  4.7 1.2 %pack.1.full_ref.refs_0_ = bf16[520,128]{1,0:T(8,128)(2,1)S(1)} custom-call(s32[1,1]{1,0:T(1,128)S(6)} %copy.5.kept, s32[1,1,3]{2,1,0:T(1,128)} %pairs_hbm.1, bf16[64,256]{1,0:T(8,128)(2,1)} %density_ref.1, bf16[1,1,3,4,4096]{4,3,2,1,0:T(4,128)(2,1)} %raw_hbm.1), custom_call_target="tpu_custom_call" | custom-call | tf_op jit(solution)/shard_map/pack/pallas_call | solution.py:178
  5.9 1.6 %collective-permute-start.2 = (bf16[520,128]{1,0:T(8,128)(2,1)S(1)}, bf16[520,128]{1,0:T(8,128)(2,1)S(1)}, u32[]{:S(2)}, u32[]{:S(2)}) collective-permute-start(bf16[520,128]{1,0:T(8,128)(2,1)S(1)} %pack.1.full_ref.refs_0_), channel_id=1, source_target_pairs={{0,1},{1,0},{2,3},{3,2},{4,7},{5,6},{6,5},{7,4},{8,9},{9,8},{10,11... | collective-permute-start | bytes 399368 | tf_op jit(solution)/shard_map/ppermute | solution.py:176
  7.5 0.3 %collective-permute-start = (bf16[72,128]{1,0:T(8,128)(2,1)S(1)}, bf16[72,128]{1,0:T(8,128)(2,1)S(1)}, u32[]{:S(2)}, u32[]{:S(2)}) collective-permute-start(bf16[72,128]{1,0:T(8,128)(2,1)S(1)} %tail.1.tail_ref), channel_id=1, source_target_pairs={{0,2},{1,3},{2,0},{3,1},{4,6},{5,7},{6,4},{7,5},{8,10},{9,11},{10,... | collective-permute-start | bytes 55304 | tf_op jit(solution)/shard_map/ppermute | solution.py:213
  7.9 2.5 %collective-permute-start.4 = (bf16[392,128]{1,0:T(8,128)(2,1)S(1)}, bf16[392,128]{1,0:T(8,128)(2,1)S(1)}, u32[]{:S(2)}, u32[]{:S(2)}) collective-permute-start(bf16[392,128]{1,0:T(8,128)(2,1)S(1)} %lean.1), channel_id=1, source_target_pairs={{0,3},{1,2},{2,1},{3,0},{4,5},{5,4},{6,7},{7,6},{8,11},{9,10},{10,... | collective-permute-start | bytes 301064 | tf_op jit(solution)/shard_map/ppermute | solution.py:176
  10.4 2.3 %collective-permute-done.refs_1_.tail = bf16[72,128]{1,0:T(8,128)(2,1)S(1)} collective-permute-done((bf16[72,128]{1,0:T(8,128)(2,1)S(1)}, bf16[72,128]{1,0:T(8,128)(2,1)S(1)}, u32[]{:S(2)}, u32[]{:S(2)}) %collective-permute-start) | collective-permute-done | bytes 18464 | tf_op jit(solution)/shard_map/ppermute | solution.py:213
  12.7 0.0 collective-permute-done.1.raw
  12.7 0.2 relay.1
  13.0 0.4 %collective-permute-done.2.refs_0_.refs_2_ = bf16[520,128]{1,0:T(8,128)(2,1)S(1)} collective-permute-done((bf16[520,128]{1,0:T(8,128)(2,1)S(1)}, bf16[520,128]{1,0:T(8,128)(2,1)S(1)}, u32[]{:S(2)}, u32[]{:S(2)}) %collective-permute-start.2) | collective-permute-done | bytes 133152 | tf_op jit(solution)/shard_map/ppermute | solution.py:176
  13.4 0.0 copy-start
  13.4 0.0 collective-permute-start.3
  13.4 1.1 %collective-permute-done.4.refs_3_ = bf16[392,128]{1,0:T(8,128)(2,1)S(1)} collective-permute-done((bf16[392,128]{1,0:T(8,128)(2,1)S(1)}, bf16[392,128]{1,0:T(8,128)(2,1)S(1)}, u32[]{:S(2)}, u32[]{:S(2)}) %collective-permute-start.4) | collective-permute-done | bytes 100384 | tf_op jit(solution)/shard_map/ppermute | solution.py:176
  14.5 0.1 collective-permute-done.3.swapped
  14.6 0.1 maximum_convert_fusion.meta_ref
  14.7 0.0 copy-done
  14.7 0.7 %exchange.1 = f32[64,256]{1,0:T(8,128)S(1)} custom-call(s32[12]{0:T(128)S(1)} %maximum_convert_fusion.meta_ref, bf16[64,256]{1,0:T(8,128)(2,1)S(1)} %copy-done, bf16[256,192]{1,0:T(8,128)(2,1)S(1)} %get-tuple-element.14.left_ref, bf16[72,128]{1,0:T(8,128)(2,1)S(1)} %collective-permute-done.refs_1_.tail, bf16[192,128]{1,0:T(8,128)(2,1)S(1)} %collective-permute-done.3.swapped, ...), custom_call_target="tpu_custom_call" | custom-call | tf_op jit(solution)/shard_map/exchange/pallas_call | solution.py:244
  15.4 0.2 collective-permute-start.5
  15.7 1.1 %collective-permute-done.5 = f32[64,256]{1,0:T(8,128)S(1)} collective-permute-done((f32[64,256]{1,0:T(8,128)S(1)}, f32[64,256]{1,0:T(8,128)S(1)}, u32[]{:S(2)}, u32[]{:S(2)}) %collective-permute-start.5) | collective-permute-done | bytes 65568 | tf_op jit(solution)/shard_map/ppermute | solution.py:263
  16.8 2.7 %collective-permute-start.8 = (f32[64,256]{1,0:T(8,128)S(1)}, f32[64,256]{1,0:T(8,128)S(1)}, u32[]{:S(2)}, u32[]{:S(2)}) collective-permute-start(f32[64,256]{1,0:T(8,128)S(1)} %add.12), channel_id=1, source_target_pairs={{0,24},{4,28},{8,16},{12,20},{16,8},{20,12},{24,0},{28,4},{1,25},{... | collective-permute-start | bytes 196616 | tf_op jit(solution)/shard_map/ppermute | solution.py:263
  19.5 0.5 %collective-permute-start.7 = (f32[64,256]{1,0:T(8,128)S(1)}, f32[64,256]{1,0:T(8,128)S(1)}, u32[]{:S(2)}, u32[]{:S(2)}) collective-permute-start(f32[64,256]{1,0:T(8,128)S(1)} %add.12), channel_id=1, source_target_pairs={{0,16},{4,20},{8,24},{12,28},{16,0},{20,4},{24,8},{28,12},{1,17},{... | collective-permute-start | bytes 196616 | tf_op jit(solution)/shard_map/ppermute | solution.py:263
  20.0 0.3 %collective-permute-start.6 = (f32[64,256]{1,0:T(8,128)S(1)}, f32[64,256]{1,0:T(8,128)S(1)}, u32[]{:S(2)}, u32[]{:S(2)}) collective-permute-start(f32[64,256]{1,0:T(8,128)S(1)} %add.12), channel_id=1, source_target_pairs={{0,8},{4,12},{8,0},{12,4},{16,24},{20,28},{24,16},{28,20},{1,9},{5... | collective-permute-start | bytes 196616 | tf_op jit(solution)/shard_map/ppermute | solution.py:263
  20.3 1.7 %collective-permute-done.8 = f32[64,256]{1,0:T(8,128)S(1)} collective-permute-done((f32[64,256]{1,0:T(8,128)S(1)}, f32[64,256]{1,0:T(8,128)S(1)}, u32[]{:S(2)}, u32[]{:S(2)}) %collective-permute-start.8) | collective-permute-done | bytes 65568 | tf_op jit(solution)/shard_map/ppermute | solution.py:263
  22.0 1.7 %collective-permute-done.7 = f32[64,256]{1,0:T(8,128)S(1)} collective-permute-done((f32[64,256]{1,0:T(8,128)S(1)}, f32[64,256]{1,0:T(8,128)S(1)}, u32[]{:S(2)}, u32[]{:S(2)}) %collective-permute-start.7) | collective-permute-done | bytes 65568 | tf_op jit(solution)/shard_map/ppermute | solution.py:263
  23.8 0.5 %collective-permute-done.6 = f32[64,256]{1,0:T(8,128)S(1)} collective-permute-done((f32[64,256]{1,0:T(8,128)S(1)}, f32[64,256]{1,0:T(8,128)S(1)}, u32[]{:S(2)}, u32[]{:S(2)}) %collective-permute-start.6) | collective-permute-done | bytes 65568 | tf_op jit(solution)/shard_map/ppermute | solution.py:263
  24.3 0.6 %add_add_fusion = f32[64,256]{1,0:T(8,128)} fusion(f32[64,256]{1,0:T(8,128)S(1)} %collective-permute-done.7, f32[64,256]{1,0:T(8,128)S(1)} %collective-permute-done.8, f32[64,256]{1,0:T(8,128)S(1)} %add.12, f32[64,256]{1,0:T(8,128)S(1)} %collective-permute-done.6), kind=kLoop, calls=%fused_computation | loop fusion | flops 49152 | bytes 327680 | tf_op jit(solution)/shard_map/add | solution.py:265
  (8 shorter events, 0.0 us)
Async XLA Ops:
  0.0 12.7 %collective-permute-start.1 = (bf16[1,1,3,4,4096]{4,3,2,1,0:T(4,128)(2,1)}, bf16[1,1,3,4,4096]{4,3,2,1,0:T(4,128)(2,1)S(1)}, u32[]{:S(2)}, u32[]{:S(2)}) collective-permute-start(bf16[1,1,3,4,4096]{4,3,2,1,0:T(4,128)(2,1)} %raw_hbm.1), channel_id=1, source_target_pairs={{0,2},{1,3},{2,0},{3,1},{4,6},{5,7},{6,4},{7,5},{8,10},{9,11},{10,... | collective-permute-start | bytes 294920 | tf_op jit(solution)/shard_map/ppermute | solution.py:212
  5.9 7.5 %collective-permute-start.2 = (bf16[520,128]{1,0:T(8,128)(2,1)S(1)}, bf16[520,128]{1,0:T(8,128)(2,1)S(1)}, u32[]{:S(2)}, u32[]{:S(2)}) collective-permute-start(bf16[520,128]{1,0:T(8,128)(2,1)S(1)} %pack.1.full_ref.refs_0_), channel_id=1, source_target_pairs={{0,1},{1,0},{2,3},{3,2},{4,7},{5,6},{6,5},{7,4},{8,9},{9,8},{10,11... | collective-permute-start | bytes 399368 | tf_op jit(solution)/shard_map/ppermute | solution.py:176
  7.5 5.2 %collective-permute-start = (bf16[72,128]{1,0:T(8,128)(2,1)S(1)}, bf16[72,128]{1,0:T(8,128)(2,1)S(1)}, u32[]{:S(2)}, u32[]{:S(2)}) collective-permute-start(bf16[72,128]{1,0:T(8,128)(2,1)S(1)} %tail.1.tail_ref), channel_id=1, source_target_pairs={{0,2},{1,3},{2,0},{3,1},{4,6},{5,7},{6,4},{7,5},{8,10},{9,11},{10,... | collective-permute-start | bytes 55304 | tf_op jit(solution)/shard_map/ppermute | solution.py:213
  7.9 6.7 %collective-permute-start.4 = (bf16[392,128]{1,0:T(8,128)(2,1)S(1)}, bf16[392,128]{1,0:T(8,128)(2,1)S(1)}, u32[]{:S(2)}, u32[]{:S(2)}) collective-permute-start(bf16[392,128]{1,0:T(8,128)(2,1)S(1)} %lean.1), channel_id=1, source_target_pairs={{0,3},{1,2},{2,1},{3,0},{4,5},{5,4},{6,7},{7,6},{8,11},{9,10},{10,... | collective-permute-start | bytes 301064 | tf_op jit(solution)/shard_map/ppermute | solution.py:176
  13.4 1.3 %copy-start = (bf16[64,256]{1,0:T(8,128)(2,1)S(1)}, bf16[64,256]{1,0:T(8,128)(2,1)}, u32[]{:S(2)}) copy-start(bf16[64,256]{1,0:T(8,128)(2,1)} %density_ref.1) | copy-start | bytes 98308
  13.4 1.2 %collective-permute-start.3 = (bf16[192,128]{1,0:T(8,128)(2,1)S(1)}, bf16[192,128]{1,0:T(8,128)(2,1)S(1)}, u32[]{:S(2)}, u32[]{:S(2)}) collective-permute-start(bf16[192,128]{1,0:T(8,128)(2,1)S(1)} %merge.1), channel_id=1, source_target_pairs={{0,4},{4,0},{8,12},{12,8},{16,20},{20,16},{24,28},{28,24},{1,5},{5... | collective-permute-start | bytes 147464 | tf_op jit(solution)/shard_map/ppermute | solution.py:226
  15.4 1.3 %collective-permute-start.5 = (f32[64,256]{1,0:T(8,128)S(1)}, f32[64,256]{1,0:T(8,128)S(1)}, u32[]{:S(2)}, u32[]{:S(2)}) collective-permute-start(f32[64,256]{1,0:T(8,128)S(1)} %exchange.1), channel_id=1, source_target_pairs={{0,4},{4,0},{8,12},{12,8},{16,20},{20,16},{24,28},{28,24},{1,5},{5... | collective-permute-start | bytes 196616 | tf_op jit(solution)/shard_map/ppermute | solution.py:263
  16.8 5.2 %collective-permute-start.8 = (f32[64,256]{1,0:T(8,128)S(1)}, f32[64,256]{1,0:T(8,128)S(1)}, u32[]{:S(2)}, u32[]{:S(2)}) collective-permute-start(f32[64,256]{1,0:T(8,128)S(1)} %add.12), channel_id=1, source_target_pairs={{0,24},{4,28},{8,16},{12,20},{16,8},{20,12},{24,0},{28,4},{1,25},{... | collective-permute-start | bytes 196616 | tf_op jit(solution)/shard_map/ppermute | solution.py:263
  19.5 4.3 %collective-permute-start.7 = (f32[64,256]{1,0:T(8,128)S(1)}, f32[64,256]{1,0:T(8,128)S(1)}, u32[]{:S(2)}, u32[]{:S(2)}) collective-permute-start(f32[64,256]{1,0:T(8,128)S(1)} %add.12), channel_id=1, source_target_pairs={{0,16},{4,20},{8,24},{12,28},{16,0},{20,4},{24,8},{28,12},{1,17},{... | collective-permute-start | bytes 196616 | tf_op jit(solution)/shard_map/ppermute | solution.py:263
  20.0 4.3 %collective-permute-start.6 = (f32[64,256]{1,0:T(8,128)S(1)}, f32[64,256]{1,0:T(8,128)S(1)}, u32[]{:S(2)}, u32[]{:S(2)}) collective-permute-start(f32[64,256]{1,0:T(8,128)S(1)} %add.12), channel_id=1, source_target_pairs={{0,8},{4,12},{8,0},{12,4},{16,24},{20,28},{24,16},{28,20},{1,9},{5... | collective-permute-start | bytes 196616 | tf_op jit(solution)/shard_map/ppermute | solution.py:263

commit v27 on v25

--- a/solution.py
+++ b/solution.py
@@ -257,9 +257,12 @@
     step = 1
     while step < aux:
         ways = 2 if step == 1 or step * 4 > aux else 4
+        if step == 2:
+            parts = parts.astype(jnp.bfloat16)
         terms = [parts]
         for way in range(1, ways):
             terms.append(lax.ppermute(parts, "aux", [(i, i ^ (way * step)) for i in range(aux)]))
+        terms = [term.astype(jnp.float32) for term in terms]
         while len(terms) > 1:
             terms = [terms[i] + terms[i + 1] for i in range(0, len(terms), 2)]
         parts = terms[0]

time: 25 us -> 24.7 us (0.988)
  waiting for transfers between devices: 8.98 us -> 8.62 us
    ppermute x4, waiting for transfers between devices: 5.03 us -> 4.67 us  [shards(): lax.ppermute(parts, 'aux', [(i, i ^ way * step) for i in range(aux)])]
    add x2 -> x1, other arithmetic: 0.66 us -> 0.65 us  [shards(): terms = [terms[i] + terms[i + 1] for i in range(0, len(terms), 2)]]
where the time goes in v27:
time: 24.7 us; the launch traced here: 24.5 us
  starting transfers between devices  12.3 us (50%)
  waiting for transfers between devices  8.62 us (35%)
  Pallas kernels  2.11 us (9%)
  other arithmetic  0.74 us (3%)
  between operations  0.71 us (3%)
    ppermute x4, waiting for transfers between devices, shards(): lax.ppermute(parts, 'aux', [(i, i ^ way * step) for i in range(aux)])  4.67 us
    ppermute x2, starting transfers between devices, shift(): return lax.ppermute(x, ('aux', 'orb'), perm)  4.18 us
    ppermute x1, starting transfers between devices, shards(): raw = lax.ppermute(tensor_blocks, 'orb', across)  4.04 us
    ppermute x4, starting transfers between devices, shards(): lax.ppermute(parts, 'aux', [(i, i ^ way * step) for i in range(aux)])  3.78 us
    ppermute x1, waiting for transfers between devices, shards(): tail_in = lax.ppermute(tail, 'orb', across)  2.3 us
    ppermute x2, waiting for transfers between devices, shift(): return lax.ppermute(x, ('aux', 'orb'), perm)  1.55 us
    pallas_call x1, Pallas kernels, shards(): pl.pallas_call(functools.partial(pack_kernel, orb), out_shape=array(size...  1.14 us
    pallas_call x1, Pallas kernels, shards(): pl.pallas_call(functools.partial(exchange_kernel, orb, slots, aux_width),...  0.73 us
  transfers between devices with their start and end apart: 9, of which 8 were waited for; matrix products, arithmetic and copies ran while one was open for 0% of the time, Pallas kernels for 6%

profile of v27, /device:TPU:0, one launch (start us, length us, event | category | flops | bytes accessed | tf_op | source)
XLA Modules:
  0.0 24.5 jit_solution(3075425928715219792)
XLA Ops:
  0.0 4.0 %collective-permute-start.1 = (bf16[1,1,3,4,4096]{4,3,2,1,0:T(4,128)(2,1)}, bf16[1,1,3,4,4096]{4,3,2,1,0:T(4,128)(2,1)S(1)}, u32[]{:S(2)}, u32[]{:S(2)}) collective-permute-start(bf16[1,1,3,4,4096]{4,3,2,1,0:T(4,128)(2,1)} %raw_hbm.1), channel_id=1, source_target_pairs={{0,2},{1,3},{2,0},{3,1},{4,6},{5,7},{6,4},{7,5},{8,10},{9,11},{10,... | collective-permute-start | bytes 294920 | tf_op jit(solution)/shard_map/ppermute | solution.py:211
  4.7 1.1 %pack.1.full_ref.refs_0_ = bf16[520,128]{1,0:T(8,128)(2,1)S(1)} custom-call(s32[1,1]{1,0:T(1,128)S(6)} %copy.5.kept, s32[1,1,3]{2,1,0:T(1,128)} %pairs_hbm.1, bf16[64,256]{1,0:T(8,128)(2,1)} %density_ref.1, bf16[1,1,3,4,4096]{4,3,2,1,0:T(4,128)(2,1)} %raw_hbm.1), custom_call_target="tpu_custom_call" | custom-call | tf_op jit(solution)/shard_map/pack/pallas_call | solution.py:177
  5.8 1.6 %collective-permute-start.2 = (bf16[520,128]{1,0:T(8,128)(2,1)S(1)}, bf16[520,128]{1,0:T(8,128)(2,1)S(1)}, u32[]{:S(2)}, u32[]{:S(2)}) collective-permute-start(bf16[520,128]{1,0:T(8,128)(2,1)S(1)} %pack.1.full_ref.refs_0_), channel_id=1, source_target_pairs={{0,1},{1,0},{2,3},{3,2},{4,7},{5,6},{6,5},{7,4},{8,9},{9,8},{10,11... | collective-permute-start | bytes 399368 | tf_op jit(solution)/shard_map/ppermute | solution.py:175
  7.5 0.3 %collective-permute-start = (bf16[72,128]{1,0:T(8,128)(2,1)S(1)}, bf16[72,128]{1,0:T(8,128)(2,1)S(1)}, u32[]{:S(2)}, u32[]{:S(2)}) collective-permute-start(bf16[72,128]{1,0:T(8,128)(2,1)S(1)} %tail.1.tail_ref), channel_id=1, source_target_pairs={{0,2},{1,3},{2,0},{3,1},{4,6},{5,7},{6,4},{7,5},{8,10},{9,11},{10,... | collective-permute-start | bytes 55304 | tf_op jit(solution)/shard_map/ppermute | solution.py:212
  7.8 2.5 %collective-permute-start.4 = (bf16[392,128]{1,0:T(8,128)(2,1)S(1)}, bf16[392,128]{1,0:T(8,128)(2,1)S(1)}, u32[]{:S(2)}, u32[]{:S(2)}) collective-permute-start(bf16[392,128]{1,0:T(8,128)(2,1)S(1)} %lean.1), channel_id=1, source_target_pairs={{0,3},{1,2},{2,1},{3,0},{4,5},{5,4},{6,7},{7,6},{8,11},{9,10},{10,... | collective-permute-start | bytes 301064 | tf_op jit(solution)/shard_map/ppermute | solution.py:175
  10.4 2.3 %collective-permute-done.refs_1_.tail = bf16[72,128]{1,0:T(8,128)(2,1)S(1)} collective-permute-done((bf16[72,128]{1,0:T(8,128)(2,1)S(1)}, bf16[72,128]{1,0:T(8,128)(2,1)S(1)}, u32[]{:S(2)}, u32[]{:S(2)}) %collective-permute-start) | collective-permute-done | bytes 18464 | tf_op jit(solution)/shard_map/ppermute | solution.py:212
  12.7 0.0 collective-permute-done.1.raw
  12.7 0.2 relay.1
  12.9 0.4 %collective-permute-done.2.refs_0_.refs_2_ = bf16[520,128]{1,0:T(8,128)(2,1)S(1)} collective-permute-done((bf16[520,128]{1,0:T(8,128)(2,1)S(1)}, bf16[520,128]{1,0:T(8,128)(2,1)S(1)}, u32[]{:S(2)}, u32[]{:S(2)}) %collective-permute-start.2) | collective-permute-done | bytes 133152 | tf_op jit(solution)/shard_map/ppermute | solution.py:175
  13.4 0.0 copy-start
  13.4 0.0 collective-permute-start.3
  13.4 1.1 %collective-permute-done.4.refs_3_ = bf16[392,128]{1,0:T(8,128)(2,1)S(1)} collective-permute-done((bf16[392,128]{1,0:T(8,128)(2,1)S(1)}, bf16[392,128]{1,0:T(8,128)(2,1)S(1)}, u32[]{:S(2)}, u32[]{:S(2)}) %collective-permute-start.4) | collective-permute-done | bytes 100384 | tf_op jit(solution)/shard_map/ppermute | solution.py:175
  14.5 0.1 collective-permute-done.3.swapped
  14.6 0.1 maximum_convert_fusion.meta_ref
  14.7 0.0 copy-done
  14.7 0.7 %exchange.1 = f32[64,256]{1,0:T(8,128)S(1)} custom-call(s32[12]{0:T(128)S(1)} %maximum_convert_fusion.meta_ref, bf16[64,256]{1,0:T(8,128)(2,1)S(1)} %copy-done, bf16[256,192]{1,0:T(8,128)(2,1)S(1)} %get-tuple-element.14.left_ref, bf16[72,128]{1,0:T(8,128)(2,1)S(1)} %collective-permute-done.refs_1_.tail, bf16[192,128]{1,0:T(8,128)(2,1)S(1)} %collective-permute-done.3.swapped, ...), custom_call_target="tpu_custom_call" | custom-call | tf_op jit(solution)/shard_map/exchange/pallas_call | solution.py:243
  15.4 0.2 collective-permute-start.5
  15.6 1.1 %collective-permute-done.5 = f32[64,256]{1,0:T(8,128)S(1)} collective-permute-done((f32[64,256]{1,0:T(8,128)S(1)}, f32[64,256]{1,0:T(8,128)S(1)}, u32[]{:S(2)}, u32[]{:S(2)}) %collective-permute-start.5) | collective-permute-done | bytes 65568 | tf_op jit(solution)/shard_map/ppermute | solution.py:264
  16.8 2.7 %collective-permute-start.8 = (bf16[64,256]{1,0:T(8,128)(2,1)S(1)}, bf16[64,256]{1,0:T(8,128)(2,1)S(1)}, u32[]{:S(2)}, u32[]{:S(2)}) collective-permute-start(bf16[64,256]{1,0:T(8,128)(2,1)S(1)} %add_convert_fusion), channel_id=1, source_target_pairs={{0,24},{4,28},{8,16},{12,20},{16,8},{20,12},{24,0},{28,4},{1,25},{... | collective-permute-start | bytes 98312 | tf_op jit(solution)/shard_map/ppermute | solution.py:264
  19.5 0.5 %collective-permute-start.7 = (bf16[64,256]{1,0:T(8,128)(2,1)S(1)}, bf16[64,256]{1,0:T(8,128)(2,1)S(1)}, u32[]{:S(2)}, u32[]{:S(2)}) collective-permute-start(bf16[64,256]{1,0:T(8,128)(2,1)S(1)} %add_convert_fusion), channel_id=1, source_target_pairs={{0,16},{4,20},{8,24},{12,28},{16,0},{20,4},{24,8},{28,12},{1,17},{... | collective-permute-start | bytes 98312 | tf_op jit(solution)/shard_map/ppermute | solution.py:264
  20.0 0.3 %collective-permute-start.6 = (bf16[64,256]{1,0:T(8,128)(2,1)S(1)}, bf16[64,256]{1,0:T(8,128)(2,1)S(1)}, u32[]{:S(2)}, u32[]{:S(2)}) collective-permute-start(bf16[64,256]{1,0:T(8,128)(2,1)S(1)} %add_convert_fusion), channel_id=1, source_target_pairs={{0,8},{4,12},{8,0},{12,4},{16,24},{20,28},{24,16},{28,20},{1,9},{5... | collective-permute-start | bytes 98312 | tf_op jit(solution)/shard_map/ppermute | solution.py:264
  20.3 1.3 %collective-permute-done.8 = bf16[64,256]{1,0:T(8,128)(2,1)S(1)} collective-permute-done((bf16[64,256]{1,0:T(8,128)(2,1)S(1)}, bf16[64,256]{1,0:T(8,128)(2,1)S(1)}, u32[]{:S(2)}, u32[]{:S(2)}) %collective-permute-start.8) | collective-permute-done | bytes 32800 | tf_op jit(solution)/shard_map/ppermute | solution.py:264
  21.6 1.7 %collective-permute-done.7 = bf16[64,256]{1,0:T(8,128)(2,1)S(1)} collective-permute-done((bf16[64,256]{1,0:T(8,128)(2,1)S(1)}, bf16[64,256]{1,0:T(8,128)(2,1)S(1)}, u32[]{:S(2)}, u32[]{:S(2)}) %collective-permute-start.7) | collective-permute-done | bytes 32800 | tf_op jit(solution)/shard_map/ppermute | solution.py:264
  23.4 0.5 %collective-permute-done.6 = bf16[64,256]{1,0:T(8,128)(2,1)S(1)} collective-permute-done((bf16[64,256]{1,0:T(8,128)(2,1)S(1)}, bf16[64,256]{1,0:T(8,128)(2,1)S(1)}, u32[]{:S(2)}, u32[]{:S(2)}) %collective-permute-start.6) | collective-permute-done | bytes 32800 | tf_op jit(solution)/shard_map/ppermute | solution.py:264
  23.9 0.6 %add_add_fusion = f32[64,256]{1,0:T(8,128)} fusion(bf16[64,256]{1,0:T(8,128)(2,1)S(1)} %collective-permute-done.8, bf16[64,256]{1,0:T(8,128)(2,1)S(1)} %collective-permute-done.7, bf16[64,256]{1,0:T(8,128)(2,1)S(1)} %collective-permute-done.6, bf16[64,256]{1,0:T(8,128)(2,1)S(1)} %add_convert_fusion), kind=kLoop, calls=%fused_computation | loop fusion | flops 114688 | bytes 196608 | tf_op jit(solution)/shard_map/add | solution.py:267
  (8 shorter events, 0.0 us)
Async XLA Ops:
  0.0 12.7 %collective-permute-start.1 = (bf16[1,1,3,4,4096]{4,3,2,1,0:T(4,128)(2,1)}, bf16[1,1,3,4,4096]{4,3,2,1,0:T(4,128)(2,1)S(1)}, u32[]{:S(2)}, u32[]{:S(2)}) collective-permute-start(bf16[1,1,3,4,4096]{4,3,2,1,0:T(4,128)(2,1)} %raw_hbm.1), channel_id=1, source_target_pairs={{0,2},{1,3},{2,0},{3,1},{4,6},{5,7},{6,4},{7,5},{8,10},{9,11},{10,... | collective-permute-start | bytes 294920 | tf_op jit(solution)/shard_map/ppermute | solution.py:211
  5.8 7.5 %collective-permute-start.2 = (bf16[520,128]{1,0:T(8,128)(2,1)S(1)}, bf16[520,128]{1,0:T(8,128)(2,1)S(1)}, u32[]{:S(2)}, u32[]{:S(2)}) collective-permute-start(bf16[520,128]{1,0:T(8,128)(2,1)S(1)} %pack.1.full_ref.refs_0_), channel_id=1, source_target_pairs={{0,1},{1,0},{2,3},{3,2},{4,7},{5,6},{6,5},{7,4},{8,9},{9,8},{10,11... | collective-permute-start | bytes 399368 | tf_op jit(solution)/shard_map/ppermute | solution.py:175
  7.5 5.2 %collective-permute-start = (bf16[72,128]{1,0:T(8,128)(2,1)S(1)}, bf16[72,128]{1,0:T(8,128)(2,1)S(1)}, u32[]{:S(2)}, u32[]{:S(2)}) collective-permute-start(bf16[72,128]{1,0:T(8,128)(2,1)S(1)} %tail.1.tail_ref), channel_id=1, source_target_pairs={{0,2},{1,3},{2,0},{3,1},{4,6},{5,7},{6,4},{7,5},{8,10},{9,11},{10,... | collective-permute-start | bytes 55304 | tf_op jit(solution)/shard_map/ppermute | solution.py:212
  7.8 6.7 %collective-permute-start.4 = (bf16[392,128]{1,0:T(8,128)(2,1)S(1)}, bf16[392,128]{1,0:T(8,128)(2,1)S(1)}, u32[]{:S(2)}, u32[]{:S(2)}) collective-permute-start(bf16[392,128]{1,0:T(8,128)(2,1)S(1)} %lean.1), channel_id=1, source_target_pairs={{0,3},{1,2},{2,1},{3,0},{4,5},{5,4},{6,7},{7,6},{8,11},{9,10},{10,... | collective-permute-start | bytes 301064 | tf_op jit(solution)/shard_map/ppermute | solution.py:175
  13.4 1.3 %copy-start = (bf16[64,256]{1,0:T(8,128)(2,1)S(1)}, bf16[64,256]{1,0:T(8,128)(2,1)}, u32[]{:S(2)}) copy-start(bf16[64,256]{1,0:T(8,128)(2,1)} %density_ref.1) | copy-start | bytes 98308
  13.4 1.2 %collective-permute-start.3 = (bf16[192,128]{1,0:T(8,128)(2,1)S(1)}, bf16[192,128]{1,0:T(8,128)(2,1)S(1)}, u32[]{:S(2)}, u32[]{:S(2)}) collective-permute-start(bf16[192,128]{1,0:T(8,128)(2,1)S(1)} %merge.1), channel_id=1, source_target_pairs={{0,4},{4,0},{8,12},{12,8},{16,20},{20,16},{24,28},{28,24},{1,5},{5... | collective-permute-start | bytes 147464 | tf_op jit(solution)/shard_map/ppermute | solution.py:225
  15.4 1.3 %collective-permute-start.5 = (f32[64,256]{1,0:T(8,128)S(1)}, f32[64,256]{1,0:T(8,128)S(1)}, u32[]{:S(2)}, u32[]{:S(2)}) collective-permute-start(f32[64,256]{1,0:T(8,128)S(1)} %exchange.1), channel_id=1, source_target_pairs={{0,4},{4,0},{8,12},{12,8},{16,20},{20,16},{24,28},{28,24},{1,5},{5... | collective-permute-start | bytes 196616 | tf_op jit(solution)/shard_map/ppermute | solution.py:264
  16.8 4.9 %collective-permute-start.8 = (bf16[64,256]{1,0:T(8,128)(2,1)S(1)}, bf16[64,256]{1,0:T(8,128)(2,1)S(1)}, u32[]{:S(2)}, u32[]{:S(2)}) collective-permute-start(bf16[64,256]{1,0:T(8,128)(2,1)S(1)} %add_convert_fusion), channel_id=1, source_target_pairs={{0,24},{4,28},{8,16},{12,20},{16,8},{20,12},{24,0},{28,4},{1,25},{... | collective-permute-start | bytes 98312 | tf_op jit(solution)/shard_map/ppermute | solution.py:264
  19.5 3.9 %collective-permute-start.7 = (bf16[64,256]{1,0:T(8,128)(2,1)S(1)}, bf16[64,256]{1,0:T(8,128)(2,1)S(1)}, u32[]{:S(2)}, u32[]{:S(2)}) collective-permute-start(bf16[64,256]{1,0:T(8,128)(2,1)S(1)} %add_convert_fusion), channel_id=1, source_target_pairs={{0,16},{4,20},{8,24},{12,28},{16,0},{20,4},{24,8},{28,12},{1,17},{... | collective-permute-start | bytes 98312 | tf_op jit(solution)/shard_map/ppermute | solution.py:264
  20.0 3.9 %collective-permute-start.6 = (bf16[64,256]{1,0:T(8,128)(2,1)S(1)}, bf16[64,256]{1,0:T(8,128)(2,1)S(1)}, u32[]{:S(2)}, u32[]{:S(2)}) collective-permute-start(bf16[64,256]{1,0:T(8,128)(2,1)S(1)} %add_convert_fusion), channel_id=1, source_target_pairs={{0,8},{4,12},{8,0},{12,4},{16,24},{20,28},{24,16},{28,20},{1,9},{5... | collective-permute-start | bytes 98312 | tf_op jit(solution)/shard_map/ppermute | solution.py:264

commit v28 on v27

--- a/solution.py
+++ b/solution.py
@@ -254,19 +254,28 @@
         name="exchange",
     )(codes, density, left, tail_in, swapped, *packs)
 
-    step = 1
+    odd = core_parity() == 1
+    beside = [(i, i ^ 1) for i in range(aux)]
+    parts = parts + lax.ppermute(parts, "aux", beside)
+    step = 2
     while step < aux:
-        ways = 2 if step == 1 or step * 4 > aux else 4
+        if step * 4 > aux:
+            parts = parts + lax.ppermute(parts, "aux", [(i, i ^ step) for i in range(aux)])
+            break
         if step == 2:
             parts = parts.astype(jnp.bfloat16)
-        terms = [parts]
-        for way in range(1, ways):
-            terms.append(lax.ppermute(parts, "aux", [(i, i ^ (way * step)) for i in range(aux)]))
-        terms = [term.astype(jnp.float32) for term in terms]
-        while len(terms) > 1:
-            terms = [terms[i] + terms[i + 1] for i in range(0, len(terms), 2)]
-        parts = terms[0]
-        step *= ways
+        mid = BS // 2
+        straight = [(i, i ^ (2 * step if i % 2 else step)) for i in range(aux)]
+        diagonal = [(i, i ^ (3 * step)) for i in range(aux)]
+        one = lax.ppermute(parts, "aux", straight)
+        two = lax.ppermute(jnp.where(odd, parts[mid:], parts[:mid]), "aux", diagonal)
+        got = jnp.concatenate([one, two], axis=0)
+        other = lax.ppermute(got, "aux", beside)
+        first = jnp.where(odd, other, got).astype(jnp.float32)
+        second = jnp.where(odd, got, other).astype(jnp.float32)
+        corner = jnp.concatenate([first[BS:], second[BS:]], axis=0)
+        parts = (parts.astype(jnp.float32) + first[:BS]) + (second[:BS] + corner)
+        step *= 4
     return parts
 
 

time: 24.7 us -> 25.3 us (1.024)
  waiting for transfers between devices: 8.62 us -> 9.41 us
  starting transfers between devices: 12.3 us -> 12 us
    ppermute x4, waiting for transfers between devices: 4.67 us -> 5.46 us  [the longest x1 2.42 us: shards(): lax.ppermute(jnp.where(odd, parts[mid:], parts[:mid]), 'aux', diagonal)]
    ppermute x4, starting transfers between devices: 3.78 us -> 3.48 us  [the longest x1 1.76 us: shards(): one = lax.ppermute(parts, 'aux', straight)]
where the time goes in v28:
time: 25.3 us; the launch traced here: 25.1 us
  starting transfers between devices  12 us (47%)
  waiting for transfers between devices  9.41 us (37%)
  Pallas kernels  2.11 us (8%)
  other arithmetic  0.76 us (3%)
  between operations  0.73 us (3%)
    ppermute x2, starting transfers between devices, shift(): return lax.ppermute(x, ('aux', 'orb'), perm)  4.18 us
    ppermute x1, starting transfers between devices, shards(): raw = lax.ppermute(tensor_blocks, 'orb', across)  4.04 us
    ppermute x1, waiting for transfers between devices, shards(): lax.ppermute(jnp.where(odd, parts[mid:], parts[:mid]), 'aux', diagonal)  2.42 us
    ppermute x1, waiting for transfers between devices, shards(): tail_in = lax.ppermute(tail, 'orb', across)  2.3 us
    ppermute x1, starting transfers between devices, shards(): one = lax.ppermute(parts, 'aux', straight)  1.76 us
    ppermute x2, waiting for transfers between devices, shift(): return lax.ppermute(x, ('aux', 'orb'), perm)  1.55 us
    ppermute x1, starting transfers between devices, shards(): lax.ppermute(jnp.where(odd, parts[mid:], parts[:mid]), 'aux', diagonal)  1.49 us
    ppermute x1, waiting for transfers between devices, shards(): other = lax.ppermute(got, 'aux', beside)  1.23 us
  transfers between devices with their start and end apart: 9, of which 8 were waited for; matrix products, arithmetic and copies ran while one was open for 0% of the time, Pallas kernels for 6%

profile of v28, /device:TPU:0, one launch (start us, length us, event | category | flops | bytes accessed | tf_op | source)
XLA Modules:
  0.0 25.1 jit_solution(8165424705154872565)
XLA Ops:
  0.0 4.0 %collective-permute-start.1 = (bf16[1,1,3,4,4096]{4,3,2,1,0:T(4,128)(2,1)}, bf16[1,1,3,4,4096]{4,3,2,1,0:T(4,128)(2,1)S(1)}, u32[]{:S(2)}, u32[]{:S(2)}) collective-permute-start(bf16[1,1,3,4,4096]{4,3,2,1,0:T(4,128)(2,1)} %raw_hbm.1), channel_id=1, source_target_pairs={{0,2},{1,3},{2,0},{3,1},{4,6},{5,7},{6,4},{7,5},{8,10},{9,11},{10,... | collective-permute-start | bytes 294920 | tf_op jit(solution)/shard_map/ppermute | solution.py:211
  4.7 1.1 %pack.1.full_ref.refs_0_ = bf16[520,128]{1,0:T(8,128)(2,1)S(1)} custom-call(s32[1,1]{1,0:T(1,128)S(6)} %copy.6.kept, s32[1,1,3]{2,1,0:T(1,128)} %pairs_hbm.1, bf16[64,256]{1,0:T(8,128)(2,1)} %density_ref.1, bf16[1,1,3,4,4096]{4,3,2,1,0:T(4,128)(2,1)} %raw_hbm.1), custom_call_target="tpu_custom_call" | custom-call | tf_op jit(solution)/shard_map/pack/pallas_call | solution.py:177
  5.8 1.6 %collective-permute-start.2 = (bf16[520,128]{1,0:T(8,128)(2,1)S(1)}, bf16[520,128]{1,0:T(8,128)(2,1)S(1)}, u32[]{:S(2)}, u32[]{:S(2)}) collective-permute-start(bf16[520,128]{1,0:T(8,128)(2,1)S(1)} %pack.1.full_ref.refs_0_), channel_id=1, source_target_pairs={{0,1},{1,0},{2,3},{3,2},{4,7},{5,6},{6,5},{7,4},{8,9},{9,8},{10,11... | collective-permute-start | bytes 399368 | tf_op jit(solution)/shard_map/ppermute | solution.py:175
  7.5 0.3 %collective-permute-start = (bf16[72,128]{1,0:T(8,128)(2,1)S(1)}, bf16[72,128]{1,0:T(8,128)(2,1)S(1)}, u32[]{:S(2)}, u32[]{:S(2)}) collective-permute-start(bf16[72,128]{1,0:T(8,128)(2,1)S(1)} %tail.1.tail_ref), channel_id=1, source_target_pairs={{0,2},{1,3},{2,0},{3,1},{4,6},{5,7},{6,4},{7,5},{8,10},{9,11},{10,... | collective-permute-start | bytes 55304 | tf_op jit(solution)/shard_map/ppermute | solution.py:212
  7.8 2.5 %collective-permute-start.4 = (bf16[392,128]{1,0:T(8,128)(2,1)S(1)}, bf16[392,128]{1,0:T(8,128)(2,1)S(1)}, u32[]{:S(2)}, u32[]{:S(2)}) collective-permute-start(bf16[392,128]{1,0:T(8,128)(2,1)S(1)} %lean.1), channel_id=1, source_target_pairs={{0,3},{1,2},{2,1},{3,0},{4,5},{5,4},{6,7},{7,6},{8,11},{9,10},{10,... | collective-permute-start | bytes 301064 | tf_op jit(solution)/shard_map/ppermute | solution.py:175
  10.4 2.3 %collective-permute-done.refs_1_.tail = bf16[72,128]{1,0:T(8,128)(2,1)S(1)} collective-permute-done((bf16[72,128]{1,0:T(8,128)(2,1)S(1)}, bf16[72,128]{1,0:T(8,128)(2,1)S(1)}, u32[]{:S(2)}, u32[]{:S(2)}) %collective-permute-start) | collective-permute-done | bytes 18464 | tf_op jit(solution)/shard_map/ppermute | solution.py:212
  12.7 0.0 collective-permute-done.1.raw
  12.7 0.2 relay.1
  12.9 0.4 %collective-permute-done.2.refs_0_.refs_2_ = bf16[520,128]{1,0:T(8,128)(2,1)S(1)} collective-permute-done((bf16[520,128]{1,0:T(8,128)(2,1)S(1)}, bf16[520,128]{1,0:T(8,128)(2,1)S(1)}, u32[]{:S(2)}, u32[]{:S(2)}) %collective-permute-start.2) | collective-permute-done | bytes 133152 | tf_op jit(solution)/shard_map/ppermute | solution.py:175
  13.4 0.0 copy-start
  13.4 0.0 collective-permute-start.3
  13.4 1.1 %collective-permute-done.4.refs_3_ = bf16[392,128]{1,0:T(8,128)(2,1)S(1)} collective-permute-done((bf16[392,128]{1,0:T(8,128)(2,1)S(1)}, bf16[392,128]{1,0:T(8,128)(2,1)S(1)}, u32[]{:S(2)}, u32[]{:S(2)}) %collective-permute-start.4) | collective-permute-done | bytes 100384 | tf_op jit(solution)/shard_map/ppermute | solution.py:175
  14.5 0.1 collective-permute-done.3.swapped
  14.6 0.1 maximum_convert_fusion.meta_ref
  14.7 0.0 copy-done
  14.7 0.7 %exchange.1 = f32[64,256]{1,0:T(8,128)S(1)} custom-call(s32[12]{0:T(128)S(1)} %maximum_convert_fusion.meta_ref, bf16[64,256]{1,0:T(8,128)(2,1)S(1)} %copy-done, bf16[256,192]{1,0:T(8,128)(2,1)S(1)} %get-tuple-element.14.left_ref, bf16[72,128]{1,0:T(8,128)(2,1)S(1)} %collective-permute-done.refs_1_.tail, bf16[192,128]{1,0:T(8,128)(2,1)S(1)} %collective-permute-done.3.swapped, ...), custom_call_target="tpu_custom_call" | custom-call | tf_op jit(solution)/shard_map/exchange/pallas_call | solution.py:243
  15.4 0.2 collective-permute-start.5
  15.6 1.1 %collective-permute-done.5 = f32[64,256]{1,0:T(8,128)S(1)} collective-permute-done((f32[64,256]{1,0:T(8,128)S(1)}, f32[64,256]{1,0:T(8,128)S(1)}, u32[]{:S(2)}, u32[]{:S(2)}) %collective-permute-start.5) | collective-permute-done | bytes 65568 | tf_op jit(solution)/shard_map/ppermute | solution.py:259
  16.8 1.8 %collective-permute-start.6 = (bf16[64,256]{1,0:T(8,128)(2,1)S(1)}, bf16[64,256]{1,0:T(8,128)(2,1)S(1)}, u32[]{:S(2)}, u32[]{:S(2)}) collective-permute-start(bf16[64,256]{1,0:T(8,128)(2,1)S(1)} %add_convert_fusion), channel_id=1, source_target_pairs={{0,8},{4,20},{8,0},{12,28},{16,24},{20,4},{24,16},{28,12},{1,9},{5... | collective-permute-start | bytes 98312 | tf_op jit(solution)/shard_map/ppermute | solution.py:270
  18.5 1.5 %collective-permute-start.7 = (bf16[32,256]{1,0:T(8,128)(2,1)S(1)}, bf16[32,256]{1,0:T(8,128)(2,1)S(1)}, u32[]{:S(2)}, u32[]{:S(2)}) collective-permute-start(bf16[32,256]{1,0:T(8,128)(2,1)S(1)} %slice_select_fusion), channel_id=1, source_target_pairs={{0,24},{4,28},{8,16},{12,20},{16,8},{20,12},{24,0},{28,4},{1,25},{... | collective-permute-start | bytes 49160 | tf_op jit(solution)/shard_map/ppermute | solution.py:271
  20.0 0.7 %collective-permute-done.6 = bf16[64,256]{1,0:T(8,128)(2,1)S(1)} collective-permute-done((bf16[64,256]{1,0:T(8,128)(2,1)S(1)}, bf16[64,256]{1,0:T(8,128)(2,1)S(1)}, u32[]{:S(2)}, u32[]{:S(2)}) %collective-permute-start.6) | collective-permute-done | bytes 32800 | tf_op jit(solution)/shard_map/ppermute | solution.py:270
  20.7 2.4 %collective-permute-done.7 = bf16[32,256]{1,0:T(8,128)(2,1)S(1)} collective-permute-done((bf16[32,256]{1,0:T(8,128)(2,1)S(1)}, bf16[32,256]{1,0:T(8,128)(2,1)S(1)}, u32[]{:S(2)}, u32[]{:S(2)}) %collective-permute-start.7) | collective-permute-done | bytes 16416 | tf_op jit(solution)/shard_map/ppermute | solution.py:271
  23.2 0.0 collective-permute-start.8
  23.2 1.2 %collective-permute-done.8 = bf16[96,256]{1,0:T(8,128)(2,1)S(1)} collective-permute-done((bf16[96,256]{1,0:T(8,128)(2,1)S(1)}, bf16[96,256]{1,0:T(8,128)(2,1)S(1)}, u32[]{:S(2)}, u32[]{:S(2)}) %collective-permute-start.8) | collective-permute-done | bytes 49184 | tf_op jit(solution)/shard_map/ppermute | solution.py:273
  24.4 0.6 %fusion = f32[64,256]{1,0:T(8,128)} fusion(f32[96,256]{1,0:T(8,128)S(1)} %get-tuple-element.18, f32[96,256]{1,0:T(8,128)S(1)} %get-tuple-element.17, f32[32,256]{1,0:T(8,128)S(1)} %slice.47, f32[32,256]{1,0:T(8,128)S(1)} %slice.46, bf16[64,256]{1,0:T(8,128)(2,1)S(1)} %add_convert_fusion), kind=kLoop, calls=%fused_computation.1 | loop fusion | flops 81920 | bytes 294912 | tf_op jit(solution)/shard_map/add | solution.py:277
  (14 shorter events, 0.1 us)
Async XLA Ops:
  0.0 12.7 %collective-permute-start.1 = (bf16[1,1,3,4,4096]{4,3,2,1,0:T(4,128)(2,1)}, bf16[1,1,3,4,4096]{4,3,2,1,0:T(4,128)(2,1)S(1)}, u32[]{:S(2)}, u32[]{:S(2)}) collective-permute-start(bf16[1,1,3,4,4096]{4,3,2,1,0:T(4,128)(2,1)} %raw_hbm.1), channel_id=1, source_target_pairs={{0,2},{1,3},{2,0},{3,1},{4,6},{5,7},{6,4},{7,5},{8,10},{9,11},{10,... | collective-permute-start | bytes 294920 | tf_op jit(solution)/shard_map/ppermute | solution.py:211
  5.8 7.5 %collective-permute-start.2 = (bf16[520,128]{1,0:T(8,128)(2,1)S(1)}, bf16[520,128]{1,0:T(8,128)(2,1)S(1)}, u32[]{:S(2)}, u32[]{:S(2)}) collective-permute-start(bf16[520,128]{1,0:T(8,128)(2,1)S(1)} %pack.1.full_ref.refs_0_), channel_id=1, source_target_pairs={{0,1},{1,0},{2,3},{3,2},{4,7},{5,6},{6,5},{7,4},{8,9},{9,8},{10,11... | collective-permute-start | bytes 399368 | tf_op jit(solution)/shard_map/ppermute | solution.py:175
  7.5 5.2 %collective-permute-start = (bf16[72,128]{1,0:T(8,128)(2,1)S(1)}, bf16[72,128]{1,0:T(8,128)(2,1)S(1)}, u32[]{:S(2)}, u32[]{:S(2)}) collective-permute-start(bf16[72,128]{1,0:T(8,128)(2,1)S(1)} %tail.1.tail_ref), channel_id=1, source_target_pairs={{0,2},{1,3},{2,0},{3,1},{4,6},{5,7},{6,4},{7,5},{8,10},{9,11},{10,... | collective-permute-start | bytes 55304 | tf_op jit(solution)/shard_map/ppermute | solution.py:212
  7.8 6.7 %collective-permute-start.4 = (bf16[392,128]{1,0:T(8,128)(2,1)S(1)}, bf16[392,128]{1,0:T(8,128)(2,1)S(1)}, u32[]{:S(2)}, u32[]{:S(2)}) collective-permute-start(bf16[392,128]{1,0:T(8,128)(2,1)S(1)} %lean.1), channel_id=1, source_target_pairs={{0,3},{1,2},{2,1},{3,0},{4,5},{5,4},{6,7},{7,6},{8,11},{9,10},{10,... | collective-permute-start | bytes 301064 | tf_op jit(solution)/shard_map/ppermute | solution.py:175
  13.4 1.3 %copy-start = (bf16[64,256]{1,0:T(8,128)(2,1)S(1)}, bf16[64,256]{1,0:T(8,128)(2,1)}, u32[]{:S(2)}) copy-start(bf16[64,256]{1,0:T(8,128)(2,1)} %density_ref.1) | copy-start | bytes 98308
  13.4 1.2 %collective-permute-start.3 = (bf16[192,128]{1,0:T(8,128)(2,1)S(1)}, bf16[192,128]{1,0:T(8,128)(2,1)S(1)}, u32[]{:S(2)}, u32[]{:S(2)}) collective-permute-start(bf16[192,128]{1,0:T(8,128)(2,1)S(1)} %merge.1), channel_id=1, source_target_pairs={{0,4},{4,0},{8,12},{12,8},{16,20},{20,16},{24,28},{28,24},{1,5},{5... | collective-permute-start | bytes 147464 | tf_op jit(solution)/shard_map/ppermute | solution.py:225
  15.4 1.3 %collective-permute-start.5 = (f32[64,256]{1,0:T(8,128)S(1)}, f32[64,256]{1,0:T(8,128)S(1)}, u32[]{:S(2)}, u32[]{:S(2)}) collective-permute-start(f32[64,256]{1,0:T(8,128)S(1)} %exchange.1), channel_id=1, source_target_pairs={{0,4},{4,0},{8,12},{12,8},{16,20},{20,16},{24,28},{28,24},{1,5},{5... | collective-permute-start | bytes 196616 | tf_op jit(solution)/shard_map/ppermute | solution.py:259
  16.8 4.0 %collective-permute-start.6 = (bf16[64,256]{1,0:T(8,128)(2,1)S(1)}, bf16[64,256]{1,0:T(8,128)(2,1)S(1)}, u32[]{:S(2)}, u32[]{:S(2)}) collective-permute-start(bf16[64,256]{1,0:T(8,128)(2,1)S(1)} %add_convert_fusion), channel_id=1, source_target_pairs={{0,8},{4,20},{8,0},{12,28},{16,24},{20,4},{24,16},{28,12},{1,9},{5... | collective-permute-start | bytes 98312 | tf_op jit(solution)/shard_map/ppermute | solution.py:270
  18.5 4.6 %collective-permute-start.7 = (bf16[32,256]{1,0:T(8,128)(2,1)S(1)}, bf16[32,256]{1,0:T(8,128)(2,1)S(1)}, u32[]{:S(2)}, u32[]{:S(2)}) collective-permute-start(bf16[32,256]{1,0:T(8,128)(2,1)S(1)} %slice_select_fusion), channel_id=1, source_target_pairs={{0,24},{4,28},{8,16},{12,20},{16,8},{20,12},{24,0},{28,4},{1,25},{... | collective-permute-start | bytes 49160 | tf_op jit(solution)/shard_map/ppermute | solution.py:271
  23.2 1.2 %collective-permute-start.8 = (bf16[96,256]{1,0:T(8,128)(2,1)S(1)}, bf16[96,256]{1,0:T(8,128)(2,1)S(1)}, u32[]{:S(2)}, u32[]{:S(2)}) collective-permute-start(bf16[96,256]{1,0:T(8,128)(2,1)S(1)} %constant_dynamic-update-slice_fusion), channel_id=1, source_target_pairs={{0,4},{4,0},{8,12},{12,8},{16,20},{20,16},{24,28},{28,24},{1,5},{5... | collective-permute-start | bytes 147464 | tf_op jit(solution)/shard_map/ppermute | solution.py:273

commit v29 on v27

--- a/solution.py
+++ b/solution.py
@@ -23,14 +23,18 @@
 
 def partner(i, step, sign, orb):
     if orb == 4:
-        return i ^ (2 - sign)
+        return i ^ (5 - sign) // 2
     return (i + sign * step) % orb
 
 
 def owner_of(me, step, sign, orb):
     if orb == 4:
-        return me ^ (2 - sign)
+        return me ^ jnp.where(sign > 0, 2, 3)
     return lax.rem(me - sign * step + orb, orb)
+
+
+def opposite(i, orb):
+    return i ^ 1 if orb == 4 else (i + orb // 2) % orb
 
 
 def core_parity():
@@ -114,7 +118,7 @@
     size = slots * aux_width * BS // LANES * BS
     near = pl.multiple_of(parity * height, height)
     far = pl.multiple_of((1 - parity) * height, height)
-    across = lax.rem(me + orb // 2, orb)
+    across = opposite(me, orb)
     owners = [me, across]
     rows[me] = density_ref[...]
     for i, full in enumerate(fulls):
@@ -207,7 +211,7 @@
         compiler_params=params,
         name="lean",
     )(full, tail)
-    across = [(i, (i + orb // 2) % orb) for i in range(orb)]
+    across = [(i, opposite(i, orb)) for i in range(orb)]
     raw = lax.ppermute(tensor_blocks, "orb", across)
     tail_in = lax.ppermute(tail, "orb", across)
     fulls = [shift(full, i, 1) for i in range(1, orb // 2)]

time: 24.7 us -> 28 us (1.13)
  waiting for transfers between devices: 8.62 us -> 12.9 us
  starting transfers between devices: 12.3 us -> 11.3 us
    ppermute x2, waiting for transfers between devices: 1.55 us -> 5.14 us  [shift(): return lax.ppermute(x, ('aux', 'orb'), perm)]
    ppermute x1, waiting for transfers between devices: 0.1 us -> 1.2 us  [shards(): swapped = lax.ppermute(merged, 'aux', [(i, i ^ 1) for i in range(aux)])]
    ppermute x1, starting transfers between devices: 4.04 us -> 3.02 us  [shards(): raw = lax.ppermute(tensor_blocks, 'orb', across)]
  transfers between devices with their start and end apart: 9 -> 9, of which waited for: 8 -> 7; matrix products, arithmetic and copies ran while one was open for 0% -> 0% of each run, Pallas kernels for 6% -> 5%
where the time goes in v29:
time: 28 us; the launch traced here: 27.8 us
  waiting for transfers between devices  12.9 us (46%)
  starting transfers between devices  11.3 us (40%)
  Pallas kernels  2.12 us (8%)
  other arithmetic  0.74 us (3%)
  between operations  0.72 us (3%)
    ppermute x2, waiting for transfers between devices, shift(): return lax.ppermute(x, ('aux', 'orb'), perm)  5.14 us
    ppermute x4, waiting for transfers between devices, shards(): lax.ppermute(parts, 'aux', [(i, i ^ way * step) for i in range(aux)])  4.48 us
    ppermute x2, starting transfers between devices, shift(): return lax.ppermute(x, ('aux', 'orb'), perm)  4.07 us
    ppermute x4, starting transfers between devices, shards(): lax.ppermute(parts, 'aux', [(i, i ^ way * step) for i in range(aux)])  3.77 us
    ppermute x1, starting transfers between devices, shards(): raw = lax.ppermute(tensor_blocks, 'orb', across)  3.02 us
    ppermute x1, waiting for transfers between devices, shards(): tail_in = lax.ppermute(tail, 'orb', across)  2.08 us
    ppermute x1, waiting for transfers between devices, shards(): swapped = lax.ppermute(merged, 'aux', [(i, i ^ 1) for i in range(aux)])  1.2 us
    pallas_call x1, Pallas kernels, shards(): pl.pallas_call(functools.partial(pack_kernel, orb), out_shape=array(size...  1.14 us
  transfers between devices with their start and end apart: 9, of which 7 were waited for; matrix products, arithmetic and copies ran while one was open for 0% of the time, Pallas kernels for 5%

profile of v29, /device:TPU:0, one launch (start us, length us, event | category | flops | bytes accessed | tf_op | source)
XLA Modules:
  0.0 27.8 jit_solution(12053774479620161822)
XLA Ops:
  0.0 3.0 %collective-permute-start.1 = (bf16[1,1,3,4,4096]{4,3,2,1,0:T(4,128)(2,1)}, bf16[1,1,3,4,4096]{4,3,2,1,0:T(4,128)(2,1)S(1)}, u32[]{:S(2)}, u32[]{:S(2)}) collective-permute-start(bf16[1,1,3,4,4096]{4,3,2,1,0:T(4,128)(2,1)} %raw_hbm.1), channel_id=1, source_target_pairs={{0,1},{1,0},{2,3},{3,2},{4,5},{5,4},{6,7},{7,6},{8,9},{9,8},{10,11... | collective-permute-start | bytes 294920 | tf_op jit(solution)/shard_map/ppermute | solution.py:215
  3.7 1.1 %pack.1.full_ref.refs_0_ = bf16[520,128]{1,0:T(8,128)(2,1)S(1)} custom-call(s32[1,1]{1,0:T(1,128)S(6)} %copy.5.kept, s32[1,1,3]{2,1,0:T(1,128)} %pairs_hbm.1, bf16[64,256]{1,0:T(8,128)(2,1)} %density_ref.1, bf16[1,1,3,4,4096]{4,3,2,1,0:T(4,128)(2,1)} %raw_hbm.1), custom_call_target="tpu_custom_call" | custom-call | tf_op jit(solution)/shard_map/pack/pallas_call | solution.py:181
  4.8 2.7 %collective-permute-start.2 = (bf16[520,128]{1,0:T(8,128)(2,1)S(1)}, bf16[520,128]{1,0:T(8,128)(2,1)S(1)}, u32[]{:S(2)}, u32[]{:S(2)}) collective-permute-start(bf16[520,128]{1,0:T(8,128)(2,1)S(1)} %pack.1.full_ref.refs_0_), channel_id=1, source_target_pairs={{0,2},{1,3},{2,0},{3,1},{4,7},{5,6},{6,5},{7,4},{8,10},{9,11},{10,... | collective-permute-start | bytes 399368 | tf_op jit(solution)/shard_map/ppermute | solution.py:179
  7.5 0.4 %collective-permute-start = (bf16[72,128]{1,0:T(8,128)(2,1)S(1)}, bf16[72,128]{1,0:T(8,128)(2,1)S(1)}, u32[]{:S(2)}, u32[]{:S(2)}) collective-permute-start(bf16[72,128]{1,0:T(8,128)(2,1)S(1)} %tail.1.tail_ref), channel_id=1, source_target_pairs={{0,1},{1,0},{2,3},{3,2},{4,5},{5,4},{6,7},{7,6},{8,9},{9,8},{10,11... | collective-permute-start | bytes 55304 | tf_op jit(solution)/shard_map/ppermute | solution.py:216
  7.9 1.4 %collective-permute-start.4 = (bf16[392,128]{1,0:T(8,128)(2,1)S(1)}, bf16[392,128]{1,0:T(8,128)(2,1)S(1)}, u32[]{:S(2)}, u32[]{:S(2)}) collective-permute-start(bf16[392,128]{1,0:T(8,128)(2,1)S(1)} %lean.1), channel_id=1, source_target_pairs={{0,3},{1,2},{2,1},{3,0},{4,6},{5,7},{6,4},{7,5},{8,11},{9,10},{10,... | collective-permute-start | bytes 301064 | tf_op jit(solution)/shard_map/ppermute | solution.py:179
  9.4 2.1 %collective-permute-done.refs_1_.tail = bf16[72,128]{1,0:T(8,128)(2,1)S(1)} collective-permute-done((bf16[72,128]{1,0:T(8,128)(2,1)S(1)}, bf16[72,128]{1,0:T(8,128)(2,1)S(1)}, u32[]{:S(2)}, u32[]{:S(2)}) %collective-permute-start) | collective-permute-done | bytes 18464 | tf_op jit(solution)/shard_map/ppermute | solution.py:216
  11.4 0.0 collective-permute-done.1.raw
  11.4 0.2 relay.1
  11.7 5.1 %collective-permute-done.2.refs_0_.refs_2_ = bf16[520,128]{1,0:T(8,128)(2,1)S(1)} collective-permute-done((bf16[520,128]{1,0:T(8,128)(2,1)S(1)}, bf16[520,128]{1,0:T(8,128)(2,1)S(1)}, u32[]{:S(2)}, u32[]{:S(2)}) %collective-permute-start.2) | collective-permute-done | bytes 133152 | tf_op jit(solution)/shard_map/ppermute | solution.py:179
  16.8 0.0 copy-start
  16.8 0.0 collective-permute-start.3
  16.8 0.0 collective-permute-done.4.refs_3_
  16.9 1.2 %collective-permute-done.3.swapped = bf16[192,128]{1,0:T(8,128)(2,1)S(1)} collective-permute-done((bf16[192,128]{1,0:T(8,128)(2,1)S(1)}, bf16[192,128]{1,0:T(8,128)(2,1)S(1)}, u32[]{:S(2)}, u32[]{:S(2)}) %collective-permute-start.3) | collective-permute-done | bytes 49184 | tf_op jit(solution)/shard_map/ppermute | solution.py:229
  18.1 0.1 maximum_convert_fusion.meta_ref
  18.1 0.0 copy-done
  18.1 0.7 %exchange.1 = f32[64,256]{1,0:T(8,128)S(1)} custom-call(s32[12]{0:T(128)S(1)} %maximum_convert_fusion.meta_ref, bf16[64,256]{1,0:T(8,128)(2,1)S(1)} %copy-done, bf16[256,192]{1,0:T(8,128)(2,1)S(1)} %get-tuple-element.14.left_ref, bf16[72,128]{1,0:T(8,128)(2,1)S(1)} %collective-permute-done.refs_1_.tail, bf16[192,128]{1,0:T(8,128)(2,1)S(1)} %collective-permute-done.3.swapped, ...), custom_call_target="tpu_custom_call" | custom-call | tf_op jit(solution)/shard_map/exchange/pallas_call | solution.py:247
  18.9 0.2 collective-permute-start.5
  19.1 1.1 %collective-permute-done.5 = f32[64,256]{1,0:T(8,128)S(1)} collective-permute-done((f32[64,256]{1,0:T(8,128)S(1)}, f32[64,256]{1,0:T(8,128)S(1)}, u32[]{:S(2)}, u32[]{:S(2)}) %collective-permute-start.5) | collective-permute-done | bytes 65568 | tf_op jit(solution)/shard_map/ppermute | solution.py:268
  20.2 2.5 %collective-permute-start.8 = (bf16[64,256]{1,0:T(8,128)(2,1)S(1)}, bf16[64,256]{1,0:T(8,128)(2,1)S(1)}, u32[]{:S(2)}, u32[]{:S(2)}) collective-permute-start(bf16[64,256]{1,0:T(8,128)(2,1)S(1)} %add_convert_fusion), channel_id=1, source_target_pairs={{0,24},{4,28},{8,16},{12,20},{16,8},{20,12},{24,0},{28,4},{1,25},{... | collective-permute-start | bytes 98312 | tf_op jit(solution)/shard_map/ppermute | solution.py:268
  22.7 0.5 %collective-permute-start.7 = (bf16[64,256]{1,0:T(8,128)(2,1)S(1)}, bf16[64,256]{1,0:T(8,128)(2,1)S(1)}, u32[]{:S(2)}, u32[]{:S(2)}) collective-permute-start(bf16[64,256]{1,0:T(8,128)(2,1)S(1)} %add_convert_fusion), channel_id=1, source_target_pairs={{0,16},{4,20},{8,24},{12,28},{16,0},{20,4},{24,8},{28,12},{1,17},{... | collective-permute-start | bytes 98312 | tf_op jit(solution)/shard_map/ppermute | solution.py:268
  23.2 0.5 %collective-permute-start.6 = (bf16[64,256]{1,0:T(8,128)(2,1)S(1)}, bf16[64,256]{1,0:T(8,128)(2,1)S(1)}, u32[]{:S(2)}, u32[]{:S(2)}) collective-permute-start(bf16[64,256]{1,0:T(8,128)(2,1)S(1)} %add_convert_fusion), channel_id=1, source_target_pairs={{0,8},{4,12},{8,0},{12,4},{16,24},{20,28},{24,16},{28,20},{1,9},{5... | collective-permute-start | bytes 98312 | tf_op jit(solution)/shard_map/ppermute | solution.py:268
  23.8 1.3 %collective-permute-done.8 = bf16[64,256]{1,0:T(8,128)(2,1)S(1)} collective-permute-done((bf16[64,256]{1,0:T(8,128)(2,1)S(1)}, bf16[64,256]{1,0:T(8,128)(2,1)S(1)}, u32[]{:S(2)}, u32[]{:S(2)}) %collective-permute-start.8) | collective-permute-done | bytes 32800 | tf_op jit(solution)/shard_map/ppermute | solution.py:268
  25.1 1.5 %collective-permute-done.7 = bf16[64,256]{1,0:T(8,128)(2,1)S(1)} collective-permute-done((bf16[64,256]{1,0:T(8,128)(2,1)S(1)}, bf16[64,256]{1,0:T(8,128)(2,1)S(1)}, u32[]{:S(2)}, u32[]{:S(2)}) %collective-permute-start.7) | collective-permute-done | bytes 32800 | tf_op jit(solution)/shard_map/ppermute | solution.py:268
  26.6 0.5 %collective-permute-done.6 = bf16[64,256]{1,0:T(8,128)(2,1)S(1)} collective-permute-done((bf16[64,256]{1,0:T(8,128)(2,1)S(1)}, bf16[64,256]{1,0:T(8,128)(2,1)S(1)}, u32[]{:S(2)}, u32[]{:S(2)}) %collective-permute-start.6) | collective-permute-done | bytes 32800 | tf_op jit(solution)/shard_map/ppermute | solution.py:268
  27.1 0.6 %add_add_fusion = f32[64,256]{1,0:T(8,128)} fusion(bf16[64,256]{1,0:T(8,128)(2,1)S(1)} %collective-permute-done.8, bf16[64,256]{1,0:T(8,128)(2,1)S(1)} %collective-permute-done.7, bf16[64,256]{1,0:T(8,128)(2,1)S(1)} %collective-permute-done.6, bf16[64,256]{1,0:T(8,128)(2,1)S(1)} %add_convert_fusion), kind=kLoop, calls=%fused_computation | loop fusion | flops 114688 | bytes 196608 | tf_op jit(solution)/shard_map/add | solution.py:271
  (8 shorter events, 0.0 us)
Async XLA Ops:
  0.0 11.4 %collective-permute-start.1 = (bf16[1,1,3,4,4096]{4,3,2,1,0:T(4,128)(2,1)}, bf16[1,1,3,4,4096]{4,3,2,1,0:T(4,128)(2,1)S(1)}, u32[]{:S(2)}, u32[]{:S(2)}) collective-permute-start(bf16[1,1,3,4,4096]{4,3,2,1,0:T(4,128)(2,1)} %raw_hbm.1), channel_id=1, source_target_pairs={{0,1},{1,0},{2,3},{3,2},{4,5},{5,4},{6,7},{7,6},{8,9},{9,8},{10,11... | collective-permute-start | bytes 294920 | tf_op jit(solution)/shard_map/ppermute | solution.py:215
  4.8 12.0 %collective-permute-start.2 = (bf16[520,128]{1,0:T(8,128)(2,1)S(1)}, bf16[520,128]{1,0:T(8,128)(2,1)S(1)}, u32[]{:S(2)}, u32[]{:S(2)}) collective-permute-start(bf16[520,128]{1,0:T(8,128)(2,1)S(1)} %pack.1.full_ref.refs_0_), channel_id=1, source_target_pairs={{0,2},{1,3},{2,0},{3,1},{4,7},{5,6},{6,5},{7,4},{8,10},{9,11},{10,... | collective-permute-start | bytes 399368 | tf_op jit(solution)/shard_map/ppermute | solution.py:179
  7.5 4.0 %collective-permute-start = (bf16[72,128]{1,0:T(8,128)(2,1)S(1)}, bf16[72,128]{1,0:T(8,128)(2,1)S(1)}, u32[]{:S(2)}, u32[]{:S(2)}) collective-permute-start(bf16[72,128]{1,0:T(8,128)(2,1)S(1)} %tail.1.tail_ref), channel_id=1, source_target_pairs={{0,1},{1,0},{2,3},{3,2},{4,5},{5,4},{6,7},{7,6},{8,9},{9,8},{10,11... | collective-permute-start | bytes 55304 | tf_op jit(solution)/shard_map/ppermute | solution.py:216
  7.9 8.9 %collective-permute-start.4 = (bf16[392,128]{1,0:T(8,128)(2,1)S(1)}, bf16[392,128]{1,0:T(8,128)(2,1)S(1)}, u32[]{:S(2)}, u32[]{:S(2)}) collective-permute-start(bf16[392,128]{1,0:T(8,128)(2,1)S(1)} %lean.1), channel_id=1, source_target_pairs={{0,3},{1,2},{2,1},{3,0},{4,6},{5,7},{6,4},{7,5},{8,11},{9,10},{10,... | collective-permute-start | bytes 301064 | tf_op jit(solution)/shard_map/ppermute | solution.py:179
  16.8 1.3 %copy-start = (bf16[64,256]{1,0:T(8,128)(2,1)S(1)}, bf16[64,256]{1,0:T(8,128)(2,1)}, u32[]{:S(2)}) copy-start(bf16[64,256]{1,0:T(8,128)(2,1)} %density_ref.1) | copy-start | bytes 98308
  16.8 1.2 %collective-permute-start.3 = (bf16[192,128]{1,0:T(8,128)(2,1)S(1)}, bf16[192,128]{1,0:T(8,128)(2,1)S(1)}, u32[]{:S(2)}, u32[]{:S(2)}) collective-permute-start(bf16[192,128]{1,0:T(8,128)(2,1)S(1)} %merge.1), channel_id=1, source_target_pairs={{0,4},{4,0},{8,12},{12,8},{16,20},{20,16},{24,28},{28,24},{1,5},{5... | collective-permute-start | bytes 147464 | tf_op jit(solution)/shard_map/ppermute | solution.py:229
  18.9 1.3 %collective-permute-start.5 = (f32[64,256]{1,0:T(8,128)S(1)}, f32[64,256]{1,0:T(8,128)S(1)}, u32[]{:S(2)}, u32[]{:S(2)}) collective-permute-start(f32[64,256]{1,0:T(8,128)S(1)} %exchange.1), channel_id=1, source_target_pairs={{0,4},{4,0},{8,12},{12,8},{16,20},{20,16},{24,28},{28,24},{1,5},{5... | collective-permute-start | bytes 196616 | tf_op jit(solution)/shard_map/ppermute | solution.py:268
  20.2 4.9 %collective-permute-start.8 = (bf16[64,256]{1,0:T(8,128)(2,1)S(1)}, bf16[64,256]{1,0:T(8,128)(2,1)S(1)}, u32[]{:S(2)}, u32[]{:S(2)}) collective-permute-start(bf16[64,256]{1,0:T(8,128)(2,1)S(1)} %add_convert_fusion), channel_id=1, source_target_pairs={{0,24},{4,28},{8,16},{12,20},{16,8},{20,12},{24,0},{28,4},{1,25},{... | collective-permute-start | bytes 98312 | tf_op jit(solution)/shard_map/ppermute | solution.py:268
  22.7 3.9 %collective-permute-start.7 = (bf16[64,256]{1,0:T(8,128)(2,1)S(1)}, bf16[64,256]{1,0:T(8,128)(2,1)S(1)}, u32[]{:S(2)}, u32[]{:S(2)}) collective-permute-start(bf16[64,256]{1,0:T(8,128)(2,1)S(1)} %add_convert_fusion), channel_id=1, source_target_pairs={{0,16},{4,20},{8,24},{12,28},{16,0},{20,4},{24,8},{28,12},{1,17},{... | collective-permute-start | bytes 98312 | tf_op jit(solution)/shard_map/ppermute | solution.py:268
  23.2 3.9 %collective-permute-start.6 = (bf16[64,256]{1,0:T(8,128)(2,1)S(1)}, bf16[64,256]{1,0:T(8,128)(2,1)S(1)}, u32[]{:S(2)}, u32[]{:S(2)}) collective-permute-start(bf16[64,256]{1,0:T(8,128)(2,1)S(1)} %add_convert_fusion), channel_id=1, source_target_pairs={{0,8},{4,12},{8,0},{12,4},{16,24},{20,28},{24,16},{28,20},{1,9},{5... | collective-permute-start | bytes 98312 | tf_op jit(solution)/shard_map/ppermute | solution.py:268

commit v30 on v27

--- a/solution.py
+++ b/solution.py
@@ -12,12 +12,12 @@
 NOTE = 8
 
 
-def lay_blocks(raw, out_ref):
+def lay_blocks(raw, out_ref, first=0):
     slots, aux_width = raw.shape[:2]
     square = raw.reshape(slots * aux_width, BS, BS)
     for tile in range(slots * aux_width // 2):
         both = jnp.concatenate([square[2 * tile], square[2 * tile + 1]], axis=1)
-        out_ref[tile * BS : (tile + 1) * BS] = both
+        out_ref[first + tile * BS : first + (tile + 1) * BS] = both
     return slots * aux_width // 2
 
 
@@ -40,13 +40,15 @@
 def pack_kernel(
     orb, kept, pairs_hbm, density_hbm, raw_hbm, full_ref, pairs, rows, raw, sems
 ):
+    slots = raw.shape[2]
+    moves = [(density_hbm, rows), (pairs_hbm, pairs)]
+    moves += [(raw_hbm.at[0, 0, j], raw.at[0, 0, j]) for j in range(slots)]
     copies = [
-        pltpu.make_async_copy(src, dst, sems.at[i])
-        for i, (src, dst) in enumerate(((raw_hbm, raw), (density_hbm, rows), (pairs_hbm, pairs)))
+        pltpu.make_async_copy(src, dst, sems.at[i]) for i, (src, dst) in enumerate(moves)
     ]
     for copy in copies:
         copy.start()
-    for copy in copies[1:]:
+    for copy in copies[:2]:
         copy.wait()
     tiles = rows.shape[1] // LANES
     size = full_ref.shape[0] - tiles * BS - NOTE
@@ -59,8 +61,9 @@
     for j in range(pairs.shape[2]):
         note = jnp.where(lane == j, jnp.where(j < kept[0, 0], pairs[0, 0, j], orb), note)
     full_ref[size + tiles * BS :] = note.astype(jnp.float32).astype(jnp.bfloat16)
-    copies[0].wait()
-    lay_blocks(raw[0, 0], full_ref)
+    for j in range(slots):
+        copies[2 + j].wait()
+        lay_blocks(raw[0, 0, j : j + 1], full_ref, j * size // slots)
 
 
 def tail_kernel(size, full_ref, out_ref):
@@ -183,7 +186,7 @@
             pltpu.SMEM(pairs.shape, jnp.int32),
             pltpu.VMEM(density.shape, jnp.bfloat16),
             pltpu.VMEM(tensor_blocks.shape, jnp.bfloat16),
-            pltpu.SemaphoreType.DMA((3,)),
+            pltpu.SemaphoreType.DMA((2 + slots,)),
         ],
         compiler_params=params,
         name="pack",

time: 24.7 us -> 24.9 us (level)
  no operation moved by 1% of the time
where the time goes in v30:
time: 24.9 us; the launch traced here: 24.8 us
  starting transfers between devices  12.3 us (49%)
  waiting for transfers between devices  8.62 us (35%)
  Pallas kernels  2.34 us (9%)
  other arithmetic  0.74 us (3%)
  between operations  0.71 us (3%)
    ppermute x4, waiting for transfers between devices, shards(): lax.ppermute(parts, 'aux', [(i, i ^ way * step) for i in range(aux)])  4.67 us
    ppermute x2, starting transfers between devices, shift(): return lax.ppermute(x, ('aux', 'orb'), perm)  4.18 us
    ppermute x1, starting transfers between devices, shards(): raw = lax.ppermute(tensor_blocks, 'orb', across)  4.04 us
    ppermute x4, starting transfers between devices, shards(): lax.ppermute(parts, 'aux', [(i, i ^ way * step) for i in range(aux)])  3.78 us
    ppermute x1, waiting for transfers between devices, shards(): tail_in = lax.ppermute(tail, 'orb', across)  2.32 us
    ppermute x2, waiting for transfers between devices, shift(): return lax.ppermute(x, ('aux', 'orb'), perm)  1.52 us
    pallas_call x1, Pallas kernels, shards(): pl.pallas_call(functools.partial(pack_kernel, orb), out_shape=array(size...  1.37 us
    pallas_call x1, Pallas kernels, shards(): pl.pallas_call(functools.partial(exchange_kernel, orb, slots, aux_width),...  0.73 us
  transfers between devices with their start and end apart: 9, of which 8 were waited for; matrix products, arithmetic and copies ran while one was open for 0% of the time, Pallas kernels for 6%

profile of v30, /device:TPU:0, one launch (start us, length us, event | category | flops | bytes accessed | tf_op | source)
XLA Modules:
  0.0 24.8 jit_solution(16642307668150970995)
XLA Ops:
  0.0 4.0 %collective-permute-start.1 = (bf16[1,1,3,4,4096]{4,3,2,1,0:T(4,128)(2,1)}, bf16[1,1,3,4,4096]{4,3,2,1,0:T(4,128)(2,1)S(1)}, u32[]{:S(2)}, u32[]{:S(2)}) collective-permute-start(bf16[1,1,3,4,4096]{4,3,2,1,0:T(4,128)(2,1)} %raw_hbm.1), channel_id=1, source_target_pairs={{0,2},{1,3},{2,0},{3,1},{4,6},{5,7},{6,4},{7,5},{8,10},{9,11},{10,... | collective-permute-start | bytes 294920 | tf_op jit(solution)/shard_map/ppermute | solution.py:214
  4.7 1.4 %pack.1.full_ref.refs_0_ = bf16[520,128]{1,0:T(8,128)(2,1)S(1)} custom-call(s32[1,1]{1,0:T(1,128)S(6)} %copy.5.kept, s32[1,1,3]{2,1,0:T(1,128)} %pairs_hbm.1, bf16[64,256]{1,0:T(8,128)(2,1)} %density_ref.1, bf16[1,1,3,4,4096]{4,3,2,1,0:T(4,128)(2,1)} %raw_hbm.1), custom_call_target="tpu_custom_call" | custom-call | tf_op jit(solution)/shard_map/pack/pallas_call | solution.py:180
  6.1 1.6 %collective-permute-start.2 = (bf16[520,128]{1,0:T(8,128)(2,1)S(1)}, bf16[520,128]{1,0:T(8,128)(2,1)S(1)}, u32[]{:S(2)}, u32[]{:S(2)}) collective-permute-start(bf16[520,128]{1,0:T(8,128)(2,1)S(1)} %pack.1.full_ref.refs_0_), channel_id=1, source_target_pairs={{0,1},{1,0},{2,3},{3,2},{4,7},{5,6},{6,5},{7,4},{8,9},{9,8},{10,11... | collective-permute-start | bytes 399368 | tf_op jit(solution)/shard_map/ppermute | solution.py:178
  7.7 0.3 %collective-permute-start = (bf16[72,128]{1,0:T(8,128)(2,1)S(1)}, bf16[72,128]{1,0:T(8,128)(2,1)S(1)}, u32[]{:S(2)}, u32[]{:S(2)}) collective-permute-start(bf16[72,128]{1,0:T(8,128)(2,1)S(1)} %tail.1.tail_ref), channel_id=1, source_target_pairs={{0,2},{1,3},{2,0},{3,1},{4,6},{5,7},{6,4},{7,5},{8,10},{9,11},{10,... | collective-permute-start | bytes 55304 | tf_op jit(solution)/shard_map/ppermute | solution.py:215
  8.1 2.5 %collective-permute-start.4 = (bf16[392,128]{1,0:T(8,128)(2,1)S(1)}, bf16[392,128]{1,0:T(8,128)(2,1)S(1)}, u32[]{:S(2)}, u32[]{:S(2)}) collective-permute-start(bf16[392,128]{1,0:T(8,128)(2,1)S(1)} %lean.1), channel_id=1, source_target_pairs={{0,3},{1,2},{2,1},{3,0},{4,5},{5,4},{6,7},{7,6},{8,11},{9,10},{10,... | collective-permute-start | bytes 301064 | tf_op jit(solution)/shard_map/ppermute | solution.py:178
  10.6 2.3 %collective-permute-done.refs_1_.tail = bf16[72,128]{1,0:T(8,128)(2,1)S(1)} collective-permute-done((bf16[72,128]{1,0:T(8,128)(2,1)S(1)}, bf16[72,128]{1,0:T(8,128)(2,1)S(1)}, u32[]{:S(2)}, u32[]{:S(2)}) %collective-permute-start) | collective-permute-done | bytes 18464 | tf_op jit(solution)/shard_map/ppermute | solution.py:215
  12.9 0.0 collective-permute-done.1.raw
  12.9 0.2 relay.1
  13.2 0.4 %collective-permute-done.2.refs_0_.refs_2_ = bf16[520,128]{1,0:T(8,128)(2,1)S(1)} collective-permute-done((bf16[520,128]{1,0:T(8,128)(2,1)S(1)}, bf16[520,128]{1,0:T(8,128)(2,1)S(1)}, u32[]{:S(2)}, u32[]{:S(2)}) %collective-permute-start.2) | collective-permute-done | bytes 133152 | tf_op jit(solution)/shard_map/ppermute | solution.py:178
  13.6 0.0 copy-start
  13.6 0.0 collective-permute-start.3
  13.6 1.1 %collective-permute-done.4.refs_3_ = bf16[392,128]{1,0:T(8,128)(2,1)S(1)} collective-permute-done((bf16[392,128]{1,0:T(8,128)(2,1)S(1)}, bf16[392,128]{1,0:T(8,128)(2,1)S(1)}, u32[]{:S(2)}, u32[]{:S(2)}) %collective-permute-start.4) | collective-permute-done | bytes 100384 | tf_op jit(solution)/shard_map/ppermute | solution.py:178
  14.7 0.1 collective-permute-done.3.swapped
  14.8 0.1 maximum_convert_fusion.meta_ref
  14.9 0.0 copy-done
  14.9 0.7 %exchange.1 = f32[64,256]{1,0:T(8,128)S(1)} custom-call(s32[12]{0:T(128)S(1)} %maximum_convert_fusion.meta_ref, bf16[64,256]{1,0:T(8,128)(2,1)S(1)} %copy-done, bf16[256,192]{1,0:T(8,128)(2,1)S(1)} %get-tuple-element.14.left_ref, bf16[72,128]{1,0:T(8,128)(2,1)S(1)} %collective-permute-done.refs_1_.tail, bf16[192,128]{1,0:T(8,128)(2,1)S(1)} %collective-permute-done.3.swapped, ...), custom_call_target="tpu_custom_call" | custom-call | tf_op jit(solution)/shard_map/exchange/pallas_call | solution.py:246
  15.6 0.2 collective-permute-start.5
  15.9 1.1 %collective-permute-done.5 = f32[64,256]{1,0:T(8,128)S(1)} collective-permute-done((f32[64,256]{1,0:T(8,128)S(1)}, f32[64,256]{1,0:T(8,128)S(1)}, u32[]{:S(2)}, u32[]{:S(2)}) %collective-permute-start.5) | collective-permute-done | bytes 65568 | tf_op jit(solution)/shard_map/ppermute | solution.py:267
  17.0 2.7 %collective-permute-start.8 = (bf16[64,256]{1,0:T(8,128)(2,1)S(1)}, bf16[64,256]{1,0:T(8,128)(2,1)S(1)}, u32[]{:S(2)}, u32[]{:S(2)}) collective-permute-start(bf16[64,256]{1,0:T(8,128)(2,1)S(1)} %add_convert_fusion), channel_id=1, source_target_pairs={{0,24},{4,28},{8,16},{12,20},{16,8},{20,12},{24,0},{28,4},{1,25},{... | collective-permute-start | bytes 98312 | tf_op jit(solution)/shard_map/ppermute | solution.py:267
  19.7 0.5 %collective-permute-start.7 = (bf16[64,256]{1,0:T(8,128)(2,1)S(1)}, bf16[64,256]{1,0:T(8,128)(2,1)S(1)}, u32[]{:S(2)}, u32[]{:S(2)}) collective-permute-start(bf16[64,256]{1,0:T(8,128)(2,1)S(1)} %add_convert_fusion), channel_id=1, source_target_pairs={{0,16},{4,20},{8,24},{12,28},{16,0},{20,4},{24,8},{28,12},{1,17},{... | collective-permute-start | bytes 98312 | tf_op jit(solution)/shard_map/ppermute | solution.py:267
  20.2 0.3 %collective-permute-start.6 = (bf16[64,256]{1,0:T(8,128)(2,1)S(1)}, bf16[64,256]{1,0:T(8,128)(2,1)S(1)}, u32[]{:S(2)}, u32[]{:S(2)}) collective-permute-start(bf16[64,256]{1,0:T(8,128)(2,1)S(1)} %add_convert_fusion), channel_id=1, source_target_pairs={{0,8},{4,12},{8,0},{12,4},{16,24},{20,28},{24,16},{28,20},{1,9},{5... | collective-permute-start | bytes 98312 | tf_op jit(solution)/shard_map/ppermute | solution.py:267
  20.5 1.3 %collective-permute-done.8 = bf16[64,256]{1,0:T(8,128)(2,1)S(1)} collective-permute-done((bf16[64,256]{1,0:T(8,128)(2,1)S(1)}, bf16[64,256]{1,0:T(8,128)(2,1)S(1)}, u32[]{:S(2)}, u32[]{:S(2)}) %collective-permute-start.8) | collective-permute-done | bytes 32800 | tf_op jit(solution)/shard_map/ppermute | solution.py:267
  21.9 1.8 %collective-permute-done.7 = bf16[64,256]{1,0:T(8,128)(2,1)S(1)} collective-permute-done((bf16[64,256]{1,0:T(8,128)(2,1)S(1)}, bf16[64,256]{1,0:T(8,128)(2,1)S(1)}, u32[]{:S(2)}, u32[]{:S(2)}) %collective-permute-start.7) | collective-permute-done | bytes 32800 | tf_op jit(solution)/shard_map/ppermute | solution.py:267
  23.6 0.5 %collective-permute-done.6 = bf16[64,256]{1,0:T(8,128)(2,1)S(1)} collective-permute-done((bf16[64,256]{1,0:T(8,128)(2,1)S(1)}, bf16[64,256]{1,0:T(8,128)(2,1)S(1)}, u32[]{:S(2)}, u32[]{:S(2)}) %collective-permute-start.6) | collective-permute-done | bytes 32800 | tf_op jit(solution)/shard_map/ppermute | solution.py:267
  24.1 0.6 %add_add_fusion = f32[64,256]{1,0:T(8,128)} fusion(bf16[64,256]{1,0:T(8,128)(2,1)S(1)} %collective-permute-done.8, bf16[64,256]{1,0:T(8,128)(2,1)S(1)} %collective-permute-done.7, bf16[64,256]{1,0:T(8,128)(2,1)S(1)} %collective-permute-done.6, bf16[64,256]{1,0:T(8,128)(2,1)S(1)} %add_convert_fusion), kind=kLoop, calls=%fused_computation | loop fusion | flops 114688 | bytes 196608 | tf_op jit(solution)/shard_map/add | solution.py:270
  (8 shorter events, 0.0 us)
Async XLA Ops:
  0.0 12.9 %collective-permute-start.1 = (bf16[1,1,3,4,4096]{4,3,2,1,0:T(4,128)(2,1)}, bf16[1,1,3,4,4096]{4,3,2,1,0:T(4,128)(2,1)S(1)}, u32[]{:S(2)}, u32[]{:S(2)}) collective-permute-start(bf16[1,1,3,4,4096]{4,3,2,1,0:T(4,128)(2,1)} %raw_hbm.1), channel_id=1, source_target_pairs={{0,2},{1,3},{2,0},{3,1},{4,6},{5,7},{6,4},{7,5},{8,10},{9,11},{10,... | collective-permute-start | bytes 294920 | tf_op jit(solution)/shard_map/ppermute | solution.py:214
  6.1 7.5 %collective-permute-start.2 = (bf16[520,128]{1,0:T(8,128)(2,1)S(1)}, bf16[520,128]{1,0:T(8,128)(2,1)S(1)}, u32[]{:S(2)}, u32[]{:S(2)}) collective-permute-start(bf16[520,128]{1,0:T(8,128)(2,1)S(1)} %pack.1.full_ref.refs_0_), channel_id=1, source_target_pairs={{0,1},{1,0},{2,3},{3,2},{4,7},{5,6},{6,5},{7,4},{8,9},{9,8},{10,11... | collective-permute-start | bytes 399368 | tf_op jit(solution)/shard_map/ppermute | solution.py:178
  7.7 5.2 %collective-permute-start = (bf16[72,128]{1,0:T(8,128)(2,1)S(1)}, bf16[72,128]{1,0:T(8,128)(2,1)S(1)}, u32[]{:S(2)}, u32[]{:S(2)}) collective-permute-start(bf16[72,128]{1,0:T(8,128)(2,1)S(1)} %tail.1.tail_ref), channel_id=1, source_target_pairs={{0,2},{1,3},{2,0},{3,1},{4,6},{5,7},{6,4},{7,5},{8,10},{9,11},{10,... | collective-permute-start | bytes 55304 | tf_op jit(solution)/shard_map/ppermute | solution.py:215
  8.1 6.7 %collective-permute-start.4 = (bf16[392,128]{1,0:T(8,128)(2,1)S(1)}, bf16[392,128]{1,0:T(8,128)(2,1)S(1)}, u32[]{:S(2)}, u32[]{:S(2)}) collective-permute-start(bf16[392,128]{1,0:T(8,128)(2,1)S(1)} %lean.1), channel_id=1, source_target_pairs={{0,3},{1,2},{2,1},{3,0},{4,5},{5,4},{6,7},{7,6},{8,11},{9,10},{10,... | collective-permute-start | bytes 301064 | tf_op jit(solution)/shard_map/ppermute | solution.py:178
  13.6 1.3 %copy-start = (bf16[64,256]{1,0:T(8,128)(2,1)S(1)}, bf16[64,256]{1,0:T(8,128)(2,1)}, u32[]{:S(2)}) copy-start(bf16[64,256]{1,0:T(8,128)(2,1)} %density_ref.1) | copy-start | bytes 98308
  13.6 1.2 %collective-permute-start.3 = (bf16[192,128]{1,0:T(8,128)(2,1)S(1)}, bf16[192,128]{1,0:T(8,128)(2,1)S(1)}, u32[]{:S(2)}, u32[]{:S(2)}) collective-permute-start(bf16[192,128]{1,0:T(8,128)(2,1)S(1)} %merge.1), channel_id=1, source_target_pairs={{0,4},{4,0},{8,12},{12,8},{16,20},{20,16},{24,28},{28,24},{1,5},{5... | collective-permute-start | bytes 147464 | tf_op jit(solution)/shard_map/ppermute | solution.py:228
  15.6 1.3 %collective-permute-start.5 = (f32[64,256]{1,0:T(8,128)S(1)}, f32[64,256]{1,0:T(8,128)S(1)}, u32[]{:S(2)}, u32[]{:S(2)}) collective-permute-start(f32[64,256]{1,0:T(8,128)S(1)} %exchange.1), channel_id=1, source_target_pairs={{0,4},{4,0},{8,12},{12,8},{16,20},{20,16},{24,28},{28,24},{1,5},{5... | collective-permute-start | bytes 196616 | tf_op jit(solution)/shard_map/ppermute | solution.py:267
  17.0 4.9 %collective-permute-start.8 = (bf16[64,256]{1,0:T(8,128)(2,1)S(1)}, bf16[64,256]{1,0:T(8,128)(2,1)S(1)}, u32[]{:S(2)}, u32[]{:S(2)}) collective-permute-start(bf16[64,256]{1,0:T(8,128)(2,1)S(1)} %add_convert_fusion), channel_id=1, source_target_pairs={{0,24},{4,28},{8,16},{12,20},{16,8},{20,12},{24,0},{28,4},{1,25},{... | collective-permute-start | bytes 98312 | tf_op jit(solution)/shard_map/ppermute | solution.py:267
  19.7 3.9 %collective-permute-start.7 = (bf16[64,256]{1,0:T(8,128)(2,1)S(1)}, bf16[64,256]{1,0:T(8,128)(2,1)S(1)}, u32[]{:S(2)}, u32[]{:S(2)}) collective-permute-start(bf16[64,256]{1,0:T(8,128)(2,1)S(1)} %add_convert_fusion), channel_id=1, source_target_pairs={{0,16},{4,20},{8,24},{12,28},{16,0},{20,4},{24,8},{28,12},{1,17},{... | collective-permute-start | bytes 98312 | tf_op jit(solution)/shard_map/ppermute | solution.py:267
  20.2 3.9 %collective-permute-start.6 = (bf16[64,256]{1,0:T(8,128)(2,1)S(1)}, bf16[64,256]{1,0:T(8,128)(2,1)S(1)}, u32[]{:S(2)}, u32[]{:S(2)}) collective-permute-start(bf16[64,256]{1,0:T(8,128)(2,1)S(1)} %add_convert_fusion), channel_id=1, source_target_pairs={{0,8},{4,12},{8,0},{12,4},{16,24},{20,28},{24,16},{28,20},{1,9},{5... | collective-permute-start | bytes 98312 | tf_op jit(solution)/shard_map/ppermute | solution.py:267

commit v31 on v27

--- a/solution.py
+++ b/solution.py
@@ -262,7 +262,7 @@
         terms = [parts]
         for way in range(1, ways):
             terms.append(lax.ppermute(parts, "aux", [(i, i ^ (way * step)) for i in range(aux)]))
-        terms = [term.astype(jnp.float32) for term in terms]
+        terms = [term.astype(jnp.float32) for term in terms[::-1]]
         while len(terms) > 1:
             terms = [terms[i] + terms[i + 1] for i in range(0, len(terms), 2)]
         parts = terms[0]

time: 24.7 us -> 25.6 us (1.036)
  waiting for transfers between devices: 8.62 us -> 9.58 us
    ppermute x4, waiting for transfers between devices: 4.67 us -> 5.63 us  [shards(): lax.ppermute(parts, 'aux', [(i, i ^ way * step) for i in range(aux)])]
  transfers between devices with their start and end apart: 9 -> 9, of which waited for: 8 -> 8; matrix products, arithmetic and copies ran while one was open for 0% -> 0% of each run, Pallas kernels for 6% -> 5%
where the time goes in v31:
time: 25.6 us; the launch traced here: 25.5 us
  starting transfers between devices  12.3 us (48%)
  waiting for transfers between devices  9.58 us (37%)
  Pallas kernels  2.11 us (8%)
  other arithmetic  0.74 us (3%)
  between operations  0.71 us (3%)
    ppermute x4, waiting for transfers between devices, shards(): lax.ppermute(parts, 'aux', [(i, i ^ way * step) for i in range(aux)])  5.63 us
    ppermute x2, starting transfers between devices, shift(): return lax.ppermute(x, ('aux', 'orb'), perm)  4.18 us
    ppermute x1, starting transfers between devices, shards(): raw = lax.ppermute(tensor_blocks, 'orb', across)  4.04 us
    ppermute x4, starting transfers between devices, shards(): lax.ppermute(parts, 'aux', [(i, i ^ way * step) for i in range(aux)])  3.78 us
    ppermute x1, waiting for transfers between devices, shards(): tail_in = lax.ppermute(tail, 'orb', across)  2.3 us
    ppermute x2, waiting for transfers between devices, shift(): return lax.ppermute(x, ('aux', 'orb'), perm)  1.55 us
    pallas_call x1, Pallas kernels, shards(): pl.pallas_call(functools.partial(pack_kernel, orb), out_shape=array(size...  1.14 us
    pallas_call x1, Pallas kernels, shards(): pl.pallas_call(functools.partial(exchange_kernel, orb, slots, aux_width),...  0.73 us
  transfers between devices with their start and end apart: 9, of which 8 were waited for; matrix products, arithmetic and copies ran while one was open for 0% of the time, Pallas kernels for 5%

profile of v31, /device:TPU:0, one launch (start us, length us, event | category | flops | bytes accessed | tf_op | source)
XLA Modules:
  0.0 25.5 jit_solution(16707049960214429216)
XLA Ops:
  0.0 4.0 %collective-permute-start.1 = (bf16[1,1,3,4,4096]{4,3,2,1,0:T(4,128)(2,1)}, bf16[1,1,3,4,4096]{4,3,2,1,0:T(4,128)(2,1)S(1)}, u32[]{:S(2)}, u32[]{:S(2)}) collective-permute-start(bf16[1,1,3,4,4096]{4,3,2,1,0:T(4,128)(2,1)} %raw_hbm.1), channel_id=1, source_target_pairs={{0,2},{1,3},{2,0},{3,1},{4,6},{5,7},{6,4},{7,5},{8,10},{9,11},{10,... | collective-permute-start | bytes 294920 | tf_op jit(solution)/shard_map/ppermute | solution.py:211
  4.7 1.1 %pack.1.full_ref.refs_0_ = bf16[520,128]{1,0:T(8,128)(2,1)S(1)} custom-call(s32[1,1]{1,0:T(1,128)S(6)} %copy.5.kept, s32[1,1,3]{2,1,0:T(1,128)} %pairs_hbm.1, bf16[64,256]{1,0:T(8,128)(2,1)} %density_ref.1, bf16[1,1,3,4,4096]{4,3,2,1,0:T(4,128)(2,1)} %raw_hbm.1), custom_call_target="tpu_custom_call" | custom-call | tf_op jit(solution)/shard_map/pack/pallas_call | solution.py:177
  5.8 1.6 %collective-permute-start.2 = (bf16[520,128]{1,0:T(8,128)(2,1)S(1)}, bf16[520,128]{1,0:T(8,128)(2,1)S(1)}, u32[]{:S(2)}, u32[]{:S(2)}) collective-permute-start(bf16[520,128]{1,0:T(8,128)(2,1)S(1)} %pack.1.full_ref.refs_0_), channel_id=1, source_target_pairs={{0,1},{1,0},{2,3},{3,2},{4,7},{5,6},{6,5},{7,4},{8,9},{9,8},{10,11... | collective-permute-start | bytes 399368 | tf_op jit(solution)/shard_map/ppermute | solution.py:175
  7.5 0.3 %collective-permute-start = (bf16[72,128]{1,0:T(8,128)(2,1)S(1)}, bf16[72,128]{1,0:T(8,128)(2,1)S(1)}, u32[]{:S(2)}, u32[]{:S(2)}) collective-permute-start(bf16[72,128]{1,0:T(8,128)(2,1)S(1)} %tail.1.tail_ref), channel_id=1, source_target_pairs={{0,2},{1,3},{2,0},{3,1},{4,6},{5,7},{6,4},{7,5},{8,10},{9,11},{10,... | collective-permute-start | bytes 55304 | tf_op jit(solution)/shard_map/ppermute | solution.py:212
  7.8 2.5 %collective-permute-start.4 = (bf16[392,128]{1,0:T(8,128)(2,1)S(1)}, bf16[392,128]{1,0:T(8,128)(2,1)S(1)}, u32[]{:S(2)}, u32[]{:S(2)}) collective-permute-start(bf16[392,128]{1,0:T(8,128)(2,1)S(1)} %lean.1), channel_id=1, source_target_pairs={{0,3},{1,2},{2,1},{3,0},{4,5},{5,4},{6,7},{7,6},{8,11},{9,10},{10,... | collective-permute-start | bytes 301064 | tf_op jit(solution)/shard_map/ppermute | solution.py:175
  10.4 2.3 %collective-permute-done.refs_1_.tail = bf16[72,128]{1,0:T(8,128)(2,1)S(1)} collective-permute-done((bf16[72,128]{1,0:T(8,128)(2,1)S(1)}, bf16[72,128]{1,0:T(8,128)(2,1)S(1)}, u32[]{:S(2)}, u32[]{:S(2)}) %collective-permute-start) | collective-permute-done | bytes 18464 | tf_op jit(solution)/shard_map/ppermute | solution.py:212
  12.7 0.0 collective-permute-done.1.raw
  12.7 0.2 relay.1
  12.9 0.4 %collective-permute-done.2.refs_0_.refs_2_ = bf16[520,128]{1,0:T(8,128)(2,1)S(1)} collective-permute-done((bf16[520,128]{1,0:T(8,128)(2,1)S(1)}, bf16[520,128]{1,0:T(8,128)(2,1)S(1)}, u32[]{:S(2)}, u32[]{:S(2)}) %collective-permute-start.2) | collective-permute-done | bytes 133152 | tf_op jit(solution)/shard_map/ppermute | solution.py:175
  13.4 0.0 copy-start
  13.4 0.0 collective-permute-start.3
  13.4 1.1 %collective-permute-done.4.refs_3_ = bf16[392,128]{1,0:T(8,128)(2,1)S(1)} collective-permute-done((bf16[392,128]{1,0:T(8,128)(2,1)S(1)}, bf16[392,128]{1,0:T(8,128)(2,1)S(1)}, u32[]{:S(2)}, u32[]{:S(2)}) %collective-permute-start.4) | collective-permute-done | bytes 100384 | tf_op jit(solution)/shard_map/ppermute | solution.py:175
  14.5 0.1 collective-permute-done.3.swapped
  14.6 0.1 maximum_convert_fusion.meta_ref
  14.7 0.0 copy-done
  14.7 0.7 %exchange.1 = f32[64,256]{1,0:T(8,128)S(1)} custom-call(s32[12]{0:T(128)S(1)} %maximum_convert_fusion.meta_ref, bf16[64,256]{1,0:T(8,128)(2,1)S(1)} %copy-done, bf16[256,192]{1,0:T(8,128)(2,1)S(1)} %get-tuple-element.14.left_ref, bf16[72,128]{1,0:T(8,128)(2,1)S(1)} %collective-permute-done.refs_1_.tail, bf16[192,128]{1,0:T(8,128)(2,1)S(1)} %collective-permute-done.3.swapped, ...), custom_call_target="tpu_custom_call" | custom-call | tf_op jit(solution)/shard_map/exchange/pallas_call | solution.py:243
  15.4 0.2 collective-permute-start.5
  15.6 1.1 %collective-permute-done.5 = f32[64,256]{1,0:T(8,128)S(1)} collective-permute-done((f32[64,256]{1,0:T(8,128)S(1)}, f32[64,256]{1,0:T(8,128)S(1)}, u32[]{:S(2)}, u32[]{:S(2)}) %collective-permute-start.5) | collective-permute-done | bytes 65568 | tf_op jit(solution)/shard_map/ppermute | solution.py:264
  16.8 1.8 %collective-permute-start.8 = (bf16[64,256]{1,0:T(8,128)(2,1)S(1)}, bf16[64,256]{1,0:T(8,128)(2,1)S(1)}, u32[]{:S(2)}, u32[]{:S(2)}) collective-permute-start(bf16[64,256]{1,0:T(8,128)(2,1)S(1)} %add_convert_fusion), channel_id=1, source_target_pairs={{0,8},{4,12},{8,0},{12,4},{16,24},{20,28},{24,16},{28,20},{1,9},{5... | collective-permute-start | bytes 98312 | tf_op jit(solution)/shard_map/ppermute | solution.py:264
  18.5 1.5 %collective-permute-start.7 = (bf16[64,256]{1,0:T(8,128)(2,1)S(1)}, bf16[64,256]{1,0:T(8,128)(2,1)S(1)}, u32[]{:S(2)}, u32[]{:S(2)}) collective-permute-start(bf16[64,256]{1,0:T(8,128)(2,1)S(1)} %add_convert_fusion), channel_id=1, source_target_pairs={{0,16},{4,20},{8,24},{12,28},{16,0},{20,4},{24,8},{28,12},{1,17},{... | collective-permute-start | bytes 98312 | tf_op jit(solution)/shard_map/ppermute | solution.py:264
  20.0 0.3 %collective-permute-start.6 = (bf16[64,256]{1,0:T(8,128)(2,1)S(1)}, bf16[64,256]{1,0:T(8,128)(2,1)S(1)}, u32[]{:S(2)}, u32[]{:S(2)}) collective-permute-start(bf16[64,256]{1,0:T(8,128)(2,1)S(1)} %add_convert_fusion), channel_id=1, source_target_pairs={{0,24},{4,28},{8,16},{12,20},{16,8},{20,12},{24,0},{28,4},{1,25},{... | collective-permute-start | bytes 98312 | tf_op jit(solution)/shard_map/ppermute | solution.py:264
  20.3 0.4 %collective-permute-done.8 = bf16[64,256]{1,0:T(8,128)(2,1)S(1)} collective-permute-done((bf16[64,256]{1,0:T(8,128)(2,1)S(1)}, bf16[64,256]{1,0:T(8,128)(2,1)S(1)}, u32[]{:S(2)}, u32[]{:S(2)}) %collective-permute-start.8) | collective-permute-done | bytes 32800 | tf_op jit(solution)/shard_map/ppermute | solution.py:264
  20.7 1.7 %collective-permute-done.7 = bf16[64,256]{1,0:T(8,128)(2,1)S(1)} collective-permute-done((bf16[64,256]{1,0:T(8,128)(2,1)S(1)}, bf16[64,256]{1,0:T(8,128)(2,1)S(1)}, u32[]{:S(2)}, u32[]{:S(2)}) %collective-permute-start.7) | collective-permute-done | bytes 32800 | tf_op jit(solution)/shard_map/ppermute | solution.py:264
  22.4 2.4 %collective-permute-done.6 = bf16[64,256]{1,0:T(8,128)(2,1)S(1)} collective-permute-done((bf16[64,256]{1,0:T(8,128)(2,1)S(1)}, bf16[64,256]{1,0:T(8,128)(2,1)S(1)}, u32[]{:S(2)}, u32[]{:S(2)}) %collective-permute-start.6) | collective-permute-done | bytes 32800 | tf_op jit(solution)/shard_map/ppermute | solution.py:264
  24.8 0.6 %add_add_fusion = f32[64,256]{1,0:T(8,128)} fusion(bf16[64,256]{1,0:T(8,128)(2,1)S(1)} %add_convert_fusion, bf16[64,256]{1,0:T(8,128)(2,1)S(1)} %collective-permute-done.8, bf16[64,256]{1,0:T(8,128)(2,1)S(1)} %collective-permute-done.7, bf16[64,256]{1,0:T(8,128)(2,1)S(1)} %collective-permute-done.6), kind=kLoop, calls=%fused_computation | loop fusion | flops 114688 | bytes 196608 | tf_op jit(solution)/shard_map/add | solution.py:267
  (8 shorter events, 0.0 us)
Async XLA Ops:
  0.0 12.7 %collective-permute-start.1 = (bf16[1,1,3,4,4096]{4,3,2,1,0:T(4,128)(2,1)}, bf16[1,1,3,4,4096]{4,3,2,1,0:T(4,128)(2,1)S(1)}, u32[]{:S(2)}, u32[]{:S(2)}) collective-permute-start(bf16[1,1,3,4,4096]{4,3,2,1,0:T(4,128)(2,1)} %raw_hbm.1), channel_id=1, source_target_pairs={{0,2},{1,3},{2,0},{3,1},{4,6},{5,7},{6,4},{7,5},{8,10},{9,11},{10,... | collective-permute-start | bytes 294920 | tf_op jit(solution)/shard_map/ppermute | solution.py:211
  5.8 7.5 %collective-permute-start.2 = (bf16[520,128]{1,0:T(8,128)(2,1)S(1)}, bf16[520,128]{1,0:T(8,128)(2,1)S(1)}, u32[]{:S(2)}, u32[]{:S(2)}) collective-permute-start(bf16[520,128]{1,0:T(8,128)(2,1)S(1)} %pack.1.full_ref.refs_0_), channel_id=1, source_target_pairs={{0,1},{1,0},{2,3},{3,2},{4,7},{5,6},{6,5},{7,4},{8,9},{9,8},{10,11... | collective-permute-start | bytes 399368 | tf_op jit(solution)/shard_map/ppermute | solution.py:175
  7.5 5.2 %collective-permute-start = (bf16[72,128]{1,0:T(8,128)(2,1)S(1)}, bf16[72,128]{1,0:T(8,128)(2,1)S(1)}, u32[]{:S(2)}, u32[]{:S(2)}) collective-permute-start(bf16[72,128]{1,0:T(8,128)(2,1)S(1)} %tail.1.tail_ref), channel_id=1, source_target_pairs={{0,2},{1,3},{2,0},{3,1},{4,6},{5,7},{6,4},{7,5},{8,10},{9,11},{10,... | collective-permute-start | bytes 55304 | tf_op jit(solution)/shard_map/ppermute | solution.py:212
  7.8 6.7 %collective-permute-start.4 = (bf16[392,128]{1,0:T(8,128)(2,1)S(1)}, bf16[392,128]{1,0:T(8,128)(2,1)S(1)}, u32[]{:S(2)}, u32[]{:S(2)}) collective-permute-start(bf16[392,128]{1,0:T(8,128)(2,1)S(1)} %lean.1), channel_id=1, source_target_pairs={{0,3},{1,2},{2,1},{3,0},{4,5},{5,4},{6,7},{7,6},{8,11},{9,10},{10,... | collective-permute-start | bytes 301064 | tf_op jit(solution)/shard_map/ppermute | solution.py:175
  13.4 1.3 %copy-start = (bf16[64,256]{1,0:T(8,128)(2,1)S(1)}, bf16[64,256]{1,0:T(8,128)(2,1)}, u32[]{:S(2)}) copy-start(bf16[64,256]{1,0:T(8,128)(2,1)} %density_ref.1) | copy-start | bytes 98308
  13.4 1.2 %collective-permute-start.3 = (bf16[192,128]{1,0:T(8,128)(2,1)S(1)}, bf16[192,128]{1,0:T(8,128)(2,1)S(1)}, u32[]{:S(2)}, u32[]{:S(2)}) collective-permute-start(bf16[192,128]{1,0:T(8,128)(2,1)S(1)} %merge.1), channel_id=1, source_target_pairs={{0,4},{4,0},{8,12},{12,8},{16,20},{20,16},{24,28},{28,24},{1,5},{5... | collective-permute-start | bytes 147464 | tf_op jit(solution)/shard_map/ppermute | solution.py:225
  15.4 1.3 %collective-permute-start.5 = (f32[64,256]{1,0:T(8,128)S(1)}, f32[64,256]{1,0:T(8,128)S(1)}, u32[]{:S(2)}, u32[]{:S(2)}) collective-permute-start(f32[64,256]{1,0:T(8,128)S(1)} %exchange.1), channel_id=1, source_target_pairs={{0,4},{4,0},{8,12},{12,8},{16,20},{20,16},{24,28},{28,24},{1,5},{5... | collective-permute-start | bytes 196616 | tf_op jit(solution)/shard_map/ppermute | solution.py:264
  16.8 4.0 %collective-permute-start.8 = (bf16[64,256]{1,0:T(8,128)(2,1)S(1)}, bf16[64,256]{1,0:T(8,128)(2,1)S(1)}, u32[]{:S(2)}, u32[]{:S(2)}) collective-permute-start(bf16[64,256]{1,0:T(8,128)(2,1)S(1)} %add_convert_fusion), channel_id=1, source_target_pairs={{0,8},{4,12},{8,0},{12,4},{16,24},{20,28},{24,16},{28,20},{1,9},{5... | collective-permute-start | bytes 98312 | tf_op jit(solution)/shard_map/ppermute | solution.py:264
  18.5 3.9 %collective-permute-start.7 = (bf16[64,256]{1,0:T(8,128)(2,1)S(1)}, bf16[64,256]{1,0:T(8,128)(2,1)S(1)}, u32[]{:S(2)}, u32[]{:S(2)}) collective-permute-start(bf16[64,256]{1,0:T(8,128)(2,1)S(1)} %add_convert_fusion), channel_id=1, source_target_pairs={{0,16},{4,20},{8,24},{12,28},{16,0},{20,4},{24,8},{28,12},{1,17},{... | collective-permute-start | bytes 98312 | tf_op jit(solution)/shard_map/ppermute | solution.py:264
  20.0 4.8 %collective-permute-start.6 = (bf16[64,256]{1,0:T(8,128)(2,1)S(1)}, bf16[64,256]{1,0:T(8,128)(2,1)S(1)}, u32[]{:S(2)}, u32[]{:S(2)}) collective-permute-start(bf16[64,256]{1,0:T(8,128)(2,1)S(1)} %add_convert_fusion), channel_id=1, source_target_pairs={{0,24},{4,28},{8,16},{12,20},{16,8},{20,12},{24,0},{28,4},{1,25},{... | collective-permute-start | bytes 98312 | tf_op jit(solution)/shard_map/ppermute | solution.py:264

commit v32 on v25

--- a/solution.py
+++ b/solution.py
@@ -9,7 +9,7 @@
 
 BS = 64
 LANES = 128
-NOTE = 8
+NOTE = 16
 
 
 def lay_blocks(raw, out_ref):

time: 25 us -> 25.2 us (level)
  no operation moved by 1% of the time
where the time goes in v32:
time: 25.2 us; the launch traced here: 25 us
  starting transfers between devices  12.3 us (49%)
  waiting for transfers between devices  9.11 us (36%)
  Pallas kernels  2.12 us (8%)
  other arithmetic  0.74 us (3%)
  between operations  0.71 us (3%)
    ppermute x4, waiting for transfers between devices, shards(): lax.ppermute(parts, 'aux', [(i, i ^ way * step) for i in range(aux)])  4.94 us
    ppermute x2, starting transfers between devices, shift(): return lax.ppermute(x, ('aux', 'orb'), perm)  4.18 us
    ppermute x1, starting transfers between devices, shards(): raw = lax.ppermute(tensor_blocks, 'orb', across)  4.04 us
    ppermute x4, starting transfers between devices, shards(): lax.ppermute(parts, 'aux', [(i, i ^ way * step) for i in range(aux)])  3.77 us
    ppermute x1, waiting for transfers between devices, shards(): tail_in = lax.ppermute(tail, 'orb', across)  2.52 us
    ppermute x2, waiting for transfers between devices, shift(): return lax.ppermute(x, ('aux', 'orb'), perm)  1.43 us
    pallas_call x1, Pallas kernels, shards(): pl.pallas_call(functools.partial(pack_kernel, orb), out_shape=array(size...  1.14 us
    pallas_call x1, Pallas kernels, shards(): pl.pallas_call(functools.partial(exchange_kernel, orb, slots, aux_width),...  0.73 us
  transfers between devices with their start and end apart: 9, of which 8 were waited for; matrix products, arithmetic and copies ran while one was open for 0% of the time, Pallas kernels for 6%

profile of v32, /device:TPU:0, one launch (start us, length us, event | category | flops | bytes accessed | tf_op | source)
XLA Modules:
  0.0 25.0 jit_solution(12635707695743062513)
XLA Ops:
  0.0 4.0 %collective-permute-start.1 = (bf16[1,1,3,4,4096]{4,3,2,1,0:T(4,128)(2,1)}, bf16[1,1,3,4,4096]{4,3,2,1,0:T(4,128)(2,1)S(1)}, u32[]{:S(2)}, u32[]{:S(2)}) collective-permute-start(bf16[1,1,3,4,4096]{4,3,2,1,0:T(4,128)(2,1)} %raw_hbm.1), channel_id=1, source_target_pairs={{0,2},{1,3},{2,0},{3,1},{4,6},{5,7},{6,4},{7,5},{8,10},{9,11},{10,... | collective-permute-start | bytes 294920 | tf_op jit(solution)/shard_map/ppermute | solution.py:211
  4.7 1.1 %pack.1.full_ref.refs_0_ = bf16[528,128]{1,0:T(8,128)(2,1)S(1)} custom-call(s32[1,1]{1,0:T(1,128)S(6)} %copy.5.kept, s32[1,1,3]{2,1,0:T(1,128)} %pairs_hbm.1, bf16[64,256]{1,0:T(8,128)(2,1)} %density_ref.1, bf16[1,1,3,4,4096]{4,3,2,1,0:T(4,128)(2,1)} %raw_hbm.1), custom_call_target="tpu_custom_call" | custom-call | tf_op jit(solution)/shard_map/pack/pallas_call | solution.py:177
  5.8 1.6 %collective-permute-start.2 = (bf16[528,128]{1,0:T(8,128)(2,1)S(1)}, bf16[528,128]{1,0:T(8,128)(2,1)S(1)}, u32[]{:S(2)}, u32[]{:S(2)}) collective-permute-start(bf16[528,128]{1,0:T(8,128)(2,1)S(1)} %pack.1.full_ref.refs_0_), channel_id=1, source_target_pairs={{0,1},{1,0},{2,3},{3,2},{4,7},{5,6},{6,5},{7,4},{8,9},{9,8},{10,11... | collective-permute-start | bytes 405512 | tf_op jit(solution)/shard_map/ppermute | solution.py:175
  7.5 0.3 %collective-permute-start = (bf16[80,128]{1,0:T(8,128)(2,1)S(1)}, bf16[80,128]{1,0:T(8,128)(2,1)S(1)}, u32[]{:S(2)}, u32[]{:S(2)}) collective-permute-start(bf16[80,128]{1,0:T(8,128)(2,1)S(1)} %tail.1.tail_ref), channel_id=1, source_target_pairs={{0,2},{1,3},{2,0},{3,1},{4,6},{5,7},{6,4},{7,5},{8,10},{9,11},{10,... | collective-permute-start | bytes 61448 | tf_op jit(solution)/shard_map/ppermute | solution.py:212
  7.8 2.5 %collective-permute-start.4 = (bf16[400,128]{1,0:T(8,128)(2,1)S(1)}, bf16[400,128]{1,0:T(8,128)(2,1)S(1)}, u32[]{:S(2)}, u32[]{:S(2)}) collective-permute-start(bf16[400,128]{1,0:T(8,128)(2,1)S(1)} %lean.1), channel_id=1, source_target_pairs={{0,3},{1,2},{2,1},{3,0},{4,5},{5,4},{6,7},{7,6},{8,11},{9,10},{10,... | collective-permute-start | bytes 307208 | tf_op jit(solution)/shard_map/ppermute | solution.py:175
  10.4 2.5 %collective-permute-done.refs_1_.tail = bf16[80,128]{1,0:T(8,128)(2,1)S(1)} collective-permute-done((bf16[80,128]{1,0:T(8,128)(2,1)S(1)}, bf16[80,128]{1,0:T(8,128)(2,1)S(1)}, u32[]{:S(2)}, u32[]{:S(2)}) %collective-permute-start) | collective-permute-done | bytes 20512 | tf_op jit(solution)/shard_map/ppermute | solution.py:212
  12.9 0.0 collective-permute-done.1.raw
  12.9 0.2 relay.1
  13.1 0.4 %collective-permute-done.2.refs_0_.refs_2_ = bf16[528,128]{1,0:T(8,128)(2,1)S(1)} collective-permute-done((bf16[528,128]{1,0:T(8,128)(2,1)S(1)}, bf16[528,128]{1,0:T(8,128)(2,1)S(1)}, u32[]{:S(2)}, u32[]{:S(2)}) %collective-permute-start.2) | collective-permute-done | bytes 135200 | tf_op jit(solution)/shard_map/ppermute | solution.py:175
  13.6 0.0 copy-start
  13.6 0.0 collective-permute-start.3
  13.6 1.0 %collective-permute-done.4.refs_3_ = bf16[400,128]{1,0:T(8,128)(2,1)S(1)} collective-permute-done((bf16[400,128]{1,0:T(8,128)(2,1)S(1)}, bf16[400,128]{1,0:T(8,128)(2,1)S(1)}, u32[]{:S(2)}, u32[]{:S(2)}) %collective-permute-start.4) | collective-permute-done | bytes 102432 | tf_op jit(solution)/shard_map/ppermute | solution.py:175
  14.6 0.2 collective-permute-done.3.swapped
  14.8 0.1 maximum_convert_fusion.meta_ref
  14.9 0.0 copy-done
  14.9 0.7 %exchange.1 = f32[64,256]{1,0:T(8,128)S(1)} custom-call(s32[12]{0:T(128)S(1)} %maximum_convert_fusion.meta_ref, bf16[64,256]{1,0:T(8,128)(2,1)S(1)} %copy-done, bf16[256,192]{1,0:T(8,128)(2,1)S(1)} %get-tuple-element.14.left_ref, bf16[80,128]{1,0:T(8,128)(2,1)S(1)} %collective-permute-done.refs_1_.tail, bf16[192,128]{1,0:T(8,128)(2,1)S(1)} %collective-permute-done.3.swapped, ...), custom_call_target="tpu_custom_call" | custom-call | tf_op jit(solution)/shard_map/exchange/pallas_call | solution.py:243
  15.6 0.2 collective-permute-start.5
  15.9 1.1 %collective-permute-done.5 = f32[64,256]{1,0:T(8,128)S(1)} collective-permute-done((f32[64,256]{1,0:T(8,128)S(1)}, f32[64,256]{1,0:T(8,128)S(1)}, u32[]{:S(2)}, u32[]{:S(2)}) %collective-permute-start.5) | collective-permute-done | bytes 65568 | tf_op jit(solution)/shard_map/ppermute | solution.py:262
  17.0 2.6 %collective-permute-start.8 = (f32[64,256]{1,0:T(8,128)S(1)}, f32[64,256]{1,0:T(8,128)S(1)}, u32[]{:S(2)}, u32[]{:S(2)}) collective-permute-start(f32[64,256]{1,0:T(8,128)S(1)} %add.12), channel_id=1, source_target_pairs={{0,24},{4,28},{8,16},{12,20},{16,8},{20,12},{24,0},{28,4},{1,25},{... | collective-permute-start | bytes 196616 | tf_op jit(solution)/shard_map/ppermute | solution.py:262
  19.6 0.5 %collective-permute-start.7 = (f32[64,256]{1,0:T(8,128)S(1)}, f32[64,256]{1,0:T(8,128)S(1)}, u32[]{:S(2)}, u32[]{:S(2)}) collective-permute-start(f32[64,256]{1,0:T(8,128)S(1)} %add.12), channel_id=1, source_target_pairs={{0,16},{4,20},{8,24},{12,28},{16,0},{20,4},{24,8},{28,12},{1,17},{... | collective-permute-start | bytes 196616 | tf_op jit(solution)/shard_map/ppermute | solution.py:262
  20.1 0.4 %collective-permute-start.6 = (f32[64,256]{1,0:T(8,128)S(1)}, f32[64,256]{1,0:T(8,128)S(1)}, u32[]{:S(2)}, u32[]{:S(2)}) collective-permute-start(f32[64,256]{1,0:T(8,128)S(1)} %add.12), channel_id=1, source_target_pairs={{0,8},{4,12},{8,0},{12,4},{16,24},{20,28},{24,16},{28,20},{1,9},{5... | collective-permute-start | bytes 196616 | tf_op jit(solution)/shard_map/ppermute | solution.py:262
  20.5 1.7 %collective-permute-done.8 = f32[64,256]{1,0:T(8,128)S(1)} collective-permute-done((f32[64,256]{1,0:T(8,128)S(1)}, f32[64,256]{1,0:T(8,128)S(1)}, u32[]{:S(2)}, u32[]{:S(2)}) %collective-permute-start.8) | collective-permute-done | bytes 65568 | tf_op jit(solution)/shard_map/ppermute | solution.py:262
  22.2 1.7 %collective-permute-done.7 = f32[64,256]{1,0:T(8,128)S(1)} collective-permute-done((f32[64,256]{1,0:T(8,128)S(1)}, f32[64,256]{1,0:T(8,128)S(1)}, u32[]{:S(2)}, u32[]{:S(2)}) %collective-permute-start.7) | collective-permute-done | bytes 65568 | tf_op jit(solution)/shard_map/ppermute | solution.py:262
  23.9 0.5 %collective-permute-done.6 = f32[64,256]{1,0:T(8,128)S(1)} collective-permute-done((f32[64,256]{1,0:T(8,128)S(1)}, f32[64,256]{1,0:T(8,128)S(1)}, u32[]{:S(2)}, u32[]{:S(2)}) %collective-permute-start.6) | collective-permute-done | bytes 65568 | tf_op jit(solution)/shard_map/ppermute | solution.py:262
  24.4 0.6 %add_add_fusion = f32[64,256]{1,0:T(8,128)} fusion(f32[64,256]{1,0:T(8,128)S(1)} %collective-permute-done.7, f32[64,256]{1,0:T(8,128)S(1)} %collective-permute-done.8, f32[64,256]{1,0:T(8,128)S(1)} %add.12, f32[64,256]{1,0:T(8,128)S(1)} %collective-permute-done.6), kind=kLoop, calls=%fused_computation | loop fusion | flops 49152 | bytes 327680 | tf_op jit(solution)/shard_map/add | solution.py:264
  (8 shorter events, 0.0 us)
Async XLA Ops:
  0.0 12.9 %collective-permute-start.1 = (bf16[1,1,3,4,4096]{4,3,2,1,0:T(4,128)(2,1)}, bf16[1,1,3,4,4096]{4,3,2,1,0:T(4,128)(2,1)S(1)}, u32[]{:S(2)}, u32[]{:S(2)}) collective-permute-start(bf16[1,1,3,4,4096]{4,3,2,1,0:T(4,128)(2,1)} %raw_hbm.1), channel_id=1, source_target_pairs={{0,2},{1,3},{2,0},{3,1},{4,6},{5,7},{6,4},{7,5},{8,10},{9,11},{10,... | collective-permute-start | bytes 294920 | tf_op jit(solution)/shard_map/ppermute | solution.py:211
  5.8 7.7 %collective-permute-start.2 = (bf16[528,128]{1,0:T(8,128)(2,1)S(1)}, bf16[528,128]{1,0:T(8,128)(2,1)S(1)}, u32[]{:S(2)}, u32[]{:S(2)}) collective-permute-start(bf16[528,128]{1,0:T(8,128)(2,1)S(1)} %pack.1.full_ref.refs_0_), channel_id=1, source_target_pairs={{0,1},{1,0},{2,3},{3,2},{4,7},{5,6},{6,5},{7,4},{8,9},{9,8},{10,11... | collective-permute-start | bytes 405512 | tf_op jit(solution)/shard_map/ppermute | solution.py:175
  7.5 5.4 %collective-permute-start = (bf16[80,128]{1,0:T(8,128)(2,1)S(1)}, bf16[80,128]{1,0:T(8,128)(2,1)S(1)}, u32[]{:S(2)}, u32[]{:S(2)}) collective-permute-start(bf16[80,128]{1,0:T(8,128)(2,1)S(1)} %tail.1.tail_ref), channel_id=1, source_target_pairs={{0,2},{1,3},{2,0},{3,1},{4,6},{5,7},{6,4},{7,5},{8,10},{9,11},{10,... | collective-permute-start | bytes 61448 | tf_op jit(solution)/shard_map/ppermute | solution.py:212
  7.8 6.8 %collective-permute-start.4 = (bf16[400,128]{1,0:T(8,128)(2,1)S(1)}, bf16[400,128]{1,0:T(8,128)(2,1)S(1)}, u32[]{:S(2)}, u32[]{:S(2)}) collective-permute-start(bf16[400,128]{1,0:T(8,128)(2,1)S(1)} %lean.1), channel_id=1, source_target_pairs={{0,3},{1,2},{2,1},{3,0},{4,5},{5,4},{6,7},{7,6},{8,11},{9,10},{10,... | collective-permute-start | bytes 307208 | tf_op jit(solution)/shard_map/ppermute | solution.py:175
  13.6 1.3 %copy-start = (bf16[64,256]{1,0:T(8,128)(2,1)S(1)}, bf16[64,256]{1,0:T(8,128)(2,1)}, u32[]{:S(2)}) copy-start(bf16[64,256]{1,0:T(8,128)(2,1)} %density_ref.1) | copy-start | bytes 98308
  13.6 1.2 %collective-permute-start.3 = (bf16[192,128]{1,0:T(8,128)(2,1)S(1)}, bf16[192,128]{1,0:T(8,128)(2,1)S(1)}, u32[]{:S(2)}, u32[]{:S(2)}) collective-permute-start(bf16[192,128]{1,0:T(8,128)(2,1)S(1)} %merge.1), channel_id=1, source_target_pairs={{0,4},{4,0},{8,12},{12,8},{16,20},{20,16},{24,28},{28,24},{1,5},{5... | collective-permute-start | bytes 147464 | tf_op jit(solution)/shard_map/ppermute | solution.py:225
  15.6 1.3 %collective-permute-start.5 = (f32[64,256]{1,0:T(8,128)S(1)}, f32[64,256]{1,0:T(8,128)S(1)}, u32[]{:S(2)}, u32[]{:S(2)}) collective-permute-start(f32[64,256]{1,0:T(8,128)S(1)} %exchange.1), channel_id=1, source_target_pairs={{0,4},{4,0},{8,12},{12,8},{16,20},{20,16},{24,28},{28,24},{1,5},{5... | collective-permute-start | bytes 196616 | tf_op jit(solution)/shard_map/ppermute | solution.py:262
  17.0 5.2 %collective-permute-start.8 = (f32[64,256]{1,0:T(8,128)S(1)}, f32[64,256]{1,0:T(8,128)S(1)}, u32[]{:S(2)}, u32[]{:S(2)}) collective-permute-start(f32[64,256]{1,0:T(8,128)S(1)} %add.12), channel_id=1, source_target_pairs={{0,24},{4,28},{8,16},{12,20},{16,8},{20,12},{24,0},{28,4},{1,25},{... | collective-permute-start | bytes 196616 | tf_op jit(solution)/shard_map/ppermute | solution.py:262
  19.6 4.3 %collective-permute-start.7 = (f32[64,256]{1,0:T(8,128)S(1)}, f32[64,256]{1,0:T(8,128)S(1)}, u32[]{:S(2)}, u32[]{:S(2)}) collective-permute-start(f32[64,256]{1,0:T(8,128)S(1)} %add.12), channel_id=1, source_target_pairs={{0,16},{4,20},{8,24},{12,28},{16,0},{20,4},{24,8},{28,12},{1,17},{... | collective-permute-start | bytes 196616 | tf_op jit(solution)/shard_map/ppermute | solution.py:262
  20.1 4.3 %collective-permute-start.6 = (f32[64,256]{1,0:T(8,128)S(1)}, f32[64,256]{1,0:T(8,128)S(1)}, u32[]{:S(2)}, u32[]{:S(2)}) collective-permute-start(f32[64,256]{1,0:T(8,128)S(1)} %add.12), channel_id=1, source_target_pairs={{0,8},{4,12},{8,0},{12,4},{16,24},{20,28},{24,16},{28,20},{1,9},{5... | collective-permute-start | bytes 196616 | tf_op jit(solution)/shard_map/ppermute | solution.py:262

commit v33 on v27

--- a/solution.py
+++ b/solution.py
@@ -139,14 +139,20 @@
             axis=1,
         )
     half_ref[orb] = jnp.zeros_like(half_ref[orb])
+    depth = aux_width * BS // LANES
     for way in range(orb):
-        codes = meta[way * slots : (way + 1) * slots]
-        held[owners[way]] = lax.dot_general(
-            jnp.concatenate([half_ref[code] for code in codes], axis=1),
-            jnp.concatenate([packs[way][at : at + BS] for at in range(0, size, BS)], axis=1),
-            (((1,), (1,)), ((), ())),
-            preferred_element_type=jnp.float32,
-        )
+        total = None
+        for j in range(slots):
+            first = j * depth * BS
+            tiles = [packs[way][at : at + BS] for at in range(first, first + depth * BS, BS)]
+            term = lax.dot_general(
+                half_ref[meta[way * slots + j]],
+                jnp.concatenate(tiles, axis=1),
+                (((1,), (1,)), ((), ())),
+                preferred_element_type=jnp.float32,
+            )
+            total = term if total is None else total + term
+        held[owners[way]] = total
     out_ref[...] = jnp.concatenate([held[n] for n in range(orb)], axis=1)
 
 

time: 24.7 us -> 24.7 us (level)
  no operation moved by 1% of the time
where the time goes in v33:
time: 24.7 us; the launch traced here: 24.5 us
  starting transfers between devices  12.3 us (50%)
  waiting for transfers between devices  8.62 us (35%)
  Pallas kernels  2.11 us (9%)
  other arithmetic  0.74 us (3%)
  between operations  0.71 us (3%)
    ppermute x4, waiting for transfers between devices, shards(): lax.ppermute(parts, 'aux', [(i, i ^ way * step) for i in range(aux)])  4.67 us
    ppermute x2, starting transfers between devices, shift(): return lax.ppermute(x, ('aux', 'orb'), perm)  4.18 us
    ppermute x1, starting transfers between devices, shards(): raw = lax.ppermute(tensor_blocks, 'orb', across)  4.04 us
    ppermute x4, starting transfers between devices, shards(): lax.ppermute(parts, 'aux', [(i, i ^ way * step) for i in range(aux)])  3.78 us
    ppermute x1, waiting for transfers between devices, shards(): tail_in = lax.ppermute(tail, 'orb', across)  2.3 us
    ppermute x2, waiting for transfers between devices, shift(): return lax.ppermute(x, ('aux', 'orb'), perm)  1.55 us
    pallas_call x1, Pallas kernels, shards(): pl.pallas_call(functools.partial(pack_kernel, orb), out_shape=array(size...  1.14 us
    pallas_call x1, Pallas kernels, shards(): pl.pallas_call(functools.partial(exchange_kernel, orb, slots, aux_width),...  0.73 us
  transfers between devices with their start and end apart: 9, of which 8 were waited for; matrix products, arithmetic and copies ran while one was open for 0% of the time, Pallas kernels for 6%

profile of v33, /device:TPU:0, one launch (start us, length us, event | category | flops | bytes accessed | tf_op | source)
XLA Modules:
  0.0 24.5 jit_solution(11640219478283925706)
XLA Ops:
  0.0 4.0 %collective-permute-start.1 = (bf16[1,1,3,4,4096]{4,3,2,1,0:T(4,128)(2,1)}, bf16[1,1,3,4,4096]{4,3,2,1,0:T(4,128)(2,1)S(1)}, u32[]{:S(2)}, u32[]{:S(2)}) collective-permute-start(bf16[1,1,3,4,4096]{4,3,2,1,0:T(4,128)(2,1)} %raw_hbm.1), channel_id=1, source_target_pairs={{0,2},{1,3},{2,0},{3,1},{4,6},{5,7},{6,4},{7,5},{8,10},{9,11},{10,... | collective-permute-start | bytes 294920 | tf_op jit(solution)/shard_map/ppermute | solution.py:217
  4.7 1.1 %pack.1.full_ref.refs_0_ = bf16[520,128]{1,0:T(8,128)(2,1)S(1)} custom-call(s32[1,1]{1,0:T(1,128)S(6)} %copy.5.kept, s32[1,1,3]{2,1,0:T(1,128)} %pairs_hbm.1, bf16[64,256]{1,0:T(8,128)(2,1)} %density_ref.1, bf16[1,1,3,4,4096]{4,3,2,1,0:T(4,128)(2,1)} %raw_hbm.1), custom_call_target="tpu_custom_call" | custom-call | tf_op jit(solution)/shard_map/pack/pallas_call | solution.py:183
  5.8 1.6 %collective-permute-start.2 = (bf16[520,128]{1,0:T(8,128)(2,1)S(1)}, bf16[520,128]{1,0:T(8,128)(2,1)S(1)}, u32[]{:S(2)}, u32[]{:S(2)}) collective-permute-start(bf16[520,128]{1,0:T(8,128)(2,1)S(1)} %pack.1.full_ref.refs_0_), channel_id=1, source_target_pairs={{0,1},{1,0},{2,3},{3,2},{4,7},{5,6},{6,5},{7,4},{8,9},{9,8},{10,11... | collective-permute-start | bytes 399368 | tf_op jit(solution)/shard_map/ppermute | solution.py:181
  7.5 0.3 %collective-permute-start = (bf16[72,128]{1,0:T(8,128)(2,1)S(1)}, bf16[72,128]{1,0:T(8,128)(2,1)S(1)}, u32[]{:S(2)}, u32[]{:S(2)}) collective-permute-start(bf16[72,128]{1,0:T(8,128)(2,1)S(1)} %tail.1.tail_ref), channel_id=1, source_target_pairs={{0,2},{1,3},{2,0},{3,1},{4,6},{5,7},{6,4},{7,5},{8,10},{9,11},{10,... | collective-permute-start | bytes 55304 | tf_op jit(solution)/shard_map/ppermute | solution.py:218
  7.8 2.5 %collective-permute-start.4 = (bf16[392,128]{1,0:T(8,128)(2,1)S(1)}, bf16[392,128]{1,0:T(8,128)(2,1)S(1)}, u32[]{:S(2)}, u32[]{:S(2)}) collective-permute-start(bf16[392,128]{1,0:T(8,128)(2,1)S(1)} %lean.1), channel_id=1, source_target_pairs={{0,3},{1,2},{2,1},{3,0},{4,5},{5,4},{6,7},{7,6},{8,11},{9,10},{10,... | collective-permute-start | bytes 301064 | tf_op jit(solution)/shard_map/ppermute | solution.py:181
  10.4 2.3 %collective-permute-done.refs_1_.tail = bf16[72,128]{1,0:T(8,128)(2,1)S(1)} collective-permute-done((bf16[72,128]{1,0:T(8,128)(2,1)S(1)}, bf16[72,128]{1,0:T(8,128)(2,1)S(1)}, u32[]{:S(2)}, u32[]{:S(2)}) %collective-permute-start) | collective-permute-done | bytes 18464 | tf_op jit(solution)/shard_map/ppermute | solution.py:218
  12.7 0.0 collective-permute-done.1.raw
  12.7 0.2 relay.1
  12.9 0.4 %collective-permute-done.2.refs_0_.refs_2_ = bf16[520,128]{1,0:T(8,128)(2,1)S(1)} collective-permute-done((bf16[520,128]{1,0:T(8,128)(2,1)S(1)}, bf16[520,128]{1,0:T(8,128)(2,1)S(1)}, u32[]{:S(2)}, u32[]{:S(2)}) %collective-permute-start.2) | collective-permute-done | bytes 133152 | tf_op jit(solution)/shard_map/ppermute | solution.py:181
  13.4 0.0 copy-start
  13.4 0.0 collective-permute-start.3
  13.4 1.1 %collective-permute-done.4.refs_3_ = bf16[392,128]{1,0:T(8,128)(2,1)S(1)} collective-permute-done((bf16[392,128]{1,0:T(8,128)(2,1)S(1)}, bf16[392,128]{1,0:T(8,128)(2,1)S(1)}, u32[]{:S(2)}, u32[]{:S(2)}) %collective-permute-start.4) | collective-permute-done | bytes 100384 | tf_op jit(solution)/shard_map/ppermute | solution.py:181
  14.5 0.1 collective-permute-done.3.swapped
  14.6 0.1 maximum_convert_fusion.meta_ref
  14.7 0.0 copy-done
  14.7 0.7 %exchange.1 = f32[64,256]{1,0:T(8,128)S(1)} custom-call(s32[12]{0:T(128)S(1)} %maximum_convert_fusion.meta_ref, bf16[64,256]{1,0:T(8,128)(2,1)S(1)} %copy-done, bf16[256,192]{1,0:T(8,128)(2,1)S(1)} %get-tuple-element.14.left_ref, bf16[72,128]{1,0:T(8,128)(2,1)S(1)} %collective-permute-done.refs_1_.tail, bf16[192,128]{1,0:T(8,128)(2,1)S(1)} %collective-permute-done.3.swapped, ...), custom_call_target="tpu_custom_call" | custom-call | tf_op jit(solution)/shard_map/exchange/pallas_call | solution.py:249
  15.4 0.2 collective-permute-start.5
  15.6 1.1 %collective-permute-done.5 = f32[64,256]{1,0:T(8,128)S(1)} collective-permute-done((f32[64,256]{1,0:T(8,128)S(1)}, f32[64,256]{1,0:T(8,128)S(1)}, u32[]{:S(2)}, u32[]{:S(2)}) %collective-permute-start.5) | collective-permute-done | bytes 65568 | tf_op jit(solution)/shard_map/ppermute | solution.py:270
  16.8 2.7 %collective-permute-start.8 = (bf16[64,256]{1,0:T(8,128)(2,1)S(1)}, bf16[64,256]{1,0:T(8,128)(2,1)S(1)}, u32[]{:S(2)}, u32[]{:S(2)}) collective-permute-start(bf16[64,256]{1,0:T(8,128)(2,1)S(1)} %add_convert_fusion), channel_id=1, source_target_pairs={{0,24},{4,28},{8,16},{12,20},{16,8},{20,12},{24,0},{28,4},{1,25},{... | collective-permute-start | bytes 98312 | tf_op jit(solution)/shard_map/ppermute | solution.py:270
  19.5 0.5 %collective-permute-start.7 = (bf16[64,256]{1,0:T(8,128)(2,1)S(1)}, bf16[64,256]{1,0:T(8,128)(2,1)S(1)}, u32[]{:S(2)}, u32[]{:S(2)}) collective-permute-start(bf16[64,256]{1,0:T(8,128)(2,1)S(1)} %add_convert_fusion), channel_id=1, source_target_pairs={{0,16},{4,20},{8,24},{12,28},{16,0},{20,4},{24,8},{28,12},{1,17},{... | collective-permute-start | bytes 98312 | tf_op jit(solution)/shard_map/ppermute | solution.py:270
  20.0 0.3 %collective-permute-start.6 = (bf16[64,256]{1,0:T(8,128)(2,1)S(1)}, bf16[64,256]{1,0:T(8,128)(2,1)S(1)}, u32[]{:S(2)}, u32[]{:S(2)}) collective-permute-start(bf16[64,256]{1,0:T(8,128)(2,1)S(1)} %add_convert_fusion), channel_id=1, source_target_pairs={{0,8},{4,12},{8,0},{12,4},{16,24},{20,28},{24,16},{28,20},{1,9},{5... | collective-permute-start | bytes 98312 | tf_op jit(solution)/shard_map/ppermute | solution.py:270
  20.3 1.3 %collective-permute-done.8 = bf16[64,256]{1,0:T(8,128)(2,1)S(1)} collective-permute-done((bf16[64,256]{1,0:T(8,128)(2,1)S(1)}, bf16[64,256]{1,0:T(8,128)(2,1)S(1)}, u32[]{:S(2)}, u32[]{:S(2)}) %collective-permute-start.8) | collective-permute-done | bytes 32800 | tf_op jit(solution)/shard_map/ppermute | solution.py:270
  21.6 1.7 %collective-permute-done.7 = bf16[64,256]{1,0:T(8,128)(2,1)S(1)} collective-permute-done((bf16[64,256]{1,0:T(8,128)(2,1)S(1)}, bf16[64,256]{1,0:T(8,128)(2,1)S(1)}, u32[]{:S(2)}, u32[]{:S(2)}) %collective-permute-start.7) | collective-permute-done | bytes 32800 | tf_op jit(solution)/shard_map/ppermute | solution.py:270
  23.4 0.5 %collective-permute-done.6 = bf16[64,256]{1,0:T(8,128)(2,1)S(1)} collective-permute-done((bf16[64,256]{1,0:T(8,128)(2,1)S(1)}, bf16[64,256]{1,0:T(8,128)(2,1)S(1)}, u32[]{:S(2)}, u32[]{:S(2)}) %collective-permute-start.6) | collective-permute-done | bytes 32800 | tf_op jit(solution)/shard_map/ppermute | solution.py:270
  23.9 0.6 %add_add_fusion = f32[64,256]{1,0:T(8,128)} fusion(bf16[64,256]{1,0:T(8,128)(2,1)S(1)} %collective-permute-done.8, bf16[64,256]{1,0:T(8,128)(2,1)S(1)} %collective-permute-done.7, bf16[64,256]{1,0:T(8,128)(2,1)S(1)} %collective-permute-done.6, bf16[64,256]{1,0:T(8,128)(2,1)S(1)} %add_convert_fusion), kind=kLoop, calls=%fused_computation | loop fusion | flops 114688 | bytes 196608 | tf_op jit(solution)/shard_map/add | solution.py:273
  (8 shorter events, 0.0 us)
Async XLA Ops:
  0.0 12.7 %collective-permute-start.1 = (bf16[1,1,3,4,4096]{4,3,2,1,0:T(4,128)(2,1)}, bf16[1,1,3,4,4096]{4,3,2,1,0:T(4,128)(2,1)S(1)}, u32[]{:S(2)}, u32[]{:S(2)}) collective-permute-start(bf16[1,1,3,4,4096]{4,3,2,1,0:T(4,128)(2,1)} %raw_hbm.1), channel_id=1, source_target_pairs={{0,2},{1,3},{2,0},{3,1},{4,6},{5,7},{6,4},{7,5},{8,10},{9,11},{10,... | collective-permute-start | bytes 294920 | tf_op jit(solution)/shard_map/ppermute | solution.py:217
  5.8 7.5 %collective-permute-start.2 = (bf16[520,128]{1,0:T(8,128)(2,1)S(1)}, bf16[520,128]{1,0:T(8,128)(2,1)S(1)}, u32[]{:S(2)}, u32[]{:S(2)}) collective-permute-start(bf16[520,128]{1,0:T(8,128)(2,1)S(1)} %pack.1.full_ref.refs_0_), channel_id=1, source_target_pairs={{0,1},{1,0},{2,3},{3,2},{4,7},{5,6},{6,5},{7,4},{8,9},{9,8},{10,11... | collective-permute-start | bytes 399368 | tf_op jit(solution)/shard_map/ppermute | solution.py:181
  7.5 5.2 %collective-permute-start = (bf16[72,128]{1,0:T(8,128)(2,1)S(1)}, bf16[72,128]{1,0:T(8,128)(2,1)S(1)}, u32[]{:S(2)}, u32[]{:S(2)}) collective-permute-start(bf16[72,128]{1,0:T(8,128)(2,1)S(1)} %tail.1.tail_ref), channel_id=1, source_target_pairs={{0,2},{1,3},{2,0},{3,1},{4,6},{5,7},{6,4},{7,5},{8,10},{9,11},{10,... | collective-permute-start | bytes 55304 | tf_op jit(solution)/shard_map/ppermute | solution.py:218
  7.8 6.7 %collective-permute-start.4 = (bf16[392,128]{1,0:T(8,128)(2,1)S(1)}, bf16[392,128]{1,0:T(8,128)(2,1)S(1)}, u32[]{:S(2)}, u32[]{:S(2)}) collective-permute-start(bf16[392,128]{1,0:T(8,128)(2,1)S(1)} %lean.1), channel_id=1, source_target_pairs={{0,3},{1,2},{2,1},{3,0},{4,5},{5,4},{6,7},{7,6},{8,11},{9,10},{10,... | collective-permute-start | bytes 301064 | tf_op jit(solution)/shard_map/ppermute | solution.py:181
  13.4 1.3 %copy-start = (bf16[64,256]{1,0:T(8,128)(2,1)S(1)}, bf16[64,256]{1,0:T(8,128)(2,1)}, u32[]{:S(2)}) copy-start(bf16[64,256]{1,0:T(8,128)(2,1)} %density_ref.1) | copy-start | bytes 98308
  13.4 1.2 %collective-permute-start.3 = (bf16[192,128]{1,0:T(8,128)(2,1)S(1)}, bf16[192,128]{1,0:T(8,128)(2,1)S(1)}, u32[]{:S(2)}, u32[]{:S(2)}) collective-permute-start(bf16[192,128]{1,0:T(8,128)(2,1)S(1)} %merge.1), channel_id=1, source_target_pairs={{0,4},{4,0},{8,12},{12,8},{16,20},{20,16},{24,28},{28,24},{1,5},{5... | collective-permute-start | bytes 147464 | tf_op jit(solution)/shard_map/ppermute | solution.py:231
  15.4 1.3 %collective-permute-start.5 = (f32[64,256]{1,0:T(8,128)S(1)}, f32[64,256]{1,0:T(8,128)S(1)}, u32[]{:S(2)}, u32[]{:S(2)}) collective-permute-start(f32[64,256]{1,0:T(8,128)S(1)} %exchange.1), channel_id=1, source_target_pairs={{0,4},{4,0},{8,12},{12,8},{16,20},{20,16},{24,28},{28,24},{1,5},{5... | collective-permute-start | bytes 196616 | tf_op jit(solution)/shard_map/ppermute | solution.py:270
  16.8 4.9 %collective-permute-start.8 = (bf16[64,256]{1,0:T(8,128)(2,1)S(1)}, bf16[64,256]{1,0:T(8,128)(2,1)S(1)}, u32[]{:S(2)}, u32[]{:S(2)}) collective-permute-start(bf16[64,256]{1,0:T(8,128)(2,1)S(1)} %add_convert_fusion), channel_id=1, source_target_pairs={{0,24},{4,28},{8,16},{12,20},{16,8},{20,12},{24,0},{28,4},{1,25},{... | collective-permute-start | bytes 98312 | tf_op jit(solution)/shard_map/ppermute | solution.py:270
  19.5 3.9 %collective-permute-start.7 = (bf16[64,256]{1,0:T(8,128)(2,1)S(1)}, bf16[64,256]{1,0:T(8,128)(2,1)S(1)}, u32[]{:S(2)}, u32[]{:S(2)}) collective-permute-start(bf16[64,256]{1,0:T(8,128)(2,1)S(1)} %add_convert_fusion), channel_id=1, source_target_pairs={{0,16},{4,20},{8,24},{12,28},{16,0},{20,4},{24,8},{28,12},{1,17},{... | collective-permute-start | bytes 98312 | tf_op jit(solution)/shard_map/ppermute | solution.py:270
  20.0 3.9 %collective-permute-start.6 = (bf16[64,256]{1,0:T(8,128)(2,1)S(1)}, bf16[64,256]{1,0:T(8,128)(2,1)S(1)}, u32[]{:S(2)}, u32[]{:S(2)}) collective-permute-start(bf16[64,256]{1,0:T(8,128)(2,1)S(1)} %add_convert_fusion), channel_id=1, source_target_pairs={{0,8},{4,12},{8,0},{12,4},{16,24},{20,28},{24,16},{28,20},{1,9},{5... | collective-permute-start | bytes 98312 | tf_op jit(solution)/shard_map/ppermute | solution.py:270

commit v34 on v27

--- a/solution.py
+++ b/solution.py
@@ -78,9 +78,16 @@
     out_ref[size:] = tail_ref[tail_ref.shape[0] - NOTE :]
 
 
-def relay_kernel(slots, aux_width, raw, full_ref, out_ref, left_ref):
-    lay_blocks(raw[0, 0], out_ref)
-    size = out_ref.shape[0]
+def turn(ref, size):
+    joined = jnp.concatenate([ref[at : at + BS] for at in range(0, size, BS)], axis=1)
+    return joined.astype(jnp.float32).T.astype(jnp.bfloat16)
+
+
+def relay_kernel(slots, aux_width, raw, full_ref, out_ref, left_ref, own_ref, laid):
+    lay_blocks(raw[0, 0], laid)
+    size = laid.shape[0]
+    out_ref[...] = turn(laid, size)
+    own_ref[...] = turn(full_ref, size)
     own = jnp.concatenate([full_ref[at : at + BS] for at in range(0, size, BS)], axis=1)
     for p in range(aux_width):
         cuts = [(j * aux_width + p) * BS for j in range(slots)]
@@ -102,7 +109,8 @@
 def exchange_kernel(
     orb, slots, aux_width, meta_ref, density_ref, left_ref, tail, swapped, *refs
 ):
-    packs, (out_ref, rows, half_ref, held) = refs[:orb], refs[orb:]
+    turned, packs = refs[:2], (None, None, *refs[2:orb])
+    out_ref, rows, half_ref, held = refs[orb:]
     fulls = packs[2::2]
     notes = meta_ref[...]
     meta = [notes[i] for i in range(orb * slots)]
@@ -141,8 +149,14 @@
     half_ref[orb] = jnp.zeros_like(half_ref[orb])
     for way in range(orb):
         codes = meta[way * slots : (way + 1) * slots]
+        joined = jnp.concatenate([half_ref[code] for code in codes], axis=1)
+        if way < 2:
+            held[owners[way]] = jnp.dot(
+                joined, turned[way][...], preferred_element_type=jnp.float32
+            )
+            continue
         held[owners[way]] = lax.dot_general(
-            jnp.concatenate([half_ref[code] for code in codes], axis=1),
+            joined,
             jnp.concatenate([packs[way][at : at + BS] for at in range(0, size, BS)], axis=1),
             (((1,), (1,)), ((), ())),
             preferred_element_type=jnp.float32,
@@ -223,19 +237,21 @@
         name="merge",
     )(*fulls, tail_in)
     swapped = lax.ppermute(merged, "aux", [(i, i ^ 1) for i in range(aux)])
-    across, left = pl.pallas_call(
+    across, left, own = pl.pallas_call(
         functools.partial(relay_kernel, slots, aux_width),
         out_shape=[
-            array(size),
+            jax.ShapeDtypeStruct((slots * aux_width * BS, BS), jnp.bfloat16),
             jax.ShapeDtypeStruct((aux_width * BS, slots * BS), jnp.bfloat16),
+            jax.ShapeDtypeStruct((slots * aux_width * BS, BS), jnp.bfloat16),
         ],
         in_specs=[vmem] * 2,
-        out_specs=[vmem] * 2,
+        out_specs=[vmem] * 3,
+        scratch_shapes=[pltpu.VMEM((size, LANES), jnp.bfloat16)],
         compiler_params=params,
         name="relay",
     )(raw, full)
     swapped, leans = lax.optimization_barrier((swapped, leans))
-    packs, notes = [full, across], [tail, tail_in]
+    packs, notes = [own, across], [tail, tail_in]
     for pair in zip(fulls, leans):
         packs += pair
         notes += pair

time: 24.7 us -> 24.7 us (level)
  no operation moved by 1% of the time
where the time goes in v34:
time: 24.7 us; the launch traced here: 24.5 us
  starting transfers between devices  12.3 us (50%)
  waiting for transfers between devices  8.46 us (34%)
  Pallas kernels  2.28 us (9%)
  other arithmetic  0.74 us (3%)
  between operations  0.72 us (3%)
    ppermute x4, waiting for transfers between devices, shards(): lax.ppermute(parts, 'aux', [(i, i ^ way * step) for i in range(aux)])  4.67 us
    ppermute x2, starting transfers between devices, shift(): return lax.ppermute(x, ('aux', 'orb'), perm)  4.18 us
    ppermute x1, starting transfers between devices, shards(): raw = lax.ppermute(tensor_blocks, 'orb', across)  4.04 us
    ppermute x4, starting transfers between devices, shards(): lax.ppermute(parts, 'aux', [(i, i ^ way * step) for i in range(aux)])  3.78 us
    ppermute x1, waiting for transfers between devices, shards(): tail_in = lax.ppermute(tail, 'orb', across)  2.3 us
    ppermute x2, waiting for transfers between devices, shift(): return lax.ppermute(x, ('aux', 'orb'), perm)  1.38 us
    pallas_call x1, Pallas kernels, shards(): pl.pallas_call(functools.partial(pack_kernel, orb), out_shape=array(size...  1.14 us
    pallas_call x1, Pallas kernels, shards(): pl.pallas_call(functools.partial(exchange_kernel, orb, slots, aux_width),...  0.73 us
  transfers between devices with their start and end apart: 9, of which 8 were waited for; matrix products, arithmetic and copies ran while one was open for 0% of the time, Pallas kernels for 6%

profile of v34, /device:TPU:0, one launch (start us, length us, event | category | flops | bytes accessed | tf_op | source)
XLA Modules:
  0.0 24.5 jit_solution(13813288610665827257)
XLA Ops:
  0.0 4.0 %collective-permute-start.1 = (bf16[1,1,3,4,4096]{4,3,2,1,0:T(4,128)(2,1)}, bf16[1,1,3,4,4096]{4,3,2,1,0:T(4,128)(2,1)S(1)}, u32[]{:S(2)}, u32[]{:S(2)}) collective-permute-start(bf16[1,1,3,4,4096]{4,3,2,1,0:T(4,128)(2,1)} %raw_hbm.1), channel_id=1, source_target_pairs={{0,2},{1,3},{2,0},{3,1},{4,6},{5,7},{6,4},{7,5},{8,10},{9,11},{10,... | collective-permute-start | bytes 294920 | tf_op jit(solution)/shard_map/ppermute | solution.py:225
  4.7 1.1 %pack.1.full_ref = bf16[520,128]{1,0:T(8,128)(2,1)S(1)} custom-call(s32[1,1]{1,0:T(1,128)S(6)} %copy.5.kept, s32[1,1,3]{2,1,0:T(1,128)} %pairs_hbm.1, bf16[64,256]{1,0:T(8,128)(2,1)} %density_ref.1, bf16[1,1,3,4,4096]{4,3,2,1,0:T(4,128)(2,1)} %raw_hbm.1), custom_call_target="tpu_custom_call" | custom-call | tf_op jit(solution)/shard_map/pack/pallas_call | solution.py:191
  5.8 1.6 %collective-permute-start.2 = (bf16[520,128]{1,0:T(8,128)(2,1)S(1)}, bf16[520,128]{1,0:T(8,128)(2,1)S(1)}, u32[]{:S(2)}, u32[]{:S(2)}) collective-permute-start(bf16[520,128]{1,0:T(8,128)(2,1)S(1)} %pack.1.full_ref), channel_id=1, source_target_pairs={{0,1},{1,0},{2,3},{3,2},{4,7},{5,6},{6,5},{7,4},{8,9},{9,8},{10,11... | collective-permute-start | bytes 399368 | tf_op jit(solution)/shard_map/ppermute | solution.py:189
  7.5 0.3 %collective-permute-start = (bf16[72,128]{1,0:T(8,128)(2,1)S(1)}, bf16[72,128]{1,0:T(8,128)(2,1)S(1)}, u32[]{:S(2)}, u32[]{:S(2)}) collective-permute-start(bf16[72,128]{1,0:T(8,128)(2,1)S(1)} %tail.1.tail_ref), channel_id=1, source_target_pairs={{0,2},{1,3},{2,0},{3,1},{4,6},{5,7},{6,4},{7,5},{8,10},{9,11},{10,... | collective-permute-start | bytes 55304 | tf_op jit(solution)/shard_map/ppermute | solution.py:226
  7.8 2.5 %collective-permute-start.4 = (bf16[392,128]{1,0:T(8,128)(2,1)S(1)}, bf16[392,128]{1,0:T(8,128)(2,1)S(1)}, u32[]{:S(2)}, u32[]{:S(2)}) collective-permute-start(bf16[392,128]{1,0:T(8,128)(2,1)S(1)} %lean.1), channel_id=1, source_target_pairs={{0,3},{1,2},{2,1},{3,0},{4,5},{5,4},{6,7},{7,6},{8,11},{9,10},{10,... | collective-permute-start | bytes 301064 | tf_op jit(solution)/shard_map/ppermute | solution.py:189
  10.4 2.3 %collective-permute-done.refs_1_.tail = bf16[72,128]{1,0:T(8,128)(2,1)S(1)} collective-permute-done((bf16[72,128]{1,0:T(8,128)(2,1)S(1)}, bf16[72,128]{1,0:T(8,128)(2,1)S(1)}, u32[]{:S(2)}, u32[]{:S(2)}) %collective-permute-start) | collective-permute-done | bytes 18464 | tf_op jit(solution)/shard_map/ppermute | solution.py:226
  12.7 0.0 collective-permute-done.1.raw
  12.7 0.4 %relay.1 = (bf16[768,64]{1,0:T(8,128)(2,1)S(1)}, bf16[256,192]{1,0:T(8,128)(2,1)S(1)}, bf16[768,64]{1,0:T(8,128)(2,1)S(1)}) custom-call(bf16[1,1,3,4,4096]{4,3,2,1,0:T(4,128)(2,1)S(1)} %collective-permute-done.1.raw, bf16[520,128]{1,0:T(8,128)(2,1)S(1)} %pack.1.full_ref), custom_call_target="tpu_custom_call" | custom-call | tf_op jit(solution)/shard_map/relay/pallas_call | solution.py:240
  13.1 0.3 %collective-permute-done.2.refs_0_.refs_2_ = bf16[520,128]{1,0:T(8,128)(2,1)S(1)} collective-permute-done((bf16[520,128]{1,0:T(8,128)(2,1)S(1)}, bf16[520,128]{1,0:T(8,128)(2,1)S(1)}, u32[]{:S(2)}, u32[]{:S(2)}) %collective-permute-start.2) | collective-permute-done | bytes 133152 | tf_op jit(solution)/shard_map/ppermute | solution.py:189
  13.4 0.0 copy-start
  13.4 0.0 collective-permute-start.3
  13.4 1.1 %collective-permute-done.4.refs_3_ = bf16[392,128]{1,0:T(8,128)(2,1)S(1)} collective-permute-done((bf16[392,128]{1,0:T(8,128)(2,1)S(1)}, bf16[392,128]{1,0:T(8,128)(2,1)S(1)}, u32[]{:S(2)}, u32[]{:S(2)}) %collective-permute-start.4) | collective-permute-done | bytes 100384 | tf_op jit(solution)/shard_map/ppermute | solution.py:189
  14.5 0.1 collective-permute-done.3.swapped
  14.6 0.1 maximum_convert_fusion.meta_ref
  14.7 0.0 copy-done
  14.7 0.7 %exchange.1 = f32[64,256]{1,0:T(8,128)S(1)} custom-call(s32[12]{0:T(128)S(1)} %maximum_convert_fusion.meta_ref, bf16[64,256]{1,0:T(8,128)(2,1)S(1)} %copy-done, bf16[256,192]{1,0:T(8,128)(2,1)S(1)} %get-tuple-element.15.left_ref, bf16[72,128]{1,0:T(8,128)(2,1)S(1)} %collective-permute-done.refs_1_.tail, bf16[192,128]{1,0:T(8,128)(2,1)S(1)} %collective-permute-done.3.swapped, ...), custom_call_target="tpu_custom_call" | custom-call | tf_op jit(solution)/shard_map/exchange/pallas_call | solution.py:259
  15.4 0.2 collective-permute-start.5
  15.6 1.1 %collective-permute-done.5 = f32[64,256]{1,0:T(8,128)S(1)} collective-permute-done((f32[64,256]{1,0:T(8,128)S(1)}, f32[64,256]{1,0:T(8,128)S(1)}, u32[]{:S(2)}, u32[]{:S(2)}) %collective-permute-start.5) | collective-permute-done | bytes 65568 | tf_op jit(solution)/shard_map/ppermute | solution.py:280
  16.8 2.7 %collective-permute-start.8 = (bf16[64,256]{1,0:T(8,128)(2,1)S(1)}, bf16[64,256]{1,0:T(8,128)(2,1)S(1)}, u32[]{:S(2)}, u32[]{:S(2)}) collective-permute-start(bf16[64,256]{1,0:T(8,128)(2,1)S(1)} %add_convert_fusion), channel_id=1, source_target_pairs={{0,24},{4,28},{8,16},{12,20},{16,8},{20,12},{24,0},{28,4},{1,25},{... | collective-permute-start | bytes 98312 | tf_op jit(solution)/shard_map/ppermute | solution.py:280
  19.5 0.5 %collective-permute-start.7 = (bf16[64,256]{1,0:T(8,128)(2,1)S(1)}, bf16[64,256]{1,0:T(8,128)(2,1)S(1)}, u32[]{:S(2)}, u32[]{:S(2)}) collective-permute-start(bf16[64,256]{1,0:T(8,128)(2,1)S(1)} %add_convert_fusion), channel_id=1, source_target_pairs={{0,16},{4,20},{8,24},{12,28},{16,0},{20,4},{24,8},{28,12},{1,17},{... | collective-permute-start | bytes 98312 | tf_op jit(solution)/shard_map/ppermute | solution.py:280
  20.0 0.3 %collective-permute-start.6 = (bf16[64,256]{1,0:T(8,128)(2,1)S(1)}, bf16[64,256]{1,0:T(8,128)(2,1)S(1)}, u32[]{:S(2)}, u32[]{:S(2)}) collective-permute-start(bf16[64,256]{1,0:T(8,128)(2,1)S(1)} %add_convert_fusion), channel_id=1, source_target_pairs={{0,8},{4,12},{8,0},{12,4},{16,24},{20,28},{24,16},{28,20},{1,9},{5... | collective-permute-start | bytes 98312 | tf_op jit(solution)/shard_map/ppermute | solution.py:280
  20.3 1.3 %collective-permute-done.8 = bf16[64,256]{1,0:T(8,128)(2,1)S(1)} collective-permute-done((bf16[64,256]{1,0:T(8,128)(2,1)S(1)}, bf16[64,256]{1,0:T(8,128)(2,1)S(1)}, u32[]{:S(2)}, u32[]{:S(2)}) %collective-permute-start.8) | collective-permute-done | bytes 32800 | tf_op jit(solution)/shard_map/ppermute | solution.py:280
  21.6 1.7 %collective-permute-done.7 = bf16[64,256]{1,0:T(8,128)(2,1)S(1)} collective-permute-done((bf16[64,256]{1,0:T(8,128)(2,1)S(1)}, bf16[64,256]{1,0:T(8,128)(2,1)S(1)}, u32[]{:S(2)}, u32[]{:S(2)}) %collective-permute-start.7) | collective-permute-done | bytes 32800 | tf_op jit(solution)/shard_map/ppermute | solution.py:280
  23.4 0.5 %collective-permute-done.6 = bf16[64,256]{1,0:T(8,128)(2,1)S(1)} collective-permute-done((bf16[64,256]{1,0:T(8,128)(2,1)S(1)}, bf16[64,256]{1,0:T(8,128)(2,1)S(1)}, u32[]{:S(2)}, u32[]{:S(2)}) %collective-permute-start.6) | collective-permute-done | bytes 32800 | tf_op jit(solution)/shard_map/ppermute | solution.py:280
  23.9 0.6 %add_add_fusion = f32[64,256]{1,0:T(8,128)} fusion(bf16[64,256]{1,0:T(8,128)(2,1)S(1)} %collective-permute-done.8, bf16[64,256]{1,0:T(8,128)(2,1)S(1)} %collective-permute-done.7, bf16[64,256]{1,0:T(8,128)(2,1)S(1)} %collective-permute-done.6, bf16[64,256]{1,0:T(8,128)(2,1)S(1)} %add_convert_fusion), kind=kLoop, calls=%fused_computation | loop fusion | flops 114688 | bytes 196608 | tf_op jit(solution)/shard_map/add | solution.py:283
  (8 shorter events, 0.0 us)
Async XLA Ops:
  0.0 12.7 %collective-permute-start.1 = (bf16[1,1,3,4,4096]{4,3,2,1,0:T(4,128)(2,1)}, bf16[1,1,3,4,4096]{4,3,2,1,0:T(4,128)(2,1)S(1)}, u32[]{:S(2)}, u32[]{:S(2)}) collective-permute-start(bf16[1,1,3,4,4096]{4,3,2,1,0:T(4,128)(2,1)} %raw_hbm.1), channel_id=1, source_target_pairs={{0,2},{1,3},{2,0},{3,1},{4,6},{5,7},{6,4},{7,5},{8,10},{9,11},{10,... | collective-permute-start | bytes 294920 | tf_op jit(solution)/shard_map/ppermute | solution.py:225
  5.8 7.5 %collective-permute-start.2 = (bf16[520,128]{1,0:T(8,128)(2,1)S(1)}, bf16[520,128]{1,0:T(8,128)(2,1)S(1)}, u32[]{:S(2)}, u32[]{:S(2)}) collective-permute-start(bf16[520,128]{1,0:T(8,128)(2,1)S(1)} %pack.1.full_ref), channel_id=1, source_target_pairs={{0,1},{1,0},{2,3},{3,2},{4,7},{5,6},{6,5},{7,4},{8,9},{9,8},{10,11... | collective-permute-start | bytes 399368 | tf_op jit(solution)/shard_map/ppermute | solution.py:189
  7.5 5.2 %collective-permute-start = (bf16[72,128]{1,0:T(8,128)(2,1)S(1)}, bf16[72,128]{1,0:T(8,128)(2,1)S(1)}, u32[]{:S(2)}, u32[]{:S(2)}) collective-permute-start(bf16[72,128]{1,0:T(8,128)(2,1)S(1)} %tail.1.tail_ref), channel_id=1, source_target_pairs={{0,2},{1,3},{2,0},{3,1},{4,6},{5,7},{6,4},{7,5},{8,10},{9,11},{10,... | collective-permute-start | bytes 55304 | tf_op jit(solution)/shard_map/ppermute | solution.py:226
  7.8 6.7 %collective-permute-start.4 = (bf16[392,128]{1,0:T(8,128)(2,1)S(1)}, bf16[392,128]{1,0:T(8,128)(2,1)S(1)}, u32[]{:S(2)}, u32[]{:S(2)}) collective-permute-start(bf16[392,128]{1,0:T(8,128)(2,1)S(1)} %lean.1), channel_id=1, source_target_pairs={{0,3},{1,2},{2,1},{3,0},{4,5},{5,4},{6,7},{7,6},{8,11},{9,10},{10,... | collective-permute-start | bytes 301064 | tf_op jit(solution)/shard_map/ppermute | solution.py:189
  13.4 1.3 %copy-start = (bf16[64,256]{1,0:T(8,128)(2,1)S(1)}, bf16[64,256]{1,0:T(8,128)(2,1)}, u32[]{:S(2)}) copy-start(bf16[64,256]{1,0:T(8,128)(2,1)} %density_ref.1) | copy-start | bytes 98308
  13.4 1.2 %collective-permute-start.3 = (bf16[192,128]{1,0:T(8,128)(2,1)S(1)}, bf16[192,128]{1,0:T(8,128)(2,1)S(1)}, u32[]{:S(2)}, u32[]{:S(2)}) collective-permute-start(bf16[192,128]{1,0:T(8,128)(2,1)S(1)} %merge.1), channel_id=1, source_target_pairs={{0,4},{4,0},{8,12},{12,8},{16,20},{20,16},{24,28},{28,24},{1,5},{5... | collective-permute-start | bytes 147464 | tf_op jit(solution)/shard_map/ppermute | solution.py:239
  15.4 1.3 %collective-permute-start.5 = (f32[64,256]{1,0:T(8,128)S(1)}, f32[64,256]{1,0:T(8,128)S(1)}, u32[]{:S(2)}, u32[]{:S(2)}) collective-permute-start(f32[64,256]{1,0:T(8,128)S(1)} %exchange.1), channel_id=1, source_target_pairs={{0,4},{4,0},{8,12},{12,8},{16,20},{20,16},{24,28},{28,24},{1,5},{5... | collective-permute-start | bytes 196616 | tf_op jit(solution)/shard_map/ppermute | solution.py:280
  16.8 4.9 %collective-permute-start.8 = (bf16[64,256]{1,0:T(8,128)(2,1)S(1)}, bf16[64,256]{1,0:T(8,128)(2,1)S(1)}, u32[]{:S(2)}, u32[]{:S(2)}) collective-permute-start(bf16[64,256]{1,0:T(8,128)(2,1)S(1)} %add_convert_fusion), channel_id=1, source_target_pairs={{0,24},{4,28},{8,16},{12,20},{16,8},{20,12},{24,0},{28,4},{1,25},{... | collective-permute-start | bytes 98312 | tf_op jit(solution)/shard_map/ppermute | solution.py:280
  19.5 3.9 %collective-permute-start.7 = (bf16[64,256]{1,0:T(8,128)(2,1)S(1)}, bf16[64,256]{1,0:T(8,128)(2,1)S(1)}, u32[]{:S(2)}, u32[]{:S(2)}) collective-permute-start(bf16[64,256]{1,0:T(8,128)(2,1)S(1)} %add_convert_fusion), channel_id=1, source_target_pairs={{0,16},{4,20},{8,24},{12,28},{16,0},{20,4},{24,8},{28,12},{1,17},{... | collective-permute-start | bytes 98312 | tf_op jit(solution)/shard_map/ppermute | solution.py:280
  20.0 3.9 %collective-permute-start.6 = (bf16[64,256]{1,0:T(8,128)(2,1)S(1)}, bf16[64,256]{1,0:T(8,128)(2,1)S(1)}, u32[]{:S(2)}, u32[]{:S(2)}) collective-permute-start(bf16[64,256]{1,0:T(8,128)(2,1)S(1)} %add_convert_fusion), channel_id=1, source_target_pairs={{0,8},{4,12},{8,0},{12,4},{16,24},{20,28},{24,16},{28,20},{1,9},{5... | collective-permute-start | bytes 98312 | tf_op jit(solution)/shard_map/ppermute | solution.py:280

commit v35 on v27

--- a/solution.py
+++ b/solution.py
@@ -260,7 +260,7 @@
         if step == 2:
             parts = parts.astype(jnp.bfloat16)
         terms = [parts]
-        for way in range(1, ways):
+        for way in (2, 1, 3) if ways == 4 else (1,):
             terms.append(lax.ppermute(parts, "aux", [(i, i ^ (way * step)) for i in range(aux)]))
         terms = [term.astype(jnp.float32) for term in terms]
         while len(terms) > 1:

time: 24.7 us -> 24.7 us (level)
  no operation moved by 1% of the time
where the time goes in v35:
time: 24.7 us; the launch traced here: 24.6 us
  starting transfers between devices  12.3 us (50%)
  waiting for transfers between devices  8.65 us (35%)
  Pallas kernels  2.11 us (9%)
  other arithmetic  0.74 us (3%)
  between operations  0.71 us (3%)
    ppermute x4, waiting for transfers between devices, shards(): lax.ppermute(parts, 'aux', [(i, i ^ way * step) for i in range(aux)])  4.7 us
    ppermute x2, starting transfers between devices, shift(): return lax.ppermute(x, ('aux', 'orb'), perm)  4.18 us
    ppermute x1, starting transfers between devices, shards(): raw = lax.ppermute(tensor_blocks, 'orb', across)  4.04 us
    ppermute x4, starting transfers between devices, shards(): lax.ppermute(parts, 'aux', [(i, i ^ way * step) for i in range(aux)])  3.78 us
    ppermute x1, waiting for transfers between devices, shards(): tail_in = lax.ppermute(tail, 'orb', across)  2.3 us
    ppermute x2, waiting for transfers between devices, shift(): return lax.ppermute(x, ('aux', 'orb'), perm)  1.55 us
    pallas_call x1, Pallas kernels, shards(): pl.pallas_call(functools.partial(pack_kernel, orb), out_shape=array(size...  1.14 us
    pallas_call x1, Pallas kernels, shards(): pl.pallas_call(functools.partial(exchange_kernel, orb, slots, aux_width),...  0.73 us
  transfers between devices with their start and end apart: 9, of which 8 were waited for; matrix products, arithmetic and copies ran while one was open for 0% of the time, Pallas kernels for 6%

profile of v35, /device:TPU:0, one launch (start us, length us, event | category | flops | bytes accessed | tf_op | source)
XLA Modules:
  0.0 24.6 jit_solution(3831410820591509535)
XLA Ops:
  0.0 4.0 %collective-permute-start.1 = (bf16[1,1,3,4,4096]{4,3,2,1,0:T(4,128)(2,1)}, bf16[1,1,3,4,4096]{4,3,2,1,0:T(4,128)(2,1)S(1)}, u32[]{:S(2)}, u32[]{:S(2)}) collective-permute-start(bf16[1,1,3,4,4096]{4,3,2,1,0:T(4,128)(2,1)} %raw_hbm.1), channel_id=1, source_target_pairs={{0,2},{1,3},{2,0},{3,1},{4,6},{5,7},{6,4},{7,5},{8,10},{9,11},{10,... | collective-permute-start | bytes 294920 | tf_op jit(solution)/shard_map/ppermute | solution.py:211
  4.7 1.1 %pack.1.full_ref.refs_0_ = bf16[520,128]{1,0:T(8,128)(2,1)S(1)} custom-call(s32[1,1]{1,0:T(1,128)S(6)} %copy.5.kept, s32[1,1,3]{2,1,0:T(1,128)} %pairs_hbm.1, bf16[64,256]{1,0:T(8,128)(2,1)} %density_ref.1, bf16[1,1,3,4,4096]{4,3,2,1,0:T(4,128)(2,1)} %raw_hbm.1), custom_call_target="tpu_custom_call" | custom-call | tf_op jit(solution)/shard_map/pack/pallas_call | solution.py:177
  5.8 1.6 %collective-permute-start.2 = (bf16[520,128]{1,0:T(8,128)(2,1)S(1)}, bf16[520,128]{1,0:T(8,128)(2,1)S(1)}, u32[]{:S(2)}, u32[]{:S(2)}) collective-permute-start(bf16[520,128]{1,0:T(8,128)(2,1)S(1)} %pack.1.full_ref.refs_0_), channel_id=1, source_target_pairs={{0,1},{1,0},{2,3},{3,2},{4,7},{5,6},{6,5},{7,4},{8,9},{9,8},{10,11... | collective-permute-start | bytes 399368 | tf_op jit(solution)/shard_map/ppermute | solution.py:175
  7.5 0.3 %collective-permute-start = (bf16[72,128]{1,0:T(8,128)(2,1)S(1)}, bf16[72,128]{1,0:T(8,128)(2,1)S(1)}, u32[]{:S(2)}, u32[]{:S(2)}) collective-permute-start(bf16[72,128]{1,0:T(8,128)(2,1)S(1)} %tail.1.tail_ref), channel_id=1, source_target_pairs={{0,2},{1,3},{2,0},{3,1},{4,6},{5,7},{6,4},{7,5},{8,10},{9,11},{10,... | collective-permute-start | bytes 55304 | tf_op jit(solution)/shard_map/ppermute | solution.py:212
  7.8 2.5 %collective-permute-start.4 = (bf16[392,128]{1,0:T(8,128)(2,1)S(1)}, bf16[392,128]{1,0:T(8,128)(2,1)S(1)}, u32[]{:S(2)}, u32[]{:S(2)}) collective-permute-start(bf16[392,128]{1,0:T(8,128)(2,1)S(1)} %lean.1), channel_id=1, source_target_pairs={{0,3},{1,2},{2,1},{3,0},{4,5},{5,4},{6,7},{7,6},{8,11},{9,10},{10,... | collective-permute-start | bytes 301064 | tf_op jit(solution)/shard_map/ppermute | solution.py:175
  10.4 2.3 %collective-permute-done.refs_1_.tail = bf16[72,128]{1,0:T(8,128)(2,1)S(1)} collective-permute-done((bf16[72,128]{1,0:T(8,128)(2,1)S(1)}, bf16[72,128]{1,0:T(8,128)(2,1)S(1)}, u32[]{:S(2)}, u32[]{:S(2)}) %collective-permute-start) | collective-permute-done | bytes 18464 | tf_op jit(solution)/shard_map/ppermute | solution.py:212
  12.7 0.0 collective-permute-done.1.raw
  12.7 0.2 relay.1
  12.9 0.4 %collective-permute-done.2.refs_0_.refs_2_ = bf16[520,128]{1,0:T(8,128)(2,1)S(1)} collective-permute-done((bf16[520,128]{1,0:T(8,128)(2,1)S(1)}, bf16[520,128]{1,0:T(8,128)(2,1)S(1)}, u32[]{:S(2)}, u32[]{:S(2)}) %collective-permute-start.2) | collective-permute-done | bytes 133152 | tf_op jit(solution)/shard_map/ppermute | solution.py:175
  13.4 0.0 copy-start
  13.4 0.0 collective-permute-start.3
  13.4 1.1 %collective-permute-done.4.refs_3_ = bf16[392,128]{1,0:T(8,128)(2,1)S(1)} collective-permute-done((bf16[392,128]{1,0:T(8,128)(2,1)S(1)}, bf16[392,128]{1,0:T(8,128)(2,1)S(1)}, u32[]{:S(2)}, u32[]{:S(2)}) %collective-permute-start.4) | collective-permute-done | bytes 100384 | tf_op jit(solution)/shard_map/ppermute | solution.py:175
  14.5 0.1 collective-permute-done.3.swapped
  14.6 0.1 maximum_convert_fusion.meta_ref
  14.7 0.0 copy-done
  14.7 0.7 %exchange.1 = f32[64,256]{1,0:T(8,128)S(1)} custom-call(s32[12]{0:T(128)S(1)} %maximum_convert_fusion.meta_ref, bf16[64,256]{1,0:T(8,128)(2,1)S(1)} %copy-done, bf16[256,192]{1,0:T(8,128)(2,1)S(1)} %get-tuple-element.14.left_ref, bf16[72,128]{1,0:T(8,128)(2,1)S(1)} %collective-permute-done.refs_1_.tail, bf16[192,128]{1,0:T(8,128)(2,1)S(1)} %collective-permute-done.3.swapped, ...), custom_call_target="tpu_custom_call" | custom-call | tf_op jit(solution)/shard_map/exchange/pallas_call | solution.py:243
  15.4 0.2 collective-permute-start.5
  15.6 1.1 %collective-permute-done.5 = f32[64,256]{1,0:T(8,128)S(1)} collective-permute-done((f32[64,256]{1,0:T(8,128)S(1)}, f32[64,256]{1,0:T(8,128)S(1)}, u32[]{:S(2)}, u32[]{:S(2)}) %collective-permute-start.5) | collective-permute-done | bytes 65568 | tf_op jit(solution)/shard_map/ppermute | solution.py:264
  16.8 2.7 %collective-permute-start.8 = (bf16[64,256]{1,0:T(8,128)(2,1)S(1)}, bf16[64,256]{1,0:T(8,128)(2,1)S(1)}, u32[]{:S(2)}, u32[]{:S(2)}) collective-permute-start(bf16[64,256]{1,0:T(8,128)(2,1)S(1)} %add_convert_fusion), channel_id=1, source_target_pairs={{0,24},{4,28},{8,16},{12,20},{16,8},{20,12},{24,0},{28,4},{1,25},{... | collective-permute-start | bytes 98312 | tf_op jit(solution)/shard_map/ppermute | solution.py:264
  19.5 0.5 %collective-permute-start.7 = (bf16[64,256]{1,0:T(8,128)(2,1)S(1)}, bf16[64,256]{1,0:T(8,128)(2,1)S(1)}, u32[]{:S(2)}, u32[]{:S(2)}) collective-permute-start(bf16[64,256]{1,0:T(8,128)(2,1)S(1)} %add_convert_fusion), channel_id=1, source_target_pairs={{0,8},{4,12},{8,0},{12,4},{16,24},{20,28},{24,16},{28,20},{1,9},{5... | collective-permute-start | bytes 98312 | tf_op jit(solution)/shard_map/ppermute | solution.py:264
  20.0 0.3 %collective-permute-start.6 = (bf16[64,256]{1,0:T(8,128)(2,1)S(1)}, bf16[64,256]{1,0:T(8,128)(2,1)S(1)}, u32[]{:S(2)}, u32[]{:S(2)}) collective-permute-start(bf16[64,256]{1,0:T(8,128)(2,1)S(1)} %add_convert_fusion), channel_id=1, source_target_pairs={{0,16},{4,20},{8,24},{12,28},{16,0},{20,4},{24,8},{28,12},{1,17},{... | collective-permute-start | bytes 98312 | tf_op jit(solution)/shard_map/ppermute | solution.py:264
  20.3 1.3 %collective-permute-done.8 = bf16[64,256]{1,0:T(8,128)(2,1)S(1)} collective-permute-done((bf16[64,256]{1,0:T(8,128)(2,1)S(1)}, bf16[64,256]{1,0:T(8,128)(2,1)S(1)}, u32[]{:S(2)}, u32[]{:S(2)}) %collective-permute-start.8) | collective-permute-done | bytes 32800 | tf_op jit(solution)/shard_map/ppermute | solution.py:264
  21.6 1.8 %collective-permute-done.7 = bf16[64,256]{1,0:T(8,128)(2,1)S(1)} collective-permute-done((bf16[64,256]{1,0:T(8,128)(2,1)S(1)}, bf16[64,256]{1,0:T(8,128)(2,1)S(1)}, u32[]{:S(2)}, u32[]{:S(2)}) %collective-permute-start.7) | collective-permute-done | bytes 32800 | tf_op jit(solution)/shard_map/ppermute | solution.py:264
  23.4 0.5 %collective-permute-done.6 = bf16[64,256]{1,0:T(8,128)(2,1)S(1)} collective-permute-done((bf16[64,256]{1,0:T(8,128)(2,1)S(1)}, bf16[64,256]{1,0:T(8,128)(2,1)S(1)}, u32[]{:S(2)}, u32[]{:S(2)}) %collective-permute-start.6) | collective-permute-done | bytes 32800 | tf_op jit(solution)/shard_map/ppermute | solution.py:264
  23.9 0.6 %add_add_fusion = f32[64,256]{1,0:T(8,128)} fusion(bf16[64,256]{1,0:T(8,128)(2,1)S(1)} %collective-permute-done.8, bf16[64,256]{1,0:T(8,128)(2,1)S(1)} %collective-permute-done.7, bf16[64,256]{1,0:T(8,128)(2,1)S(1)} %collective-permute-done.6, bf16[64,256]{1,0:T(8,128)(2,1)S(1)} %add_convert_fusion), kind=kLoop, calls=%fused_computation | loop fusion | flops 114688 | bytes 196608 | tf_op jit(solution)/shard_map/add | solution.py:267
  (8 shorter events, 0.0 us)
Async XLA Ops:
  0.0 12.7 %collective-permute-start.1 = (bf16[1,1,3,4,4096]{4,3,2,1,0:T(4,128)(2,1)}, bf16[1,1,3,4,4096]{4,3,2,1,0:T(4,128)(2,1)S(1)}, u32[]{:S(2)}, u32[]{:S(2)}) collective-permute-start(bf16[1,1,3,4,4096]{4,3,2,1,0:T(4,128)(2,1)} %raw_hbm.1), channel_id=1, source_target_pairs={{0,2},{1,3},{2,0},{3,1},{4,6},{5,7},{6,4},{7,5},{8,10},{9,11},{10,... | collective-permute-start | bytes 294920 | tf_op jit(solution)/shard_map/ppermute | solution.py:211
  5.8 7.5 %collective-permute-start.2 = (bf16[520,128]{1,0:T(8,128)(2,1)S(1)}, bf16[520,128]{1,0:T(8,128)(2,1)S(1)}, u32[]{:S(2)}, u32[]{:S(2)}) collective-permute-start(bf16[520,128]{1,0:T(8,128)(2,1)S(1)} %pack.1.full_ref.refs_0_), channel_id=1, source_target_pairs={{0,1},{1,0},{2,3},{3,2},{4,7},{5,6},{6,5},{7,4},{8,9},{9,8},{10,11... | collective-permute-start | bytes 399368 | tf_op jit(solution)/shard_map/ppermute | solution.py:175
  7.5 5.2 %collective-permute-start = (bf16[72,128]{1,0:T(8,128)(2,1)S(1)}, bf16[72,128]{1,0:T(8,128)(2,1)S(1)}, u32[]{:S(2)}, u32[]{:S(2)}) collective-permute-start(bf16[72,128]{1,0:T(8,128)(2,1)S(1)} %tail.1.tail_ref), channel_id=1, source_target_pairs={{0,2},{1,3},{2,0},{3,1},{4,6},{5,7},{6,4},{7,5},{8,10},{9,11},{10,... | collective-permute-start | bytes 55304 | tf_op jit(solution)/shard_map/ppermute | solution.py:212
  7.8 6.7 %collective-permute-start.4 = (bf16[392,128]{1,0:T(8,128)(2,1)S(1)}, bf16[392,128]{1,0:T(8,128)(2,1)S(1)}, u32[]{:S(2)}, u32[]{:S(2)}) collective-permute-start(bf16[392,128]{1,0:T(8,128)(2,1)S(1)} %lean.1), channel_id=1, source_target_pairs={{0,3},{1,2},{2,1},{3,0},{4,5},{5,4},{6,7},{7,6},{8,11},{9,10},{10,... | collective-permute-start | bytes 301064 | tf_op jit(solution)/shard_map/ppermute | solution.py:175
  13.4 1.3 %copy-start = (bf16[64,256]{1,0:T(8,128)(2,1)S(1)}, bf16[64,256]{1,0:T(8,128)(2,1)}, u32[]{:S(2)}) copy-start(bf16[64,256]{1,0:T(8,128)(2,1)} %density_ref.1) | copy-start | bytes 98308
  13.4 1.2 %collective-permute-start.3 = (bf16[192,128]{1,0:T(8,128)(2,1)S(1)}, bf16[192,128]{1,0:T(8,128)(2,1)S(1)}, u32[]{:S(2)}, u32[]{:S(2)}) collective-permute-start(bf16[192,128]{1,0:T(8,128)(2,1)S(1)} %merge.1), channel_id=1, source_target_pairs={{0,4},{4,0},{8,12},{12,8},{16,20},{20,16},{24,28},{28,24},{1,5},{5... | collective-permute-start | bytes 147464 | tf_op jit(solution)/shard_map/ppermute | solution.py:225
  15.4 1.3 %collective-permute-start.5 = (f32[64,256]{1,0:T(8,128)S(1)}, f32[64,256]{1,0:T(8,128)S(1)}, u32[]{:S(2)}, u32[]{:S(2)}) collective-permute-start(f32[64,256]{1,0:T(8,128)S(1)} %exchange.1), channel_id=1, source_target_pairs={{0,4},{4,0},{8,12},{12,8},{16,20},{20,16},{24,28},{28,24},{1,5},{5... | collective-permute-start | bytes 196616 | tf_op jit(solution)/shard_map/ppermute | solution.py:264
  16.8 4.9 %collective-permute-start.8 = (bf16[64,256]{1,0:T(8,128)(2,1)S(1)}, bf16[64,256]{1,0:T(8,128)(2,1)S(1)}, u32[]{:S(2)}, u32[]{:S(2)}) collective-permute-start(bf16[64,256]{1,0:T(8,128)(2,1)S(1)} %add_convert_fusion), channel_id=1, source_target_pairs={{0,24},{4,28},{8,16},{12,20},{16,8},{20,12},{24,0},{28,4},{1,25},{... | collective-permute-start | bytes 98312 | tf_op jit(solution)/shard_map/ppermute | solution.py:264
  19.5 3.9 %collective-permute-start.7 = (bf16[64,256]{1,0:T(8,128)(2,1)S(1)}, bf16[64,256]{1,0:T(8,128)(2,1)S(1)}, u32[]{:S(2)}, u32[]{:S(2)}) collective-permute-start(bf16[64,256]{1,0:T(8,128)(2,1)S(1)} %add_convert_fusion), channel_id=1, source_target_pairs={{0,8},{4,12},{8,0},{12,4},{16,24},{20,28},{24,16},{28,20},{1,9},{5... | collective-permute-start | bytes 98312 | tf_op jit(solution)/shard_map/ppermute | solution.py:264
  20.0 3.9 %collective-permute-start.6 = (bf16[64,256]{1,0:T(8,128)(2,1)S(1)}, bf16[64,256]{1,0:T(8,128)(2,1)S(1)}, u32[]{:S(2)}, u32[]{:S(2)}) collective-permute-start(bf16[64,256]{1,0:T(8,128)(2,1)S(1)} %add_convert_fusion), channel_id=1, source_target_pairs={{0,16},{4,20},{8,24},{12,28},{16,0},{20,4},{24,8},{28,12},{1,17},{... | collective-permute-start | bytes 98312 | tf_op jit(solution)/shard_map/ppermute | solution.py:264

commit v36 on v35

--- a/solution.py
+++ b/solution.py
@@ -105,7 +105,11 @@
     packs, (out_ref, rows, half_ref, held) = refs[:orb], refs[orb:]
     fulls = packs[2::2]
     notes = meta_ref[...]
-    meta = [notes[i] for i in range(orb * slots)]
+    bits = orb.bit_length()
+    meta = []
+    for way in range(orb):
+        word = notes[way]
+        meta += [(word >> (bits * j)) & ((1 << bits) - 1) for j in range(slots)]
     me = lax.axis_index("orb")
     parity = core_parity()
     sign = 1 - 2 * parity
@@ -240,6 +244,8 @@
         packs += pair
         notes += pair
     codes = jnp.concatenate([n[-NOTE, :slots] for n in notes]).astype(jnp.int32)
+    places = 1 << (orb.bit_length() * jnp.arange(slots, dtype=jnp.int32))
+    codes = jnp.sum(codes.reshape(orb, slots) * places, axis=1, dtype=jnp.int32)
     parts = pl.pallas_call(
         functools.partial(exchange_kernel, orb, slots, aux_width),
         out_shape=jax.ShapeDtypeStruct((BS, full_width), jnp.float32),

time: 24.7 us -> 24.9 us (level)
  no operation moved by 1% of the time
where the time goes in v36:
time: 24.9 us; the launch traced here: 24.7 us
  starting transfers between devices  12.3 us (49%)
  waiting for transfers between devices  8.65 us (35%)
  Pallas kernels  2.06 us (8%)
  other arithmetic  0.86 us (3%)
  between operations  0.72 us (3%)
    ppermute x4, waiting for transfers between devices, shards(): lax.ppermute(parts, 'aux', [(i, i ^ way * step) for i in range(aux)])  4.71 us
    ppermute x2, starting transfers between devices, shift(): return lax.ppermute(x, ('aux', 'orb'), perm)  4.18 us
    ppermute x1, starting transfers between devices, shards(): raw = lax.ppermute(tensor_blocks, 'orb', across)  4.04 us
    ppermute x4, starting transfers between devices, shards(): lax.ppermute(parts, 'aux', [(i, i ^ way * step) for i in range(aux)])  3.78 us
    ppermute x1, waiting for transfers between devices, shards(): tail_in = lax.ppermute(tail, 'orb', across)  2.3 us
    ppermute x2, waiting for transfers between devices, shift(): return lax.ppermute(x, ('aux', 'orb'), perm)  1.55 us
    pallas_call x1, Pallas kernels, shards(): pl.pallas_call(functools.partial(pack_kernel, orb), out_shape=array(size...  1.14 us
    pallas_call x1, Pallas kernels, shards(): pl.pallas_call(functools.partial(exchange_kernel, orb, slots, aux_width),...  0.67 us
  transfers between devices with their start and end apart: 9, of which 8 were waited for; matrix products, arithmetic and copies ran while one was open for 0% of the time, Pallas kernels for 6%

profile of v36, /device:TPU:0, one launch (start us, length us, event | category | flops | bytes accessed | tf_op | source)
XLA Modules:
  0.0 24.7 jit_solution(1923228034720089100)
XLA Ops:
  0.0 4.0 %collective-permute-start.1 = (bf16[1,1,3,4,4096]{4,3,2,1,0:T(4,128)(2,1)}, bf16[1,1,3,4,4096]{4,3,2,1,0:T(4,128)(2,1)S(1)}, u32[]{:S(2)}, u32[]{:S(2)}) collective-permute-start(bf16[1,1,3,4,4096]{4,3,2,1,0:T(4,128)(2,1)} %raw_hbm.1), channel_id=1, source_target_pairs={{0,2},{1,3},{2,0},{3,1},{4,6},{5,7},{6,4},{7,5},{8,10},{9,11},{10,... | collective-permute-start | bytes 294920 | tf_op jit(solution)/shard_map/ppermute | solution.py:215
  4.7 1.1 %pack.1.full_ref.refs_0_ = bf16[520,128]{1,0:T(8,128)(2,1)S(1)} custom-call(s32[1,1]{1,0:T(1,128)S(6)} %copy.5.kept, s32[1,1,3]{2,1,0:T(1,128)} %pairs_hbm.1, bf16[64,256]{1,0:T(8,128)(2,1)} %density_ref.1, bf16[1,1,3,4,4096]{4,3,2,1,0:T(4,128)(2,1)} %raw_hbm.1), custom_call_target="tpu_custom_call" | custom-call | tf_op jit(solution)/shard_map/pack/pallas_call | solution.py:181
  5.8 1.6 %collective-permute-start.2 = (bf16[520,128]{1,0:T(8,128)(2,1)S(1)}, bf16[520,128]{1,0:T(8,128)(2,1)S(1)}, u32[]{:S(2)}, u32[]{:S(2)}) collective-permute-start(bf16[520,128]{1,0:T(8,128)(2,1)S(1)} %pack.1.full_ref.refs_0_), channel_id=1, source_target_pairs={{0,1},{1,0},{2,3},{3,2},{4,7},{5,6},{6,5},{7,4},{8,9},{9,8},{10,11... | collective-permute-start | bytes 399368 | tf_op jit(solution)/shard_map/ppermute | solution.py:179
  7.5 0.3 %collective-permute-start = (bf16[72,128]{1,0:T(8,128)(2,1)S(1)}, bf16[72,128]{1,0:T(8,128)(2,1)S(1)}, u32[]{:S(2)}, u32[]{:S(2)}) collective-permute-start(bf16[72,128]{1,0:T(8,128)(2,1)S(1)} %tail.1.tail_ref), channel_id=1, source_target_pairs={{0,2},{1,3},{2,0},{3,1},{4,6},{5,7},{6,4},{7,5},{8,10},{9,11},{10,... | collective-permute-start | bytes 55304 | tf_op jit(solution)/shard_map/ppermute | solution.py:216
  7.8 2.5 %collective-permute-start.4 = (bf16[392,128]{1,0:T(8,128)(2,1)S(1)}, bf16[392,128]{1,0:T(8,128)(2,1)S(1)}, u32[]{:S(2)}, u32[]{:S(2)}) collective-permute-start(bf16[392,128]{1,0:T(8,128)(2,1)S(1)} %lean.1), channel_id=1, source_target_pairs={{0,3},{1,2},{2,1},{3,0},{4,5},{5,4},{6,7},{7,6},{8,11},{9,10},{10,... | collective-permute-start | bytes 301064 | tf_op jit(solution)/shard_map/ppermute | solution.py:179
  10.4 2.3 %collective-permute-done.refs_1_.tail = bf16[72,128]{1,0:T(8,128)(2,1)S(1)} collective-permute-done((bf16[72,128]{1,0:T(8,128)(2,1)S(1)}, bf16[72,128]{1,0:T(8,128)(2,1)S(1)}, u32[]{:S(2)}, u32[]{:S(2)}) %collective-permute-start) | collective-permute-done | bytes 18464 | tf_op jit(solution)/shard_map/ppermute | solution.py:216
  12.7 0.0 collective-permute-done.1.raw
  12.7 0.2 relay.1
  12.9 0.4 %collective-permute-done.2.refs_0_.refs_2_ = bf16[520,128]{1,0:T(8,128)(2,1)S(1)} collective-permute-done((bf16[520,128]{1,0:T(8,128)(2,1)S(1)}, bf16[520,128]{1,0:T(8,128)(2,1)S(1)}, u32[]{:S(2)}, u32[]{:S(2)}) %collective-permute-start.2) | collective-permute-done | bytes 133152 | tf_op jit(solution)/shard_map/ppermute | solution.py:179
  13.4 0.0 copy-start
  13.4 0.0 collective-permute-start.3
  13.4 1.1 %collective-permute-done.4.refs_3_ = bf16[392,128]{1,0:T(8,128)(2,1)S(1)} collective-permute-done((bf16[392,128]{1,0:T(8,128)(2,1)S(1)}, bf16[392,128]{1,0:T(8,128)(2,1)S(1)}, u32[]{:S(2)}, u32[]{:S(2)}) %collective-permute-start.4) | collective-permute-done | bytes 100384 | tf_op jit(solution)/shard_map/ppermute | solution.py:179
  14.5 0.1 collective-permute-done.3.swapped
  14.6 0.1 maximum_convert_fusion
  14.7 0.1 reshape.9
  14.8 0.1 multiply_reduce_fusion.meta_ref
  14.9 0.0 copy-done
  14.9 0.7 %exchange.1 = f32[64,256]{1,0:T(8,128)S(1)} custom-call(s32[4]{0:T(128)S(1)} %multiply_reduce_fusion.meta_ref, bf16[64,256]{1,0:T(8,128)(2,1)S(1)} %copy-done, bf16[256,192]{1,0:T(8,128)(2,1)S(1)} %get-tuple-element.14.left_ref, bf16[72,128]{1,0:T(8,128)(2,1)S(1)} %collective-permute-done.refs_1_.tail, bf16[192,128]{1,0:T(8,128)(2,1)S(1)} %collective-permute-done.3.swapped, ...), custom_call_target="tpu_custom_call" | custom-call | tf_op jit(solution)/shard_map/exchange/pallas_call | solution.py:249
  15.6 0.2 collective-permute-start.5
  15.8 1.1 %collective-permute-done.5 = f32[64,256]{1,0:T(8,128)S(1)} collective-permute-done((f32[64,256]{1,0:T(8,128)S(1)}, f32[64,256]{1,0:T(8,128)S(1)}, u32[]{:S(2)}, u32[]{:S(2)}) %collective-permute-start.5) | collective-permute-done | bytes 65568 | tf_op jit(solution)/shard_map/ppermute | solution.py:270
  16.9 2.7 %collective-permute-start.8 = (bf16[64,256]{1,0:T(8,128)(2,1)S(1)}, bf16[64,256]{1,0:T(8,128)(2,1)S(1)}, u32[]{:S(2)}, u32[]{:S(2)}) collective-permute-start(bf16[64,256]{1,0:T(8,128)(2,1)S(1)} %add_convert_fusion), channel_id=1, source_target_pairs={{0,24},{4,28},{8,16},{12,20},{16,8},{20,12},{24,0},{28,4},{1,25},{... | collective-permute-start | bytes 98312 | tf_op jit(solution)/shard_map/ppermute | solution.py:270
  19.6 0.5 %collective-permute-start.7 = (bf16[64,256]{1,0:T(8,128)(2,1)S(1)}, bf16[64,256]{1,0:T(8,128)(2,1)S(1)}, u32[]{:S(2)}, u32[]{:S(2)}) collective-permute-start(bf16[64,256]{1,0:T(8,128)(2,1)S(1)} %add_convert_fusion), channel_id=1, source_target_pairs={{0,8},{4,12},{8,0},{12,4},{16,24},{20,28},{24,16},{28,20},{1,9},{5... | collective-permute-start | bytes 98312 | tf_op jit(solution)/shard_map/ppermute | solution.py:270
  20.2 0.3 %collective-permute-start.6 = (bf16[64,256]{1,0:T(8,128)(2,1)S(1)}, bf16[64,256]{1,0:T(8,128)(2,1)S(1)}, u32[]{:S(2)}, u32[]{:S(2)}) collective-permute-start(bf16[64,256]{1,0:T(8,128)(2,1)S(1)} %add_convert_fusion), channel_id=1, source_target_pairs={{0,16},{4,20},{8,24},{12,28},{16,0},{20,4},{24,8},{28,12},{1,17},{... | collective-permute-start | bytes 98312 | tf_op jit(solution)/shard_map/ppermute | solution.py:270
  20.5 1.3 %collective-permute-done.8 = bf16[64,256]{1,0:T(8,128)(2,1)S(1)} collective-permute-done((bf16[64,256]{1,0:T(8,128)(2,1)S(1)}, bf16[64,256]{1,0:T(8,128)(2,1)S(1)}, u32[]{:S(2)}, u32[]{:S(2)}) %collective-permute-start.8) | collective-permute-done | bytes 32800 | tf_op jit(solution)/shard_map/ppermute | solution.py:270
  21.8 1.8 %collective-permute-done.7 = bf16[64,256]{1,0:T(8,128)(2,1)S(1)} collective-permute-done((bf16[64,256]{1,0:T(8,128)(2,1)S(1)}, bf16[64,256]{1,0:T(8,128)(2,1)S(1)}, u32[]{:S(2)}, u32[]{:S(2)}) %collective-permute-start.7) | collective-permute-done | bytes 32800 | tf_op jit(solution)/shard_map/ppermute | solution.py:270
  23.5 0.5 %collective-permute-done.6 = bf16[64,256]{1,0:T(8,128)(2,1)S(1)} collective-permute-done((bf16[64,256]{1,0:T(8,128)(2,1)S(1)}, bf16[64,256]{1,0:T(8,128)(2,1)S(1)}, u32[]{:S(2)}, u32[]{:S(2)}) %collective-permute-start.6) | collective-permute-done | bytes 32800 | tf_op jit(solution)/shard_map/ppermute | solution.py:270
  24.1 0.6 %add_add_fusion = f32[64,256]{1,0:T(8,128)} fusion(bf16[64,256]{1,0:T(8,128)(2,1)S(1)} %collective-permute-done.8, bf16[64,256]{1,0:T(8,128)(2,1)S(1)} %collective-permute-done.7, bf16[64,256]{1,0:T(8,128)(2,1)S(1)} %collective-permute-done.6, bf16[64,256]{1,0:T(8,128)(2,1)S(1)} %add_convert_fusion), kind=kLoop, calls=%fused_computation | loop fusion | flops 114688 | bytes 196608 | tf_op jit(solution)/shard_map/add | solution.py:273
  (9 shorter events, 0.0 us)
Async XLA Ops:
  0.0 12.7 %collective-permute-start.1 = (bf16[1,1,3,4,4096]{4,3,2,1,0:T(4,128)(2,1)}, bf16[1,1,3,4,4096]{4,3,2,1,0:T(4,128)(2,1)S(1)}, u32[]{:S(2)}, u32[]{:S(2)}) collective-permute-start(bf16[1,1,3,4,4096]{4,3,2,1,0:T(4,128)(2,1)} %raw_hbm.1), channel_id=1, source_target_pairs={{0,2},{1,3},{2,0},{3,1},{4,6},{5,7},{6,4},{7,5},{8,10},{9,11},{10,... | collective-permute-start | bytes 294920 | tf_op jit(solution)/shard_map/ppermute | solution.py:215
  5.8 7.5 %collective-permute-start.2 = (bf16[520,128]{1,0:T(8,128)(2,1)S(1)}, bf16[520,128]{1,0:T(8,128)(2,1)S(1)}, u32[]{:S(2)}, u32[]{:S(2)}) collective-permute-start(bf16[520,128]{1,0:T(8,128)(2,1)S(1)} %pack.1.full_ref.refs_0_), channel_id=1, source_target_pairs={{0,1},{1,0},{2,3},{3,2},{4,7},{5,6},{6,5},{7,4},{8,9},{9,8},{10,11... | collective-permute-start | bytes 399368 | tf_op jit(solution)/shard_map/ppermute | solution.py:179
  7.5 5.2 %collective-permute-start = (bf16[72,128]{1,0:T(8,128)(2,1)S(1)}, bf16[72,128]{1,0:T(8,128)(2,1)S(1)}, u32[]{:S(2)}, u32[]{:S(2)}) collective-permute-start(bf16[72,128]{1,0:T(8,128)(2,1)S(1)} %tail.1.tail_ref), channel_id=1, source_target_pairs={{0,2},{1,3},{2,0},{3,1},{4,6},{5,7},{6,4},{7,5},{8,10},{9,11},{10,... | collective-permute-start | bytes 55304 | tf_op jit(solution)/shard_map/ppermute | solution.py:216
  7.8 6.7 %collective-permute-start.4 = (bf16[392,128]{1,0:T(8,128)(2,1)S(1)}, bf16[392,128]{1,0:T(8,128)(2,1)S(1)}, u32[]{:S(2)}, u32[]{:S(2)}) collective-permute-start(bf16[392,128]{1,0:T(8,128)(2,1)S(1)} %lean.1), channel_id=1, source_target_pairs={{0,3},{1,2},{2,1},{3,0},{4,5},{5,4},{6,7},{7,6},{8,11},{9,10},{10,... | collective-permute-start | bytes 301064 | tf_op jit(solution)/shard_map/ppermute | solution.py:179
  13.4 1.5 %copy-start = (bf16[64,256]{1,0:T(8,128)(2,1)S(1)}, bf16[64,256]{1,0:T(8,128)(2,1)}, u32[]{:S(2)}) copy-start(bf16[64,256]{1,0:T(8,128)(2,1)} %density_ref.1) | copy-start | bytes 98308
  13.4 1.2 %collective-permute-start.3 = (bf16[192,128]{1,0:T(8,128)(2,1)S(1)}, bf16[192,128]{1,0:T(8,128)(2,1)S(1)}, u32[]{:S(2)}, u32[]{:S(2)}) collective-permute-start(bf16[192,128]{1,0:T(8,128)(2,1)S(1)} %merge.1), channel_id=1, source_target_pairs={{0,4},{4,0},{8,12},{12,8},{16,20},{20,16},{24,28},{28,24},{1,5},{5... | collective-permute-start | bytes 147464 | tf_op jit(solution)/shard_map/ppermute | solution.py:229
  15.6 1.3 %collective-permute-start.5 = (f32[64,256]{1,0:T(8,128)S(1)}, f32[64,256]{1,0:T(8,128)S(1)}, u32[]{:S(2)}, u32[]{:S(2)}) collective-permute-start(f32[64,256]{1,0:T(8,128)S(1)} %exchange.1), channel_id=1, source_target_pairs={{0,4},{4,0},{8,12},{12,8},{16,20},{20,16},{24,28},{28,24},{1,5},{5... | collective-permute-start | bytes 196616 | tf_op jit(solution)/shard_map/ppermute | solution.py:270
  16.9 4.9 %collective-permute-start.8 = (bf16[64,256]{1,0:T(8,128)(2,1)S(1)}, bf16[64,256]{1,0:T(8,128)(2,1)S(1)}, u32[]{:S(2)}, u32[]{:S(2)}) collective-permute-start(bf16[64,256]{1,0:T(8,128)(2,1)S(1)} %add_convert_fusion), channel_id=1, source_target_pairs={{0,24},{4,28},{8,16},{12,20},{16,8},{20,12},{24,0},{28,4},{1,25},{... | collective-permute-start | bytes 98312 | tf_op jit(solution)/shard_map/ppermute | solution.py:270
  19.6 3.9 %collective-permute-start.7 = (bf16[64,256]{1,0:T(8,128)(2,1)S(1)}, bf16[64,256]{1,0:T(8,128)(2,1)S(1)}, u32[]{:S(2)}, u32[]{:S(2)}) collective-permute-start(bf16[64,256]{1,0:T(8,128)(2,1)S(1)} %add_convert_fusion), channel_id=1, source_target_pairs={{0,8},{4,12},{8,0},{12,4},{16,24},{20,28},{24,16},{28,20},{1,9},{5... | collective-permute-start | bytes 98312 | tf_op jit(solution)/shard_map/ppermute | solution.py:270
  20.2 3.9 %collective-permute-start.6 = (bf16[64,256]{1,0:T(8,128)(2,1)S(1)}, bf16[64,256]{1,0:T(8,128)(2,1)S(1)}, u32[]{:S(2)}, u32[]{:S(2)}) collective-permute-start(bf16[64,256]{1,0:T(8,128)(2,1)S(1)} %add_convert_fusion), channel_id=1, source_target_pairs={{0,16},{4,20},{8,24},{12,28},{16,0},{20,4},{24,8},{28,12},{1,17},{... | collective-permute-start | bytes 98312 | tf_op jit(solution)/shard_map/ppermute | solution.py:270
